TPU v7x, 32 devices: a whole 2x2x4 slice. The times are simulated.
32 devices in a mesh: seq: 8 (over z, y), ch: 4 (over x, core).
Axes of the slice: x: 2, y: 2, z: 4, core: 2. Of those that a mesh axis runs over, the one named last changes fastest.
Arguments:
- projected: bfloat16 [2048, 3, 8192], P('seq', None, 'ch'), may hold values from -6 to 6
- short_taps: float32 [3, 7, 8192], P(None, None, 'ch'), may hold values from -2 to 2
- filter_taps: float32 [128, 8192], P('seq', 'ch'), may hold values from -1 to 1
- decay: float32 [8192], P('ch'), may hold values from 0.003 to 0.1
- cotangent: bfloat16 [2048, 8192], P('seq', 'ch'), may hold values from -18 to 18
Outputs:
- gated: bfloat16 [2048, 8192], P('seq', 'ch')
- grad_projected: bfloat16 [2048, 3, 8192], P('seq', None, 'ch')
- grad_short: float32 [3, 7, 8192], P(None, None, 'ch')
- grad_filter: float32 [128, 8192], P('seq', 'ch')
All inputs are finite; a program needn't handle non-finite values.
Results may differ from a plain program's by a relative error of at most 0.005.
Values may be sent and summed in bfloat16 or wider, within the bound.
No kernel may reach another device: no remote copies, remote signals or barrier semaphores. Data moves between devices by JAX's collectives and lax.ppermute only.
A program may use at most 128 MiB of HBM per device.

v0:
```python
import math

import jax
import jax.numpy as jnp
from jax import lax
from jax.sharding import PartitionSpec as P

D = 8192
K = 128
FK = 7


def from_behind(value, axis, by):
    count = lax.axis_size(axis)
    pairs = [(i, i + by) for i in range(count) if 0 <= i + by < count]
    return lax.ppermute(value, axis, pairs)


def shortened(value):

    def short(part):
        return part.astype(jnp.bfloat16) if part.dtype == jnp.float32 else part

    return jax.tree.map(short, value)


def depthwise(signal, weights):
    return lax.conv_general_dilated(
        signal,
        weights,
        (1,),
        "VALID",
        dimension_numbers=("NWC", "WIO", "NWC"),
        feature_group_count=signal.shape[2],
        precision=lax.Precision.HIGHEST,
    )


def featurize(extended, short, count):
    total = jnp.zeros((count,) + extended.shape[1:], jnp.float32)
    for lag in range(FK):
        total = total + short[:, lag, :] * extended[FK - 1 - lag : FK - 1 - lag + count]
    return total


def shards(projected, short_taps, filter_taps, decay, cotangent):
    length = projected.shape[0]
    kernel_taps = lax.all_gather(filter_taps, "seq", axis=0, tiled=True)
    lags = jnp.arange(K, dtype=jnp.float32)
    falloff = jnp.exp(-decay[None, :] * lags[:, None])
    kernel = kernel_taps * falloff
    before = from_behind(projected[length - (FK - 1) :], "seq", 1)
    leading = jnp.concatenate([before, projected], axis=0)
    feat = featurize(leading, short_taps, length)
    mixed = feat[:, 1, :] * feat[:, 2, :]
    prior = from_behind(mixed[length - (K - 1) :].astype(jnp.bfloat16), "seq", 1).astype(
        jnp.float32
    )
    mixed_ext = jnp.concatenate([prior, mixed], axis=0)
    filtered = depthwise(mixed_ext[None], kernel[::-1][:, None, :])[0]
    gate = feat[:, 0, :]
    gated = (gate * filtered).astype(jnp.bfloat16)
    grad_out = cotangent.astype(jnp.float32)
    grad_filtered = grad_out * gate
    grad_gate = grad_out * filtered
    after = from_behind(grad_filtered[: K - 1].astype(jnp.bfloat16), "seq", -1).astype(jnp.float32)
    grad_ext = jnp.concatenate([grad_filtered, after], axis=0)
    grad_mixed = depthwise(grad_ext[None], kernel[:, None, :])[0]
    correlation = depthwise(mixed_ext[None], grad_filtered[:, None, :])[0]
    filter_part = correlation[::-1] * falloff
    grad_feat = jnp.stack(
        [grad_gate, grad_mixed * feat[:, 2, :], grad_mixed * feat[:, 1, :]], axis=1
    )
    later = from_behind(shortened(grad_feat[: FK - 1]), "seq", -1)
    grad_feat_ext = jnp.concatenate([grad_feat, later], axis=0)
    grad_proj = jnp.zeros(grad_feat.shape, jnp.float32)
    for lag in range(FK):
        grad_proj = grad_proj + short_taps[:, lag, :] * grad_feat_ext[lag : lag + length]
    grad_projected = grad_proj.astype(jnp.bfloat16)
    short_part = jnp.stack(
        [
            jnp.sum(grad_feat * leading[FK - 1 - lag : FK - 1 - lag + length], axis=0)
            for lag in range(FK)
        ],
        axis=1,
    )
    filter_raw = lax.psum_scatter(filter_part, "seq", scatter_dimension=0, tiled=True)
    short_raw = lax.psum(short_part, "seq")
    squares = jnp.sum(filter_raw * filter_raw) + jnp.sum(short_raw * short_raw) / lax.axis_size(
        "seq"
    )
    total = lax.psum(squares, ("seq", "ch"))
    limit = math.sqrt(K * D + 3 * FK * D)
    scale = jnp.minimum(1.0, limit / jnp.sqrt(total))
    return (gated, grad_projected, scale * short_raw, scale * filter_raw)


def solution(mesh):
    placed = (P("seq", None, "ch"), P(None, None, "ch"), P("seq", "ch"), P("ch"), P("seq", "ch"))
    return jax.shard_map(
        shards,
        mesh=mesh,
        in_specs=placed,
        out_specs=(P("seq", "ch"), P("seq", None, "ch"), P(None, None, "ch"), P("seq", "ch")),
        check_vma=False,
    )
```

profile of v0, /device:TPU:0, one launch (start us, length us, event | category | flops | bytes accessed | tf_op | source)
XLA Modules:
  0.0 394.5 jit_solution(1783919932120694297)
XLA Ops:
  7.2 0.0 copy-start.6
  7.2 0.0 all-gather.2.cloned.1.call-start
  7.2 0.7 all-gather.2.cloned.1.call-update
  7.9 0.0 all-reduce.2.cloned.1.call-start
  8.0 0.9 slice.99
  8.9 4.9 %collective-permute-start = (bf16[6,3,2048]{2,0,1:T(8,128)(2,1)S(1)}, bf16[6,3,2048]{2,0,1:T(8,128)(2,1)S(1)}, u32[]{:S(2)}, u32[]{:S(2)}) collective-permute-start(bf16[6,3,2048]{2,0,1:T(8,128)(2,1)S(1)} %slice.99), channel_id=1, source_target_pairs={{0,4},{4,8},{8,12},{12,16},{16,20},{20,24},{24,28},{1,5},{5,9},{9,... | collective-permute-start | bytes 221192 | tf_op jit(solution)/shard_map/ppermute | solution.py:16
  13.8 2.3 fusion.37
  16.1 0.0 copy-start.15
  16.1 0.0 copy-start.17
  16.2 0.0 copy-start.23
  16.2 0.0 collective-permute-done
  16.3 0.0 copy-start.12
  16.3 0.0 copy-start.29
  16.3 13.1 %fusion.5 = f32[256,3,2048]{2,0,1:T(8,128)S(1)} fusion(bf16[256,3,2048]{2,0,1:T(8,128)(2,1)} %param.5, bf16[6,3,2048]{2,0,1:T(8,128)(2,1)S(1)} %collective-permute-done, f32[3,2048]{1,0:T(4,128)S(1)} %get-tuple-element.31, f32[3,2048]{1,0:T(4,128)S(1)} %get-tuple-element.32, f32[3,2048]{1,0:T(4,128)S(1)} %get-tuple-element.33, ...), kind=kLoop, calls=%fused_computation.25 | loop fusion | flops 59768832 | bytes 9682944 | tf_op jit(solution)/shard_map/add | solution.py:42
  29.4 2.6 copy-done.2
  32.0 0.0 copy-done.6
  32.0 0.3 convert_multiply_fusion.14
  32.5 0.1 slice.249
  32.5 1.3 collective-permute-start.2
  33.8 19.6 %collective-permute-done.2 = bf16[127,2048]{1,0:T(8,128)(2,1)S(1)} collective-permute-done((bf16[127,2048]{1,0:T(8,128)(2,1)S(1)}, bf16[127,2048]{1,0:T(8,128)(2,1)S(1)}, u32[]{:S(2)}, u32[]{:S(2)}) %collective-permute-start.2) | collective-permute-done | bytes 520224 | tf_op jit(solution)/shard_map/ppermute | solution.py:16
  53.4 0.1 convert_element_type.63
  53.5 0.4 maximum_bitcast_fusion
  53.9 4.1 %all-gather.2.cloned.1.call-done = f32[128,2048]{1,0:T(8,128)} async-done(((f32[16,2048]{1,0:T(8,128)}), f32[128,2048]{1,0:T(8,128)}) %all-gather.2.cloned.1.call-update) | async-done | bytes 1048592 | tf_op jit(solution)/shard_map/all_gather | solution.py:48
  58.0 1.4 fusion.40
  59.4 21.5 %fusion.25 = f32[1,256,2048]{2,0,1:T(1,128)S(1)} fusion(f32[1,383,2048]{2,1,0:T(8,128)S(1)} %maximum_bitcast_fusion, f32[128,1,2048]{2,0,1:T(8,128)S(1)} %fusion.40), kind=kOutput, calls=%fused_computation.55 | convolution fusion | flops 805306368 | bytes 6283264 | tf_op jit(solution)/shard_map/conv_general_dilated | solution.py:28
  80.9 4.9 %bitcast_multiply_fusion.1 = (f32[256,1,2048]{2,0,1:T(8,128)S(1)}, f32[256,1,2048]{2,0,1:T(8,128)}, f32[256,1,2048]{2,0,1:T(8,128)S(1)}) fusion(f32[256,3,2048]{2,0,1:T(8,128)} %copy-done.2, f32[1,256,2048]{2,0,1:T(1,128)S(1)} %fusion.25), kind=kLoop, calls=%fused_computation.62 | loop fusion | flops 1572864 | bytes 12582912 | tf_op jit(solution)/shard_map/mul | solution.py:72
  85.8 1.3 copy-done.4
  87.2 0.9 fusion.36
  88.1 5.1 %collective-permute-start.1 = (bf16[127,2048]{1,0:T(8,128)(2,1)}, bf16[127,2048]{1,0:T(8,128)(2,1)}, u32[]{:S(2)}, u32[]{:S(2)}) collective-permute-start(bf16[127,2048]{1,0:T(8,128)(2,1)} %fusion.36), channel_id=1, source_target_pairs={{0,4},{4,8},{8,12},{12,16},{16,20},{20,24},{24,28},{1,5},{5,9},{9,... | collective-permute-start | bytes 1560584 | tf_op jit(solution)/shard_map/ppermute | solution.py:16
  93.2 0.2 fusion.35
  93.4 5.2 %rev.6 = f32[128,2048]{1,0:T(8,128)} reverse(f32[128,2048]{1,0:T(8,128)S(1)} %fusion.35), dimensions={0} | reverse | bytes 2097152 | tf_op jit(solution)/shard_map/rev | solution.py:60
  98.6 5.2 %collective-permute-done.1 = bf16[127,2048]{1,0:T(8,128)(2,1)} collective-permute-done((bf16[127,2048]{1,0:T(8,128)(2,1)}, bf16[127,2048]{1,0:T(8,128)(2,1)}, u32[]{:S(2)}, u32[]{:S(2)}) %collective-permute-start.1) | collective-permute-done | bytes 520224 | tf_op jit(solution)/shard_map/ppermute | solution.py:16
  103.7 1.1 convert_element_type.60
  104.8 3.6 pad_maximum_fusion.3
  108.5 5.8 %broadcast_in_dim.18 = f32[1,383,2048]{2,0,1:T(1,128)} reshape(f32[383,2048]{1,0:T(8,128)} %pad_maximum_fusion.3) | data formatting | bytes 6275072 | tf_op jit(solution)/shard_map/broadcast_in_dim | solution.py:60
  114.2 20.8 %fusion.29 = f32[1,128,2048]{2,0,1:T(1,128)S(1)} fusion(f32[1,383,2048]{2,0,1:T(1,128)} %broadcast_in_dim.18, f32[256,1,2048]{2,0,1:T(8,128)} %bitcast.59), kind=kOutput, calls=%fused_computation.65 | convolution fusion | flops 805306368 | bytes 6283264 | tf_op jit(solution)/shard_map/conv_general_dilated | solution.py:28
  135.0 0.0 copy-start.7
  135.1 21.4 %fusion.32 = f32[1,256,2048]{2,0,1:T(1,128)S(1)} fusion(f32[1,383,2048]{2,0,1:T(1,128)S(1)} %copy-done.8, f32[128,1,2048]{2,0,1:T(8,128)S(1)} %bitcast.62), kind=kOutput, calls=%fused_computation.72 | convolution fusion | flops 805306368 | bytes 6283264 | tf_op jit(solution)/shard_map/conv_general_dilated | solution.py:28
  156.5 0.0 copy-start.13
  156.5 4.5 %fusion.27 = (f32[256,1,2048]{2,0,1:T(8,128)}, bf16[256,2048]{1,0:T(8,128)(2,1)}) fusion(bf16[256,2048]{1,0:T(8,128)(2,1)S(1)} %copy-done.7, f32[1,256,2048]{2,0,1:T(1,128)S(1)} %fusion.32, f32[256,3,2048]{2,0,1:T(8,128)} %copy-done.2), kind=kLoop, calls=%fused_computation.59 | loop fusion | flops 2097152 | bytes 8388608 | tf_op jit(solution)/shard_map/stack | solution.py:71
  161.0 1.3 copy.48
  162.3 6.8 %rev.7 = f32[128,2048]{1,0:T(8,128)S(1)} reverse(f32[128,2048]{1,0:T(8,128)} %bitcast.61), dimensions={0} | reverse | bytes 2097152 | tf_op jit(solution)/shard_map/rev | solution.py:70
  169.2 16.4 %fusion.11 = (f32[3,2048]{1,0:T(4,128)S(1)}, f32[3,2048]{1,0:T(4,128)S(1)}, f32[3,2048]{1,0:T(4,128)S(1)}, f32[3,2048]{1,0:T(4,128)S(1)}, f32[3,2048]{1,0:T(4,12...) fusion(bf16[256,3,2048]{2,0,1:T(8,128)(2,1)} %param.5, bf16[6,3,2048]{2,0,1:T(8,128)(2,1)S(1)} %copy-done.13, ...), kind=kLoop, calls=%fused_computation.31 | loop fusion | flops 64444416 | bytes 9682944 | tf_op jit(solution)/shard_map/reduce_sum | solution.py:82
  185.8 0.7 copy-done.14
  186.5 0.0 all-reduce.2.cloned.1.call-update
  186.5 0.0 reduce-scatter.2.cloned.1.call-start
  186.5 1.1 fusion.34
  187.7 0.0 reduce-scatter.2.cloned.1.call-update
  187.7 3.0 pad_maximum_fusion.1
  190.7 1.5 collective-permute-start.3
  192.3 5.5 %collective-permute-done.3 = bf16[6,3,2048]{2,0,1:T(8,128)(2,1)S(1)} collective-permute-done((bf16[6,3,2048]{2,0,1:T(8,128)(2,1)S(1)}, bf16[6,3,2048]{2,0,1:T(8,128)(2,1)S(1)}, u32[]{:S(2)}, u32[]{:S(2)}) %collective-permute-start.3) | collective-permute-done | bytes 73760 | tf_op jit(solution)/shard_map/ppermute | solution.py:16
  197.8 0.0 copy-start.24
  197.8 0.0 copy-start.26
  197.8 0.0 copy-start.28
  197.8 3.0 pad_maximum_fusion
  200.9 57.5 %all-reduce.2.cloned.1.call-done = f32[3,7,2048]{2,0,1:T(4,128)} async-done(((f32[3,7,2048]{2,0,1:T(4,128)}), f32[3,7,2048]{2,0,1:T(4,128)}) %all-reduce.2.cloned.1.call-update) | async-done | bytes 172048 | tf_op jit(solution)/shard_map/psum | solution.py:88
  258.4 1.7 multiply_reduce_fusion
  260.7 64.8 %reduce-scatter.2.cloned.1.call-done = f32[16,2048]{1,0:T(8,128)} async-done(((f32[128,2048]{1,0:T(8,128)}), f32[16,2048]{1,0:T(8,128)}) %reduce-scatter.2.cloned.1.call-update) | async-done | bytes 131088 | tf_op jit(solution)/shard_map/reduce_scatter | solution.py:87
  325.4 1.5 multiply_reduce_fusion.1
  327.7 18.1 %fusion.14 = bf16[256,3,2048]{2,0,1:T(8,128)(2,1)} fusion(f32[262,3,2048]{2,0,1:T(8,128)} %pad_maximum_fusion, f32[3,2048]{1,0:T(4,128)S(1)} %copy-done.24, f32[3,2048]{1,0:T(4,128)S(1)} %copy-done.26, f32[3,2048]{1,0:T(4,128)S(1)} %copy-done.16, f32[3,2048]{1,0:T(4,128)S(1)} %copy-done.18, f32[3,2048]{1,0:T(4,128)S(1)} %copy-done.20, ...), kind=kLoop, calls=%fused_computation.35 | loop fusion | flops 25165824 | bytes 47357952 | tf_op jit(solution)/shard_map/convert_element_type | solution.py:79
  345.8 39.9 %psum.15 = f32[]{:T(128)} all-reduce(f32[]{:T(128)S(6)} %add.57), channel_id=1, replica_groups=mesh['seq'=8,'ch'=4] {'seq','ch'}, use_global_device_ids=true, to_apply=%region_11.0 | all-reduce | flops 1 | bytes 8 | tf_op jit(solution)/shard_map/psum | solution.py:92
  386.4 0.0 copy-done.10
  386.5 0.8 copy.17
  387.3 0.7 broadcast_multiply_fusion.1
  (59 shorter events, 0.4 us)
Async XLA Ops:
  7.2 24.9 %copy-start.6 = (bf16[256,2048]{1,0:T(8,128)(2,1)S(1)}, bf16[256,2048]{1,0:T(8,128)(2,1)}, u32[]{:S(2)}) copy-start(bf16[256,2048]{1,0:T(8,128)(2,1)} %param.9) | copy-start | bytes 3145732
  7.2 50.8 %all-gather.2.cloned.1.call-start = ((), (), s32[]{:S(2)}) async-start(), calls=%async_computation.1 | async-start | bytes 1179648 | tf_op jit(solution)/shard_map/all_gather | solution.py:48
  7.9 250.4 %all-reduce.2.cloned.1.call-start = ((), (), s32[]{:S(2)}) async-start(), calls=%async_computation.3 | async-start | bytes 458752 | tf_op jit(solution)/shard_map/psum | solution.py:88
  8.9 7.4 %collective-permute-start = (bf16[6,3,2048]{2,0,1:T(8,128)(2,1)S(1)}, bf16[6,3,2048]{2,0,1:T(8,128)(2,1)S(1)}, u32[]{:S(2)}, u32[]{:S(2)}) collective-permute-start(bf16[6,3,2048]{2,0,1:T(8,128)(2,1)S(1)} %slice.99), channel_id=1, source_target_pairs={{0,4},{4,8},{8,12},{12,16},{16,20},{20,24},{24,28},{1,5},{5,9},{9,... | collective-permute-start | bytes 221192 | tf_op jit(solution)/shard_map/ppermute | solution.py:16
  16.1 16.3 %copy-start.15 = (f32[3,2048]{1,0:T(4,128)}, f32[3,2048]{1,0:T(4,128)S(1)}, u32[]{:S(2)}) copy-start(f32[3,2048]{1,0:T(4,128)S(1)} %get-tuple-element.33) | copy-start | bytes 73732
  16.1 16.3 %copy-start.17 = (f32[3,2048]{1,0:T(4,128)}, f32[3,2048]{1,0:T(4,128)S(1)}, u32[]{:S(2)}) copy-start(f32[3,2048]{1,0:T(4,128)S(1)} %get-tuple-element.34) | copy-start | bytes 73732
  16.1 16.3 %copy-start.19 = (f32[3,2048]{1,0:T(4,128)}, f32[3,2048]{1,0:T(4,128)S(1)}, u32[]{:S(2)}) copy-start(f32[3,2048]{1,0:T(4,128)S(1)} %get-tuple-element.35) | copy-start | bytes 73732
  16.1 16.3 %copy-start.21 = (f32[3,2048]{1,0:T(4,128)}, f32[3,2048]{1,0:T(4,128)S(1)}, u32[]{:S(2)}) copy-start(f32[3,2048]{1,0:T(4,128)S(1)} %get-tuple-element.36) | copy-start | bytes 73732
  16.2 16.2 %copy-start.23 = (f32[3,2048]{1,0:T(4,128)}, f32[3,2048]{1,0:T(4,128)S(1)}, u32[]{:S(2)}) copy-start(f32[3,2048]{1,0:T(4,128)S(1)} %get-tuple-element.31) | copy-start | bytes 73732
  16.2 16.2 %copy-start.25 = (f32[3,2048]{1,0:T(4,128)}, f32[3,2048]{1,0:T(4,128)S(1)}, u32[]{:S(2)}) copy-start(f32[3,2048]{1,0:T(4,128)S(1)} %get-tuple-element.32) | copy-start | bytes 73732
  16.2 16.2 %copy-start.27 = (f32[3,1,2048]{2,0,1:T(4,128)}, f32[3,1,2048]{2,0,1:T(4,128)S(1)}, u32[]{:S(2)}) copy-start(f32[3,1,2048]{2,0,1:T(4,128)S(1)} %copy.49) | copy-start | bytes 73732
  16.3 16.2 %copy-start.12 = (bf16[6,3,2048]{2,0,1:T(8,128)(2,1)}, bf16[6,3,2048]{2,0,1:T(8,128)(2,1)S(1)}, u32[]{:S(2)}) copy-start(bf16[6,3,2048]{2,0,1:T(8,128)(2,1)S(1)} %collective-permute-done) | copy-start | bytes 221188
  16.3 17.6 %copy-start.29 = (f32[2048]{0:T(1024)S(1)}, f32[2048]{0:T(1024)}, u32[]{:S(2)}) copy-start(f32[2048]{0:T(1024)} %param.8) | copy-start | bytes 24580
  29.4 2.6 copy-start.2
  32.4 21.1 %copy-start.3 = (f32[256,2048]{1,0:T(8,128)}, f32[256,2048]{1,0:T(8,128)S(1)}, u32[]{:S(2)}) copy-start(f32[256,2048]{1,0:T(8,128)S(1)} %convert_multiply_fusion.14) | copy-start | bytes 6291460
  32.5 20.9 %collective-permute-start.2 = (bf16[127,2048]{1,0:T(8,128)(2,1)S(1)}, bf16[127,2048]{1,0:T(8,128)(2,1)S(1)}, u32[]{:S(2)}, u32[]{:S(2)}) collective-permute-start(bf16[127,2048]{1,0:T(8,128)(2,1)S(1)} %slice.249), channel_id=1, source_target_pairs={{4,0},{8,4},{12,8},{16,12},{20,16},{24,20},{28,24},{5,1},{9,5},{13... | collective-permute-start | bytes 1560584 | tf_op jit(solution)/shard_map/ppermute | solution.py:16
  80.9 12.3 %copy-start.5 = (f32[128,2048]{1,0:T(8,128)S(1)}, f32[128,2048]{1,0:T(8,128)}, u32[]{:S(2)}) copy-start(f32[128,2048]{1,0:T(8,128)} %all-gather.2.cloned.1.call-done) | copy-start | bytes 3145732
  85.8 1.3 copy-start.4
  88.1 15.7 %collective-permute-start.1 = (bf16[127,2048]{1,0:T(8,128)(2,1)}, bf16[127,2048]{1,0:T(8,128)(2,1)}, u32[]{:S(2)}, u32[]{:S(2)}) collective-permute-start(bf16[127,2048]{1,0:T(8,128)(2,1)} %fusion.36), channel_id=1, source_target_pairs={{0,4},{4,8},{8,12},{12,16},{16,20},{20,24},{24,28},{1,5},{5,9},{9,... | collective-permute-start | bytes 1560584 | tf_op jit(solution)/shard_map/ppermute | solution.py:16
  114.2 20.8 %copy-start.8 = (f32[1,383,2048]{2,0,1:T(1,128)S(1)}, f32[1,383,2048]{2,0,1:T(1,128)}, u32[]{:S(2)}) copy-start(f32[1,383,2048]{2,0,1:T(1,128)} %broadcast_in_dim.18) | copy-start | bytes 9412612
  114.2 20.8 %copy-start.9 = (f32[128,2048]{1,0:T(8,128)S(1)}, f32[128,2048]{1,0:T(8,128)}, u32[]{:S(2)}) copy-start(f32[128,2048]{1,0:T(8,128)} %rev.6) | copy-start | bytes 3145732
  135.0 21.5 %copy-start.7 = (bf16[256,2048]{1,0:T(8,128)(2,1)S(1)}, bf16[256,2048]{1,0:T(8,128)(2,1)}, u32[]{:S(2)}) copy-start(bf16[256,2048]{1,0:T(8,128)(2,1)} %param.9) | copy-start | bytes 3145732
  156.5 12.7 %copy-start.13 = (bf16[6,3,2048]{2,0,1:T(8,128)(2,1)S(1)}, bf16[6,3,2048]{2,0,1:T(8,128)(2,1)}, u32[]{:S(2)}) copy-start(bf16[6,3,2048]{2,0,1:T(8,128)(2,1)} %copy-done.12) | copy-start | bytes 221188
  185.8 0.7 copy-start.14
  186.5 138.9 %reduce-scatter.2.cloned.1.call-start = ((), (), s32[]{:S(2)}) async-start(), calls=%async_computation.2 | async-start | bytes 1179648 | tf_op jit(solution)/shard_map/reduce_scatter | solution.py:87
  187.7 10.0 %copy-start = (f32[256,1,2048]{2,0,1:T(8,128)S(1)}, f32[256,1,2048]{2,0,1:T(8,128)}, u32[]{:S(2)}) copy-start(f32[256,1,2048]{2,0,1:T(8,128)} %get-tuple-element.20) | copy-start | bytes 6291460
  187.7 10.0 %copy-start.1 = (f32[256,1,2048]{2,0,1:T(8,128)S(1)}, f32[256,1,2048]{2,0,1:T(8,128)}, u32[]{:S(2)}) copy-start(f32[256,1,2048]{2,0,1:T(8,128)} %get-tuple-element.22) | copy-start | bytes 6291460
  190.7 7.0 %collective-permute-start.3 = (bf16[6,3,2048]{2,0,1:T(8,128)(2,1)S(1)}, bf16[6,3,2048]{2,0,1:T(8,128)(2,1)S(1)}, u32[]{:S(2)}, u32[]{:S(2)}) collective-permute-start(bf16[6,3,2048]{2,0,1:T(8,128)(2,1)S(1)} %slice.250), channel_id=1, source_target_pairs={{4,0},{8,4},{12,8},{16,12},{20,16},{24,20},{28,24},{5,1},{9,5},{13... | collective-permute-start | bytes 221192 | tf_op jit(solution)/shard_map/ppermute | solution.py:16
  197.8 129.9 %copy-start.16 = (f32[3,2048]{1,0:T(4,128)S(1)}, f32[3,2048]{1,0:T(4,128)}, u32[]{:S(2)}) copy-start(f32[3,2048]{1,0:T(4,128)} %copy-done.15) | copy-start | bytes 73732
  197.8 129.9 %copy-start.18 = (f32[3,2048]{1,0:T(4,128)S(1)}, f32[3,2048]{1,0:T(4,128)}, u32[]{:S(2)}) copy-start(f32[3,2048]{1,0:T(4,128)} %copy-done.17) | copy-start | bytes 73732
  197.8 129.9 %copy-start.20 = (f32[3,2048]{1,0:T(4,128)S(1)}, f32[3,2048]{1,0:T(4,128)}, u32[]{:S(2)}) copy-start(f32[3,2048]{1,0:T(4,128)} %copy-done.19) | copy-start | bytes 73732
  197.8 129.9 %copy-start.22 = (f32[3,2048]{1,0:T(4,128)S(1)}, f32[3,2048]{1,0:T(4,128)}, u32[]{:S(2)}) copy-start(f32[3,2048]{1,0:T(4,128)} %copy-done.21) | copy-start | bytes 73732
  197.8 129.9 %copy-start.24 = (f32[3,2048]{1,0:T(4,128)S(1)}, f32[3,2048]{1,0:T(4,128)}, u32[]{:S(2)}) copy-start(f32[3,2048]{1,0:T(4,128)} %copy-done.23) | copy-start | bytes 73732
  197.8 129.9 %copy-start.26 = (f32[3,2048]{1,0:T(4,128)S(1)}, f32[3,2048]{1,0:T(4,128)}, u32[]{:S(2)}) copy-start(f32[3,2048]{1,0:T(4,128)} %copy-done.25) | copy-start | bytes 73732
  197.8 129.9 %copy-start.28 = (f32[3,1,2048]{2,0,1:T(4,128)S(1)}, f32[3,1,2048]{2,0,1:T(4,128)}, u32[]{:S(2)}) copy-start(f32[3,1,2048]{2,0,1:T(4,128)} %copy-done.27) | copy-start | bytes 73732
  327.7 58.7 %copy-start.10 = (f32[3,7,2048]{2,0,1:T(4,128)S(1)}, f32[3,7,2048]{2,0,1:T(4,128)}, u32[]{:S(2)}) copy-start(f32[3,7,2048]{2,0,1:T(4,128)} %all-reduce.2.cloned.1.call-done) | copy-start | bytes 516100
  327.7 59.6 %copy-start.11 = (f32[16,2048]{1,0:T(8,128)S(1)}, f32[16,2048]{1,0:T(8,128)}, u32[]{:S(2)}) copy-start(f32[16,2048]{1,0:T(8,128)} %reduce-scatter.2.cloned.1.call-done) | copy-start | bytes 393220
Sparse Core Ops, SparseCore 0:
  10.1 47.8 all-gather.1
  186.6 71.6 all-reduce.1
  262.7 62.6 reduce-scatter.1
where the time goes:
time: 395 us; the launch traced here: 394 us
  waiting for transfers between devices  157 us (40%)
  other arithmetic  75.2 us (19%)
  matrix products  63.7 us (16%)
  blocking collectives  39.9 us (10%)
  local copies, waits for them, and re-layouts  29 us (7%)
  between operations  16.4 us (4%)
  starting transfers between devices  12.9 us (3%)
    reduce_scatter x1, waiting for transfers between devices, shards(): lax.psum_scatter(filter_part, 'seq', scatter_dimension=0, tiled=True)  64.8 us
    conv_general_dilated x3, matrix products, depthwise(): lax.conv_general_dilated(signal, weights, (1,), 'VALID', dimension_number...  63.7 us
    psum x1, waiting for transfers between devices, shards(): short_raw = lax.psum(short_part, 'seq')  57.5 us
    psum x1, blocking collectives, shards(): total = lax.psum(squares, ('seq', 'ch'))  39.9 us
    ppermute x4, waiting for transfers between devices, from_behind(): return lax.ppermute(value, axis, pairs)  30.2 us
    convert_element_type x1, other arithmetic, shards(): grad_projected = grad_proj.astype(jnp.bfloat16)  18.1 us
    reduce_sum x1, other arithmetic, shards(): jnp.sum(grad_feat * leading[FK - 1 - lag:FK - 1 - lag + length], axis=0)  16.4 us
    add x1, other arithmetic, featurize(): total + short[:, lag, :] * extended[FK - 1 - lag:FK - 1 - lag + count]  13.1 us
  transfers between devices with their start and end apart: 7, of which 6 were waited for; matrix products, arithmetic and copies ran while one was open for 8% of the time, Pallas kernels for 0%

commit v1 on v0

v1 whole, which is shorter than its diff:
```python
import functools
import math

import jax
import jax.numpy as jnp
import ml_dtypes
import numpy as np
from jax import lax
from jax.experimental import pallas as pl
from jax.experimental.pallas import tpu as pltpu
from jax.sharding import PartitionSpec as P


FK = 7
BF16 = jnp.bfloat16
F32 = jnp.float32
HALO = 160


def from_behind(value, axis, by):
    count = lax.axis_size(axis)
    pairs = [(i, i + by) for i in range(count) if 0 <= i + by < count]
    return lax.ppermute(value, axis, pairs)


def interleaved(span, first=0, low=0):
    return np.array([first + s * span + r for r in range(low, span) for s in range(8)])


def pick(positions, count):
    out = np.zeros((len(positions), count), np.float32)
    for row, at in enumerate(positions):
        if 0 <= at < count:
            out[row, at] = 1.0
    return out.astype(ml_dtypes.bfloat16)


def halves(matrix):
    high = matrix.astype(np.float32).astype(ml_dtypes.bfloat16)
    low = (matrix - high.astype(np.float64)).astype(np.float32).astype(ml_dtypes.bfloat16)
    return np.stack([high, low])


def analysis(positions, size, pad=0):
    freq = np.arange(size // 2)[:, None]
    angle = np.pi * (((2 * freq + 1) * np.asarray(positions)[None, :]) % (2 * size)) / size
    matrix = np.concatenate([np.cos(angle), -np.sin(angle)], axis=0)
    return halves(np.pad(matrix, ((0, 0), (0, pad))))


def synthesis(positions, size):
    freq = np.arange(size // 2)[None, :]
    angle = np.pi * (((2 * freq + 1) * np.asarray(positions)[:, None]) % (2 * size)) / size
    return halves(np.concatenate([np.cos(angle), -np.sin(angle)], axis=1) * (2.0 / size))


def mm(a, b):
    return jnp.dot(a, b, preferred_element_type=F32)


def split(value):
    high = value.astype(BF16)
    return high, (value - high.astype(F32)).astype(BF16)


def product(matrix, value):
    high, low = split(value)
    return mm(matrix[0], high) + (mm(matrix[1], high) + mm(matrix[0], low))


def edges_kernel(proj, cot, short, p_tail, p_head, forward, backward):
    length, width = cot.shape
    tail, head = p_tail.shape[0] // 8 - (FK - 1), p_head.shape[0] // 8 - (FK - 1)

    def conv(x, taps, count):
        x = x.reshape(-1, 8, width)
        total = taps[0:1] * x[FK - 1 : FK - 1 + count]
        for lag in range(1, FK):
            total = total + taps[lag : lag + 1] * x[FK - 1 - lag : FK - 1 - lag + count]
        return total

    mixed = conv(mm(p_tail[...], proj[1]), short[1], tail) * conv(mm(p_tail[...], proj[2]), short[2], tail)
    ends = [proj[i, length - 16 :, :].astype(F32)[8:] for i in range(3)]
    forward[...] = jnp.concatenate(
        [mixed.reshape(tail * 8, width)] + ends + [jnp.zeros((8, width), F32)], axis=0
    ).astype(BF16)
    gate = conv(mm(p_head[...], proj[0]), short[0], head).reshape(head * 8, width)
    grad = gate * mm(p_head[(FK - 1) * 8 :, :], cot[...])
    starts = [ref[:16, :].astype(F32)[:8] for ref in (cot, proj.at[1], proj.at[2])]
    backward[...] = jnp.concatenate([grad] + starts, axis=0).astype(BF16)


def main_kernel(
    proj, cot, prev, later, short, taps, decay,
    e_own, e_prev, e_next, e_taps, s_own, s_lags, p_in, p_out,
    gated, grad_proj, filter_part, short_part,
    px, feat, grad, cots,
):
    length, width = cot.shape
    span = length // 8
    edge = FK - 1
    lanes = [slice(at, at + 128) for at in range(0, width, 128)]
    row8 = lax.broadcasted_iota(jnp.int32, (8, width), 0)

    before = prev[...].astype(F32)
    after = later[...].astype(F32)
    prev8 = [before[128 + 8 * i : 136 + 8 * i] for i in range(3)]
    cot_next = after[136:144]
    next8 = [None, after[144:152], after[152:160]]

    for i in range(3):
        x = mm(p_in[...], proj[i]).reshape(span + edge, 8, width)
        px[i, edge:] = x[edge:]
        for k in range(1, FK):
            px[i, edge - k] = jnp.where(row8 == 0, pltpu.roll(prev8[i], k, 0), x[edge - k])
    cots[...] = mm(p_in[edge * 8 :, :], cot[...]).reshape(span, 8, width)

    step = 8
    for i in range(3):
        for lane in lanes:
            weights = [jnp.broadcast_to(short[i, lag : lag + 1, lane], (8, 128)) for lag in range(FK)]
            for r in range(0, span, step):
                total = weights[0] * px[i, r + edge : r + edge + step, :, lane]
                for lag in range(1, FK):
                    total = total + weights[lag] * px[i, r + edge - lag : r + edge - lag + step, :, lane]
                feat[i, r : r + step, :, lane] = total

    def conv8(last, first, weights, whole):
        total = weights[0:1] * first if whole else jnp.zeros((8, width), F32)
        for lag in range(1, FK):
            rolled = pltpu.roll(first, lag, 0) if whole else 0.0
            total = total + weights[lag : lag + 1] * jnp.where(row8 < lag, pltpu.roll(last, lag, 0), rolled)
        return total

    ends = [proj[i, length - 16 :, :].astype(F32)[8:] for i in range(3)]
    feat_next = [None] + [conv8(ends[i], next8[i], short[i], True) for i in (1, 2)]
    mixed_next = feat_next[1] * feat_next[2]
    grad_next = after[:136]
    fix = cot_next * conv8(ends[0], None, short[0], False)
    rows = [grad_next[8 * r : 8 * r + 8] for r in range(17)]
    for r in range(edge):
        rows[r] = rows[r] + jnp.where(row8 == 0, pltpu.roll(fix, (8 - r) % 8, 0), 0.0)
    grad_next = jnp.concatenate(rows + [jnp.zeros((8, width), F32)], axis=0).astype(BF16)
    mixed_edge = jnp.concatenate([before[:128], mixed_next, jnp.zeros((8, width), F32)], axis=0).astype(BF16)

    lags = lax.broadcasted_iota(jnp.int32, (taps.shape[0], width), 0).astype(F32)
    falloff = jnp.exp(-decay[...] * lags)
    k_spec = product(e_taps, taps[...].astype(F32) * falloff)

    flat = lambda value: value.reshape(length, width)
    m_spec = product(e_own, flat(feat[1] * feat[2])) + (mm(e_prev[0], mixed_edge) + mm(e_prev[1], mixed_edge))
    g_own = product(e_own, flat(cots[...] * feat[0]))
    g_spec = g_own + (mm(e_next[0], grad_next) + mm(e_next[1], grad_next))

    half = k_spec.shape[0] // 2
    parts = lambda value: (value[:half], value[half:])
    (kr, ki), (mr, mi), (gr, gi), (hr, hi) = parts(k_spec), parts(m_spec), parts(g_spec), parts(g_own)
    lag_sums = product(s_lags, jnp.concatenate([hr * mr + hi * mi, hi * mr - hr * mi], axis=0))
    filter_part[...] = (lag_sums * falloff).astype(BF16)
    filtered = product(s_own, jnp.concatenate([mr * kr - mi * ki, mr * ki + mi * kr], axis=0))
    grad_mixed = product(s_own, jnp.concatenate([gr * kr + gi * ki, gi * kr - gr * ki], axis=0))

    own = filtered[:length].reshape(span, 8, width)
    gated[...] = mm(p_out[...], flat(feat[0] * own).astype(BF16)).astype(BF16)
    back = grad_mixed[:length].reshape(span, 8, width)
    grad[0, :span] = cots[...] * own
    grad[1, :span] = back * feat[2]
    grad[2, :span] = back * feat[1]
    back_next = grad_mixed[length:]
    edge_next = [cot_next * filtered[length:], back_next * feat_next[2], back_next * feat_next[1]]
    for i in range(3):
        for k in range(edge):
            grad[i, span + k] = jnp.where(row8 == 7, pltpu.roll(edge_next[i], 7 - k, 0), pltpu.roll(grad[i, k], 7, 0))

    for i in range(3):
        columns = []
        for lane in lanes:
            weights = [jnp.broadcast_to(short[i, lag : lag + 1, lane], (8, 128)) for lag in range(FK)]
            sums = [jnp.zeros((8, 128), F32)] * FK
            chunks = []
            for r in range(0, span, step):
                total = jnp.zeros((step, 8, 128), F32)
                here = px[i, r + edge : r + edge + step, :, lane]
                for lag in range(FK):
                    value = grad[i, r + lag : r + lag + step, :, lane]
                    total = total + weights[lag] * value
                    sums[lag] = sums[lag] + jnp.sum(here * value, axis=0)
                chunks.append(total)
            columns.append(jnp.concatenate(chunks, axis=0))
            for lag in range(FK):
                short_part[i, lag : lag + 1, lane] = jnp.sum(sums[lag], axis=0, keepdims=True)
        short_part[i, FK:, :] = jnp.zeros((1, width), F32)
        result = flat(jnp.concatenate(columns, axis=2)).astype(BF16)
        grad_proj[i] = mm(p_out[...], result).astype(BF16)


def whole(array):
    return pl.BlockSpec(array.shape, lambda c: (0,) * array.ndim)


def columns(rows, width):
    lead = (0,) * len(rows)
    return pl.BlockSpec(tuple(rows) + (width,), lambda c: lead + (c,))


def edges(proj, cot, short, width):
    length, channels = cot.shape
    p_tail = jnp.asarray(pick(interleaved(16, length - 128, 1 - FK), length))
    p_head = jnp.asarray(pick(interleaved(17, 0, 1 - FK), length))
    return pl.pallas_call(
        edges_kernel,
        grid=(channels // width,),
        in_specs=[
            columns((3, length), width), columns((length,), width), columns((3, FK), width),
            whole(p_tail), whole(p_head),
        ],
        out_specs=[columns((HALO,), width)] * 2,
        out_shape=[jax.ShapeDtypeStruct((HALO, channels), BF16)] * 2,
        compiler_params=pltpu.CompilerParams(vmem_limit_bytes=48 << 20),
        name="edges",
    )(proj, cot, short, p_tail, p_head)


def main(proj, cot, prev, later, short, taps, decay, width):
    length, channels = cot.shape
    count = taps.shape[0]
    size = 2 * length
    own = interleaved(length // 8)
    constants = [
        analysis(own, size),
        analysis(np.concatenate([interleaved(16, -128), length + np.arange(8)]), size, 8),
        analysis(interleaved(17, length), size, 8),
        analysis(np.arange(count), size),
        synthesis(np.concatenate([own, length + np.arange(8)]), size),
        synthesis(np.arange(count), size),
        pick(interleaved(length // 8, 0, 1 - FK), length),
        pick(own, length).T,
    ]
    constants = [jnp.asarray(constant) for constant in constants]
    span = length // 8
    return pl.pallas_call(
        main_kernel,
        grid=(channels // width,),
        in_specs=[
            columns((3, length), width), columns((length,), width), columns((HALO,), width),
            columns((HALO,), width), columns((3, FK), width), columns((count,), width), columns((1,), width),
        ] + [whole(constant) for constant in constants],
        out_specs=[
            columns((length,), width), columns((3, length), width), columns((count,), width),
            columns((3, FK + 1), width),
        ],
        out_shape=[
            jax.ShapeDtypeStruct((length, channels), BF16),
            jax.ShapeDtypeStruct((3, length, channels), BF16),
            jax.ShapeDtypeStruct((count, channels), BF16),
            jax.ShapeDtypeStruct((3, FK + 1, channels), F32),
        ],
        scratch_shapes=[
            pltpu.VMEM((3, span + FK - 1, 8, width), F32),
            pltpu.VMEM((3, span, 8, width), F32),
            pltpu.VMEM((3, span + FK - 1, 8, width), F32),
            pltpu.VMEM((span, 8, width), F32),
        ],
        compiler_params=pltpu.CompilerParams(vmem_limit_bytes=56 << 20),
        name="operator",
    )(proj, cot, prev, later, short, taps, decay, *constants)


def everyone(value, axis, count):
    return lax.all_to_all(jnp.broadcast_to(value[None], (count,) + value.shape), axis, 0, 0)


def shards(projected, short_taps, filter_taps, decay, cotangent):
    length, _, channels = projected.shape
    ranks = lax.axis_size("seq")
    rows = filter_taps.shape[0]
    width = min(256, channels)
    proj = jnp.transpose(projected, (1, 0, 2))
    forward, backward = edges(proj, cotangent, short_taps, width)
    prev = from_behind(forward, "seq", 1)
    later = from_behind(backward, "seq", -1)
    taps = everyone(filter_taps.astype(BF16), "seq", ranks).reshape(rows * ranks, channels)
    gated, grad_proj, filter_part, short_part = main(
        proj, cotangent, prev, later, short_taps, taps, decay[None], width
    )
    filter_all = lax.all_to_all(filter_part.reshape(ranks, rows, channels), "seq", 0, 0)
    filter_raw = jnp.sum(filter_all.astype(F32), axis=0)
    share = channels // ranks
    short_all = jnp.transpose(short_part.reshape(3 * (FK + 1), ranks, share), (1, 0, 2))
    short_raw = jnp.sum(lax.all_to_all(short_all, "seq", 0, 0), axis=0)
    squares = jnp.sum(filter_raw * filter_raw) + jnp.sum(short_raw * short_raw)
    total = jnp.sum(everyone(jnp.full((8, 128), squares), ("seq", "ch"), ranks * lax.axis_size("ch"))[:, 0, 0])
    short_sum = jnp.transpose(everyone(short_raw, "seq", ranks), (1, 0, 2)).reshape(3, FK + 1, channels)[:, :FK]
    entries = (rows * ranks + 3 * FK) * channels * lax.axis_size("ch")
    scale = jnp.minimum(1.0, math.sqrt(entries) / jnp.sqrt(total))
    return (gated, jnp.transpose(grad_proj, (1, 0, 2)), scale * short_sum, scale * filter_raw)


def solution(mesh):
    placed = (P("seq", None, "ch"), P(None, None, "ch"), P("seq", "ch"), P("ch"), P("seq", "ch"))
    return jax.shard_map(
        shards,
        mesh=mesh,
        in_specs=placed,
        out_specs=(P("seq", "ch"), P("seq", None, "ch"), P(None, None, "ch"), P("seq", "ch")),
        check_vma=False,
    )
```

time: 395 us -> 140 us (0.35)
  waiting for transfers between devices: 157 us -> 53.4 us
  other arithmetic: 75.2 us -> 4.22 us
  matrix products: 63.7 us -> 0 us
  Pallas kernels: 0 us -> 31.4 us
  blocking collectives: 39.9 us -> 14.2 us
  local copies, waits for them, and re-layouts: 29 us -> 10.4 us
  between operations: 16.4 us -> 2.64 us
  starting transfers between devices: 12.9 us -> 22.7 us
    reduce_scatter x1 -> x0, waiting for transfers between devices: 64.8 us -> none  [shards(): lax.psum_scatter(filter_part, 'seq', scatter_dimension=0, tiled=True)]
    conv_general_dilated x3 -> x0, matrix products: 63.7 us -> none  [depthwise(): lax.conv_general_dilated(signal, weights, (1,), 'VALID', dimension_number...]
    psum x1 -> x0, waiting for transfers between devices: 57.5 us -> none  [shards(): short_raw = lax.psum(short_part, 'seq')]
    psum x1 -> x0, blocking collectives: 39.9 us -> none  [shards(): total = lax.psum(squares, ('seq', 'ch'))]
    pallas_call x0 -> x2, Pallas kernels: none -> 31.4 us  [the longest x1 27.6 us: main(): pl.pallas_call(main_kernel, grid=(channels // width,), in_specs=[columns(...]
    all_to_all x0 -> x4, waiting for transfers between devices: none -> 27.3 us  [the longest x1 13.9 us: shards(): lax.all_to_all(filter_part.reshape(ranks, rows, channels), 'seq', 0, 0)]
    convert_element_type x4 -> x1, other arithmetic: 19.4 us -> 0.91 us  [shards(): filter_taps.astype(BF16)]
    reduce_sum x3 -> x5, other arithmetic: 19.6 us -> 1.95 us  [the longest x2 1.23 us: shards(): squares = jnp.sum(filter_raw * filter_raw) + jnp.sum(short_raw * short_raw)]
  transfers between devices with their start and end apart: 7 -> 6, of which waited for: 6 -> 4; matrix products, arithmetic and copies ran while one was open for 8% -> 1% of each run, Pallas kernels for 0% -> 3%
where the time goes in v1:
time: 140 us; the launch traced here: 139 us
  waiting for transfers between devices  53.4 us (38%)
  Pallas kernels  31.4 us (22%)
  starting transfers between devices  22.7 us (16%)
  blocking collectives  14.2 us (10%)
  local copies, waits for them, and re-layouts  10.4 us (7%)
  other arithmetic  4.22 us (3%)
  between operations  2.64 us (2%)
    pallas_call x1, Pallas kernels, main(): pl.pallas_call(main_kernel, grid=(channels // width,), in_specs=[columns(...  27.6 us
    ppermute x2, waiting for transfers between devices, from_behind(): return lax.ppermute(value, axis, pairs)  26.1 us
    all_to_all x1, blocking collectives, shards(): short_raw = jnp.sum(lax.all_to_all(short_all, 'seq', 0, 0), axis=0)  14.2 us
    all_to_all x3, starting transfers between devices, everyone(): lax.all_to_all(jnp.broadcast_to(value[None], (count,) + value.shape), axi...  14 us
    all_to_all x1, waiting for transfers between devices, shards(): lax.all_to_all(filter_part.reshape(ranks, rows, channels), 'seq', 0, 0)  13.9 us
    all_to_all x3, waiting for transfers between devices, everyone(): lax.all_to_all(jnp.broadcast_to(value[None], (count,) + value.shape), axi...  13.4 us
    unnamed x17, local copies, waits for them, and re-layouts  8.04 us
    ppermute x2, starting transfers between devices, from_behind(): return lax.ppermute(value, axis, pairs)  5.26 us
  transfers between devices with their start and end apart: 6, of which 4 were waited for; matrix products, arithmetic and copies ran while one was open for 1% of the time, Pallas kernels for 3%

profile of v1, /device:TPU:0, one launch (start us, length us, event | category | flops | bytes accessed | tf_op | source)
XLA Modules:
  0.0 139.0 jit_solution(7471361173296978426)
XLA Ops:
  0.6 0.9 convert_element_type.6
  1.5 0.8 broadcast_in_dim.6
  2.4 7.3 %all-to-all-start = ((bf16[8,16,2048]{2,1,0:T(8,128)(2,1)}), bf16[8,16,2048]{2,1,0:T(8,128)(2,1)S(1)}, u32[]{:S(2)}, u32[]{:S(2)}) async-start(bf16[8,16,2048]{2,1,0:T(8,128)(2,1)} %broadcast_in_dim.6), calls=%async_computation | async-start | bytes 1048576 | tf_op jit(solution)/shard_map/all_to_all | solution.py:270
  9.7 0.0 copy-start
  9.7 1.9 %copy-done = bf16[256,3,2048]{2,0,1:T(8,128)(2,1)S(1)} copy-done((bf16[256,3,2048]{2,0,1:T(8,128)(2,1)S(1)}, bf16[256,3,2048]{2,0,1:T(8,128)(2,1)}, u32[]{:S(2)}) %copy-start) | copy-done | bytes 3145752
  11.6 0.0 copy-start.1
  11.6 1.2 copy-done.1
  12.8 0.0 copy-start.2
  12.8 0.9 copy-done.2
  13.7 0.0 copy-start.3
  13.7 0.9 copy-done.3
  14.6 0.0 copy-start.4
  14.6 0.9 copy-done.4
  15.5 3.7 %edges.1 = (bf16[160,2048]{1,0:T(8,128)(2,1)S(1)}, bf16[160,2048]{1,0:T(8,128)(2,1)S(1)}) custom-call(bf16[3,256,2048]{2,1,0:T(8,128)(2,1)S(1)} %bitcast.13, bf16[256,2048]{1,0:T(8,128)(2,1)S(1)} %copy-done.1, f32[3,7,2048]{2,1,0:T(8,128)S(1)} %copy-done.2, bf16[176,256]{1,0:T(8,128)(2,1)S(1)} %copy-done.4, bf16[184,256]{1,0:T(8,128)(2,1)S(1)} %copy-done.3), custom_call_target="tpu_custom_call" | custom-call | tf_op jit(solution)/shard_map/edges/pallas_call | solution.py:210
  19.2 4.0 %collective-permute-start = (bf16[160,2048]{1,0:T(8,128)(2,1)S(1)}, bf16[160,2048]{1,0:T(8,128)(2,1)S(1)}, u32[]{:S(2)}, u32[]{:S(2)}) collective-permute-start(bf16[160,2048]{1,0:T(8,128)(2,1)S(1)} %get-tuple-element.10), channel_id=1, source_target_pairs={{0,4},{4,8},{8,12},{12,16},{16,20},{20,24},{24,28},{1,5},{5,9},{9,... | collective-permute-start | bytes 1966088 | tf_op jit(solution)/shard_map/ppermute | solution.py:23
  23.2 1.3 collective-permute-start.1
  24.5 26.1 %collective-permute-done.prev = bf16[160,2048]{1,0:T(8,128)(2,1)S(1)} collective-permute-done((bf16[160,2048]{1,0:T(8,128)(2,1)S(1)}, bf16[160,2048]{1,0:T(8,128)(2,1)S(1)}, u32[]{:S(2)}, u32[]{:S(2)}) %collective-permute-start) | collective-permute-done | bytes 655392 | tf_op jit(solution)/shard_map/ppermute | solution.py:23
  50.6 0.0 copy-start.6
  50.6 0.0 collective-permute-done.1.later
  50.6 0.0 copy-start.7
  50.6 0.0 all-to-all-done
  50.6 0.0 copy-start.5
  50.7 0.8 copy-done.6
  51.5 0.2 copy-done.7
  51.7 0.2 copy-done.5
  51.9 27.6 %operator.1 = (bf16[256,2048]{1,0:T(8,128)(2,1)}, bf16[3,256,2048]{2,1,0:T(8,128)(2,1)}, bf16[128,2048]{1,0:T(8,128)(2,1)}, f32[3,8,2048]{2,1,0:T(8,128)}) custom-call(bf16[3,256,2048]{2,1,0:T(8,128)(2,1)} %bitcast.12, bf16[256,2048]{1,0:T(8,128)(2,1)} %cot.3, bf16[160,2048]{1,0:T(8,128)(2,1)} %copy-done.6, bf16[160,2048]{1,0:T(8,128)(2,1)} %copy-done.7, ...), custom_call_target="tpu_custom_call" | custom-call | tf_op jit(solution)/shard_map/operator/pallas_call | solution.py:241
  79.5 1.0 copy.28
  80.5 0.1 copy.30
  80.6 14.2 %all_to_all.25 = f32[8,24,256]{2,1,0:T(8,128)S(1)} all-to-all(f32[8,24,256]{2,1,0:T(8,128)S(1)} %bitcast.17), channel_id=1, replica_groups=mesh['seq'=8,'ch'=4] {'seq'}, dimensions={0} | all-to-all | bytes 393216 | tf_op jit(solution)/shard_map/all_to_all | solution.py:290
  94.8 3.5 %all-to-all-start.1 = ((bf16[8,16,2048]{2,1,0:T(8,128)(2,1)}), bf16[8,16,2048]{2,1,0:T(8,128)(2,1)S(1)}, u32[]{:S(2)}, u32[]{:S(2)}) async-start(bf16[8,16,2048]{2,1,0:T(8,128)(2,1)} %bitcast.18), calls=%async_computation.1 | async-start | bytes 1048576 | tf_op jit(solution)/shard_map/all_to_all | solution.py:286
  98.3 13.9 %all-to-all-done.1 = bf16[8,16,2048]{2,1,0:T(8,128)(2,1)S(1)} async-done(((bf16[8,16,2048]{2,1,0:T(8,128)(2,1)}), bf16[8,16,2048]{2,1,0:T(8,128)(2,1)S(1)}, u32[]{:S(2)}, u32[]{:S(2)}) %all-to-all-start.1) | async-done | bytes 524320 | tf_op jit(solution)/shard_map/all_to_all | solution.py:286
  112.2 0.7 broadcast_in_dim.8
  112.9 3.6 %all-to-all-start.4 = ((f32[8,24,256]{2,1,0:T(8,128)}), f32[8,24,256]{2,1,0:T(8,128)S(1)}, u32[]{:S(2)}, u32[]{:S(2)}) async-start(f32[8,24,256]{2,1,0:T(8,128)} %broadcast_in_dim.8), calls=%async_computation.4 | async-start | bytes 393216 | tf_op jit(solution)/shard_map/all_to_all | solution.py:270
  116.5 0.6 multiply_reduce_fusion.1
  117.1 0.1 convert_reduce_fusion
  117.2 0.6 multiply_reduce_fusion
  119.0 5.3 %all-to-all-done.4 = f32[8,24,256]{2,1,0:T(8,128)S(1)} async-done(((f32[8,24,256]{2,1,0:T(8,128)}), f32[8,24,256]{2,1,0:T(8,128)S(1)}, u32[]{:S(2)}, u32[]{:S(2)}) %all-to-all-start.4) | async-done | bytes 196640 | tf_op jit(solution)/shard_map/all_to_all | solution.py:270
  124.3 0.7 broadcast_in_dim_broadcast_in_dim_broadcast_in_dim.3
  125.0 3.1 %all-to-all-start.3 = ((f32[32,8,128]{2,1,0:T(8,128)}), f32[32,8,128]{2,1,0:T(8,128)S(1)}, u32[]{:S(2)}, u32[]{:S(2)}) async-start(f32[32,8,128]{2,1,0:T(8,128)} %broadcast_in_dim_broadcast_in_dim_broadcast_in_dim.3), calls=%async_computation.3 | async-start | bytes 262144 | tf_op jit(solution)/shard_map/all_to_all | solution.py:270
  128.1 0.1 copy.26
  128.2 8.1 %all-to-all-done.3 = f32[32,8,128]{2,1,0:T(8,128)S(1)} async-done(((f32[32,8,128]{2,1,0:T(8,128)}), f32[32,8,128]{2,1,0:T(8,128)S(1)}, u32[]{:S(2)}, u32[]{:S(2)}) %all-to-all-start.3) | async-done | bytes 131104 | tf_op jit(solution)/shard_map/all_to_all | solution.py:270
  136.3 0.6 slice_reduce_fusion
  137.6 0.7 broadcast_multiply_fusion
  138.3 0.7 slice_multiply_fusion
  (2 shorter events, 0.1 us)
Async XLA Ops:
  2.4 48.3 %all-to-all-start = ((bf16[8,16,2048]{2,1,0:T(8,128)(2,1)}), bf16[8,16,2048]{2,1,0:T(8,128)(2,1)S(1)}, u32[]{:S(2)}, u32[]{:S(2)}) async-start(bf16[8,16,2048]{2,1,0:T(8,128)(2,1)} %broadcast_in_dim.6), calls=%async_computation | async-start | bytes 1048576 | tf_op jit(solution)/shard_map/all_to_all | solution.py:270
  9.7 1.9 %copy-start = (bf16[256,3,2048]{2,0,1:T(8,128)(2,1)S(1)}, bf16[256,3,2048]{2,0,1:T(8,128)(2,1)}, u32[]{:S(2)}) copy-start(bf16[256,3,2048]{2,0,1:T(8,128)(2,1)} %param.15) | copy-start | bytes 9437188
  11.6 1.2 copy-start.1
  12.8 0.9 copy-start.2
  13.7 0.9 copy-start.3
  14.6 0.9 copy-start.4
  19.2 31.4 %collective-permute-start = (bf16[160,2048]{1,0:T(8,128)(2,1)S(1)}, bf16[160,2048]{1,0:T(8,128)(2,1)S(1)}, u32[]{:S(2)}, u32[]{:S(2)}) collective-permute-start(bf16[160,2048]{1,0:T(8,128)(2,1)S(1)} %get-tuple-element.10), channel_id=1, source_target_pairs={{0,4},{4,8},{8,12},{12,16},{16,20},{20,24},{24,28},{1,5},{5,9},{9,... | collective-permute-start | bytes 1966088 | tf_op jit(solution)/shard_map/ppermute | solution.py:23
  23.2 27.4 %collective-permute-start.1 = (bf16[160,2048]{1,0:T(8,128)(2,1)S(1)}, bf16[160,2048]{1,0:T(8,128)(2,1)S(1)}, u32[]{:S(2)}, u32[]{:S(2)}) collective-permute-start(bf16[160,2048]{1,0:T(8,128)(2,1)S(1)} %get-tuple-element.11), channel_id=1, source_target_pairs={{4,0},{8,4},{12,8},{16,12},{20,16},{24,20},{28,24},{5,1},{9,5},{13... | collective-permute-start | bytes 1966088 | tf_op jit(solution)/shard_map/ppermute | solution.py:23
  50.6 0.8 copy-start.6
  50.6 1.1 copy-start.7
  50.6 1.2 copy-start.5
  94.8 17.4 %all-to-all-start.1 = ((bf16[8,16,2048]{2,1,0:T(8,128)(2,1)}), bf16[8,16,2048]{2,1,0:T(8,128)(2,1)S(1)}, u32[]{:S(2)}, u32[]{:S(2)}) async-start(bf16[8,16,2048]{2,1,0:T(8,128)(2,1)} %bitcast.18), calls=%async_computation.1 | async-start | bytes 1048576 | tf_op jit(solution)/shard_map/all_to_all | solution.py:286
  112.9 11.4 %all-to-all-start.4 = ((f32[8,24,256]{2,1,0:T(8,128)}), f32[8,24,256]{2,1,0:T(8,128)S(1)}, u32[]{:S(2)}, u32[]{:S(2)}) async-start(f32[8,24,256]{2,1,0:T(8,128)} %broadcast_in_dim.8), calls=%async_computation.4 | async-start | bytes 393216 | tf_op jit(solution)/shard_map/all_to_all | solution.py:270
  125.0 11.3 %all-to-all-start.3 = ((f32[32,8,128]{2,1,0:T(8,128)}), f32[32,8,128]{2,1,0:T(8,128)S(1)}, u32[]{:S(2)}, u32[]{:S(2)}) async-start(f32[32,8,128]{2,1,0:T(8,128)} %broadcast_in_dim_broadcast_in_dim_broadcast_in_dim.3), calls=%async_computation.3 | async-start | bytes 262144 | tf_op jit(solution)/shard_map/all_to_all | solution.py:270

commit v2 on v1

v2 whole, which is shorter than its diff:
```python
import functools
import math

import jax
import jax.numpy as jnp
import ml_dtypes
import numpy as np
from jax import lax
from jax.experimental import pallas as pl
from jax.experimental.pallas import tpu as pltpu
from jax.sharding import PartitionSpec as P


FK = 7
BF16 = jnp.bfloat16
F32 = jnp.float32
CHUNKS = 4


def from_behind(value, axis, by):
    count = lax.axis_size(axis)
    pairs = [(i, i + by) for i in range(count) if 0 <= i + by < count]
    return lax.ppermute(value, axis, pairs)


def interleaved(span, first=0, low=0):
    return np.array([first + s * span + r for r in range(low, span) for s in range(8)])


def pick(positions, count):
    out = np.zeros((len(positions), count), np.float32)
    for row, at in enumerate(positions):
        if 0 <= at < count:
            out[row, at] = 1.0
    return out.astype(ml_dtypes.bfloat16)


def halves(matrix):
    high = matrix.astype(np.float32).astype(ml_dtypes.bfloat16)
    low = (matrix - high.astype(np.float64)).astype(np.float32).astype(ml_dtypes.bfloat16)
    return np.stack([high, low])


def analysis(positions, size, pad=0):
    freq = np.arange(size // 2)[:, None]
    angle = np.pi * (((2 * freq + 1) * np.asarray(positions)[None, :]) % (2 * size)) / size
    matrix = np.concatenate([np.cos(angle), -np.sin(angle)], axis=0)
    return halves(np.pad(matrix, ((0, 0), (0, pad))))


def synthesis(positions, size):
    freq = np.arange(size // 2)[None, :]
    angle = np.pi * (((2 * freq + 1) * np.asarray(positions)[:, None]) % (2 * size)) / size
    return halves(np.concatenate([np.cos(angle), -np.sin(angle)], axis=1) * (2.0 / size))


def mm(a, b):
    return jnp.dot(a, b, preferred_element_type=F32)


def edges_kernel(proj, cot, short, p_tail, p_head, *refs):
    forward, backward = refs[-2:]
    length, width = cot.shape
    tail, head = p_tail.shape[0] // 8 - (FK - 1), p_head.shape[0] // 8 - (FK - 1)

    def conv(x, taps, count):
        x = x.reshape(-1, 8, width)
        total = taps[0:1] * x[FK - 1 : FK - 1 + count]
        for lag in range(1, FK):
            total = total + taps[lag : lag + 1] * x[FK - 1 - lag : FK - 1 - lag + count]
        return total

    mixed = conv(mm(p_tail[...], proj[1]), short[1], tail) * conv(mm(p_tail[...], proj[2]), short[2], tail)
    ends = [proj[i, length - 16 :, :].astype(F32)[8:] for i in range(3)]
    forward[...] = jnp.concatenate([mixed.reshape(tail * 8, width)] + ends, axis=0).astype(BF16)
    gate = conv(mm(p_head[...], proj[0]), short[0], head).reshape(head * 8, width)
    grad = gate * mm(p_head[(FK - 1) * 8 :, :], cot[...])
    starts = [ref[:16, :].astype(F32)[:8] for ref in (cot, proj.at[1], proj.at[2])]
    backward[...] = jnp.concatenate([grad] + starts, axis=0).astype(BF16)
    if len(refs) > 2:
        taps, spread = refs[:2]
        spread[...] = jnp.broadcast_to(taps[...].astype(BF16)[None], spread.shape)


def main_kernel(
    proj, cot, prev, later, short, taps, decay,
    e_own, e_prev, e_next, e_taps, s_own, s_lags, p_in, p_out, *refs,
):
    gated, grad_proj, sums_out, px, feat, grad, cots = refs[-7:]
    length, width = cot.shape
    span = length // 8
    edge = FK - 1
    lanes = [slice(at, at + 128) for at in range(0, width, 128)]
    row8 = lax.broadcasted_iota(jnp.int32, (8, width), 0)

    before = prev[...].astype(F32)
    after = later[...].astype(F32)
    prev8 = [before[128 + 8 * i : 136 + 8 * i] for i in range(3)]
    cot_next = after[136:144]
    next8 = [None, after[144:152], after[152:160]]

    lags = lax.broadcasted_iota(jnp.int32, (taps.shape[0], width), 0).astype(F32)
    falloff = jnp.exp(-decay[...] * lags)
    kernel = taps[...].astype(F32) * falloff
    high = kernel.astype(BF16)
    low = (kernel - high.astype(F32)).astype(BF16)
    k_spec = mm(e_taps[...], jnp.concatenate([high, high, low], axis=0))

    for i in range(3):
        x = mm(p_in[...], proj[i]).reshape(span + edge, 8, width)
        px[i, edge:] = x[edge:]
        for k in range(1, FK):
            px[i, edge - k] = jnp.where(row8 == 0, pltpu.roll(prev8[i], k, 0), x[edge - k])
    cots[...] = mm(p_in[edge * 8 :, :], cot[...]).reshape(span, 8, width)

    step = 8
    for i in range(3):
        for lane in lanes:
            weights = [jnp.broadcast_to(short[i, lag : lag + 1, lane], (8, 128)) for lag in range(FK)]
            for r in range(0, span, step):
                total = weights[0] * px[i, r + edge : r + edge + step, :, lane]
                for lag in range(1, FK):
                    total = total + weights[lag] * px[i, r + edge - lag : r + edge - lag + step, :, lane]
                feat[i, r : r + step, :, lane] = total

    def conv8(last, first, weights, whole):
        total = weights[0:1] * first if whole else jnp.zeros((8, width), F32)
        for lag in range(1, FK):
            rolled = pltpu.roll(first, lag, 0) if whole else 0.0
            total = total + weights[lag : lag + 1] * jnp.where(row8 < lag, pltpu.roll(last, lag, 0), rolled)
        return total

    ends = [proj[i, length - 16 :, :].astype(F32)[8:] for i in range(3)]
    feat_next = [None] + [conv8(ends[i], next8[i], short[i], True) for i in (1, 2)]
    mixed_next = feat_next[1] * feat_next[2]
    grad_next = after[:136]
    fix = cot_next * conv8(ends[0], None, short[0], False)
    rows = [grad_next[8 * r : 8 * r + 8] for r in range(17)]
    for r in range(edge):
        rows[r] = rows[r] + jnp.where(row8 == 0, pltpu.roll(fix, (8 - r) % 8, 0), 0.0)
    grad_next = jnp.concatenate(rows + [jnp.zeros((8, width), F32)], axis=0).astype(BF16)
    mixed_edge = jnp.concatenate([before[:128], mixed_next, jnp.zeros((8, width), F32)], axis=0).astype(BF16)

    flat = lambda value: value.reshape(length, width)
    mixed = flat(feat[1] * feat[2]).astype(BF16)
    grad_own = flat(cots[...] * feat[0]).astype(BF16)
    m_spec = mm(e_own[...], jnp.concatenate([mixed, mixed], axis=0)) + mm(e_prev[...], mixed_edge)
    g_own = mm(e_own[...], jnp.concatenate([grad_own, grad_own], axis=0))
    g_spec = g_own + mm(e_next[...], grad_next)

    half = k_spec.shape[0] // 2
    parts = lambda value: (value[:half], value[half:])
    (kr, ki), (mr, mi), (gr, gi), (hr, hi) = parts(k_spec), parts(m_spec), parts(g_spec), parts(g_own)

    def back_to(matrix, real, imaginary):
        spectrum = jnp.concatenate([real, imaginary], axis=0).astype(BF16)
        return mm(matrix[...], jnp.concatenate([spectrum, spectrum], axis=0))

    filtered = back_to(s_own, mr * kr - mi * ki, mr * ki + mi * kr)
    grad_mixed = back_to(s_own, gr * kr + gi * ki, gi * kr - gr * ki)
    filter_sums = back_to(s_lags, hr * mr + hi * mi, hi * mr - hr * mi) * falloff

    own = filtered[:length].reshape(span, 8, width)
    gated[...] = mm(p_out[...], flat(feat[0] * own).astype(BF16)).astype(BF16)
    back = grad_mixed[:length].reshape(span, 8, width)
    grad[0, :span] = cots[...] * own
    grad[1, :span] = back * feat[2]
    grad[2, :span] = back * feat[1]
    back_next = grad_mixed[length:]
    edge_next = [cot_next * filtered[length:], back_next * feat_next[2], back_next * feat_next[1]]
    for i in range(3):
        for k in range(edge):
            grad[i, span + k] = jnp.where(row8 == 7, pltpu.roll(edge_next[i], 7 - k, 0), pltpu.roll(grad[i, k], 7, 0))

    short_rows = []
    for i in range(3):
        columns, rows = [], [[] for _ in range(FK)]
        for lane in lanes:
            weights = [jnp.broadcast_to(short[i, lag : lag + 1, lane], (8, 128)) for lag in range(FK)]
            sums = [jnp.zeros((8, 128), F32)] * FK
            chunks = []
            for r in range(0, span, step):
                total = jnp.zeros((step, 8, 128), F32)
                here = px[i, r + edge : r + edge + step, :, lane]
                for lag in range(FK):
                    value = grad[i, r + lag : r + lag + step, :, lane]
                    total = total + weights[lag] * value
                    sums[lag] = sums[lag] + jnp.sum(here * value, axis=0)
                chunks.append(total)
            columns.append(jnp.concatenate(chunks, axis=0))
            for lag in range(FK):
                rows[lag].append(jnp.sum(sums[lag], axis=0, keepdims=True))
        short_rows += [jnp.concatenate(row, axis=1) for row in rows] + [jnp.zeros((1, width), F32)]
        result = flat(jnp.concatenate(columns, axis=2)).astype(BF16)
        grad_proj[i] = mm(p_out[...], result).astype(BF16)

    ranks, slots, _ = sums_out.shape
    per, each = filter_sums.shape[0] // ranks, -(-len(short_rows) // ranks)
    short_rows += [jnp.zeros((1, width), F32)] * (ranks * each - len(short_rows))
    empty = [jnp.zeros((slots - per - each, width), F32)]
    blocks = []
    for rank in range(ranks):
        blocks += [filter_sums[rank * per : rank * per + per]] + short_rows[rank * each : rank * each + each] + empty
    sums_out[...] = jnp.concatenate(blocks, axis=0).reshape(ranks, slots, width).astype(BF16)


def resident(array):
    return pl.BlockSpec(memory_space=pltpu.VMEM)


def columns(rows, width, first=0):
    lead = (0,) * len(rows)
    return pl.BlockSpec(tuple(rows) + (width,), lambda c: lead + (first + c,))


def edges(proj, cot, short, width, first, blocks, taps=None, ranks=None):
    length = cot.shape[0]
    constants = [
        jnp.asarray(pick(interleaved(16, length - 128, 1 - FK), length)),
        jnp.asarray(pick(interleaved(17, 0, 1 - FK), length)),
    ]
    in_specs = [
        columns((3, length), width, first), columns((length,), width, first), columns((3, FK), width, first),
    ] + [resident(constant) for constant in constants]
    out_specs = [columns((152,), width), columns((160,), width)]
    out_shape = [jax.ShapeDtypeStruct((rows, blocks * width), BF16) for rows in (152, 160)]
    operands = [proj, cot, short] + constants
    if taps is not None:
        rows, channels = taps.shape
        in_specs.append(columns((rows,), channels // blocks))
        operands.append(taps)
        out_specs.insert(0, columns((ranks, rows), channels // blocks))
        out_shape.insert(0, pltpu.HBM((ranks, rows, channels), BF16))
    return pl.pallas_call(
        edges_kernel,
        grid=(blocks,),
        in_specs=in_specs,
        out_specs=out_specs,
        out_shape=out_shape,
        compiler_params=pltpu.CompilerParams(vmem_limit_bytes=32 << 20),
        cost_estimate=pl.CostEstimate(flops=0, bytes_accessed=blocks * width * 10000, transcendentals=0),
        name="edges",
    )(*operands)


def main(proj, cot, prev, later, short, taps, decay, width, first, blocks, ranks, slots, group, at, held):
    length, channels = cot.shape
    count = taps.shape[0]
    size = 2 * length
    span = length // 8
    own = interleaved(span)
    high, low = analysis(own, size)
    k_high, k_low = analysis(np.arange(count), size)
    constants = [
        np.concatenate([high, low], axis=1),
        analysis(np.concatenate([interleaved(16, -128), length + np.arange(8)]), size, 8)[0],
        analysis(interleaved(17, length), size, 8)[0],
        np.concatenate([k_high, k_low, k_high], axis=1),
        np.concatenate(list(synthesis(np.concatenate([own, length + np.arange(8)]), size)), axis=1),
        np.concatenate(list(synthesis(np.arange(count), size)), axis=1),
        pick(interleaved(span, 0, 1 - FK), length),
        pick(own, length).T,
    ]
    constants = [jnp.asarray(constant) for constant in constants]
    operands = [proj, cot, prev, later, short, taps, decay] + constants
    aliases = {}
    for index, value in enumerate(held):
        if value is not None:
            aliases[len(operands)] = index
            operands.append(value)
    return pl.pallas_call(
        main_kernel,
        grid=(blocks,),
        in_specs=[
            columns((3, length), width, first), columns((length,), width, first), columns((prev.shape[0],), width),
            columns((later.shape[0],), width), columns((3, FK), width, first), columns((count,), width, first),
            columns((1,), width, first),
        ] + [resident(constant) for constant in constants] + [pl.BlockSpec(memory_space=pl.ANY)] * len(aliases),
        out_specs=[
            columns((length,), width, first), columns((3, length), width, first), columns((ranks, slots), width, at),
        ],
        out_shape=[
            jax.ShapeDtypeStruct((length, channels), BF16),
            jax.ShapeDtypeStruct((3, length, channels), BF16),
            pltpu.HBM((ranks, slots, group), BF16),
        ],
        scratch_shapes=[
            pltpu.VMEM((3, span + FK - 1, 8, width), F32),
            pltpu.VMEM((3, span, 8, width), F32),
            pltpu.VMEM((3, span + FK - 1, 8, width), F32),
            pltpu.VMEM((span, 8, width), F32),
        ],
        input_output_aliases=aliases,
        compiler_params=pltpu.CompilerParams(vmem_limit_bytes=40 << 20),
        cost_estimate=pl.CostEstimate(flops=blocks * 4 * 10**9, bytes_accessed=blocks * 2 * 10**6, transcendentals=0),
        name="operator",
    )(*operands)


def everyone(value, axis, count):
    return lax.all_to_all(jnp.broadcast_to(value[None], (count,) + value.shape), axis, 0, 0)


def shards(projected, short_taps, filter_taps, decay, cotangent):
    length, _, channels = projected.shape
    ranks = lax.axis_size("seq")
    rows = filter_taps.shape[0]
    width = min(256, channels // CHUNKS)
    blocks = channels // width // CHUNKS
    chunk = blocks * width
    proj = pltpu.with_memory_space_constraint(jnp.transpose(projected, (1, 0, 2)), pltpu.HBM)
    cotangent = pltpu.with_memory_space_constraint(cotangent, pltpu.HBM)

    each = -(-3 * (FK + 1) // ranks)
    slots = -(-(rows + each) // 8) * 8

    sent, prev, later, spread = [], [], [], None
    for k in range(CHUNKS):
        made = edges(
            proj, cotangent, short_taps, width, k * blocks, blocks, filter_taps if k == 1 else None, ranks
        )
        if k == 1:
            spread = made[0]
        sent.append(made[-2:])
    for k in range(CHUNKS):
        forward, backward = sent[k]
        if k:
            forward, prev[k - 1] = lax.optimization_barrier((forward, prev[k - 1]))
            backward, later[k - 1] = lax.optimization_barrier((backward, later[k - 1]))
        prev.append(from_behind(forward, "seq", 1))
        later.append(from_behind(backward, "seq", -1))
    taps = lax.all_to_all(spread, "seq", 0, 0).reshape(rows * ranks, channels)

    gated = grad_proj = sums = None
    groups = []
    for k in range(CHUNKS):
        last = k == CHUNKS - 1
        gated, grad_proj, sums = main(
            proj, cotangent, prev[k], later[k], short_taps, taps, decay[None], width, k * blocks, blocks, ranks,
            slots, chunk if last else chunk * (CHUNKS - 1), 0 if last else k * blocks,
            [gated, grad_proj, None if last else sums],
        )
        if k >= CHUNKS - 2:
            groups.append(lax.all_to_all(sums, "seq", 0, 0))

    raw = [jnp.sum(group.astype(F32), axis=0) for group in groups]
    total = sum(jnp.sum(part[: rows + each] * part[: rows + each]) for part in raw)
    filter_raw = jnp.concatenate([part[:rows] for part in raw], axis=1)
    short_raw = jnp.concatenate([part[rows : rows + each] for part in raw], axis=1)
    short_raw, total = lax.optimization_barrier((short_raw, total))
    totals = everyone(jnp.full((8, 128), total), ("seq", "ch"), ranks * lax.axis_size("ch"))
    short_all = everyone(short_raw.reshape(8 * each, channels // 8), "seq", ranks)
    short_all = short_all.reshape(ranks * each, channels)[: 3 * (FK + 1)].reshape(3, FK + 1, channels)[:, :FK]
    entries = (rows * ranks + 3 * FK) * channels * lax.axis_size("ch")
    scale = jnp.minimum(1.0, math.sqrt(entries) / jnp.sqrt(jnp.sum(totals[:, 0, 0])))
    return (gated, jnp.transpose(grad_proj, (1, 0, 2)), scale * short_all, scale * filter_raw)


def solution(mesh):
    placed = (P("seq", None, "ch"), P(None, None, "ch"), P("seq", "ch"), P("ch"), P("seq", "ch"))
    return jax.shard_map(
        shards,
        mesh=mesh,
        in_specs=placed,
        out_specs=(P("seq", "ch"), P("seq", None, "ch"), P(None, None, "ch"), P("seq", "ch")),
        check_vma=False,
    )
```

time: 140 us -> 146 us (1.043)
  starting transfers between devices: 22.7 us -> 41.1 us
  waiting for transfers between devices: 53.4 us -> 36.8 us
  Pallas kernels: 31.4 us -> 35 us
  blocking collectives: 14.2 us -> 15.8 us
    ppermute x2 -> x8, starting transfers between devices: 5.26 us -> 23.2 us  [from_behind(): return lax.ppermute(value, axis, pairs)]
    ppermute x2 -> x8, waiting for transfers between devices: 26.1 us -> 11.8 us  [from_behind(): return lax.ppermute(value, axis, pairs)]
    all_to_all x1 -> x2, starting transfers between devices: 3.49 us -> 10.8 us  [the longest x1 7.28 us: shards(): taps = lax.all_to_all(spread, 'seq', 0, 0).reshape(rows * ranks, channels)]
    all_to_all x3 -> x2, starting transfers between devices: 14 us -> 7.07 us  [everyone(): lax.all_to_all(jnp.broadcast_to(value[None], (count,) + value.shape), axi...]
    all_to_all x1 -> x2, waiting for transfers between devices: 13.9 us -> 10.2 us  [the longest x1 10.2 us: shards(): groups.append(lax.all_to_all(sums, 'seq', 0, 0))]
    pallas_call x2 -> x8, Pallas kernels: 31.4 us -> 35 us  [the longest x4 27 us: main(): pl.pallas_call(main_kernel, grid=(blocks,), in_specs=[columns((3, length)...]
    all_to_all x1, blocking collectives: 14.2 us -> 15.8 us  [shards(): groups.append(lax.all_to_all(sums, 'seq', 0, 0))]
    all_to_all x3 -> x2, waiting for transfers between devices: 13.4 us -> 14.7 us  [everyone(): lax.all_to_all(jnp.broadcast_to(value[None], (count,) + value.shape), axi...]
  transfers between devices with their start and end apart: 6 -> 12, of which waited for: 4 -> 7; matrix products, arithmetic and copies ran while one was open for 1% -> 1% of each run, Pallas kernels for 3% -> 18%
where the time goes in v2:
time: 146 us; the launch traced here: 145 us
  starting transfers between devices  41.1 us (28%)
  waiting for transfers between devices  36.8 us (25%)
  Pallas kernels  35 us (24%)
  blocking collectives  15.8 us (11%)
  local copies, waits for them, and re-layouts  9.84 us (7%)
  other arithmetic  3.37 us (2%)
  between operations  2.94 us (2%)
    pallas_call x4, Pallas kernels, main(): pl.pallas_call(main_kernel, grid=(blocks,), in_specs=[columns((3, length)...  27 us
    ppermute x8, starting transfers between devices, from_behind(): return lax.ppermute(value, axis, pairs)  23.2 us
    all_to_all x1, blocking collectives, shards(): groups.append(lax.all_to_all(sums, 'seq', 0, 0))  15.8 us
    all_to_all x2, waiting for transfers between devices, everyone(): lax.all_to_all(jnp.broadcast_to(value[None], (count,) + value.shape), axi...  14.7 us
    ppermute x8, waiting for transfers between devices, from_behind(): return lax.ppermute(value, axis, pairs)  11.8 us
    all_to_all x1, waiting for transfers between devices, shards(): groups.append(lax.all_to_all(sums, 'seq', 0, 0))  10.2 us
    unnamed x38, local copies, waits for them, and re-layouts  8.41 us
    pallas_call x4, Pallas kernels, edges(): pl.pallas_call(edges_kernel, grid=(blocks,), in_specs=in_specs, out_specs...  7.99 us
  transfers between devices with their start and end apart: 12, of which 7 were waited for; matrix products, arithmetic and copies ran while one was open for 1% of the time, Pallas kernels for 18%

profile of v2, /device:TPU:0, one launch (start us, length us, event | category | flops | bytes accessed | tf_op | source)
XLA Modules:
  0.0 144.8 jit_solution(18088485782832813561)
XLA Ops:
  0.6 0.0 copy-start
  0.6 0.9 copy-done
  1.6 0.9 copy-done.2
  2.5 0.9 copy-done.4
  3.3 0.9 copy-done.6
  4.3 2.4 %edges.6 = (bf16[8,16,2048]{2,1,0:T(8,128)(2,1)}, bf16[152,512]{1,0:T(8,128)(2,1)S(1)}, bf16[160,512]{1,0:T(8,128)(2,1)S(1)}) custom-call(bf16[3,256,2048]{2,1,0:T(8,128)(2,1)} %bitcast.12, bf16[256,2048]{1,0:T(8,128)(2,1)} %cot.15, f32[3,7,2048]{2,1,0:T(8,128)S(1)} %copy-done, bf16[176,256]{1,0:T(8,128)(2,1)S(1)} %copy-done.4, ...), custom_call_target="tpu_custom_call" | custom-call | bytes 5120000 | tf_op jit(solution)/shard_map/edges/pallas_call | solution.py:234
  6.7 7.3 %all-to-all-start = ((bf16[8,16,2048]{2,1,0:T(8,128)(2,1)}), bf16[8,16,2048]{2,1,0:T(8,128)(2,1)S(1)}, u32[]{:S(2)}, u32[]{:S(2)}) async-start(bf16[8,16,2048]{2,1,0:T(8,128)(2,1)} %get-tuple-element.53), calls=%async_computation | async-start | bytes 1048576 | tf_op jit(solution)/shard_map/all_to_all | solution.py:332
  14.0 0.0 copy-done.1
  14.0 0.0 copy-done.3
  14.0 0.0 copy-done.5
  14.0 1.8 %edges.7 = (bf16[152,512]{1,0:T(8,128)(2,1)S(1)}, bf16[160,512]{1,0:T(8,128)(2,1)S(1)}) custom-call(bf16[3,256,2048]{2,1,0:T(8,128)(2,1)} %bitcast.13, bf16[256,2048]{1,0:T(8,128)(2,1)} %cot.15, f32[3,7,2048]{2,1,0:T(8,128)S(1)} %copy-done.1, bf16[176,256]{1,0:T(8,128)(2,1)S(1)} %copy-done.5, bf16[184,256]{1,0:T(8,128)(2,1)S(1)} %copy-done.3), custom_call_target="tpu_custom_call" | custom-call | bytes 5120000 | tf_op jit(solution)/shard_map/edges/pallas_call | solution.py:234
  15.9 1.3 collective-permute-start.4
  17.2 4.6 %collective-permute-start = (bf16[152,512]{1,0:T(8,128)(2,1)S(1)}, bf16[152,512]{1,0:T(8,128)(2,1)S(1)}, u32[]{:S(2)}, u32[]{:S(2)}) collective-permute-start(bf16[152,512]{1,0:T(8,128)(2,1)S(1)} %get-tuple-element.42), channel_id=1, source_target_pairs={{0,4},{4,8},{8,12},{12,16},{16,20},{20,24},{24,28},{1,5},{5,9},{9,... | collective-permute-start | bytes 466952 | tf_op jit(solution)/shard_map/ppermute | solution.py:23
  21.7 3.8 %collective-permute-done.4.later = bf16[160,512]{1,0:T(8,128)(2,1)S(1)} collective-permute-done((bf16[160,512]{1,0:T(8,128)(2,1)S(1)}, bf16[160,512]{1,0:T(8,128)(2,1)S(1)}, u32[]{:S(2)}, u32[]{:S(2)}) %collective-permute-start.4) | collective-permute-done | bytes 163872 | tf_op jit(solution)/shard_map/ppermute | solution.py:23
  25.5 1.3 collective-permute-start.5
  26.8 2.0 %collective-permute-done.prev = bf16[152,512]{1,0:T(8,128)(2,1)S(1)} collective-permute-done((bf16[152,512]{1,0:T(8,128)(2,1)S(1)}, bf16[152,512]{1,0:T(8,128)(2,1)S(1)}, u32[]{:S(2)}, u32[]{:S(2)}) %collective-permute-start) | collective-permute-done | bytes 155680 | tf_op jit(solution)/shard_map/ppermute | solution.py:23
  28.8 4.4 %collective-permute-start.1 = (bf16[152,512]{1,0:T(8,128)(2,1)S(1)}, bf16[152,512]{1,0:T(8,128)(2,1)S(1)}, u32[]{:S(2)}, u32[]{:S(2)}) collective-permute-start(bf16[152,512]{1,0:T(8,128)(2,1)S(1)} %get-tuple-element.43), channel_id=1, source_target_pairs={{0,4},{4,8},{8,12},{12,16},{16,20},{20,24},{24,28},{1,5},{5,9},{9,... | collective-permute-start | bytes 466952 | tf_op jit(solution)/shard_map/ppermute | solution.py:23
  33.2 1.9 %edges.5 = (bf16[152,512]{1,0:T(8,128)(2,1)S(1)}, bf16[160,512]{1,0:T(8,128)(2,1)S(1)}) custom-call(bf16[3,256,2048]{2,1,0:T(8,128)(2,1)} %bitcast.14, bf16[256,2048]{1,0:T(8,128)(2,1)} %cot.15, f32[3,7,2048]{2,1,0:T(8,128)S(1)} %copy-done.1, bf16[176,256]{1,0:T(8,128)(2,1)S(1)} %copy-done.5, bf16[184,256]{1,0:T(8,128)(2,1)S(1)} %copy-done.3), custom_call_target="tpu_custom_call" | custom-call | bytes 5120000 | tf_op jit(solution)/shard_map/edges/pallas_call | solution.py:234
  35.1 0.0 copy-start.7
  35.1 0.0 copy-start.8
  35.1 0.0 copy-start.9
  35.1 0.0 copy-start.18
  35.1 0.0 collective-permute-done.5.later
  35.1 1.4 collective-permute-start.6
  36.5 3.2 %collective-permute-done.1.prev = bf16[152,512]{1,0:T(8,128)(2,1)S(1)} collective-permute-done((bf16[152,512]{1,0:T(8,128)(2,1)S(1)}, bf16[152,512]{1,0:T(8,128)(2,1)S(1)}, u32[]{:S(2)}, u32[]{:S(2)}) %collective-permute-start.1) | collective-permute-done | bytes 155680 | tf_op jit(solution)/shard_map/ppermute | solution.py:23
  39.7 4.4 %collective-permute-start.2 = (bf16[152,512]{1,0:T(8,128)(2,1)S(1)}, bf16[152,512]{1,0:T(8,128)(2,1)S(1)}, u32[]{:S(2)}, u32[]{:S(2)}) collective-permute-start(bf16[152,512]{1,0:T(8,128)(2,1)S(1)} %get-tuple-element.44), channel_id=1, source_target_pairs={{0,4},{4,8},{8,12},{12,16},{16,20},{20,24},{24,28},{1,5},{5,9},{9,... | collective-permute-start | bytes 466952 | tf_op jit(solution)/shard_map/ppermute | solution.py:23
  44.1 1.9 %edges.4 = (bf16[152,512]{1,0:T(8,128)(2,1)S(1)}, bf16[160,512]{1,0:T(8,128)(2,1)S(1)}) custom-call(bf16[3,256,2048]{2,1,0:T(8,128)(2,1)} %bitcast.15, bf16[256,2048]{1,0:T(8,128)(2,1)} %cot.15, f32[3,7,2048]{2,1,0:T(8,128)S(1)} %copy-done.1, bf16[176,256]{1,0:T(8,128)(2,1)S(1)} %copy-done.5, bf16[184,256]{1,0:T(8,128)(2,1)S(1)} %copy-done.3), custom_call_target="tpu_custom_call" | custom-call | bytes 5120000 | tf_op jit(solution)/shard_map/edges/pallas_call | solution.py:234
  46.0 2.8 %collective-permute-done.2.prev = bf16[152,512]{1,0:T(8,128)(2,1)S(1)} collective-permute-done((bf16[152,512]{1,0:T(8,128)(2,1)S(1)}, bf16[152,512]{1,0:T(8,128)(2,1)S(1)}, u32[]{:S(2)}, u32[]{:S(2)}) %collective-permute-start.2) | collective-permute-done | bytes 155680 | tf_op jit(solution)/shard_map/ppermute | solution.py:23
  48.8 4.4 %collective-permute-start.3 = (bf16[152,512]{1,0:T(8,128)(2,1)S(1)}, bf16[152,512]{1,0:T(8,128)(2,1)S(1)}, u32[]{:S(2)}, u32[]{:S(2)}) collective-permute-start(bf16[152,512]{1,0:T(8,128)(2,1)S(1)} %get-tuple-element.45), channel_id=1, source_target_pairs={{0,4},{4,8},{8,12},{12,16},{16,20},{20,24},{24,28},{1,5},{5,9},{9,... | collective-permute-start | bytes 466952 | tf_op jit(solution)/shard_map/ppermute | solution.py:23
  53.2 0.0 collective-permute-done.6.later
  53.2 1.5 %collective-permute-start.7 = (bf16[160,512]{1,0:T(8,128)(2,1)S(1)}, bf16[160,512]{1,0:T(8,128)(2,1)S(1)}, u32[]{:S(2)}, u32[]{:S(2)}) collective-permute-start(bf16[160,512]{1,0:T(8,128)(2,1)S(1)} %get-tuple-element.52), channel_id=1, source_target_pairs={{4,0},{8,4},{12,8},{16,12},{20,16},{24,20},{28,24},{5,1},{9,5},{13... | collective-permute-start | bytes 491528 | tf_op jit(solution)/shard_map/ppermute | solution.py:23
  54.7 0.0 all-to-all-done
  54.7 0.0 copy-done.7
  54.7 0.0 copy-done.8
  54.7 0.0 copy-done.9
  54.7 0.0 copy-start.10
  54.7 1.0 copy-done.10
  55.7 0.9 copy-done.11
  56.7 0.9 copy-done.13
  57.6 0.9 copy-done.15
  58.6 0.9 copy-done.17
  59.5 6.8 %operator.4 = (bf16[256,2048]{1,0:T(8,128)(2,1)}, bf16[3,256,2048]{2,1,0:T(8,128)(2,1)}, bf16[8,24,1536]{2,1,0:T(8,128)(2,1)}) custom-call(bf16[3,256,2048]{2,1,0:T(8,128)(2,1)} %bitcast.16, bf16[256,2048]{1,0:T(8,128)(2,1)} %cot.15, bf16[152,512]{1,0:T(8,128)(2,1)S(1)} %collective-permute-done.prev, bf16[160,512]{1,0:T(8,128)(2,1)S(1)} %collective-permute-done.4.later, ...), custom_call_target="tpu_custom_call" | custom-call | flops 8000000000 | bytes 4000000 | tf_op jit(solution)/shard_map/operator/pallas_call | solution.py:271
  66.3 0.0 copy-done.14
  66.3 0.0 copy-done.16
  66.3 6.8 %operator.5 = (bf16[256,2048]{1,0:T(8,128)(2,1)}, bf16[3,256,2048]{2,1,0:T(8,128)(2,1)}, bf16[8,24,1536]{2,1,0:T(8,128)(2,1)}) custom-call(bf16[3,256,2048]{2,1,0:T(8,128)(2,1)} %bitcast.17, bf16[256,2048]{1,0:T(8,128)(2,1)} %cot.15, bf16[152,512]{1,0:T(8,128)(2,1)S(1)} %collective-permute-done.1.prev, ...), custom_call_target="tpu_custom_call", output_to_operand_aliasing={{0}: (15, {}), {1}: (16, {}), {2}: (17, {})} | custom-call | flops 8000000000 | bytes 4000000 | tf_op jit(solution)/shard_map/operator/pallas_call | solution.py:271
  73.1 6.7 %operator.6 = (bf16[256,2048]{1,0:T(8,128)(2,1)}, bf16[3,256,2048]{2,1,0:T(8,128)(2,1)}, bf16[8,24,1536]{2,1,0:T(8,128)(2,1)}) custom-call(bf16[3,256,2048]{2,1,0:T(8,128)(2,1)} %bitcast.18, bf16[256,2048]{1,0:T(8,128)(2,1)} %cot.15, bf16[152,512]{1,0:T(8,128)(2,1)S(1)} %collective-permute-done.2.prev, ...), custom_call_target="tpu_custom_call", output_to_operand_aliasing={{0}: (15, {}), {1}: (16, {}), {2}: (17, {})} | custom-call | flops 8000000000 | bytes 4000000 | tf_op jit(solution)/shard_map/operator/pallas_call | solution.py:271
  79.8 0.0 collective-permute-done.3.prev
  79.8 0.0 collective-permute-done.7.later
  79.8 6.7 %operator.7 = (bf16[256,2048]{1,0:T(8,128)(2,1)}, bf16[3,256,2048]{2,1,0:T(8,128)(2,1)}, bf16[8,24,512]{2,1,0:T(8,128)(2,1)}) custom-call(bf16[3,256,2048]{2,1,0:T(8,128)(2,1)} %bitcast.19, bf16[256,2048]{1,0:T(8,128)(2,1)} %cot.15, bf16[152,512]{1,0:T(8,128)(2,1)S(1)} %collective-permute-done.3.prev, ...), custom_call_target="tpu_custom_call", output_to_operand_aliasing={{0}: (15, {}), {1}: (16, {})} | custom-call | flops 8000000000 | bytes 4000000 | tf_op jit(solution)/shard_map/operator/pallas_call | solution.py:271
  86.5 15.8 %all_to_all.25 = bf16[8,24,512]{2,1,0:T(8,128)(2,1)S(1)} all-to-all(bf16[8,24,512]{2,1,0:T(8,128)(2,1)} %get-tuple-element.71), channel_id=1, replica_groups=mesh['seq'=8,'ch'=4] {'seq'}, dimensions={0} | all-to-all | bytes 393216 | tf_op jit(solution)/shard_map/all_to_all | solution.py:344
  102.3 3.5 %all-to-all-start.1 = ((bf16[8,24,1536]{2,1,0:T(8,128)(2,1)}), bf16[8,24,1536]{2,1,0:T(8,128)(2,1)S(1)}, u32[]{:S(2)}, u32[]{:S(2)}) async-start(bf16[8,24,1536]{2,1,0:T(8,128)(2,1)} %get-tuple-element.70), calls=%async_computation.1 | async-start | bytes 1179648 | tf_op jit(solution)/shard_map/all_to_all | solution.py:344
  105.9 0.6 fusion.1
  106.5 10.2 %all-to-all-done.1 = bf16[8,24,1536]{2,1,0:T(8,128)(2,1)S(1)} async-done(((bf16[8,24,1536]{2,1,0:T(8,128)(2,1)}), bf16[8,24,1536]{2,1,0:T(8,128)(2,1)S(1)}, u32[]{:S(2)}, u32[]{:S(2)}) %all-to-all-start.1) | async-done | bytes 589856 | tf_op jit(solution)/shard_map/all_to_all | solution.py:344
  116.8 0.1 convert_reduce_fusion
  116.9 0.6 fusion
  118.8 0.7 broadcast_in_dim_broadcast_in_dim_broadcast_in_dim.3
  119.5 3.7 %all-to-all-start.3 = ((f32[32,8,128]{2,1,0:T(8,128)}), f32[32,8,128]{2,1,0:T(8,128)S(1)}, u32[]{:S(2)}, u32[]{:S(2)}) async-start(f32[32,8,128]{2,1,0:T(8,128)} %broadcast_in_dim_broadcast_in_dim_broadcast_in_dim.3), calls=%async_computation.3 | async-start | bytes 262144 | tf_op jit(solution)/shard_map/all_to_all | solution.py:301
  123.2 8.2 %all-to-all-done.3 = f32[32,8,128]{2,1,0:T(8,128)S(1)} async-done(((f32[32,8,128]{2,1,0:T(8,128)}), f32[32,8,128]{2,1,0:T(8,128)S(1)}, u32[]{:S(2)}, u32[]{:S(2)}) %all-to-all-start.3) | async-done | bytes 131104 | tf_op jit(solution)/shard_map/all_to_all | solution.py:301
  131.4 0.7 broadcast_in_dim.15
  132.1 3.4 %all-to-all-start.4 = ((f32[8,24,256]{2,1,0:T(8,128)}), f32[8,24,256]{2,1,0:T(8,128)S(1)}, u32[]{:S(2)}, u32[]{:S(2)}) async-start(f32[8,24,256]{2,1,0:T(8,128)} %broadcast_in_dim.15), calls=%async_computation.4 | async-start | bytes 393216 | tf_op jit(solution)/shard_map/all_to_all | solution.py:301
  135.5 0.6 slice_reduce_fusion
  136.8 0.7 maximum_multiply_fusion
  137.5 6.6 %all-to-all-done.4 = f32[8,24,256]{2,1,0:T(8,128)S(1)} async-done(((f32[8,24,256]{2,1,0:T(8,128)}), f32[8,24,256]{2,1,0:T(8,128)S(1)}, u32[]{:S(2)}, u32[]{:S(2)}) %all-to-all-start.4) | async-done | bytes 196640 | tf_op jit(solution)/shard_map/all_to_all | solution.py:301
  144.1 0.7 slice_multiply_fusion
  (23 shorter events, 0.1 us)
Async XLA Ops:
  0.6 0.9 copy-start
  1.6 0.9 copy-start.2
  2.5 0.9 copy-start.4
  3.3 0.9 copy-start.6
  4.2 9.7 %copy-start.1 = (f32[3,7,2048]{2,1,0:T(8,128)S(1)}, f32[3,7,2048]{2,1,0:T(8,128)}, u32[]{:S(2)}) copy-start(f32[3,7,2048]{2,1,0:T(8,128)} %short.15) | copy-start | bytes 516100
  4.2 9.7 %copy-start.3 = (bf16[184,256]{1,0:T(8,128)(2,1)S(1)}, bf16[184,256]{1,0:T(8,128)(2,1)}, u32[]{:S(2)}) copy-start(bf16[184,256]{1,0:T(8,128)(2,1)} %constant.27.clone.p_head) | copy-start | bytes 282628
  4.3 9.7 %copy-start.5 = (bf16[176,256]{1,0:T(8,128)(2,1)S(1)}, bf16[176,256]{1,0:T(8,128)(2,1)}, u32[]{:S(2)}) copy-start(bf16[176,256]{1,0:T(8,128)(2,1)} %constant.26.clone.p_tail) | copy-start | bytes 270340
  6.7 48.0 %all-to-all-start = ((bf16[8,16,2048]{2,1,0:T(8,128)(2,1)}), bf16[8,16,2048]{2,1,0:T(8,128)(2,1)S(1)}, u32[]{:S(2)}, u32[]{:S(2)}) async-start(bf16[8,16,2048]{2,1,0:T(8,128)(2,1)} %get-tuple-element.53), calls=%async_computation | async-start | bytes 1048576 | tf_op jit(solution)/shard_map/all_to_all | solution.py:332
  15.9 9.7 %collective-permute-start.4 = (bf16[160,512]{1,0:T(8,128)(2,1)S(1)}, bf16[160,512]{1,0:T(8,128)(2,1)S(1)}, u32[]{:S(2)}, u32[]{:S(2)}) collective-permute-start(bf16[160,512]{1,0:T(8,128)(2,1)S(1)} %get-tuple-element.49), channel_id=1, source_target_pairs={{4,0},{8,4},{12,8},{16,12},{20,16},{24,20},{28,24},{5,1},{9,5},{13... | collective-permute-start | bytes 491528 | tf_op jit(solution)/shard_map/ppermute | solution.py:23
  17.2 11.7 %collective-permute-start = (bf16[152,512]{1,0:T(8,128)(2,1)S(1)}, bf16[152,512]{1,0:T(8,128)(2,1)S(1)}, u32[]{:S(2)}, u32[]{:S(2)}) collective-permute-start(bf16[152,512]{1,0:T(8,128)(2,1)S(1)} %get-tuple-element.42), channel_id=1, source_target_pairs={{0,4},{4,8},{8,12},{12,16},{16,20},{20,24},{24,28},{1,5},{5,9},{9,... | collective-permute-start | bytes 466952 | tf_op jit(solution)/shard_map/ppermute | solution.py:23
  25.5 9.6 %collective-permute-start.5 = (bf16[160,512]{1,0:T(8,128)(2,1)S(1)}, bf16[160,512]{1,0:T(8,128)(2,1)S(1)}, u32[]{:S(2)}, u32[]{:S(2)}) collective-permute-start(bf16[160,512]{1,0:T(8,128)(2,1)S(1)} %get-tuple-element.50), channel_id=1, source_target_pairs={{4,0},{8,4},{12,8},{16,12},{20,16},{24,20},{28,24},{5,1},{9,5},{13... | collective-permute-start | bytes 491528 | tf_op jit(solution)/shard_map/ppermute | solution.py:23
  28.8 10.9 %collective-permute-start.1 = (bf16[152,512]{1,0:T(8,128)(2,1)S(1)}, bf16[152,512]{1,0:T(8,128)(2,1)S(1)}, u32[]{:S(2)}, u32[]{:S(2)}) collective-permute-start(bf16[152,512]{1,0:T(8,128)(2,1)S(1)} %get-tuple-element.43), channel_id=1, source_target_pairs={{0,4},{4,8},{8,12},{12,16},{16,20},{20,24},{24,28},{1,5},{5,9},{9,... | collective-permute-start | bytes 466952 | tf_op jit(solution)/shard_map/ppermute | solution.py:23
  35.1 19.6 %copy-start.7 = (f32[2048]{0:T(1024)S(1)}, f32[2048]{0:T(1024)}, u32[]{:S(2)}) copy-start(f32[2048]{0:T(1024)} %param.48) | copy-start | bytes 24580
  35.1 19.6 %copy-start.8 = (bf16[264,1024]{1,0:T(8,128)(2,1)S(1)}, bf16[264,1024]{1,0:T(8,128)(2,1)}, u32[]{:S(2)}) copy-start(bf16[264,1024]{1,0:T(8,128)(2,1)} %constant.32.clone.s_own) | copy-start | bytes 1622020
  35.1 19.6 %copy-start.9 = (bf16[512,512]{1,0:T(8,128)(2,1)S(1)}, bf16[512,512]{1,0:T(8,128)(2,1)}, u32[]{:S(2)}) copy-start(bf16[512,512]{1,0:T(8,128)(2,1)} %constant.28.clone.e_own) | copy-start | bytes 1572868
  35.1 19.6 %copy-start.18 = (bf16[256,256]{1,0:T(8,128)(2,1)S(1)}, bf16[256,256]{1,0:T(8,128)(2,1)}, u32[]{:S(2)}) copy-start(bf16[256,256]{1,0:T(8,128)(2,1)} %constant.35.clone.p_out) | copy-start | bytes 393220
  35.1 18.1 %collective-permute-start.6 = (bf16[160,512]{1,0:T(8,128)(2,1)S(1)}, bf16[160,512]{1,0:T(8,128)(2,1)S(1)}, u32[]{:S(2)}, u32[]{:S(2)}) collective-permute-start(bf16[160,512]{1,0:T(8,128)(2,1)S(1)} %get-tuple-element.51), channel_id=1, source_target_pairs={{4,0},{8,4},{12,8},{16,12},{20,16},{24,20},{28,24},{5,1},{9,5},{13... | collective-permute-start | bytes 491528 | tf_op jit(solution)/shard_map/ppermute | solution.py:23
  39.7 9.1 %collective-permute-start.2 = (bf16[152,512]{1,0:T(8,128)(2,1)S(1)}, bf16[152,512]{1,0:T(8,128)(2,1)S(1)}, u32[]{:S(2)}, u32[]{:S(2)}) collective-permute-start(bf16[152,512]{1,0:T(8,128)(2,1)S(1)} %get-tuple-element.44), channel_id=1, source_target_pairs={{0,4},{4,8},{8,12},{12,16},{16,20},{20,24},{24,28},{1,5},{5,9},{9,... | collective-permute-start | bytes 466952 | tf_op jit(solution)/shard_map/ppermute | solution.py:23
  48.8 31.0 %collective-permute-start.3 = (bf16[152,512]{1,0:T(8,128)(2,1)S(1)}, bf16[152,512]{1,0:T(8,128)(2,1)S(1)}, u32[]{:S(2)}, u32[]{:S(2)}) collective-permute-start(bf16[152,512]{1,0:T(8,128)(2,1)S(1)} %get-tuple-element.45), channel_id=1, source_target_pairs={{0,4},{4,8},{8,12},{12,16},{16,20},{20,24},{24,28},{1,5},{5,9},{9,... | collective-permute-start | bytes 466952 | tf_op jit(solution)/shard_map/ppermute | solution.py:23
  53.2 26.6 %collective-permute-start.7 = (bf16[160,512]{1,0:T(8,128)(2,1)S(1)}, bf16[160,512]{1,0:T(8,128)(2,1)S(1)}, u32[]{:S(2)}, u32[]{:S(2)}) collective-permute-start(bf16[160,512]{1,0:T(8,128)(2,1)S(1)} %get-tuple-element.52), channel_id=1, source_target_pairs={{4,0},{8,4},{12,8},{16,12},{20,16},{24,20},{28,24},{5,1},{9,5},{13... | collective-permute-start | bytes 491528 | tf_op jit(solution)/shard_map/ppermute | solution.py:23
  54.7 1.0 copy-start.10
  55.7 0.9 copy-start.11
  56.7 0.9 copy-start.13
  57.6 0.9 copy-start.15
  58.6 0.9 copy-start.17
  59.5 6.8 %copy-start.12 = (bf16[512,144]{1,0:T(8,128)(2,1)S(1)}, bf16[512,144]{1,0:T(8,128)(2,1)}, u32[]{:S(2)}) copy-start(bf16[512,144]{1,0:T(8,128)(2,1)} %constant.29.clone.e_prev) | copy-start | bytes 442372
  59.5 6.8 %copy-start.14 = (bf16[512,144]{1,0:T(8,128)(2,1)S(1)}, bf16[512,144]{1,0:T(8,128)(2,1)}, u32[]{:S(2)}) copy-start(bf16[512,144]{1,0:T(8,128)(2,1)} %constant.30.clone.e_next) | copy-start | bytes 442372
  59.5 6.8 %copy-start.16 = (bf16[128,1024]{1,0:T(8,128)(2,1)S(1)}, bf16[128,1024]{1,0:T(8,128)(2,1)}, u32[]{:S(2)}) copy-start(bf16[128,1024]{1,0:T(8,128)(2,1)} %constant.33.clone.s_lags) | copy-start | bytes 786436
  102.3 14.4 %all-to-all-start.1 = ((bf16[8,24,1536]{2,1,0:T(8,128)(2,1)}), bf16[8,24,1536]{2,1,0:T(8,128)(2,1)S(1)}, u32[]{:S(2)}, u32[]{:S(2)}) async-start(bf16[8,24,1536]{2,1,0:T(8,128)(2,1)} %get-tuple-element.70), calls=%async_computation.1 | async-start | bytes 1179648 | tf_op jit(solution)/shard_map/all_to_all | solution.py:344
  119.5 11.9 %all-to-all-start.3 = ((f32[32,8,128]{2,1,0:T(8,128)}), f32[32,8,128]{2,1,0:T(8,128)S(1)}, u32[]{:S(2)}, u32[]{:S(2)}) async-start(f32[32,8,128]{2,1,0:T(8,128)} %broadcast_in_dim_broadcast_in_dim_broadcast_in_dim.3), calls=%async_computation.3 | async-start | bytes 262144 | tf_op jit(solution)/shard_map/all_to_all | solution.py:301
  132.1 11.9 %all-to-all-start.4 = ((f32[8,24,256]{2,1,0:T(8,128)}), f32[8,24,256]{2,1,0:T(8,128)S(1)}, u32[]{:S(2)}, u32[]{:S(2)}) async-start(f32[8,24,256]{2,1,0:T(8,128)} %broadcast_in_dim.15), calls=%async_computation.4 | async-start | bytes 393216 | tf_op jit(solution)/shard_map/all_to_all | solution.py:301

commit v3 on v2

--- a/solution.py
+++ b/solution.py
@@ -14,7 +14,7 @@
 FK = 7
 BF16 = jnp.bfloat16
 F32 = jnp.float32
-CHUNKS = 4
+CHUNKS = 2
 
 
 def from_behind(value, axis, by):
@@ -58,10 +58,18 @@
     return jnp.dot(a, b, preferred_element_type=F32)
 
 
-def edges_kernel(proj, cot, short, p_tail, p_head, *refs):
+def picked(span, first, length):
+    shape = ((span + FK - 1) * 8, length)
+    row, column = (lax.broadcasted_iota(jnp.int32, shape, axis) for axis in (0, 1))
+    position = first + (row & 7) * span + (row >> 3) - (FK - 1)
+    return jnp.where(position == column, 1.0, 0.0).astype(BF16)
+
+
+def edges_kernel(proj, cot, short, *refs):
     forward, backward = refs[-2:]
     length, width = cot.shape
-    tail, head = p_tail.shape[0] // 8 - (FK - 1), p_head.shape[0] // 8 - (FK - 1)
+    tail, head = 16, 17
+    p_tail, p_head = picked(tail, length - 128, length), picked(head, 0, length)
 
     def conv(x, taps, count):
         x = x.reshape(-1, 8, width)
@@ -70,11 +78,11 @@
             total = total + taps[lag : lag + 1] * x[FK - 1 - lag : FK - 1 - lag + count]
         return total
 
-    mixed = conv(mm(p_tail[...], proj[1]), short[1], tail) * conv(mm(p_tail[...], proj[2]), short[2], tail)
+    mixed = conv(mm(p_tail, proj[1]), short[1], tail) * conv(mm(p_tail, proj[2]), short[2], tail)
     ends = [proj[i, length - 16 :, :].astype(F32)[8:] for i in range(3)]
     forward[...] = jnp.concatenate([mixed.reshape(tail * 8, width)] + ends, axis=0).astype(BF16)
-    gate = conv(mm(p_head[...], proj[0]), short[0], head).reshape(head * 8, width)
-    grad = gate * mm(p_head[(FK - 1) * 8 :, :], cot[...])
+    gate = conv(mm(p_head, proj[0]), short[0], head).reshape(head * 8, width)
+    grad = gate * mm(p_head[(FK - 1) * 8 :], cot[...])
     starts = [ref[:16, :].astype(F32)[:8] for ref in (cot, proj.at[1], proj.at[2])]
     backward[...] = jnp.concatenate([grad] + starts, axis=0).astype(BF16)
     if len(refs) > 2:
@@ -197,10 +205,12 @@
     ranks, slots, _ = sums_out.shape
     per, each = filter_sums.shape[0] // ranks, -(-len(short_rows) // ranks)
     short_rows += [jnp.zeros((1, width), F32)] * (ranks * each - len(short_rows))
-    empty = [jnp.zeros((slots - per - each, width), F32)]
+    gaps = [-per % 8, -each % 8]
+    gaps = [[jnp.zeros((gap, width), F32)] if gap else [] for gap in gaps]
     blocks = []
     for rank in range(ranks):
-        blocks += [filter_sums[rank * per : rank * per + per]] + short_rows[rank * each : rank * each + each] + empty
+        blocks += [filter_sums[rank * per : rank * per + per]] + gaps[0]
+        blocks += short_rows[rank * each : rank * each + each] + gaps[1]
     sums_out[...] = jnp.concatenate(blocks, axis=0).reshape(ranks, slots, width).astype(BF16)
 
 
@@ -215,16 +225,12 @@
 
 def edges(proj, cot, short, width, first, blocks, taps=None, ranks=None):
     length = cot.shape[0]
-    constants = [
-        jnp.asarray(pick(interleaved(16, length - 128, 1 - FK), length)),
-        jnp.asarray(pick(interleaved(17, 0, 1 - FK), length)),
-    ]
     in_specs = [
         columns((3, length), width, first), columns((length,), width, first), columns((3, FK), width, first),
-    ] + [resident(constant) for constant in constants]
+    ]
     out_specs = [columns((152,), width), columns((160,), width)]
     out_shape = [jax.ShapeDtypeStruct((rows, blocks * width), BF16) for rows in (152, 160)]
-    operands = [proj, cot, short] + constants
+    operands = [proj, cot, short]
     if taps is not None:
         rows, channels = taps.shape
         in_specs.append(columns((rows,), channels // blocks))
@@ -243,7 +249,7 @@
     )(*operands)
 
 
-def main(proj, cot, prev, later, short, taps, decay, width, first, blocks, ranks, slots, group, at, held):
+def main(proj, cot, prev, later, short, taps, decay, width, first, blocks, ranks, slots, held):
     length, channels = cot.shape
     count = taps.shape[0]
     size = 2 * length
@@ -277,12 +283,12 @@
             columns((1,), width, first),
         ] + [resident(constant) for constant in constants] + [pl.BlockSpec(memory_space=pl.ANY)] * len(aliases),
         out_specs=[
-            columns((length,), width, first), columns((3, length), width, first), columns((ranks, slots), width, at),
+            columns((length,), width, first), columns((3, length), width, first), columns((ranks, slots), width, first),
         ],
         out_shape=[
             jax.ShapeDtypeStruct((length, channels), BF16),
             jax.ShapeDtypeStruct((3, length, channels), BF16),
-            pltpu.HBM((ranks, slots, group), BF16),
+            pltpu.HBM((ranks, slots, channels), BF16),
         ],
         scratch_shapes=[
             pltpu.VMEM((3, span + FK - 1, 8, width), F32),
@@ -297,63 +303,108 @@
     )(*operands)
 
 
-def everyone(value, axis, count):
-    return lax.all_to_all(jnp.broadcast_to(value[None], (count,) + value.shape), axis, 0, 0)
+def squares_kernel(sums, raw, payload):
+    ranks, slots, channels = sums.shape
+    total = sums[0].astype(F32)
+    for rank in range(1, ranks):
+        total = total + sums[rank].astype(F32)
+    raw[...] = total
+    squares = jnp.sum(total * total, keepdims=True)
+    high = squares.astype(BF16).astype(F32)
+    everyone, rows, width = payload.shape
+    each, cuts = rows // 8 - 1, channels // width
+    first = slots - 8 * (-(-each // 8))
+    pieces = [
+        total[row : row + 1, cut * width : (cut + 1) * width]
+        for row in range(first, first + each)
+        for cut in range(cuts)
+    ]
+    half = (8, width // 2)
+    ends = [jnp.broadcast_to(high, half), jnp.broadcast_to(squares - high, half)]
+    block = jnp.concatenate(pieces + [jnp.concatenate(ends, axis=1)], axis=0).astype(BF16)
+    for other in range(everyone):
+        payload[other] = block
+
+
+def scale_kernel(entries, mine, raw, gathered, grad_short, grad_filter):
+    everyone, rows, width = gathered.shape
+    each, channels = rows // 8 - 1, raw.shape[1]
+    cuts = channels // width
+    total = jnp.zeros((8, width), F32)
+    for other in range(everyone):
+        total = total + gathered[other].astype(F32)[rows - 8 :]
+    total = total[:1, :1] + total[:1, width // 2 : width // 2 + 1]
+    scale = jnp.minimum(1.0, math.sqrt(entries) / jnp.sqrt(total))
+    grad_filter[...] = scale * raw[: grad_filter.shape[0], :]
+    step = mine[1]
+    for i in range(3):
+        for lag in range(FK):
+            rank, row = divmod(i * (FK + 1) + lag, each)
+            block = gathered[rank * step + mine[0]].astype(F32) * scale
+            for cut in range(cuts):
+                at = row * cuts + cut
+                grad_short[i, lag : lag + 1, cut * width : (cut + 1) * width] = block[at : at + 1]
 
 
 def shards(projected, short_taps, filter_taps, decay, cotangent):
     length, _, channels = projected.shape
-    ranks = lax.axis_size("seq")
+    ranks, groups = lax.axis_size("seq"), lax.axis_size("ch")
     rows = filter_taps.shape[0]
     width = min(256, channels // CHUNKS)
     blocks = channels // width // CHUNKS
-    chunk = blocks * width
-    proj = pltpu.with_memory_space_constraint(jnp.transpose(projected, (1, 0, 2)), pltpu.HBM)
-    cotangent = pltpu.with_memory_space_constraint(cotangent, pltpu.HBM)
+    proj = jnp.transpose(projected, (1, 0, 2))
+    proj, cotangent, short_taps, filter_taps, decay = (
+        pltpu.with_memory_space_constraint(array, pltpu.HBM)
+        for array in (proj, cotangent, short_taps, filter_taps, decay[None])
+    )
 
     each = -(-3 * (FK + 1) // ranks)
-    slots = -(-(rows + each) // 8) * 8
-
-    sent, prev, later, spread = [], [], [], None
-    for k in range(CHUNKS):
-        made = edges(
-            proj, cotangent, short_taps, width, k * blocks, blocks, filter_taps if k == 1 else None, ranks
-        )
-        if k == 1:
-            spread = made[0]
-        sent.append(made[-2:])
-    for k in range(CHUNKS):
-        forward, backward = sent[k]
-        if k:
-            forward, prev[k - 1] = lax.optimization_barrier((forward, prev[k - 1]))
-            backward, later[k - 1] = lax.optimization_barrier((backward, later[k - 1]))
-        prev.append(from_behind(forward, "seq", 1))
-        later.append(from_behind(backward, "seq", -1))
-    taps = lax.all_to_all(spread, "seq", 0, 0).reshape(rows * ranks, channels)
-
-    gated = grad_proj = sums = None
-    groups = []
+    slots = -(-rows // 8) * 8 + -(-each // 8) * 8
+
+    prev, later, spread = [], [], None
     for k in range(CHUNKS):
         last = k == CHUNKS - 1
-        gated, grad_proj, sums = main(
-            proj, cotangent, prev[k], later[k], short_taps, taps, decay[None], width, k * blocks, blocks, ranks,
-            slots, chunk if last else chunk * (CHUNKS - 1), 0 if last else k * blocks,
-            [gated, grad_proj, None if last else sums],
+        made = edges(proj, cotangent, short_taps, width, k * blocks, blocks, filter_taps if last else None, ranks)
+        spread = made[0] if last else None
+        prev.append(from_behind(made[-2], "seq", 1))
+        later.append(from_behind(made[-1], "seq", -1))
+    taps = lax.all_to_all(spread, "seq", 0, 0).reshape(rows * ranks, channels)
+
+    held = [None] * 3
+    for k in range(CHUNKS):
+        held = main(
+            proj, cotangent, prev[k], later[k], short_taps, taps, decay, width, k * blocks, blocks, ranks, slots, held
         )
-        if k >= CHUNKS - 2:
-            groups.append(lax.all_to_all(sums, "seq", 0, 0))
-
-    raw = [jnp.sum(group.astype(F32), axis=0) for group in groups]
-    total = sum(jnp.sum(part[: rows + each] * part[: rows + each]) for part in raw)
-    filter_raw = jnp.concatenate([part[:rows] for part in raw], axis=1)
-    short_raw = jnp.concatenate([part[rows : rows + each] for part in raw], axis=1)
-    short_raw, total = lax.optimization_barrier((short_raw, total))
-    totals = everyone(jnp.full((8, 128), total), ("seq", "ch"), ranks * lax.axis_size("ch"))
-    short_all = everyone(short_raw.reshape(8 * each, channels // 8), "seq", ranks)
-    short_all = short_all.reshape(ranks * each, channels)[: 3 * (FK + 1)].reshape(3, FK + 1, channels)[:, :FK]
-    entries = (rows * ranks + 3 * FK) * channels * lax.axis_size("ch")
-    scale = jnp.minimum(1.0, math.sqrt(entries) / jnp.sqrt(jnp.sum(totals[:, 0, 0])))
-    return (gated, jnp.transpose(grad_proj, (1, 0, 2)), scale * short_all, scale * filter_raw)
+    gated, grad_proj, sums = held
+    sums = lax.all_to_all(sums, "seq", 0, 0)
+
+    vmem = pl.BlockSpec(memory_space=pltpu.VMEM)
+    raw, payload = pl.pallas_call(
+        squares_kernel,
+        in_specs=[vmem],
+        out_specs=[vmem] * 2,
+        out_shape=[
+            jax.ShapeDtypeStruct((slots, channels), F32),
+            jax.ShapeDtypeStruct((ranks * groups, 8 * each + 8, channels // 8), BF16),
+        ],
+        compiler_params=pltpu.CompilerParams(vmem_limit_bytes=32 << 20),
+        name="squares",
+    )(sums)
+    gathered = lax.all_to_all(payload, ("seq", "ch"), 0, 0)
+    mine = jnp.stack([lax.axis_index("ch"), jnp.int32(groups)])
+    entries = (rows * ranks + 3 * FK) * channels * groups
+    grad_short, grad_filter = pl.pallas_call(
+        functools.partial(scale_kernel, entries),
+        in_specs=[pl.BlockSpec(memory_space=pltpu.SMEM), vmem, vmem],
+        out_specs=[vmem] * 2,
+        out_shape=[
+            jax.ShapeDtypeStruct((3, FK, channels), F32),
+            jax.ShapeDtypeStruct((rows, channels), F32),
+        ],
+        compiler_params=pltpu.CompilerParams(vmem_limit_bytes=32 << 20),
+        name="scale",
+    )(mine, raw, gathered)
+    return (gated, jnp.transpose(grad_proj, (1, 0, 2)), grad_short, grad_filter)
 
 
 def solution(mesh):

time: 146 us -> 118 us (0.81)
  starting transfers between devices: 41.1 us -> 23.6 us
  blocking collectives: 15.8 us -> 24.1 us
  waiting for transfers between devices: 36.8 us -> 29.6 us
  local copies, waits for them, and re-layouts: 9.84 us -> 5.67 us
  other arithmetic: 3.37 us -> 0.08 us
  between operations: 2.94 us -> 0.74 us
    ppermute x8 -> x4, starting transfers between devices: 23.2 us -> 12.6 us  [from_behind(): return lax.ppermute(value, axis, pairs)]
    all_to_all x3 -> x1, waiting for transfers between devices: 25 us -> 15.5 us  [shards(): gathered = lax.all_to_all(payload, ('seq', 'ch'), 0, 0)]
    all_to_all x1, blocking collectives: 15.8 us -> 24.1 us  [shards(): sums = lax.all_to_all(sums, 'seq', 0, 0)]
    all_to_all x3 -> x1, starting transfers between devices: 10.6 us -> 3.61 us  [shards(): gathered = lax.all_to_all(payload, ('seq', 'ch'), 0, 0)]
    pallas_call x4 -> x2, Pallas kernels: 27 us -> 23.7 us  [main(): pl.pallas_call(main_kernel, grid=(blocks,), in_specs=[columns((3, length)...]
    unnamed x38 -> x22, local copies, waits for them, and re-layouts: 8.41 us -> 5.67 us
    pallas_call x0 -> x2, Pallas kernels: none -> 2.48 us  [the longest x1 1.37 us: shards(): pl.pallas_call(functools.partial(scale_kernel, entries), in_specs=[pl.Blo...]
    ppermute x8 -> x4, waiting for transfers between devices: 11.8 us -> 14.1 us  [from_behind(): return lax.ppermute(value, axis, pairs)]
  transfers between devices with their start and end apart: 12 -> 6, of which waited for: 7 -> 2; matrix products, arithmetic and copies ran while one was open for 1% -> 0% of each run, Pallas kernels for 18% -> 13%
where the time goes in v3:
time: 118 us
  Pallas kernels  33.8 us (29%)
  waiting for transfers between devices  29.6 us (25%)
  blocking collectives  24.1 us (20%)
  starting transfers between devices  23.6 us (20%)
  local copies, waits for them, and re-layouts  5.67 us (5%)
    all_to_all x1, blocking collectives, shards(): sums = lax.all_to_all(sums, 'seq', 0, 0)  24.1 us
    pallas_call x2, Pallas kernels, main(): pl.pallas_call(main_kernel, grid=(blocks,), in_specs=[columns((3, length)...  23.7 us
    all_to_all x1, waiting for transfers between devices, shards(): gathered = lax.all_to_all(payload, ('seq', 'ch'), 0, 0)  15.5 us
    ppermute x4, waiting for transfers between devices, from_behind(): return lax.ppermute(value, axis, pairs)  14.1 us
    ppermute x4, starting transfers between devices, from_behind(): return lax.ppermute(value, axis, pairs)  12.6 us
    pallas_call x2, Pallas kernels, edges(): pl.pallas_call(edges_kernel, grid=(blocks,), in_specs=in_specs, out_specs...  7.63 us
    all_to_all x1, starting transfers between devices, shards(): taps = lax.all_to_all(spread, 'seq', 0, 0).reshape(rows * ranks, channels)  7.42 us
    unnamed x22, local copies, waits for them, and re-layouts  5.67 us
  transfers between devices with their start and end apart: 6, of which 2 were waited for; matrix products, arithmetic and copies ran while one was open for 0% of the time, Pallas kernels for 13%

profile of v3, /device:TPU:0, one launch (start us, length us, event | category | flops | bytes accessed | tf_op | source)
XLA Modules:
  0.0 117.6 jit_solution(4951737662389132142)
XLA Ops:
  0.6 4.3 %edges.2 = (bf16[8,16,2048]{2,1,0:T(8,128)(2,1)}, bf16[152,1024]{1,0:T(8,128)(2,1)S(1)}, bf16[160,1024]{1,0:T(8,128)(2,1)S(1)}) custom-call(bf16[3,256,2048]{2,1,0:T(8,128)(2,1)} %bitcast.7, bf16[256,2048]{1,0:T(8,128)(2,1)} %cot.7, f32[3,7,2048]{2,1,0:T(8,128)} %short.7, f32[16,2048]{1,0:T(8,128)} %refs_0_.1), custom_call_target="tpu_custom_call" | custom-call | bytes 10240000 | tf_op jit(solution)/shard_map/edges/pallas_call | solution.py:240
  4.9 0.0 copy-start
  4.9 0.0 copy-start.1
  4.9 7.4 %all-to-all-start = ((bf16[8,16,2048]{2,1,0:T(8,128)(2,1)}), bf16[8,16,2048]{2,1,0:T(8,128)(2,1)S(1)}, u32[]{:S(2)}, u32[]{:S(2)}) async-start(bf16[8,16,2048]{2,1,0:T(8,128)(2,1)} %get-tuple-element.21), calls=%async_computation | async-start | bytes 1048576 | tf_op jit(solution)/shard_map/all_to_all | solution.py:371
  12.3 3.4 %edges.3 = (bf16[152,1024]{1,0:T(8,128)(2,1)S(1)}, bf16[160,1024]{1,0:T(8,128)(2,1)S(1)}) custom-call(bf16[3,256,2048]{2,1,0:T(8,128)(2,1)} %bitcast.8, bf16[256,2048]{1,0:T(8,128)(2,1)} %cot.7, f32[3,7,2048]{2,1,0:T(8,128)} %short.7), custom_call_target="tpu_custom_call" | custom-call | bytes 10240000 | tf_op jit(solution)/shard_map/edges/pallas_call | solution.py:240
  15.7 1.3 %collective-permute-start.3 = (bf16[160,1024]{1,0:T(8,128)(2,1)S(1)}, bf16[160,1024]{1,0:T(8,128)(2,1)S(1)}, u32[]{:S(2)}, u32[]{:S(2)}) collective-permute-start(bf16[160,1024]{1,0:T(8,128)(2,1)S(1)} %get-tuple-element.23), channel_id=1, source_target_pairs={{4,0},{8,4},{12,8},{16,12},{20,16},{24,20},{28,24},{5,1},{9,5},{13... | collective-permute-start | bytes 983048 | tf_op jit(solution)/shard_map/ppermute | solution.py:23
  17.0 4.6 %collective-permute-start.2 = (bf16[152,1024]{1,0:T(8,128)(2,1)S(1)}, bf16[152,1024]{1,0:T(8,128)(2,1)S(1)}, u32[]{:S(2)}, u32[]{:S(2)}) collective-permute-start(bf16[152,1024]{1,0:T(8,128)(2,1)S(1)} %get-tuple-element.22), channel_id=1, source_target_pairs={{0,4},{4,8},{8,12},{12,16},{16,20},{20,24},{24,28},{1,5},{5,9},{9,... | collective-permute-start | bytes 933896 | tf_op jit(solution)/shard_map/ppermute | solution.py:23
  21.6 1.3 %collective-permute-start.1 = (bf16[160,1024]{1,0:T(8,128)(2,1)S(1)}, bf16[160,1024]{1,0:T(8,128)(2,1)S(1)}, u32[]{:S(2)}, u32[]{:S(2)}) collective-permute-start(bf16[160,1024]{1,0:T(8,128)(2,1)S(1)} %get-tuple-element.20), channel_id=1, source_target_pairs={{4,0},{8,4},{12,8},{16,12},{20,16},{24,20},{28,24},{5,1},{9,5},{13... | collective-permute-start | bytes 983048 | tf_op jit(solution)/shard_map/ppermute | solution.py:23
  22.9 5.4 %collective-permute-start = (bf16[152,1024]{1,0:T(8,128)(2,1)S(1)}, bf16[152,1024]{1,0:T(8,128)(2,1)S(1)}, u32[]{:S(2)}, u32[]{:S(2)}) collective-permute-start(bf16[152,1024]{1,0:T(8,128)(2,1)S(1)} %get-tuple-element.19), channel_id=1, source_target_pairs={{0,4},{4,8},{8,12},{12,16},{16,20},{20,24},{24,28},{1,5},{5,9},{9,... | collective-permute-start | bytes 933896 | tf_op jit(solution)/shard_map/ppermute | solution.py:23
  28.3 14.1 %collective-permute-done.2.prev = bf16[152,1024]{1,0:T(8,128)(2,1)S(1)} collective-permute-done((bf16[152,1024]{1,0:T(8,128)(2,1)S(1)}, bf16[152,1024]{1,0:T(8,128)(2,1)S(1)}, u32[]{:S(2)}, u32[]{:S(2)}) %collective-permute-start.2) | collective-permute-done | bytes 311328 | tf_op jit(solution)/shard_map/ppermute | solution.py:23
  42.4 0.0 collective-permute-done.3.later
  42.4 0.0 all-to-all-done
  42.4 0.0 copy-done
  42.4 0.0 copy-done.1
  42.5 0.0 copy-start.2
  42.5 1.0 copy-done.2
  43.5 0.0 copy-start.4
  43.5 0.9 copy-done.4
  44.4 0.0 copy-start.6
  44.4 0.9 copy-done.6
  45.4 0.0 copy-start.8
  45.4 0.9 copy-done.8
  46.3 0.0 copy-start.9
  46.3 0.9 copy-done.9
  47.2 0.0 copy-start.10
  47.2 0.9 copy-done.10
  48.1 0.0 copy-start.3
  48.1 0.0 copy-start.5
  48.1 0.0 copy-start.7
  48.1 11.9 %operator.2 = (bf16[256,2048]{1,0:T(8,128)(2,1)}, bf16[3,256,2048]{2,1,0:T(8,128)(2,1)}, bf16[8,24,2048]{2,1,0:T(8,128)(2,1)}) custom-call(bf16[3,256,2048]{2,1,0:T(8,128)(2,1)} %bitcast.9, bf16[256,2048]{1,0:T(8,128)(2,1)} %cot.7, bf16[152,1024]{1,0:T(8,128)(2,1)S(1)} %collective-permute-done.2.prev, bf16[160,1024]{1,0:T(8,128)(2,1)S(1)} %collective-permute-done.3.later, ...), custom_call_target="tpu_custom_call" | custom-call | flops 16000000000 | bytes 8000000 | tf_op jit(solution)/shard_map/operator/pallas_call | solution.py:277
  60.1 0.0 collective-permute-done.prev
  60.1 0.0 collective-permute-done.1.later
  60.1 0.0 copy-done.3
  60.1 0.0 copy-done.5
  60.1 0.0 copy-done.7
  60.1 11.7 %operator.3 = (bf16[256,2048]{1,0:T(8,128)(2,1)}, bf16[3,256,2048]{2,1,0:T(8,128)(2,1)}, bf16[8,24,2048]{2,1,0:T(8,128)(2,1)}) custom-call(bf16[3,256,2048]{2,1,0:T(8,128)(2,1)} %bitcast.10, bf16[256,2048]{1,0:T(8,128)(2,1)} %cot.7, bf16[152,1024]{1,0:T(8,128)(2,1)S(1)} %collective-permute-done.prev, ...), custom_call_target="tpu_custom_call", output_to_operand_aliasing={{0}: (15, {}), {1}: (16, {}), {2}: (17, {})} | custom-call | flops 16000000000 | bytes 8000000 | tf_op jit(solution)/shard_map/operator/pallas_call | solution.py:277
  71.8 24.1 %all_to_all.15.sums = bf16[8,24,2048]{2,1,0:T(8,128)(2,1)S(1)} all-to-all(bf16[8,24,2048]{2,1,0:T(8,128)(2,1)} %get-tuple-element.29), channel_id=1, replica_groups=mesh['seq'=8,'ch'=4] {'seq'}, dimensions={0} | all-to-all | bytes 1572864 | tf_op jit(solution)/shard_map/all_to_all | solution.py:379
  96.0 1.1 squares.1
  97.1 3.6 %all-to-all-start.2 = ((bf16[32,32,256]{2,1,0:T(8,128)(2,1)}), bf16[32,32,256]{2,1,0:T(8,128)(2,1)S(1)}, u32[]{:S(2)}, u32[]{:S(2)}) async-start(bf16[32,32,256]{2,1,0:T(8,128)(2,1)} %get-tuple-element.31), calls=%async_computation.2 | async-start | bytes 1048576 | tf_op jit(solution)/shard_map/all_to_all | solution.py:393
  100.7 0.1 pad_add_fusion.mine
  100.8 15.5 %all-to-all-done.2.gathered = bf16[32,32,256]{2,1,0:T(8,128)(2,1)S(1)} async-done(((bf16[32,32,256]{2,1,0:T(8,128)(2,1)}), bf16[32,32,256]{2,1,0:T(8,128)(2,1)S(1)}, u32[]{:S(2)}, u32[]{:S(2)}) %all-to-all-start.2) | async-done | bytes 524320 | tf_op jit(solution)/shard_map/all_to_all | solution.py:393
  116.2 1.4 %scale.1 = (f32[3,7,2048]{2,1,0:T(8,128)}, f32[16,2048]{1,0:T(8,128)}) custom-call(s32[2]{0:T(128)S(1)} %pad_add_fusion.mine, f32[24,2048]{1,0:T(8,128)S(1)} %get-tuple-element.30.raw, bf16[32,32,256]{2,1,0:T(8,128)(2,1)S(1)} %all-to-all-done.2.gathered), custom_call_target="tpu_custom_call" | custom-call | tf_op jit(solution)/shard_map/scale/pallas_call | solution.py:396
Async XLA Ops:
  4.9 37.6 %copy-start = (bf16[264,1024]{1,0:T(8,128)(2,1)S(1)}, bf16[264,1024]{1,0:T(8,128)(2,1)}, u32[]{:S(2)}) copy-start(bf16[264,1024]{1,0:T(8,128)(2,1)} %constant.26.clone.s_own) | copy-start | bytes 1622020
  4.9 37.6 %copy-start.1 = (bf16[512,512]{1,0:T(8,128)(2,1)S(1)}, bf16[512,512]{1,0:T(8,128)(2,1)}, u32[]{:S(2)}) copy-start(bf16[512,512]{1,0:T(8,128)(2,1)} %constant.22.clone.e_own) | copy-start | bytes 1572868
  4.9 37.5 %all-to-all-start = ((bf16[8,16,2048]{2,1,0:T(8,128)(2,1)}), bf16[8,16,2048]{2,1,0:T(8,128)(2,1)S(1)}, u32[]{:S(2)}, u32[]{:S(2)}) async-start(bf16[8,16,2048]{2,1,0:T(8,128)(2,1)} %get-tuple-element.21), calls=%async_computation | async-start | bytes 1048576 | tf_op jit(solution)/shard_map/all_to_all | solution.py:371
  15.7 26.7 %collective-permute-start.3 = (bf16[160,1024]{1,0:T(8,128)(2,1)S(1)}, bf16[160,1024]{1,0:T(8,128)(2,1)S(1)}, u32[]{:S(2)}, u32[]{:S(2)}) collective-permute-start(bf16[160,1024]{1,0:T(8,128)(2,1)S(1)} %get-tuple-element.23), channel_id=1, source_target_pairs={{4,0},{8,4},{12,8},{16,12},{20,16},{24,20},{28,24},{5,1},{9,5},{13... | collective-permute-start | bytes 983048 | tf_op jit(solution)/shard_map/ppermute | solution.py:23
  17.0 25.4 %collective-permute-start.2 = (bf16[152,1024]{1,0:T(8,128)(2,1)S(1)}, bf16[152,1024]{1,0:T(8,128)(2,1)S(1)}, u32[]{:S(2)}, u32[]{:S(2)}) collective-permute-start(bf16[152,1024]{1,0:T(8,128)(2,1)S(1)} %get-tuple-element.22), channel_id=1, source_target_pairs={{0,4},{4,8},{8,12},{12,16},{16,20},{20,24},{24,28},{1,5},{5,9},{9,... | collective-permute-start | bytes 933896 | tf_op jit(solution)/shard_map/ppermute | solution.py:23
  21.6 38.5 %collective-permute-start.1 = (bf16[160,1024]{1,0:T(8,128)(2,1)S(1)}, bf16[160,1024]{1,0:T(8,128)(2,1)S(1)}, u32[]{:S(2)}, u32[]{:S(2)}) collective-permute-start(bf16[160,1024]{1,0:T(8,128)(2,1)S(1)} %get-tuple-element.20), channel_id=1, source_target_pairs={{4,0},{8,4},{12,8},{16,12},{20,16},{24,20},{28,24},{5,1},{9,5},{13... | collective-permute-start | bytes 983048 | tf_op jit(solution)/shard_map/ppermute | solution.py:23
  22.9 37.2 %collective-permute-start = (bf16[152,1024]{1,0:T(8,128)(2,1)S(1)}, bf16[152,1024]{1,0:T(8,128)(2,1)S(1)}, u32[]{:S(2)}, u32[]{:S(2)}) collective-permute-start(bf16[152,1024]{1,0:T(8,128)(2,1)S(1)} %get-tuple-element.19), channel_id=1, source_target_pairs={{0,4},{4,8},{8,12},{12,16},{16,20},{20,24},{24,28},{1,5},{5,9},{9,... | collective-permute-start | bytes 933896 | tf_op jit(solution)/shard_map/ppermute | solution.py:23
  42.5 1.0 copy-start.2
  43.5 0.9 copy-start.4
  44.4 0.9 copy-start.6
  45.4 0.9 copy-start.8
  46.3 0.9 copy-start.9
  47.2 0.9 copy-start.10
  48.1 12.0 %copy-start.3 = (bf16[512,384]{1,0:T(8,128)(2,1)S(1)}, bf16[512,384]{1,0:T(8,128)(2,1)}, u32[]{:S(2)}) copy-start(bf16[512,384]{1,0:T(8,128)(2,1)} %constant.25.clone.e_taps) | copy-start | bytes 1179652
  48.1 12.0 %copy-start.5 = (bf16[512,144]{1,0:T(8,128)(2,1)S(1)}, bf16[512,144]{1,0:T(8,128)(2,1)}, u32[]{:S(2)}) copy-start(bf16[512,144]{1,0:T(8,128)(2,1)} %constant.23.clone.e_prev) | copy-start | bytes 442372
  48.1 12.0 %copy-start.7 = (bf16[512,144]{1,0:T(8,128)(2,1)S(1)}, bf16[512,144]{1,0:T(8,128)(2,1)}, u32[]{:S(2)}) copy-start(bf16[512,144]{1,0:T(8,128)(2,1)} %constant.24.clone.e_next) | copy-start | bytes 442372
  97.1 19.2 %all-to-all-start.2 = ((bf16[32,32,256]{2,1,0:T(8,128)(2,1)}), bf16[32,32,256]{2,1,0:T(8,128)(2,1)S(1)}, u32[]{:S(2)}, u32[]{:S(2)}) async-start(bf16[32,32,256]{2,1,0:T(8,128)(2,1)} %get-tuple-element.31), calls=%async_computation.2 | async-start | bytes 1048576 | tf_op jit(solution)/shard_map/all_to_all | solution.py:393

commit v4 on v3

--- a/solution.py
+++ b/solution.py
@@ -15,6 +15,7 @@
 BF16 = jnp.bfloat16
 F32 = jnp.float32
 CHUNKS = 2
+SHORT = 32
 
 
 def from_behind(value, axis, by):
@@ -65,8 +66,7 @@
     return jnp.where(position == column, 1.0, 0.0).astype(BF16)
 
 
-def edges_kernel(proj, cot, short, *refs):
-    forward, backward = refs[-2:]
+def edges_kernel(proj, cot, short, forward, backward):
     length, width = cot.shape
     tail, head = 16, 17
     p_tail, p_head = picked(tail, length - 128, length), picked(head, 0, length)
@@ -85,16 +85,17 @@
     grad = gate * mm(p_head[(FK - 1) * 8 :], cot[...])
     starts = [ref[:16, :].astype(F32)[:8] for ref in (cot, proj.at[1], proj.at[2])]
     backward[...] = jnp.concatenate([grad] + starts, axis=0).astype(BF16)
-    if len(refs) > 2:
-        taps, spread = refs[:2]
-        spread[...] = jnp.broadcast_to(taps[...].astype(BF16)[None], spread.shape)
+
+
+def spread_kernel(taps, spread):
+    spread[...] = jnp.broadcast_to(taps[...].astype(BF16)[None], spread.shape)
 
 
 def main_kernel(
-    proj, cot, prev, later, short, taps, decay,
+    first, proj, cot, prev, later, short, taps, decay,
     e_own, e_prev, e_next, e_taps, s_own, s_lags, p_in, p_out, *refs,
 ):
-    gated, grad_proj, sums_out, px, feat, grad, cots = refs[-7:]
+    gated, grad_proj, sums_out, px, feat, grad, cots, filter_held, short_held, done = refs[-10:]
     length, width = cot.shape
     span = length // 8
     edge = FK - 1
@@ -198,24 +199,50 @@
             columns.append(jnp.concatenate(chunks, axis=0))
             for lag in range(FK):
                 rows[lag].append(jnp.sum(sums[lag], axis=0, keepdims=True))
-        short_rows += [jnp.concatenate(row, axis=1) for row in rows] + [jnp.zeros((1, width), F32)]
+        short_rows += [jnp.concatenate(row, axis=1) for row in rows]
         result = flat(jnp.concatenate(columns, axis=2)).astype(BF16)
         grad_proj[i] = mm(p_out[...], result).astype(BF16)
 
-    ranks, slots, _ = sums_out.shape
-    per, each = filter_sums.shape[0] // ranks, -(-len(short_rows) // ranks)
-    short_rows += [jnp.zeros((1, width), F32)] * (ranks * each - len(short_rows))
-    gaps = [-per % 8, -each % 8]
-    gaps = [[jnp.zeros((gap, width), F32)] if gap else [] for gap in gaps]
-    blocks = []
-    for rank in range(ranks):
-        blocks += [filter_sums[rank * per : rank * per + per]] + gaps[0]
-        blocks += short_rows[rank * each : rank * each + each] + gaps[1]
-    sums_out[...] = jnp.concatenate(blocks, axis=0).reshape(ranks, slots, width).astype(BF16)
-
-
-def resident(array):
-    return pl.BlockSpec(memory_space=pltpu.VMEM)
+    step, block = pl.program_id(0), first + pl.program_id(0)
+    ranks, slot, _ = filter_held.shape
+    per, share = filter_sums.shape[0] // ranks, short_held.shape[0]
+    copies = [
+        pltpu.make_async_copy(
+            filter_held, sums_out.at[:, pl.ds(pl.multiple_of(block * slot, slot), slot), :], done.at[0]
+        ),
+        pltpu.make_async_copy(
+            short_held,
+            sums_out.at[pl.ds(block * share, share), pl.ds(sums_out.shape[1] - SHORT, SHORT), :],
+            done.at[1],
+        ),
+    ]
+
+    @pl.when(step > 0)
+    def _():
+        for copy in copies:
+            copy.wait()
+
+    by_rank = filter_sums.reshape(ranks, per, width) if per % 8 == 0 else jnp.stack(
+        [filter_sums[rank * per : rank * per + per] for rank in range(ranks)]
+    )
+    if slot > per:
+        by_rank = jnp.concatenate([by_rank, jnp.zeros((ranks, slot - per, width), F32)], axis=1)
+    filter_held[...] = by_rank.astype(BF16)
+    sums = jnp.concatenate(short_rows + [jnp.zeros((SHORT - len(short_rows), width), F32)], axis=0)
+    for rank in range(share):
+        held = pltpu.roll(sums, width - rank * (width // share), 1) if rank else sums
+        short_held[rank] = held.astype(BF16)
+    for copy in copies:
+        copy.start()
+
+    @pl.when(step == pl.num_programs(0) - 1)
+    def _():
+        for copy in copies:
+            copy.wait()
+
+
+def whole(array):
+    return pl.BlockSpec(array.shape, lambda c: (0,) * array.ndim)
 
 
 def columns(rows, width, first=0):
@@ -223,37 +250,28 @@
     return pl.BlockSpec(tuple(rows) + (width,), lambda c: lead + (first + c,))
 
 
-def edges(proj, cot, short, width, first, blocks, taps=None, ranks=None):
+def edges(proj, cot, short, width, first, blocks):
     length = cot.shape[0]
-    in_specs = [
-        columns((3, length), width, first), columns((length,), width, first), columns((3, FK), width, first),
-    ]
-    out_specs = [columns((152,), width), columns((160,), width)]
-    out_shape = [jax.ShapeDtypeStruct((rows, blocks * width), BF16) for rows in (152, 160)]
-    operands = [proj, cot, short]
-    if taps is not None:
-        rows, channels = taps.shape
-        in_specs.append(columns((rows,), channels // blocks))
-        operands.append(taps)
-        out_specs.insert(0, columns((ranks, rows), channels // blocks))
-        out_shape.insert(0, pltpu.HBM((ranks, rows, channels), BF16))
     return pl.pallas_call(
         edges_kernel,
         grid=(blocks,),
-        in_specs=in_specs,
-        out_specs=out_specs,
-        out_shape=out_shape,
+        in_specs=[
+            columns((3, length), width, first), columns((length,), width, first), columns((3, FK), width, first),
+        ],
+        out_specs=[columns((152,), width), columns((160,), width)],
+        out_shape=[jax.ShapeDtypeStruct((rows, blocks * width), BF16) for rows in (152, 160)],
         compiler_params=pltpu.CompilerParams(vmem_limit_bytes=32 << 20),
         cost_estimate=pl.CostEstimate(flops=0, bytes_accessed=blocks * width * 10000, transcendentals=0),
         name="edges",
-    )(*operands)
-
-
-def main(proj, cot, prev, later, short, taps, decay, width, first, blocks, ranks, slots, held):
+    )(proj, cot, short)
+
+
+def main(proj, cot, prev, later, short, taps, decay, width, first, blocks, ranks, slot, held):
     length, channels = cot.shape
     count = taps.shape[0]
     size = 2 * length
     span = length // 8
+    share = ranks * width // channels
     own = interleaved(span)
     high, low = analysis(own, size)
     k_high, k_low = analysis(np.arange(count), size)
@@ -267,7 +285,7 @@
         pick(interleaved(span, 0, 1 - FK), length),
         pick(own, length).T,
     ]
-    constants = [jnp.asarray(constant) for constant in constants]
+    constants = [pltpu.with_memory_space_constraint(jnp.asarray(constant), pltpu.HBM) for constant in constants]
     operands = [proj, cot, prev, later, short, taps, decay] + constants
     aliases = {}
     for index, value in enumerate(held):
@@ -275,26 +293,29 @@
             aliases[len(operands)] = index
             operands.append(value)
     return pl.pallas_call(
-        main_kernel,
+        functools.partial(main_kernel, first),
         grid=(blocks,),
         in_specs=[
             columns((3, length), width, first), columns((length,), width, first), columns((prev.shape[0],), width),
             columns((later.shape[0],), width), columns((3, FK), width, first), columns((count,), width, first),
             columns((1,), width, first),
-        ] + [resident(constant) for constant in constants] + [pl.BlockSpec(memory_space=pl.ANY)] * len(aliases),
+        ] + [whole(constant) for constant in constants] + [pl.BlockSpec(memory_space=pl.ANY)] * len(aliases),
         out_specs=[
-            columns((length,), width, first), columns((3, length), width, first), columns((ranks, slots), width, first),
+            columns((length,), width, first), columns((3, length), width, first), pl.BlockSpec(memory_space=pl.ANY),
         ],
         out_shape=[
             jax.ShapeDtypeStruct((length, channels), BF16),
             jax.ShapeDtypeStruct((3, length, channels), BF16),
-            pltpu.HBM((ranks, slots, channels), BF16),
+            pltpu.HBM((ranks, channels // width * slot + SHORT, width), BF16),
         ],
         scratch_shapes=[
             pltpu.VMEM((3, span + FK - 1, 8, width), F32),
             pltpu.VMEM((3, span, 8, width), F32),
             pltpu.VMEM((3, span + FK - 1, 8, width), F32),
             pltpu.VMEM((span, 8, width), F32),
+            pltpu.VMEM((ranks, slot, width), BF16),
+            pltpu.VMEM((share, SHORT, width), BF16),
+            pltpu.SemaphoreType.DMA((2,)),
         ],
         input_output_aliases=aliases,
         compiler_params=pltpu.CompilerParams(vmem_limit_bytes=40 << 20),
@@ -303,47 +324,39 @@
     )(*operands)
 
 
-def squares_kernel(sums, raw, payload):
-    ranks, slots, channels = sums.shape
+def squares_kernel(rows, share, sums, raw, payload):
+    ranks, slots, width = sums.shape
     total = sums[0].astype(F32)
     for rank in range(1, ranks):
         total = total + sums[rank].astype(F32)
-    raw[...] = total
-    squares = jnp.sum(total * total, keepdims=True)
+    slot = -(-rows // 16) * 16
+    pieces = [total[at : at + rows] for at in range(0, slots - SHORT, slot)]
+    raw[...] = jnp.concatenate(pieces, axis=1)
+    lane = lax.broadcasted_iota(jnp.int32, (SHORT, width), 1)
+    short = jnp.where(lane < share, total[slots - SHORT :], 0.0)
+    squares = jnp.sum(short * short, keepdims=True)
+    for piece in pieces:
+        squares = squares + jnp.sum(piece * piece, keepdims=True)
     high = squares.astype(BF16).astype(F32)
-    everyone, rows, width = payload.shape
-    each, cuts = rows // 8 - 1, channels // width
-    first = slots - 8 * (-(-each // 8))
-    pieces = [
-        total[row : row + 1, cut * width : (cut + 1) * width]
-        for row in range(first, first + each)
-        for cut in range(cuts)
-    ]
-    half = (8, width // 2)
-    ends = [jnp.broadcast_to(high, half), jnp.broadcast_to(squares - high, half)]
-    block = jnp.concatenate(pieces + [jnp.concatenate(ends, axis=1)], axis=0).astype(BF16)
-    for other in range(everyone):
+    row = lax.broadcasted_iota(jnp.int32, (24, width), 0)
+    block = jnp.where(row < 3 * FK, short[:24], jnp.where(row == 3 * FK, high, squares - high)).astype(BF16)
+    for other in range(payload.shape[0]):
         payload[other] = block
 
 
-def scale_kernel(entries, mine, raw, gathered, grad_short, grad_filter):
+def scale_kernel(entries, share, mine, raw, gathered, grad_short, grad_filter):
     everyone, rows, width = gathered.shape
-    each, channels = rows // 8 - 1, raw.shape[1]
-    cuts = channels // width
     total = jnp.zeros((8, width), F32)
     for other in range(everyone):
-        total = total + gathered[other].astype(F32)[rows - 8 :]
-    total = total[:1, :1] + total[:1, width // 2 : width // 2 + 1]
+        total = total + gathered[other].astype(F32)[16:]
+    total = total[5:6, :1] + total[6:7, :1]
     scale = jnp.minimum(1.0, math.sqrt(entries) / jnp.sqrt(total))
-    grad_filter[...] = scale * raw[: grad_filter.shape[0], :]
+    grad_filter[...] = scale * raw[...]
     step = mine[1]
-    for i in range(3):
-        for lag in range(FK):
-            rank, row = divmod(i * (FK + 1) + lag, each)
-            block = gathered[rank * step + mine[0]].astype(F32) * scale
-            for cut in range(cuts):
-                at = row * cuts + cut
-                grad_short[i, lag : lag + 1, cut * width : (cut + 1) * width] = block[at : at + 1]
+    for rank in range(raw.shape[1] // share):
+        block = gathered[rank * step + mine[0]].astype(F32) * scale
+        for i in range(3):
+            grad_short[i, :, rank * share : (rank + 1) * share] = block[i * FK : (i + 1) * FK, :share]
 
 
 def shards(projected, short_taps, filter_taps, decay, cotangent):
@@ -353,39 +366,48 @@
     width = min(256, channels // CHUNKS)
     blocks = channels // width // CHUNKS
     proj = jnp.transpose(projected, (1, 0, 2))
-    proj, cotangent, short_taps, filter_taps, decay = (
+    proj, cotangent, short_taps, decay = (
         pltpu.with_memory_space_constraint(array, pltpu.HBM)
-        for array in (proj, cotangent, short_taps, filter_taps, decay[None])
+        for array in (proj, cotangent, short_taps, decay[None])
     )
 
-    each = -(-3 * (FK + 1) // ranks)
-    slots = -(-rows // 8) * 8 + -(-each // 8) * 8
-
-    prev, later, spread = [], [], None
+    slot = -(-rows // 16) * 16
+    share = channels // ranks
+
+    def constrained(*values):
+        return lax.optimization_barrier(values)
+
+    prev, later = [], []
     for k in range(CHUNKS):
-        last = k == CHUNKS - 1
-        made = edges(proj, cotangent, short_taps, width, k * blocks, blocks, filter_taps if last else None, ranks)
-        spread = made[0] if last else None
-        prev.append(from_behind(made[-2], "seq", 1))
-        later.append(from_behind(made[-1], "seq", -1))
+        forward, backward = edges(proj, cotangent, short_taps, width, k * blocks, blocks)
+        if k:
+            forward, backward, later[-1] = constrained(forward, backward, later[-1])
+        prev.append(from_behind(forward, "seq", 1))
+        later.append(from_behind(backward, "seq", -1))
+    filter_taps, prev[0] = constrained(filter_taps, prev[0])
+    spread = pl.pallas_call(
+        spread_kernel,
+        out_shape=pltpu.HBM((ranks, rows, channels), BF16),
+        name="spread",
+    )(filter_taps)
     taps = lax.all_to_all(spread, "seq", 0, 0).reshape(rows * ranks, channels)
 
     held = [None] * 3
     for k in range(CHUNKS):
         held = main(
-            proj, cotangent, prev[k], later[k], short_taps, taps, decay, width, k * blocks, blocks, ranks, slots, held
+            proj, cotangent, prev[k], later[k], short_taps, taps, decay, width, k * blocks, blocks, ranks, slot, held
         )
     gated, grad_proj, sums = held
     sums = lax.all_to_all(sums, "seq", 0, 0)
 
     vmem = pl.BlockSpec(memory_space=pltpu.VMEM)
     raw, payload = pl.pallas_call(
-        squares_kernel,
+        functools.partial(squares_kernel, rows, share),
         in_specs=[vmem],
         out_specs=[vmem] * 2,
         out_shape=[
-            jax.ShapeDtypeStruct((slots, channels), F32),
-            jax.ShapeDtypeStruct((ranks * groups, 8 * each + 8, channels // 8), BF16),
+            jax.ShapeDtypeStruct((rows, channels), F32),
+            jax.ShapeDtypeStruct((ranks * groups, 24, width), BF16),
         ],
         compiler_params=pltpu.CompilerParams(vmem_limit_bytes=32 << 20),
         name="squares",
@@ -394,7 +416,7 @@
     mine = jnp.stack([lax.axis_index("ch"), jnp.int32(groups)])
     entries = (rows * ranks + 3 * FK) * channels * groups
     grad_short, grad_filter = pl.pallas_call(
-        functools.partial(scale_kernel, entries),
+        functools.partial(scale_kernel, entries, share),
         in_specs=[pl.BlockSpec(memory_space=pltpu.SMEM), vmem, vmem],
         out_specs=[vmem] * 2,
         out_shape=[

time: 118 us -> 116 us (0.983)
  local copies, waits for them, and re-layouts: 5.67 us -> 0 us
  Pallas kernels: 33.8 us -> 37.4 us
  blocking collectives: 24.1 us -> 22.7 us
    unnamed x22 -> x0, local copies, waits for them, and re-layouts: 5.67 us -> none
    pallas_call x6 -> x7, Pallas kernels: 33.8 us -> 37.4 us  [the longest x2 26.5 us: main(): pl.pallas_call(functools.partial(main_kernel, first), grid=(blocks,), in_...]
    ppermute x4, waiting for transfers between devices: 14.1 us -> 16.9 us  [from_behind(): return lax.ppermute(value, axis, pairs)]
    all_to_all x1, waiting for transfers between devices: 15.5 us -> 13.1 us  [shards(): gathered = lax.all_to_all(payload, ('seq', 'ch'), 0, 0)]
    ppermute x4, starting transfers between devices: 12.6 us -> 14.3 us  [from_behind(): return lax.ppermute(value, axis, pairs)]
    all_to_all x1, blocking collectives: 24.1 us -> 22.7 us  [shards(): sums = lax.all_to_all(sums, 'seq', 0, 0)]
  transfers between devices with their start and end apart: 6 -> 6, of which waited for: 2 -> 3; matrix products, arithmetic and copies ran while one was open for 0% -> 0% of each run, Pallas kernels for 13% -> 14%
where the time goes in v4:
time: 116 us; the launch traced here: 115 us
  Pallas kernels  37.4 us (32%)
  waiting for transfers between devices  30 us (26%)
  starting transfers between devices  24.3 us (21%)
  blocking collectives  22.7 us (20%)
    pallas_call x2, Pallas kernels, main(): pl.pallas_call(functools.partial(main_kernel, first), grid=(blocks,), in_...  26.5 us
    all_to_all x1, blocking collectives, shards(): sums = lax.all_to_all(sums, 'seq', 0, 0)  22.7 us
    ppermute x4, waiting for transfers between devices, from_behind(): return lax.ppermute(value, axis, pairs)  16.9 us
    ppermute x4, starting transfers between devices, from_behind(): return lax.ppermute(value, axis, pairs)  14.3 us
    all_to_all x1, waiting for transfers between devices, shards(): gathered = lax.all_to_all(payload, ('seq', 'ch'), 0, 0)  13.1 us
    pallas_call x2, Pallas kernels, edges(): pl.pallas_call(edges_kernel, grid=(blocks,), in_specs=[columns((3, length...  6.8 us
    all_to_all x1, starting transfers between devices, shards(): taps = lax.all_to_all(spread, 'seq', 0, 0).reshape(rows * ranks, channels)  6.8 us
    all_to_all x1, starting transfers between devices, shards(): gathered = lax.all_to_all(payload, ('seq', 'ch'), 0, 0)  3.29 us
  transfers between devices with their start and end apart: 6, of which 3 were waited for; matrix products, arithmetic and copies ran while one was open for 0% of the time, Pallas kernels for 14%

profile of v4, /device:TPU:0, one launch (start us, length us, event | category | flops | bytes accessed | tf_op | source)
XLA Modules:
  0.0 115.2 jit_solution(8265419057707043337)
XLA Ops:
  0.6 3.4 %edges.3 = (bf16[152,1024]{1,0:T(8,128)(2,1)S(1)}, bf16[160,1024]{1,0:T(8,128)(2,1)S(1)}) custom-call(bf16[3,256,2048]{2,1,0:T(8,128)(2,1)} %bitcast.7, bf16[256,2048]{1,0:T(8,128)(2,1)} %cot.7, f32[3,7,2048]{2,1,0:T(8,128)} %short.7), custom_call_target="tpu_custom_call" | custom-call | bytes 10240000 | tf_op jit(solution)/shard_map/edges/pallas_call | solution.py:255
  4.0 4.9 %collective-permute-start.3 = (bf16[152,1024]{1,0:T(8,128)(2,1)S(1)}, bf16[152,1024]{1,0:T(8,128)(2,1)S(1)}, u32[]{:S(2)}, u32[]{:S(2)}) collective-permute-start(bf16[152,1024]{1,0:T(8,128)(2,1)S(1)} %get-tuple-element.28), channel_id=1, source_target_pairs={{0,4},{4,8},{8,12},{12,16},{16,20},{20,24},{24,28},{1,5},{5,9},{9,... | collective-permute-start | bytes 933896 | tf_op jit(solution)/shard_map/ppermute | solution.py:24
  8.9 6.6 %collective-permute-done.3.prev = bf16[152,1024]{1,0:T(8,128)(2,1)S(1)} collective-permute-done((bf16[152,1024]{1,0:T(8,128)(2,1)S(1)}, bf16[152,1024]{1,0:T(8,128)(2,1)S(1)}, u32[]{:S(2)}, u32[]{:S(2)}) %collective-permute-start.3) | collective-permute-done | bytes 311328 | tf_op jit(solution)/shard_map/ppermute | solution.py:24
  15.5 1.7 %spread.1 = bf16[8,16,2048]{2,1,0:T(8,128)(2,1)} custom-call(f32[16,2048]{1,0:T(8,128)} %taps), custom_call_target="tpu_custom_call" | custom-call | tf_op jit(solution)/shard_map/spread/pallas_call | solution.py:388
  17.2 6.8 %all-to-all-start = ((bf16[8,16,2048]{2,1,0:T(8,128)(2,1)}), bf16[8,16,2048]{2,1,0:T(8,128)(2,1)S(1)}, u32[]{:S(2)}, u32[]{:S(2)}) async-start(bf16[8,16,2048]{2,1,0:T(8,128)(2,1)} %spread.1), calls=%async_computation | async-start | bytes 1048576 | tf_op jit(solution)/shard_map/all_to_all | solution.py:393
  24.0 1.3 %collective-permute-start = (bf16[160,1024]{1,0:T(8,128)(2,1)S(1)}, bf16[160,1024]{1,0:T(8,128)(2,1)S(1)}, u32[]{:S(2)}, u32[]{:S(2)}) collective-permute-start(bf16[160,1024]{1,0:T(8,128)(2,1)S(1)} %get-tuple-element.25), channel_id=1, source_target_pairs={{4,0},{8,4},{12,8},{16,12},{20,16},{24,20},{28,24},{5,1},{9,5},{13... | collective-permute-start | bytes 983048 | tf_op jit(solution)/shard_map/ppermute | solution.py:24
  25.3 3.4 %edges.2 = (bf16[152,1024]{1,0:T(8,128)(2,1)S(1)}, bf16[160,1024]{1,0:T(8,128)(2,1)S(1)}) custom-call(bf16[3,256,2048]{2,1,0:T(8,128)(2,1)} %bitcast.8, bf16[256,2048]{1,0:T(8,128)(2,1)} %cot.7, f32[3,7,2048]{2,1,0:T(8,128)} %short.7), custom_call_target="tpu_custom_call" | custom-call | bytes 10240000 | tf_op jit(solution)/shard_map/edges/pallas_call | solution.py:255
  28.7 10.3 %collective-permute-done.later = bf16[160,1024]{1,0:T(8,128)(2,1)S(1)} collective-permute-done((bf16[160,1024]{1,0:T(8,128)(2,1)S(1)}, bf16[160,1024]{1,0:T(8,128)(2,1)S(1)}, u32[]{:S(2)}, u32[]{:S(2)}) %collective-permute-start) | collective-permute-done | bytes 327712 | tf_op jit(solution)/shard_map/ppermute | solution.py:24
  39.0 1.3 %collective-permute-start.2 = (bf16[160,1024]{1,0:T(8,128)(2,1)S(1)}, bf16[160,1024]{1,0:T(8,128)(2,1)S(1)}, u32[]{:S(2)}, u32[]{:S(2)}) collective-permute-start(bf16[160,1024]{1,0:T(8,128)(2,1)S(1)} %get-tuple-element.27), channel_id=1, source_target_pairs={{4,0},{8,4},{12,8},{16,12},{20,16},{24,20},{28,24},{5,1},{9,5},{13... | collective-permute-start | bytes 983048 | tf_op jit(solution)/shard_map/ppermute | solution.py:24
  40.3 6.8 %collective-permute-start.1 = (bf16[152,1024]{1,0:T(8,128)(2,1)S(1)}, bf16[152,1024]{1,0:T(8,128)(2,1)S(1)}, u32[]{:S(2)}, u32[]{:S(2)}) collective-permute-start(bf16[152,1024]{1,0:T(8,128)(2,1)S(1)} %get-tuple-element.26), channel_id=1, source_target_pairs={{0,4},{4,8},{8,12},{12,16},{16,20},{20,24},{24,28},{1,5},{5,9},{9,... | collective-permute-start | bytes 933896 | tf_op jit(solution)/shard_map/ppermute | solution.py:24
  47.1 0.0 all-to-all-done
  47.2 13.2 %operator.2 = (bf16[256,2048]{1,0:T(8,128)(2,1)}, bf16[3,256,2048]{2,1,0:T(8,128)(2,1)}, bf16[8,160,256]{2,1,0:T(8,128)(2,1)}) custom-call(bf16[3,256,2048]{2,1,0:T(8,128)(2,1)} %bitcast.9, bf16[256,2048]{1,0:T(8,128)(2,1)} %cot.7, bf16[152,1024]{1,0:T(8,128)(2,1)S(1)} %collective-permute-done.3.prev, bf16[160,1024]{1,0:T(8,128)(2,1)S(1)} %collective-permute-done.later, ...), custom_call_target="tpu_custom_call" | custom-call | flops 16000000000 | bytes 8000000 | tf_op jit(solution)/shard_map/operator/pallas_call | solution.py:295
  60.4 0.0 collective-permute-done.1.prev
  60.4 0.0 collective-permute-done.2.later
  60.4 13.3 %operator.3 = (bf16[256,2048]{1,0:T(8,128)(2,1)}, bf16[3,256,2048]{2,1,0:T(8,128)(2,1)}, bf16[8,160,256]{2,1,0:T(8,128)(2,1)}) custom-call(bf16[3,256,2048]{2,1,0:T(8,128)(2,1)} %bitcast.10, bf16[256,2048]{1,0:T(8,128)(2,1)} %cot.7, bf16[152,1024]{1,0:T(8,128)(2,1)S(1)} %collective-permute-done.1.prev, ...), custom_call_target="tpu_custom_call", output_to_operand_aliasing={{0}: (15, {}), {1}: (16, {}), {2}: (17, {})} | custom-call | flops 16000000000 | bytes 8000000 | tf_op jit(solution)/shard_map/operator/pallas_call | solution.py:295
  73.7 22.7 %all_to_all.15.sums = bf16[8,160,256]{2,1,0:T(8,128)(2,1)S(1)} all-to-all(bf16[8,160,256]{2,1,0:T(8,128)(2,1)} %get-tuple-element.37), channel_id=1, replica_groups=mesh['seq'=8,'ch'=4] {'seq'}, dimensions={0} | all-to-all | bytes 1310720 | tf_op jit(solution)/shard_map/all_to_all | solution.py:401
  96.4 1.0 squares.1
  97.3 3.3 %all-to-all-start.2 = ((bf16[32,24,256]{2,1,0:T(8,128)(2,1)}), bf16[32,24,256]{2,1,0:T(8,128)(2,1)S(1)}, u32[]{:S(2)}, u32[]{:S(2)}) async-start(bf16[32,24,256]{2,1,0:T(8,128)(2,1)} %get-tuple-element.39), calls=%async_computation.2 | async-start | bytes 786432 | tf_op jit(solution)/shard_map/all_to_all | solution.py:415
  100.6 0.1 pad_add_fusion.mine
  100.7 13.1 %all-to-all-done.2.gathered = bf16[32,24,256]{2,1,0:T(8,128)(2,1)S(1)} async-done(((bf16[32,24,256]{2,1,0:T(8,128)(2,1)}), bf16[32,24,256]{2,1,0:T(8,128)(2,1)S(1)}, u32[]{:S(2)}, u32[]{:S(2)}) %all-to-all-start.2) | async-done | bytes 393248 | tf_op jit(solution)/shard_map/all_to_all | solution.py:415
  113.8 1.4 %scale.1 = (f32[3,7,2048]{2,1,0:T(8,128)}, f32[16,2048]{1,0:T(8,128)}) custom-call(s32[2]{0:T(128)S(1)} %pad_add_fusion.mine, f32[16,2048]{1,0:T(8,128)S(1)} %get-tuple-element.38.raw, bf16[32,24,256]{2,1,0:T(8,128)(2,1)S(1)} %all-to-all-done.2.gathered), custom_call_target="tpu_custom_call" | custom-call | tf_op jit(solution)/shard_map/scale/pallas_call | solution.py:418
Async XLA Ops:
  4.0 11.5 %collective-permute-start.3 = (bf16[152,1024]{1,0:T(8,128)(2,1)S(1)}, bf16[152,1024]{1,0:T(8,128)(2,1)S(1)}, u32[]{:S(2)}, u32[]{:S(2)}) collective-permute-start(bf16[152,1024]{1,0:T(8,128)(2,1)S(1)} %get-tuple-element.28), channel_id=1, source_target_pairs={{0,4},{4,8},{8,12},{12,16},{16,20},{20,24},{24,28},{1,5},{5,9},{9,... | collective-permute-start | bytes 933896 | tf_op jit(solution)/shard_map/ppermute | solution.py:24
  17.2 29.9 %all-to-all-start = ((bf16[8,16,2048]{2,1,0:T(8,128)(2,1)}), bf16[8,16,2048]{2,1,0:T(8,128)(2,1)S(1)}, u32[]{:S(2)}, u32[]{:S(2)}) async-start(bf16[8,16,2048]{2,1,0:T(8,128)(2,1)} %spread.1), calls=%async_computation | async-start | bytes 1048576 | tf_op jit(solution)/shard_map/all_to_all | solution.py:393
  24.0 15.0 %collective-permute-start = (bf16[160,1024]{1,0:T(8,128)(2,1)S(1)}, bf16[160,1024]{1,0:T(8,128)(2,1)S(1)}, u32[]{:S(2)}, u32[]{:S(2)}) collective-permute-start(bf16[160,1024]{1,0:T(8,128)(2,1)S(1)} %get-tuple-element.25), channel_id=1, source_target_pairs={{4,0},{8,4},{12,8},{16,12},{20,16},{24,20},{28,24},{5,1},{9,5},{13... | collective-permute-start | bytes 983048 | tf_op jit(solution)/shard_map/ppermute | solution.py:24
  39.0 21.4 %collective-permute-start.2 = (bf16[160,1024]{1,0:T(8,128)(2,1)S(1)}, bf16[160,1024]{1,0:T(8,128)(2,1)S(1)}, u32[]{:S(2)}, u32[]{:S(2)}) collective-permute-start(bf16[160,1024]{1,0:T(8,128)(2,1)S(1)} %get-tuple-element.27), channel_id=1, source_target_pairs={{4,0},{8,4},{12,8},{16,12},{20,16},{24,20},{28,24},{5,1},{9,5},{13... | collective-permute-start | bytes 983048 | tf_op jit(solution)/shard_map/ppermute | solution.py:24
  40.3 20.1 %collective-permute-start.1 = (bf16[152,1024]{1,0:T(8,128)(2,1)S(1)}, bf16[152,1024]{1,0:T(8,128)(2,1)S(1)}, u32[]{:S(2)}, u32[]{:S(2)}) collective-permute-start(bf16[152,1024]{1,0:T(8,128)(2,1)S(1)} %get-tuple-element.26), channel_id=1, source_target_pairs={{0,4},{4,8},{8,12},{12,16},{16,20},{20,24},{24,28},{1,5},{5,9},{9,... | collective-permute-start | bytes 933896 | tf_op jit(solution)/shard_map/ppermute | solution.py:24
  97.3 16.5 %all-to-all-start.2 = ((bf16[32,24,256]{2,1,0:T(8,128)(2,1)}), bf16[32,24,256]{2,1,0:T(8,128)(2,1)S(1)}, u32[]{:S(2)}, u32[]{:S(2)}) async-start(bf16[32,24,256]{2,1,0:T(8,128)(2,1)} %get-tuple-element.39), calls=%async_computation.2 | async-start | bytes 786432 | tf_op jit(solution)/shard_map/all_to_all | solution.py:415

commit v5 on v4

v5 whole, which is shorter than its diff:
```python
import functools
import math

import jax
import jax.numpy as jnp
import ml_dtypes
import numpy as np
from jax import lax
from jax.experimental import pallas as pl
from jax.experimental.pallas import tpu as pltpu
from jax.sharding import PartitionSpec as P


FK = 7
BF16 = jnp.bfloat16
F32 = jnp.float32
SHORT = 32


def from_behind(value, axis, by):
    count = lax.axis_size(axis)
    pairs = [(i, i + by) for i in range(count) if 0 <= i + by < count]
    return lax.ppermute(value, axis, pairs)


def interleaved(span, first=0, low=0):
    return np.array([first + s * span + r for r in range(low, span) for s in range(8)])


def pick(positions, count):
    out = np.zeros((len(positions), count), np.float32)
    for row, at in enumerate(positions):
        if 0 <= at < count:
            out[row, at] = 1.0
    return out.astype(ml_dtypes.bfloat16)


def halves(matrix):
    high = matrix.astype(np.float32).astype(ml_dtypes.bfloat16)
    low = (matrix - high.astype(np.float64)).astype(np.float32).astype(ml_dtypes.bfloat16)
    return np.stack([high, low])


def analysis(positions, size, pad=0):
    freq = np.arange(size // 2)[:, None]
    angle = np.pi * (((2 * freq + 1) * np.asarray(positions)[None, :]) % (2 * size)) / size
    matrix = np.concatenate([np.cos(angle), -np.sin(angle)], axis=0)
    return halves(np.pad(matrix, ((0, 0), (0, pad))))


def synthesis(positions, size):
    freq = np.arange(size // 2)[None, :]
    angle = np.pi * (((2 * freq + 1) * np.asarray(positions)[:, None]) % (2 * size)) / size
    return halves(np.concatenate([np.cos(angle), -np.sin(angle)], axis=1) * (2.0 / size))


def mm(a, b):
    return jnp.dot(a, b, preferred_element_type=F32)


def picked(span, first, length):
    shape = ((span + FK - 1) * 8, length)
    row, column = (lax.broadcasted_iota(jnp.int32, shape, axis) for axis in (0, 1))
    position = first + (row & 7) * span + (row >> 3) - (FK - 1)
    return jnp.where(position == column, 1.0, 0.0).astype(BF16)


def edges_kernel(proj, cot, short, taps, forward, backward, spread):
    length, width = cot.shape
    tail, head = 16, 17
    p_tail, p_head = picked(tail, length - 128, length), picked(head, 0, length)

    def conv(x, taps, count):
        x = x.reshape(-1, 8, width)
        total = taps[0:1] * x[FK - 1 : FK - 1 + count]
        for lag in range(1, FK):
            total = total + taps[lag : lag + 1] * x[FK - 1 - lag : FK - 1 - lag + count]
        return total

    mixed = conv(mm(p_tail, proj[1]), short[1], tail) * conv(mm(p_tail, proj[2]), short[2], tail)
    ends = [proj[i, length - 16 :, :].astype(F32)[8:] for i in range(3)]
    forward[...] = jnp.concatenate([mixed.reshape(tail * 8, width)] + ends, axis=0).astype(BF16)
    gate = conv(mm(p_head, proj[0]), short[0], head).reshape(head * 8, width)
    grad = gate * mm(p_head[(FK - 1) * 8 :], cot[...])
    starts = [ref[:16, :].astype(F32)[:8] for ref in (cot, proj.at[1], proj.at[2])]
    backward[...] = jnp.concatenate([grad] + starts, axis=0).astype(BF16)
    spread[...] = jnp.broadcast_to(taps[...].astype(BF16)[None], spread.shape)


def conv8(last, first, taps):
    row = lax.broadcasted_iota(jnp.int32, last.shape, 0)
    total = jnp.zeros(last.shape, F32) if first is None else taps[0:1] * first
    for lag in range(1, FK):
        rolled = 0.0 if first is None else pltpu.roll(first, lag, 0)
        total = total + taps[lag : lag + 1] * jnp.where(row < lag, pltpu.roll(last, lag, 0), rolled)
    return total


def own_kernel(proj, cot, short, taps, decay, e_own, e_taps, p_in, feat, px, cots, m_part, g_part, k_spec):
    length, width = cot.shape
    span = length // 8
    edge = FK - 1
    lags = lax.broadcasted_iota(jnp.int32, (taps.shape[0], width), 0).astype(F32)
    kernel = taps[...].astype(F32) * jnp.exp(-decay[...] * lags)
    high = kernel.astype(BF16)
    low = (kernel - high.astype(F32)).astype(BF16)
    k_spec[...] = mm(e_taps[...], jnp.concatenate([high, high, low], axis=0))

    step = 8
    for i in range(3):
        x = mm(p_in[...], proj[i])
        px[i] = x[edge * 8 :].astype(BF16)
        x = x.reshape(span + edge, 8, width)
        for at in range(0, width, 128):
            lane = slice(at, at + 128)
            weights = [jnp.broadcast_to(short[i, lag : lag + 1, lane], (8, 128)) for lag in range(FK)]
            for r in range(0, span, step):
                total = weights[0] * x[r + edge : r + edge + step, :, lane]
                for lag in range(1, FK):
                    total = total + weights[lag] * x[r + edge - lag : r + edge - lag + step, :, lane]
                feat[i, r * 8 : (r + step) * 8, lane] = total.reshape(step * 8, 128)
    moved = mm(p_in[edge * 8 :, :], cot[...])
    cots[...] = moved.astype(BF16)
    mixed = (feat[1] * feat[2]).astype(BF16)
    m_part[...] = mm(e_own[...], jnp.concatenate([mixed, mixed], axis=0))
    grad = (moved * feat[0]).astype(BF16)
    g_part[...] = mm(e_own[...], jnp.concatenate([grad, grad], axis=0))


def finish_kernel(
    prev, later, feat, px, cots, m_part, g_part, k_spec, ends, starts, short, decay,
    e_prev, e_next, e_first, s_own, s_lags,
    product, grad, sums_out, filter_held, short_held, done,
):
    length, width = cots.shape
    span = length // 8
    edge = FK - 1
    step, steps = pl.program_id(0), pl.num_programs(0)
    row8 = lax.broadcasted_iota(jnp.int32, (8, width), 0)
    before = prev[...].astype(F32)
    after = later[...].astype(F32)
    prev8 = [before[128 + 8 * i : 136 + 8 * i] for i in range(3)]
    cot_next = after[136:144]
    next8 = [None, after[144:152], after[152:160]]
    ends8 = [ends[i].astype(F32)[8:] for i in range(3)]
    cot_first = starts[...].astype(F32)[:8]

    fixes = [conv8(prev8[i], None, short[i]) for i in range(3)]
    heads = []
    for i in range(3):
        rows, natural = [], jnp.zeros((8, width), F32)
        for r in range(edge):
            part = feat[i, 8 * r : 8 * r + 8, :]
            natural = natural + jnp.where(row8 == r, pltpu.roll(part, r, 0) if r else part, 0.0)
            moved = pltpu.roll(fixes[i], 8 - r, 0) if r else fixes[i]
            rows.append(part + jnp.where(row8 == 0, moved, 0.0))
        heads.append((jnp.concatenate(rows, axis=0), natural))
    features = lambda i: jnp.concatenate([heads[i][0], feat[i, edge * 8 :, :]], axis=0)
    inside = row8 < edge
    (first1, first2), (fix1, fix2) = (heads[1][1], heads[2][1]), fixes[1:]
    mixed_fix = jnp.where(inside, (first1 + fix1) * (first2 + fix2) - first1 * first2, 0.0)
    grad_fix = jnp.where(inside, cot_first * fixes[0], 0.0)

    feat_next = [None] + [conv8(ends8[i], next8[i], short[i]) for i in (1, 2)]
    fix = cot_next * conv8(ends8[0], None, short[0])
    rows = [after[8 * r : 8 * r + 8] for r in range(17)]
    for r in range(edge):
        rows[r] = rows[r] + jnp.where(row8 == 0, pltpu.roll(fix, (8 - r) % 8, 0), 0.0)
    grad_edge = jnp.concatenate(rows + [grad_fix], axis=0).astype(BF16)
    mixed_edge = jnp.concatenate([before[:128], feat_next[1] * feat_next[2], mixed_fix], axis=0).astype(BF16)
    grad_first = jnp.concatenate([grad_fix, jnp.zeros((8, width), F32)], axis=0).astype(BF16)

    m_spec = m_part[...] + mm(e_prev[...], mixed_edge)
    g_own = g_part[...] + mm(e_first[...], grad_first)
    g_spec = g_part[...] + mm(e_next[...], grad_edge)

    half = k_spec.shape[0] // 2
    parts = lambda value: (value[:half], value[half:])
    (kr, ki), (mr, mi), (gr, gi), (hr, hi) = parts(k_spec[...]), parts(m_spec), parts(g_spec), parts(g_own)

    def back_to(matrix, real, imaginary):
        spectrum = jnp.concatenate([real, imaginary], axis=0).astype(BF16)
        return mm(matrix[...], jnp.concatenate([spectrum, spectrum], axis=0))

    filtered = back_to(s_own, mr * kr - mi * ki, mr * ki + mi * kr)
    grad_mixed = back_to(s_own, gr * kr + gi * ki, gi * kr - gr * ki)
    filter_sums = back_to(s_lags, hr * mr + hi * mi, hi * mr - hr * mi)
    lags = lax.broadcasted_iota(jnp.int32, filter_sums.shape, 0).astype(F32)
    filter_sums = filter_sums * jnp.exp(-decay[...] * lags)

    own, back = filtered[:length], grad_mixed[:length]
    product[...] = (features(0) * own).astype(BF16)
    grad[0, :length] = cots[...].astype(F32) * own
    grad[1, :length] = back * features(2)
    grad[2, :length] = back * features(1)
    back_next = grad_mixed[length:]
    edge_next = [cot_next * filtered[length:], back_next * feat_next[2], back_next * feat_next[1]]
    for i in range(3):
        for k in range(edge):
            at = length + 8 * k
            moved = pltpu.roll(grad[i, 8 * k : 8 * k + 8, :], 7, 0)
            grad[i, at : at + 8, :] = jnp.where(row8 == 7, pltpu.roll(edge_next[i], 7 - k, 0), moved)

    short_rows = []
    chunk = 64
    for i in range(3):
        rows = [[] for _ in range(FK)]
        for at in range(0, width, 128):
            lane = slice(at, at + 128)
            sums = [jnp.zeros((8, 128), F32)] * FK
            for r in range(0, length, chunk):
                here = px[i, r : r + chunk, lane].astype(F32).reshape(chunk // 8, 8, 128)
                for lag in range(FK):
                    value = grad[i, r + 8 * lag : r + 8 * lag + chunk, lane].reshape(chunk // 8, 8, 128)
                    sums[lag] = sums[lag] + jnp.sum(here * value, axis=0)
            for lag in range(FK):
                rows[lag].append(jnp.sum(sums[lag], axis=0, keepdims=True))
        short_rows += [jnp.concatenate(row, axis=1) for row in rows]

    ranks, slot, _ = filter_held.shape
    per, share = filter_sums.shape[0] // ranks, short_held.shape[0]
    copies = [
        pltpu.make_async_copy(
            filter_held, sums_out.at[:, pl.ds(pl.multiple_of(step * slot, slot), slot), :], done.at[0]
        ),
        pltpu.make_async_copy(
            short_held,
            sums_out.at[pl.ds(step * share, share), pl.ds(sums_out.shape[1] - SHORT, SHORT), :],
            done.at[1],
        ),
    ]

    @pl.when(step > 0)
    def _():
        for copy in copies:
            copy.wait()

    if per % 8 == 0:
        by_rank = filter_sums.reshape(ranks, per, width)
    else:
        by_rank = jnp.stack([filter_sums[rank * per : rank * per + per] for rank in range(ranks)])
    if slot > per:
        by_rank = jnp.concatenate([by_rank, jnp.zeros((ranks, slot - per, width), F32)], axis=1)
    filter_held[...] = by_rank.astype(BF16)
    sums = jnp.concatenate(short_rows + [jnp.zeros((SHORT - len(short_rows), width), F32)], axis=0)
    for rank in range(share):
        held = pltpu.roll(sums, width - rank * (width // share), 1) if rank else sums
        short_held[rank] = held.astype(BF16)
    for copy in copies:
        copy.start()

    @pl.when(step == steps - 1)
    def _():
        for copy in copies:
            copy.wait()


def outputs_kernel(product, grad, short, p_out, gated, grad_proj):
    length, width = product.shape
    gated[...] = mm(p_out[...], product[...]).astype(BF16)
    chunk = 64
    for i in range(3):
        columns = []
        for at in range(0, width, 128):
            lane = slice(at, at + 128)
            weights = [jnp.broadcast_to(short[i, lag : lag + 1, lane], (8, 128)) for lag in range(FK)]
            chunks = []
            for r in range(0, length, chunk):
                total = jnp.zeros((chunk // 8, 8, 128), F32)
                for lag in range(FK):
                    value = grad[i, r + 8 * lag : r + 8 * lag + chunk, lane].reshape(chunk // 8, 8, 128)
                    total = total + weights[lag] * value
                chunks.append(total.reshape(chunk, 128))
            columns.append(jnp.concatenate(chunks, axis=0))
        result = jnp.concatenate(columns, axis=1).astype(BF16)
        grad_proj[i] = mm(p_out[...], result).astype(BF16)


def whole(array):
    return pl.BlockSpec(array.shape, lambda c: (0,) * array.ndim)


def columns(rows, width, first=0):
    lead = (0,) * len(rows)
    return pl.BlockSpec(tuple(rows) + (width,), lambda c: lead + (first + c,))


def call(kernel, name, operands, outputs, width, constants=(), cost=1, **options):
    spec = lambda rows: rows if isinstance(rows, pl.BlockSpec) else columns(rows, width)
    constants = [pltpu.with_memory_space_constraint(jnp.asarray(constant), pltpu.HBM) for constant in constants]
    operands = [
        (pltpu.with_memory_space_constraint(array, pltpu.HBM) if array.dtype == F32 else array, rows)
        for array, rows in operands
    ]
    return pl.pallas_call(
        kernel,
        grid=(operands[0][0].shape[-1] // width,),
        in_specs=[spec(rows) for _, rows in operands] + [whole(constant) for constant in constants],
        out_specs=[spec(rows) for _, rows in outputs],
        out_shape=[shape for shape, _ in outputs],
        compiler_params=pltpu.CompilerParams(vmem_limit_bytes=40 << 20),
        cost_estimate=pl.CostEstimate(flops=cost * 10**9, bytes_accessed=10**6, transcendentals=0),
        name=name,
        **options,
    )(*[array for array, _ in operands], *constants)


def squares_kernel(rows, share, sums, raw, payload):
    ranks, slots, width = sums.shape
    total = sums[0].astype(F32)
    for rank in range(1, ranks):
        total = total + sums[rank].astype(F32)
    slot = -(-rows // 16) * 16
    pieces = [total[at : at + rows] for at in range(0, slots - SHORT, slot)]
    raw[...] = jnp.concatenate(pieces, axis=1)
    lane = lax.broadcasted_iota(jnp.int32, (SHORT, width), 1)
    short = jnp.where(lane < share, total[slots - SHORT :], 0.0)
    squares = jnp.sum(short * short, keepdims=True)
    for piece in pieces:
        squares = squares + jnp.sum(piece * piece, keepdims=True)
    high = squares.astype(BF16).astype(F32)
    row = lax.broadcasted_iota(jnp.int32, (24, width), 0)
    block = jnp.where(row < 3 * FK, short[:24], jnp.where(row == 3 * FK, high, squares - high)).astype(BF16)
    for other in range(payload.shape[0]):
        payload[other] = block


def scale_kernel(entries, share, mine, raw, gathered, grad_short, grad_filter):
    everyone, rows, width = gathered.shape
    total = jnp.zeros((8, width), F32)
    for other in range(everyone):
        total = total + gathered[other].astype(F32)[16:]
    total = total[5:6, :1] + total[6:7, :1]
    scale = jnp.minimum(1.0, math.sqrt(entries) / jnp.sqrt(total))
    grad_filter[...] = scale * raw[...]
    step = mine[1]
    for rank in range(raw.shape[1] // share):
        block = gathered[rank * step + mine[0]].astype(F32) * scale
        for i in range(3):
            grad_short[i, :, rank * share : (rank + 1) * share] = block[i * FK : (i + 1) * FK, :share]


def shards(projected, short_taps, filter_taps, decay, cotangent):
    length, _, channels = projected.shape
    ranks, groups = lax.axis_size("seq"), lax.axis_size("ch")
    rows = filter_taps.shape[0]
    count = rows * ranks
    width = min(256, channels)
    share = channels // ranks
    slot = -(-rows // 16) * 16
    size, span = 2 * length, length // 8
    extended = length + 8 * (FK - 1)
    proj, cot, short, decay = (
        pltpu.with_memory_space_constraint(array, pltpu.HBM)
        for array in (jnp.transpose(projected, (1, 0, 2)), cotangent, short_taps, decay[None])
    )
    floats = lambda *shape: pltpu.HBM(shape + (channels,), F32)
    halves_of = lambda *shape: jax.ShapeDtypeStruct(shape + (channels,), BF16)
    own = interleaved(span)
    after = length + np.arange(8)

    forward, backward, spread = call(
        edges_kernel, "edges",
        [(proj, (3, length)), (cot, (length,)), (short, (3, FK)), (filter_taps, (rows,))],
        [
            (halves_of(152), (152,)), (halves_of(160), (160,)),
            (pltpu.HBM((ranks, rows, channels), BF16), (ranks, rows)),
        ],
        width, cost=3,
    )
    taps = lax.all_to_all(spread, "seq", 0, 0).reshape(count, channels)
    prev = from_behind(forward, "seq", 1)
    later = from_behind(backward, "seq", -1)

    e_high, e_low = analysis(own, size)
    k_high, k_low = analysis(np.arange(count), size)
    feat, px, cots, m_part, g_part, k_spec = call(
        own_kernel, "own",
        [(proj, (3, length)), (cot, (length,)), (short, (3, FK)), (taps, (count,)), (decay, (1,))],
        [
            (floats(3, length), (3, length)), (halves_of(3, length), (3, length)), (halves_of(length), (length,)),
            (floats(size), (size,)), (floats(size), (size,)), (floats(size), (size,)),
        ],
        width,
        [
            np.concatenate([e_high, e_low], axis=1), np.concatenate([k_high, k_low, k_high], axis=1),
            pick(interleaved(span, 0, 1 - FK), length),
        ],
        cost=10,
    )

    s_own = synthesis(np.concatenate([own, after]), size)
    s_lags = synthesis(np.arange(count), size)
    product, grad, sums = call(
        finish_kernel, "finish",
        [
            (prev, (152,)), (later, (160,)), (feat, (3, length)), (px, (3, length)), (cots, (length,)),
            (m_part, (size,)), (g_part, (size,)), (k_spec, (size,)),
            (proj, pl.BlockSpec((3, 16, width), lambda c: (0, length // 16 - 1, c))), (cot, (16,)),
            (short, (3, FK)), (decay, (1,)),
        ],
        [
            (halves_of(length), (length,)), (floats(3, extended), (3, extended)),
            (pltpu.HBM((ranks, channels // width * slot + SHORT, width), BF16), pl.BlockSpec(memory_space=pl.ANY)),
        ],
        width,
        [
            analysis(np.concatenate([interleaved(16, -128), after, np.arange(8)]), size)[0],
            analysis(np.concatenate([interleaved(17, length), np.arange(8)]), size)[0],
            analysis(np.arange(8), size, 8)[0],
            np.concatenate(list(s_own), axis=1), np.concatenate(list(s_lags), axis=1),
        ],
        cost=12,
        scratch_shapes=[
            pltpu.VMEM((ranks, slot, width), BF16),
            pltpu.VMEM((ranks * width // channels, SHORT, width), BF16),
            pltpu.SemaphoreType.DMA((2,)),
        ],
    )
    gated, grad_proj = call(
        outputs_kernel, "outputs",
        [(product, (length,)), (grad, (3, extended)), (short, (3, FK))],
        [(halves_of(length), (length,)), (halves_of(3, length), (3, length))],
        width, [pick(own, length).T], cost=8,
    )
    sums, gated, grad_proj = lax.optimization_barrier((lax.all_to_all(sums, "seq", 0, 0), gated, grad_proj))

    vmem = pl.BlockSpec(memory_space=pltpu.VMEM)
    raw, payload = pl.pallas_call(
        functools.partial(squares_kernel, rows, share),
        in_specs=[vmem],
        out_specs=[vmem] * 2,
        out_shape=[
            jax.ShapeDtypeStruct((rows, channels), F32),
            jax.ShapeDtypeStruct((ranks * groups, 24, width), BF16),
        ],
        compiler_params=pltpu.CompilerParams(vmem_limit_bytes=32 << 20),
        name="squares",
    )(sums)
    gathered = lax.all_to_all(payload, ("seq", "ch"), 0, 0)
    mine = jnp.stack([lax.axis_index("ch"), jnp.int32(groups)])
    entries = (rows * ranks + 3 * FK) * channels * groups
    grad_short, grad_filter = pl.pallas_call(
        functools.partial(scale_kernel, entries, share),
        in_specs=[pl.BlockSpec(memory_space=pltpu.SMEM), vmem, vmem],
        out_specs=[vmem] * 2,
        out_shape=[
            jax.ShapeDtypeStruct((3, FK, channels), F32),
            jax.ShapeDtypeStruct((rows, channels), F32),
        ],
        compiler_params=pltpu.CompilerParams(vmem_limit_bytes=32 << 20),
        name="scale",
    )(mine, raw, gathered)
    return (gated, jnp.transpose(grad_proj, (1, 0, 2)), grad_short, grad_filter)


def solution(mesh):
    placed = (P("seq", None, "ch"), P(None, None, "ch"), P("seq", "ch"), P("ch"), P("seq", "ch"))
    return jax.shard_map(
        shards,
        mesh=mesh,
        in_specs=placed,
        out_specs=(P("seq", "ch"), P("seq", None, "ch"), P(None, None, "ch"), P("seq", "ch")),
        check_vma=False,
    )
```

time: 116 us -> 110 us (0.948)
  blocking collectives: 22.7 us -> 0 us
  Pallas kernels: 37.4 us -> 48.6 us
  waiting for transfers between devices: 30 us -> 36.7 us
  starting transfers between devices: 24.3 us -> 23.1 us
    all_to_all x1 -> x0, blocking collectives: 22.7 us -> none  [shards(): sums = lax.all_to_all(sums, 'seq', 0, 0)]
    all_to_all x1 -> x2, waiting for transfers between devices: 0.01 us -> 18.2 us  [the longest x1 10.1 us: shards(): taps = lax.all_to_all(spread, 'seq', 0, 0).reshape(count, channels)]
    ppermute x4 -> x2, waiting for transfers between devices: 16.9 us -> 5.4 us  [from_behind(): return lax.ppermute(value, axis, pairs)]
    pallas_call x5 -> x4, Pallas kernels: 35 us -> 46.3 us  [call(): pl.pallas_call(kernel, grid=(operands[0][0].shape[-1] // width,), in_spec...]
    ppermute x4 -> x2, starting transfers between devices: 14.3 us -> 5.87 us  [from_behind(): return lax.ppermute(value, axis, pairs)]
    all_to_all x1 -> x2, starting transfers between devices: 6.8 us -> 13.6 us  [the longest x1 7.28 us: shards(): taps = lax.all_to_all(spread, 'seq', 0, 0).reshape(count, channels)]
  transfers between devices with their start and end apart: 6 -> 5, of which waited for: 3 -> 4; matrix products, arithmetic and copies ran while one was open for 0% -> 0% of each run, Pallas kernels for 14% -> 20%
where the time goes in v5:
time: 110 us; the launch traced here: 109 us
  Pallas kernels  48.6 us (44%)
  waiting for transfers between devices  36.7 us (33%)
  starting transfers between devices  23.1 us (21%)
    pallas_call x4, Pallas kernels, call(): pl.pallas_call(kernel, grid=(operands[0][0].shape[-1] // width,), in_spec...  46.3 us
    all_to_all x1, waiting for transfers between devices, shards(): gathered = lax.all_to_all(payload, ('seq', 'ch'), 0, 0)  13.1 us
    all_to_all x1, waiting for transfers between devices, shards(): taps = lax.all_to_all(spread, 'seq', 0, 0).reshape(count, channels)  10.1 us
    all_to_all x1, waiting for transfers between devices, shards(): lax.all_to_all(sums, 'seq', 0, 0)  8.09 us
    all_to_all x1, starting transfers between devices, shards(): taps = lax.all_to_all(spread, 'seq', 0, 0).reshape(count, channels)  7.28 us
    all_to_all x1, starting transfers between devices, shards(): lax.all_to_all(sums, 'seq', 0, 0)  6.28 us
    ppermute x2, starting transfers between devices, from_behind(): return lax.ppermute(value, axis, pairs)  5.87 us
    ppermute x2, waiting for transfers between devices, from_behind(): return lax.ppermute(value, axis, pairs)  5.4 us
  transfers between devices with their start and end apart: 5, of which 4 were waited for; matrix products, arithmetic and copies ran while one was open for 0% of the time, Pallas kernels for 20%

profile of v5, /device:TPU:0, one launch (start us, length us, event | category | flops | bytes accessed | tf_op | source)
XLA Modules:
  0.0 109.1 jit_solution(14077681550246925876)
XLA Ops:
  0.6 7.3 %edges.1 = (bf16[152,2048]{1,0:T(8,128)(2,1)S(1)}, bf16[160,2048]{1,0:T(8,128)(2,1)S(1)}, bf16[8,16,2048]{2,1,0:T(8,128)(2,1)}) custom-call(bf16[3,256,2048]{2,1,0:T(8,128)(2,1)} %bitcast.6, bf16[256,2048]{1,0:T(8,128)(2,1)} %starts.1, f32[3,7,2048]{2,1,0:T(8,128)} %short.7, f32[16,2048]{1,0:T(8,128)} %taps.1), custom_call_target="tpu_custom_call" | custom-call | flops 3000000000 | bytes 1000000 | tf_op jit(solution)/shard_map/edges/pallas_call | solution.py:295
  7.9 7.3 %all-to-all-start = ((bf16[8,16,2048]{2,1,0:T(8,128)(2,1)}), bf16[8,16,2048]{2,1,0:T(8,128)(2,1)S(1)}, u32[]{:S(2)}, u32[]{:S(2)}) async-start(bf16[8,16,2048]{2,1,0:T(8,128)(2,1)} %get-tuple-element.27), calls=%async_computation | async-start | bytes 1048576 | tf_op jit(solution)/shard_map/all_to_all | solution.py:371
  15.2 1.3 %collective-permute-start.1 = (bf16[160,2048]{1,0:T(8,128)(2,1)S(1)}, bf16[160,2048]{1,0:T(8,128)(2,1)S(1)}, u32[]{:S(2)}, u32[]{:S(2)}) collective-permute-start(bf16[160,2048]{1,0:T(8,128)(2,1)S(1)} %get-tuple-element.26), channel_id=1, source_target_pairs={{4,0},{8,4},{12,8},{16,12},{20,16},{24,20},{28,24},{5,1},{9,5},{13... | collective-permute-start | bytes 1966088 | tf_op jit(solution)/shard_map/ppermute | solution.py:23
  16.5 4.6 %collective-permute-start = (bf16[152,2048]{1,0:T(8,128)(2,1)S(1)}, bf16[152,2048]{1,0:T(8,128)(2,1)S(1)}, u32[]{:S(2)}, u32[]{:S(2)}) collective-permute-start(bf16[152,2048]{1,0:T(8,128)(2,1)S(1)} %get-tuple-element.25), channel_id=1, source_target_pairs={{0,4},{4,8},{8,12},{12,16},{16,20},{20,24},{24,28},{1,5},{5,9},{9,... | collective-permute-start | bytes 1867784 | tf_op jit(solution)/shard_map/ppermute | solution.py:23
  21.1 10.1 %all-to-all-done = bf16[8,16,2048]{2,1,0:T(8,128)(2,1)S(1)} async-done(((bf16[8,16,2048]{2,1,0:T(8,128)(2,1)}), bf16[8,16,2048]{2,1,0:T(8,128)(2,1)S(1)}, u32[]{:S(2)}, u32[]{:S(2)}) %all-to-all-start) | async-done | bytes 524320 | tf_op jit(solution)/shard_map/all_to_all | solution.py:371
  31.1 12.8 %own.1 = (f32[3,256,2048]{2,1,0:T(8,128)}, bf16[3,256,2048]{2,1,0:T(8,128)(2,1)S(1)}, bf16[256,2048]{1,0:T(8,128)(2,1)S(1)}, f32[512,2048]{1,0:T(8,128)}, f32[512,2048]{1,0:T(8,128)}, /*index=5*/f32[512,2048]{1,0:T(8,128)}) custom-call(bf16[3,256,2048]{2,1,0:T(8,128)(2,1)} %bitcast.7, bf16[256,2048]{1,0:T(8,128)(2,1)} %starts.1, f32[3,7,2048]{2,1,0:T(8,128)} %short.7, ...), custom_call_target="tpu_custom_call" | custom-call | flops 10000000000 | bytes 1000000 | tf_op jit(solution)/shard_map/own/pallas_call | solution.py:295
  43.9 5.4 %collective-permute-done.prev = bf16[152,2048]{1,0:T(8,128)(2,1)S(1)} collective-permute-done((bf16[152,2048]{1,0:T(8,128)(2,1)S(1)}, bf16[152,2048]{1,0:T(8,128)(2,1)S(1)}, u32[]{:S(2)}, u32[]{:S(2)}) %collective-permute-start) | collective-permute-done | bytes 622624 | tf_op jit(solution)/shard_map/ppermute | solution.py:23
  49.3 0.0 collective-permute-done.1.later
  49.3 17.2 %finish.1 = (bf16[256,2048]{1,0:T(8,128)(2,1)S(1)}, f32[3,304,2048]{2,1,0:T(8,128)}, bf16[8,160,256]{2,1,0:T(8,128)(2,1)}) custom-call(bf16[152,2048]{1,0:T(8,128)(2,1)S(1)} %collective-permute-done.prev, bf16[160,2048]{1,0:T(8,128)(2,1)S(1)} %collective-permute-done.1.later, f32[3,256,2048]{2,1,0:T(8,128)} %get-tuple-element.28.feat, ...), custom_call_target="tpu_custom_call" | custom-call | flops 12000000000 | bytes 1000000 | tf_op jit(solution)/shard_map/finish/pallas_call | solution.py:295
  66.5 6.3 %all-to-all-start.1 = ((bf16[8,160,256]{2,1,0:T(8,128)(2,1)}), bf16[8,160,256]{2,1,0:T(8,128)(2,1)S(1)}, u32[]{:S(2)}, u32[]{:S(2)}) async-start(bf16[8,160,256]{2,1,0:T(8,128)(2,1)} %get-tuple-element.34), calls=%async_computation.1 | async-start | bytes 1310720 | tf_op jit(solution)/shard_map/all_to_all | solution.py:426
  72.8 9.1 %outputs.1 = (bf16[256,2048]{1,0:T(8,128)(2,1)}, bf16[3,256,2048]{2,1,0:T(8,128)(2,1)}) custom-call(bf16[256,2048]{1,0:T(8,128)(2,1)S(1)} %get-tuple-element.35.product, f32[3,304,2048]{2,1,0:T(8,128)} %get-tuple-element.36.grad, f32[3,7,2048]{2,1,0:T(8,128)} %short.7, bf16[256,256]{1,0:T(8,128)(2,1)} %constant.32.clone.p_out), custom_call_target="tpu_custom_call" | custom-call | flops 8000000000 | bytes 1000000 | tf_op jit(solution)/shard_map/outputs/pallas_call | solution.py:295
  81.8 8.1 %all-to-all-done.1.sums = bf16[8,160,256]{2,1,0:T(8,128)(2,1)S(1)} async-done(((bf16[8,160,256]{2,1,0:T(8,128)(2,1)}), bf16[8,160,256]{2,1,0:T(8,128)(2,1)S(1)}, u32[]{:S(2)}, u32[]{:S(2)}) %all-to-all-start.1) | async-done | bytes 655392 | tf_op jit(solution)/shard_map/all_to_all | solution.py:426
  89.9 1.0 squares.1
  90.9 3.7 %all-to-all-start.2 = ((bf16[32,24,256]{2,1,0:T(8,128)(2,1)}), bf16[32,24,256]{2,1,0:T(8,128)(2,1)S(1)}, u32[]{:S(2)}, u32[]{:S(2)}) async-start(bf16[32,24,256]{2,1,0:T(8,128)(2,1)} %get-tuple-element.43), calls=%async_computation.2 | async-start | bytes 786432 | tf_op jit(solution)/shard_map/all_to_all | solution.py:440
  94.6 0.1 pad_add_fusion.mine
  94.7 13.1 %all-to-all-done.2.gathered = bf16[32,24,256]{2,1,0:T(8,128)(2,1)S(1)} async-done(((bf16[32,24,256]{2,1,0:T(8,128)(2,1)}), bf16[32,24,256]{2,1,0:T(8,128)(2,1)S(1)}, u32[]{:S(2)}, u32[]{:S(2)}) %all-to-all-start.2) | async-done | bytes 393248 | tf_op jit(solution)/shard_map/all_to_all | solution.py:440
  107.8 1.4 %scale.1 = (f32[3,7,2048]{2,1,0:T(8,128)}, f32[16,2048]{1,0:T(8,128)}) custom-call(s32[2]{0:T(128)S(1)} %pad_add_fusion.mine, f32[16,2048]{1,0:T(8,128)S(1)} %get-tuple-element.42.raw, bf16[32,24,256]{2,1,0:T(8,128)(2,1)S(1)} %all-to-all-done.2.gathered), custom_call_target="tpu_custom_call" | custom-call | tf_op jit(solution)/shard_map/scale/pallas_call | solution.py:443
Async XLA Ops:
  7.9 23.2 %all-to-all-start = ((bf16[8,16,2048]{2,1,0:T(8,128)(2,1)}), bf16[8,16,2048]{2,1,0:T(8,128)(2,1)S(1)}, u32[]{:S(2)}, u32[]{:S(2)}) async-start(bf16[8,16,2048]{2,1,0:T(8,128)(2,1)} %get-tuple-element.27), calls=%async_computation | async-start | bytes 1048576 | tf_op jit(solution)/shard_map/all_to_all | solution.py:371
  15.2 34.1 %collective-permute-start.1 = (bf16[160,2048]{1,0:T(8,128)(2,1)S(1)}, bf16[160,2048]{1,0:T(8,128)(2,1)S(1)}, u32[]{:S(2)}, u32[]{:S(2)}) collective-permute-start(bf16[160,2048]{1,0:T(8,128)(2,1)S(1)} %get-tuple-element.26), channel_id=1, source_target_pairs={{4,0},{8,4},{12,8},{16,12},{20,16},{24,20},{28,24},{5,1},{9,5},{13... | collective-permute-start | bytes 1966088 | tf_op jit(solution)/shard_map/ppermute | solution.py:23
  16.5 32.9 %collective-permute-start = (bf16[152,2048]{1,0:T(8,128)(2,1)S(1)}, bf16[152,2048]{1,0:T(8,128)(2,1)S(1)}, u32[]{:S(2)}, u32[]{:S(2)}) collective-permute-start(bf16[152,2048]{1,0:T(8,128)(2,1)S(1)} %get-tuple-element.25), channel_id=1, source_target_pairs={{0,4},{4,8},{8,12},{12,16},{16,20},{20,24},{24,28},{1,5},{5,9},{9,... | collective-permute-start | bytes 1867784 | tf_op jit(solution)/shard_map/ppermute | solution.py:23
  66.5 23.4 %all-to-all-start.1 = ((bf16[8,160,256]{2,1,0:T(8,128)(2,1)}), bf16[8,160,256]{2,1,0:T(8,128)(2,1)S(1)}, u32[]{:S(2)}, u32[]{:S(2)}) async-start(bf16[8,160,256]{2,1,0:T(8,128)(2,1)} %get-tuple-element.34), calls=%async_computation.1 | async-start | bytes 1310720 | tf_op jit(solution)/shard_map/all_to_all | solution.py:426
  90.9 16.8 %all-to-all-start.2 = ((bf16[32,24,256]{2,1,0:T(8,128)(2,1)}), bf16[32,24,256]{2,1,0:T(8,128)(2,1)S(1)}, u32[]{:S(2)}, u32[]{:S(2)}) async-start(bf16[32,24,256]{2,1,0:T(8,128)(2,1)} %get-tuple-element.43), calls=%async_computation.2 | async-start | bytes 786432 | tf_op jit(solution)/shard_map/all_to_all | solution.py:440

commit v6 on v5

--- a/solution.py
+++ b/solution.py
@@ -14,6 +14,7 @@
 FK = 7
 BF16 = jnp.bfloat16
 F32 = jnp.float32
+CHUNKS = 2
 SHORT = 32
 
 
@@ -65,10 +66,17 @@
     return jnp.where(position == column, 1.0, 0.0).astype(BF16)
 
 
-def edges_kernel(proj, cot, short, taps, forward, backward, spread):
+def edges_kernel(proj, cot, short, *refs):
+    forward, backward = refs[-4:-2]
+    p_tail, p_head = refs[-2:]
     length, width = cot.shape
     tail, head = 16, 17
-    p_tail, p_head = picked(tail, length - 128, length), picked(head, 0, length)
+
+    @pl.when(pl.program_id(0) == 0)
+    def _():
+        p_tail[...] = picked(tail, length - 128, length)
+        p_head[...] = picked(head, 0, length)
+
 
     def conv(x, taps, count):
         x = x.reshape(-1, 8, width)
@@ -77,14 +85,16 @@
             total = total + taps[lag : lag + 1] * x[FK - 1 - lag : FK - 1 - lag + count]
         return total
 
-    mixed = conv(mm(p_tail, proj[1]), short[1], tail) * conv(mm(p_tail, proj[2]), short[2], tail)
+    mixed = conv(mm(p_tail[...], proj[1]), short[1], tail) * conv(mm(p_tail[...], proj[2]), short[2], tail)
     ends = [proj[i, length - 16 :, :].astype(F32)[8:] for i in range(3)]
     forward[...] = jnp.concatenate([mixed.reshape(tail * 8, width)] + ends, axis=0).astype(BF16)
-    gate = conv(mm(p_head, proj[0]), short[0], head).reshape(head * 8, width)
-    grad = gate * mm(p_head[(FK - 1) * 8 :], cot[...])
+    gate = conv(mm(p_head[...], proj[0]), short[0], head).reshape(head * 8, width)
+    grad = gate * mm(p_head[(FK - 1) * 8 :, :], cot[...])
     starts = [ref[:16, :].astype(F32)[:8] for ref in (cot, proj.at[1], proj.at[2])]
     backward[...] = jnp.concatenate([grad] + starts, axis=0).astype(BF16)
-    spread[...] = jnp.broadcast_to(taps[...].astype(BF16)[None], spread.shape)
+    if len(refs) > 4:
+        taps, spread = refs[:2]
+        spread[...] = jnp.broadcast_to(taps[...].astype(BF16)[None], spread.shape)
 
 
 def conv8(last, first, taps):
@@ -96,16 +106,10 @@
     return total
 
 
-def own_kernel(proj, cot, short, taps, decay, e_own, e_taps, p_in, feat, px, cots, m_part, g_part, k_spec):
+def own_kernel(proj, cot, short, e_own, p_in, feat, px, cots, m_part, g_part):
     length, width = cot.shape
     span = length // 8
     edge = FK - 1
-    lags = lax.broadcasted_iota(jnp.int32, (taps.shape[0], width), 0).astype(F32)
-    kernel = taps[...].astype(F32) * jnp.exp(-decay[...] * lags)
-    high = kernel.astype(BF16)
-    low = (kernel - high.astype(F32)).astype(BF16)
-    k_spec[...] = mm(e_taps[...], jnp.concatenate([high, high, low], axis=0))
-
     step = 8
     for i in range(3):
         x = mm(p_in[...], proj[i])
@@ -128,10 +132,10 @@
 
 
 def finish_kernel(
-    prev, later, feat, px, cots, m_part, g_part, k_spec, ends, starts, short, decay,
-    e_prev, e_next, e_first, s_own, s_lags,
-    product, grad, sums_out, filter_held, short_held, done,
+    first, prev, later, feat, px, cots, m_part, g_part, taps, ends, starts, short, decay,
+    e_prev, e_next, e_first, e_taps, s_own, s_lags, *refs,
 ):
+    product, grad, sums_out, filter_held, short_held, done = refs[-6:]
     length, width = cots.shape
     span = length // 8
     edge = FK - 1
@@ -174,9 +178,16 @@
     g_own = g_part[...] + mm(e_first[...], grad_first)
     g_spec = g_part[...] + mm(e_next[...], grad_edge)
 
+    lags = lax.broadcasted_iota(jnp.int32, (taps.shape[0], width), 0).astype(F32)
+    falloff = jnp.exp(-decay[...] * lags)
+    kernel = taps[...].astype(F32) * falloff
+    high = kernel.astype(BF16)
+    low = (kernel - high.astype(F32)).astype(BF16)
+    k_spec = mm(e_taps[...], jnp.concatenate([high, high, low], axis=0))
+
     half = k_spec.shape[0] // 2
     parts = lambda value: (value[:half], value[half:])
-    (kr, ki), (mr, mi), (gr, gi), (hr, hi) = parts(k_spec[...]), parts(m_spec), parts(g_spec), parts(g_own)
+    (kr, ki), (mr, mi), (gr, gi), (hr, hi) = parts(k_spec), parts(m_spec), parts(g_spec), parts(g_own)
 
     def back_to(matrix, real, imaginary):
         spectrum = jnp.concatenate([real, imaginary], axis=0).astype(BF16)
@@ -184,9 +195,7 @@
 
     filtered = back_to(s_own, mr * kr - mi * ki, mr * ki + mi * kr)
     grad_mixed = back_to(s_own, gr * kr + gi * ki, gi * kr - gr * ki)
-    filter_sums = back_to(s_lags, hr * mr + hi * mi, hi * mr - hr * mi)
-    lags = lax.broadcasted_iota(jnp.int32, filter_sums.shape, 0).astype(F32)
-    filter_sums = filter_sums * jnp.exp(-decay[...] * lags)
+    filter_sums = back_to(s_lags, hr * mr + hi * mi, hi * mr - hr * mi) * falloff
 
     own, back = filtered[:length], grad_mixed[:length]
     product[...] = (features(0) * own).astype(BF16)
@@ -218,14 +227,14 @@
         short_rows += [jnp.concatenate(row, axis=1) for row in rows]
 
     ranks, slot, _ = filter_held.shape
-    per, share = filter_sums.shape[0] // ranks, short_held.shape[0]
+    per, share, block = filter_sums.shape[0] // ranks, short_held.shape[0], first + step
     copies = [
         pltpu.make_async_copy(
-            filter_held, sums_out.at[:, pl.ds(pl.multiple_of(step * slot, slot), slot), :], done.at[0]
+            filter_held, sums_out.at[:, pl.ds(pl.multiple_of(block * slot, slot), slot), :], done.at[0]
         ),
         pltpu.make_async_copy(
             short_held,
-            sums_out.at[pl.ds(step * share, share), pl.ds(sums_out.shape[1] - SHORT, SHORT), :],
+            sums_out.at[pl.ds(block * share, share), pl.ds(sums_out.shape[1] - SHORT, SHORT), :],
             done.at[1],
         ),
     ]
@@ -285,8 +294,9 @@
     return pl.BlockSpec(tuple(rows) + (width,), lambda c: lead + (first + c,))
 
 
-def call(kernel, name, operands, outputs, width, constants=(), cost=1, **options):
-    spec = lambda rows: rows if isinstance(rows, pl.BlockSpec) else columns(rows, width)
+def call(kernel, name, operands, outputs, width, constants=(), cost=1, first=0, blocks=None, held=(), **options):
+    spec = lambda rows: rows if isinstance(rows, pl.BlockSpec) else columns(rows, width, first)
+    aliases = {len(operands) + len(constants) + at: at for at in range(len(held))}
     constants = [pltpu.with_memory_space_constraint(jnp.asarray(constant), pltpu.HBM) for constant in constants]
     operands = [
         (pltpu.with_memory_space_constraint(array, pltpu.HBM) if array.dtype == F32 else array, rows)
@@ -294,15 +304,17 @@
     ]
     return pl.pallas_call(
         kernel,
-        grid=(operands[0][0].shape[-1] // width,),
-        in_specs=[spec(rows) for _, rows in operands] + [whole(constant) for constant in constants],
+        grid=(blocks or operands[0][0].shape[-1] // width,),
+        in_specs=[spec(rows) for _, rows in operands] + [whole(constant) for constant in constants]
+        + [pl.BlockSpec(memory_space=pl.ANY)] * len(held),
         out_specs=[spec(rows) for _, rows in outputs],
         out_shape=[shape for shape, _ in outputs],
         compiler_params=pltpu.CompilerParams(vmem_limit_bytes=40 << 20),
         cost_estimate=pl.CostEstimate(flops=cost * 10**9, bytes_accessed=10**6, transcendentals=0),
+        input_output_aliases=aliases,
         name=name,
         **options,
-    )(*[array for array, _ in operands], *constants)
+    )(*[array for array, _ in operands], *constants, *held)
 
 
 def squares_kernel(rows, share, sums, raw, payload):
@@ -345,7 +357,7 @@
     ranks, groups = lax.axis_size("seq"), lax.axis_size("ch")
     rows = filter_taps.shape[0]
     count = rows * ranks
-    width = min(256, channels)
+    width = min(256, channels // CHUNKS)
     share = channels // ranks
     slot = -(-rows // 16) * 16
     size, span = 2 * length, length // 8
@@ -359,64 +371,74 @@
     own = interleaved(span)
     after = length + np.arange(8)
 
-    forward, backward, spread = call(
-        edges_kernel, "edges",
-        [(proj, (3, length)), (cot, (length,)), (short, (3, FK)), (filter_taps, (rows,))],
-        [
-            (halves_of(152), (152,)), (halves_of(160), (160,)),
-            (pltpu.HBM((ranks, rows, channels), BF16), (ranks, rows)),
-        ],
-        width, cost=3,
-    )
-    taps = lax.all_to_all(spread, "seq", 0, 0).reshape(count, channels)
-    prev = from_behind(forward, "seq", 1)
-    later = from_behind(backward, "seq", -1)
-
-    e_high, e_low = analysis(own, size)
-    k_high, k_low = analysis(np.arange(count), size)
-    feat, px, cots, m_part, g_part, k_spec = call(
+    blocks = channels // width // CHUNKS
+    prev, later, taps = [], [], None
+    for k in range(CHUNKS):
+        operands = [(proj, (3, length)), (cot, (length,)), (short, (3, FK))]
+        results = [
+            (jax.ShapeDtypeStruct((count, blocks * width), BF16), columns((count,), width)) for count in (152, 160)
+        ]
+        if k == 0:
+            operands.append((filter_taps, columns((rows,), channels // blocks)))
+            results.insert(0, (pltpu.HBM((ranks, rows, channels), BF16), columns((ranks, rows), channels // blocks)))
+        *spread, forward, backward = call(
+            edges_kernel, "edges", operands, results, width, cost=1, first=k * blocks, blocks=blocks,
+            scratch_shapes=[pltpu.VMEM(((at + FK - 1) * 8, length), BF16) for at in (16, 17)],
+        )
+        if k == 0:
+            taps = lax.all_to_all(spread[0], "seq", 0, 0).reshape(count, channels)
+        else:
+            forward, backward, prev[-1], later[-1] = lax.optimization_barrier((forward, backward, prev[-1], later[-1]))
+        prev.append(from_behind(forward, "seq", 1))
+        later.append(from_behind(backward, "seq", -1))
+
+    feat, px, cots, m_part, g_part = call(
         own_kernel, "own",
-        [(proj, (3, length)), (cot, (length,)), (short, (3, FK)), (taps, (count,)), (decay, (1,))],
+        [(proj, (3, length)), (cot, (length,)), (short, (3, FK))],
         [
             (floats(3, length), (3, length)), (halves_of(3, length), (3, length)), (halves_of(length), (length,)),
-            (floats(size), (size,)), (floats(size), (size,)), (floats(size), (size,)),
+            (floats(size), (size,)), (floats(size), (size,)),
         ],
         width,
-        [
-            np.concatenate([e_high, e_low], axis=1), np.concatenate([k_high, k_low, k_high], axis=1),
-            pick(interleaved(span, 0, 1 - FK), length),
-        ],
+        [np.concatenate(list(analysis(own, size)), axis=1), pick(interleaved(span, 0, 1 - FK), length)],
         cost=10,
     )
 
-    s_own = synthesis(np.concatenate([own, after]), size)
-    s_lags = synthesis(np.arange(count), size)
-    product, grad, sums = call(
-        finish_kernel, "finish",
-        [
-            (prev, (152,)), (later, (160,)), (feat, (3, length)), (px, (3, length)), (cots, (length,)),
-            (m_part, (size,)), (g_part, (size,)), (k_spec, (size,)),
-            (proj, pl.BlockSpec((3, 16, width), lambda c: (0, length // 16 - 1, c))), (cot, (16,)),
-            (short, (3, FK)), (decay, (1,)),
-        ],
-        [
-            (halves_of(length), (length,)), (floats(3, extended), (3, extended)),
-            (pltpu.HBM((ranks, channels // width * slot + SHORT, width), BF16), pl.BlockSpec(memory_space=pl.ANY)),
-        ],
-        width,
-        [
-            analysis(np.concatenate([interleaved(16, -128), after, np.arange(8)]), size)[0],
-            analysis(np.concatenate([interleaved(17, length), np.arange(8)]), size)[0],
-            analysis(np.arange(8), size, 8)[0],
-            np.concatenate(list(s_own), axis=1), np.concatenate(list(s_lags), axis=1),
-        ],
-        cost=12,
-        scratch_shapes=[
-            pltpu.VMEM((ranks, slot, width), BF16),
-            pltpu.VMEM((ranks * width // channels, SHORT, width), BF16),
-            pltpu.SemaphoreType.DMA((2,)),
-        ],
-    )
+    k_high, k_low = analysis(np.arange(count), size)
+    constants = [
+        analysis(np.concatenate([interleaved(16, -128), after, np.arange(8)]), size)[0],
+        analysis(np.concatenate([interleaved(17, length), np.arange(8)]), size)[0],
+        analysis(np.arange(8), size, 8)[0],
+        np.concatenate([k_high, k_low, k_high], axis=1),
+        np.concatenate(list(synthesis(np.concatenate([own, after]), size)), axis=1),
+        np.concatenate(list(synthesis(np.arange(count), size)), axis=1),
+    ]
+    held = ()
+    for k in range(CHUNKS):
+        first = k * blocks
+        held = call(
+            functools.partial(finish_kernel, first), "finish",
+            [
+                (prev[k], columns((152,), width)), (later[k], columns((160,), width)), (feat, (3, length)),
+                (px, (3, length)), (cots, (length,)), (m_part, (size,)), (g_part, (size,)), (taps, (count,)),
+                (proj, pl.BlockSpec((3, 16, width), lambda c, first=first: (0, length // 16 - 1, first + c))),
+                (cot, (16,)), (short, (3, FK)), (decay, (1,)),
+            ],
+            [
+                (halves_of(length), (length,)), (floats(3, extended), (3, extended)),
+                (
+                    pltpu.HBM((ranks, channels // width * slot + SHORT, width), BF16),
+                    pl.BlockSpec(memory_space=pl.ANY),
+                ),
+            ],
+            width, constants, cost=6, first=first, blocks=blocks, held=held,
+            scratch_shapes=[
+                pltpu.VMEM((ranks, slot, width), BF16),
+                pltpu.VMEM((ranks * width // channels, SHORT, width), BF16),
+                pltpu.SemaphoreType.DMA((2,)),
+            ],
+        )
+    product, grad, sums = held
     gated, grad_proj = call(
         outputs_kernel, "outputs",
         [(product, (length,)), (grad, (3, extended)), (short, (3, FK))],

time: 110 us -> 110 us (level)
  waiting for transfers between devices: 36.7 us -> 18.5 us
  Pallas kernels: 48.6 us -> 55.2 us
  local copies, waits for them, and re-layouts: 0 us -> 6.08 us
  starting transfers between devices: 23.1 us -> 28.6 us
    all_to_all x1, waiting for transfers between devices: 10.1 us -> 0.01 us  [shards(): taps = lax.all_to_all(spread[0], 'seq', 0, 0).reshape(count, channels)]
    ppermute x2 -> x4, starting transfers between devices: 5.87 us -> 14.1 us  [from_behind(): return lax.ppermute(value, axis, pairs)]
    pallas_call x4 -> x6, Pallas kernels: 46.3 us -> 52.8 us  [call(): pl.pallas_call(kernel, grid=(blocks or operands[0][0].shape[-1] // width,...]
    unnamed x0 -> x12, local copies, waits for them, and re-layouts: none -> 6.08 us
    ppermute x2 -> x4, waiting for transfers between devices: 5.4 us -> 0.01 us  [from_behind(): return lax.ppermute(value, axis, pairs)]
    all_to_all x1, waiting for transfers between devices: 8.09 us -> 5.34 us  [shards(): lax.all_to_all(sums, 'seq', 0, 0)]
    all_to_all x1, starting transfers between devices: 7.28 us -> 5.5 us  [shards(): taps = lax.all_to_all(spread[0], 'seq', 0, 0).reshape(count, channels)]
  transfers between devices with their start and end apart: 5 -> 7, of which waited for: 4 -> 2; matrix products, arithmetic and copies ran while one was open for 0% -> 0% of each run, Pallas kernels for 20% -> 34%
where the time goes in v6:
time: 110 us; the launch traced here: 109 us
  Pallas kernels  55.2 us (50%)
  starting transfers between devices  28.6 us (26%)
  waiting for transfers between devices  18.5 us (17%)
  local copies, waits for them, and re-layouts  6.08 us (6%)
    pallas_call x6, Pallas kernels, call(): pl.pallas_call(kernel, grid=(blocks or operands[0][0].shape[-1] // width,...  52.8 us
    ppermute x4, starting transfers between devices, from_behind(): return lax.ppermute(value, axis, pairs)  14.1 us
    all_to_all x1, waiting for transfers between devices, shards(): gathered = lax.all_to_all(payload, ('seq', 'ch'), 0, 0)  13.1 us
    unnamed x12, local copies, waits for them, and re-layouts  6.08 us
    all_to_all x1, starting transfers between devices, shards(): taps = lax.all_to_all(spread[0], 'seq', 0, 0).reshape(count, channels)  5.5 us
    all_to_all x1, waiting for transfers between devices, shards(): lax.all_to_all(sums, 'seq', 0, 0)  5.34 us
    all_to_all x1, starting transfers between devices, shards(): lax.all_to_all(sums, 'seq', 0, 0)  5.29 us
    all_to_all x1, starting transfers between devices, shards(): gathered = lax.all_to_all(payload, ('seq', 'ch'), 0, 0)  3.7 us
  transfers between devices with their start and end apart: 7, of which 2 were waited for; matrix products, arithmetic and copies ran while one was open for 0% of the time, Pallas kernels for 34%

profile of v6, /device:TPU:0, one launch (start us, length us, event | category | flops | bytes accessed | tf_op | source)
XLA Modules:
  0.0 109.1 jit_solution(11797161238324205182)
XLA Ops:
  0.6 4.4 %edges.3 = (bf16[8,16,2048]{2,1,0:T(8,128)(2,1)}, bf16[152,1024]{1,0:T(8,128)(2,1)}, bf16[160,1024]{1,0:T(8,128)(2,1)}) custom-call(bf16[3,256,2048]{2,1,0:T(8,128)(2,1)} %bitcast.5, bf16[256,2048]{1,0:T(8,128)(2,1)} %starts.3, f32[3,7,2048]{2,1,0:T(8,128)} %short.11, f32[16,2048]{1,0:T(8,128)} %refs_0_.1), custom_call_target="tpu_custom_call" | custom-call | flops 1000000000 | bytes 1000000 | tf_op jit(solution)/shard_map/edges/pallas_call | solution.py:305
  5.0 1.3 %collective-permute-start.1 = (bf16[160,1024]{1,0:T(8,128)(2,1)}, bf16[160,1024]{1,0:T(8,128)(2,1)S(1)}, u32[]{:S(2)}, u32[]{:S(2)}) collective-permute-start(bf16[160,1024]{1,0:T(8,128)(2,1)} %get-tuple-element.36), channel_id=1, source_target_pairs={{4,0},{8,4},{12,8},{16,12},{20,16},{24,20},{28,24},{5,1},{9,5},{13... | collective-permute-start | bytes 983048 | tf_op jit(solution)/shard_map/ppermute | solution.py:24
  6.3 6.2 %collective-permute-start = (bf16[152,1024]{1,0:T(8,128)(2,1)}, bf16[152,1024]{1,0:T(8,128)(2,1)}, u32[]{:S(2)}, u32[]{:S(2)}) collective-permute-start(bf16[152,1024]{1,0:T(8,128)(2,1)} %get-tuple-element.35), channel_id=1, source_target_pairs={{0,4},{4,8},{8,12},{12,16},{16,20},{20,24},{24,28},{1,5},{5,9},{9,... | collective-permute-start | bytes 933896 | tf_op jit(solution)/shard_map/ppermute | solution.py:24
  12.5 5.5 %all-to-all-start = ((bf16[8,16,2048]{2,1,0:T(8,128)(2,1)}), bf16[8,16,2048]{2,1,0:T(8,128)(2,1)}, u32[]{:S(2)}, u32[]{:S(2)}) async-start(bf16[8,16,2048]{2,1,0:T(8,128)(2,1)} %get-tuple-element.44), calls=%async_computation | async-start | bytes 1048576 | tf_op jit(solution)/shard_map/all_to_all | solution.py:389
  18.0 12.1 %own.1 = (f32[3,256,2048]{2,1,0:T(8,128)}, bf16[3,256,2048]{2,1,0:T(8,128)(2,1)S(1)}, bf16[256,2048]{1,0:T(8,128)(2,1)S(1)}, f32[512,2048]{1,0:T(8,128)}, f32[512,2048]{1,0:T(8,128)}) custom-call(bf16[3,256,2048]{2,1,0:T(8,128)(2,1)} %bitcast.6, bf16[256,2048]{1,0:T(8,128)(2,1)} %starts.3, f32[3,7,2048]{2,1,0:T(8,128)} %short.11, ...), custom_call_target="tpu_custom_call" | custom-call | flops 10000000000 | bytes 1000000 | tf_op jit(solution)/shard_map/own/pallas_call | solution.py:305
  30.1 0.0 copy-start
  30.2 1.0 copy-done
  31.1 4.2 %edges.2 = (bf16[152,1024]{1,0:T(8,128)(2,1)}, bf16[160,1024]{1,0:T(8,128)(2,1)}) custom-call(bf16[3,256,2048]{2,1,0:T(8,128)(2,1)} %bitcast.7, bf16[256,2048]{1,0:T(8,128)(2,1)} %starts.3, f32[3,7,2048]{2,1,0:T(8,128)} %short.11), custom_call_target="tpu_custom_call" | custom-call | flops 1000000000 | bytes 1000000 | tf_op jit(solution)/shard_map/edges/pallas_call | solution.py:305
  35.4 0.0 collective-permute-done.prev
  35.4 0.0 collective-permute-done.1.later
  35.4 0.0 copy-start.4
  35.4 0.7 copy-done.4
  36.1 1.3 %collective-permute-start.3 = (bf16[160,1024]{1,0:T(8,128)(2,1)}, bf16[160,1024]{1,0:T(8,128)(2,1)S(1)}, u32[]{:S(2)}, u32[]{:S(2)}) collective-permute-start(bf16[160,1024]{1,0:T(8,128)(2,1)} %get-tuple-element.38), channel_id=1, source_target_pairs={{4,0},{8,4},{12,8},{16,12},{20,16},{24,20},{28,24},{5,1},{9,5},{13... | collective-permute-start | bytes 983048 | tf_op jit(solution)/shard_map/ppermute | solution.py:24
  37.4 5.3 %collective-permute-start.2 = (bf16[152,1024]{1,0:T(8,128)(2,1)}, bf16[152,1024]{1,0:T(8,128)(2,1)}, u32[]{:S(2)}, u32[]{:S(2)}) collective-permute-start(bf16[152,1024]{1,0:T(8,128)(2,1)} %get-tuple-element.37), channel_id=1, source_target_pairs={{0,4},{4,8},{8,12},{12,16},{16,20},{20,24},{24,28},{1,5},{5,9},{9,... | collective-permute-start | bytes 933896 | tf_op jit(solution)/shard_map/ppermute | solution.py:24
  42.7 0.0 all-to-all-done
  42.7 0.0 copy-start.1
  42.7 1.2 %copy-done.1 = bf16[256,2048]{1,0:T(8,128)(2,1)S(1)} copy-done((bf16[256,2048]{1,0:T(8,128)(2,1)S(1)}, bf16[256,2048]{1,0:T(8,128)(2,1)}, u32[]{:S(2)}) %copy-start.1) | copy-done | bytes 1048600
  43.9 0.0 copy-start.5
  43.9 1.0 copy-done.5
  44.9 11.5 %finish.2 = (bf16[256,2048]{1,0:T(8,128)(2,1)S(1)}, f32[3,304,2048]{2,1,0:T(8,128)}, bf16[8,160,256]{2,1,0:T(8,128)(2,1)}) custom-call(bf16[152,1024]{1,0:T(8,128)(2,1)} %collective-permute-done.prev, bf16[160,1024]{1,0:T(8,128)(2,1)S(1)} %copy-done.5, f32[3,256,2048]{2,1,0:T(8,128)} %get-tuple-element.39.feat, ...), custom_call_target="tpu_custom_call" | custom-call | flops 6000000000 | bytes 1000000 | tf_op jit(solution)/shard_map/finish/pallas_call | solution.py:305
  56.4 0.0 collective-permute-done.2.prev
  56.4 0.0 collective-permute-done.3.later
  56.4 11.5 %finish.3 = (bf16[256,2048]{1,0:T(8,128)(2,1)S(1)}, f32[3,304,2048]{2,1,0:T(8,128)}, bf16[8,160,256]{2,1,0:T(8,128)(2,1)}) custom-call(bf16[152,1024]{1,0:T(8,128)(2,1)} %collective-permute-done.2.prev, bf16[160,1024]{1,0:T(8,128)(2,1)S(1)} %collective-permute-done.3.later, ...), custom_call_target="tpu_custom_call", output_to_operand_aliasing={{0}: (18, {}), {1}: (19, {}), {2}: (20, {})} | custom-call | flops 6000000000 | bytes 1000000 | tf_op jit(solution)/shard_map/finish/pallas_call | solution.py:305
  68.0 0.0 copy-start.2
  68.0 1.0 copy-done.2
  68.9 5.3 %all-to-all-start.1 = ((bf16[8,160,256]{2,1,0:T(8,128)(2,1)}), bf16[8,160,256]{2,1,0:T(8,128)(2,1)S(1)}, u32[]{:S(2)}, u32[]{:S(2)}) async-start(bf16[8,160,256]{2,1,0:T(8,128)(2,1)} %get-tuple-element.50), calls=%async_computation.1 | async-start | bytes 1310720 | tf_op jit(solution)/shard_map/all_to_all | solution.py:448
  74.2 0.0 copy-start.3
  74.2 1.2 %copy-done.3 = bf16[256,2048]{1,0:T(8,128)(2,1)S(1)} copy-done((bf16[256,2048]{1,0:T(8,128)(2,1)S(1)}, bf16[256,2048]{1,0:T(8,128)(2,1)}, u32[]{:S(2)}) %copy-start.3) | copy-done | bytes 1048600
  75.5 9.0 %outputs.1 = (bf16[256,2048]{1,0:T(8,128)(2,1)}, bf16[3,256,2048]{2,1,0:T(8,128)(2,1)}) custom-call(bf16[256,2048]{1,0:T(8,128)(2,1)S(1)} %copy-done.3, f32[3,304,2048]{2,1,0:T(8,128)} %get-tuple-element.52.grad, f32[3,7,2048]{2,1,0:T(8,128)} %short.11, bf16[256,256]{1,0:T(8,128)(2,1)} %constant.32.clone.p_out), custom_call_target="tpu_custom_call" | custom-call | flops 8000000000 | bytes 1000000 | tf_op jit(solution)/shard_map/outputs/pallas_call | solution.py:305
  84.5 5.3 %all-to-all-done.1.sums = bf16[8,160,256]{2,1,0:T(8,128)(2,1)S(1)} async-done(((bf16[8,160,256]{2,1,0:T(8,128)(2,1)}), bf16[8,160,256]{2,1,0:T(8,128)(2,1)S(1)}, u32[]{:S(2)}, u32[]{:S(2)}) %all-to-all-start.1) | async-done | bytes 655392 | tf_op jit(solution)/shard_map/all_to_all | solution.py:448
  89.8 1.0 squares.1
  90.8 3.7 %all-to-all-start.2 = ((bf16[32,24,256]{2,1,0:T(8,128)(2,1)}), bf16[32,24,256]{2,1,0:T(8,128)(2,1)S(1)}, u32[]{:S(2)}, u32[]{:S(2)}) async-start(bf16[32,24,256]{2,1,0:T(8,128)(2,1)} %get-tuple-element.59), calls=%async_computation.2 | async-start | bytes 786432 | tf_op jit(solution)/shard_map/all_to_all | solution.py:462
  94.6 0.1 pad_add_fusion.mine
  94.6 13.1 %all-to-all-done.2.gathered = bf16[32,24,256]{2,1,0:T(8,128)(2,1)S(1)} async-done(((bf16[32,24,256]{2,1,0:T(8,128)(2,1)}), bf16[32,24,256]{2,1,0:T(8,128)(2,1)S(1)}, u32[]{:S(2)}, u32[]{:S(2)}) %all-to-all-start.2) | async-done | bytes 393248 | tf_op jit(solution)/shard_map/all_to_all | solution.py:462
  107.7 1.4 %scale.1 = (f32[3,7,2048]{2,1,0:T(8,128)}, f32[16,2048]{1,0:T(8,128)}) custom-call(s32[2]{0:T(128)S(1)} %pad_add_fusion.mine, f32[16,2048]{1,0:T(8,128)S(1)} %get-tuple-element.58.raw, bf16[32,24,256]{2,1,0:T(8,128)(2,1)S(1)} %all-to-all-done.2.gathered), custom_call_target="tpu_custom_call" | custom-call | tf_op jit(solution)/shard_map/scale/pallas_call | solution.py:465
Async XLA Ops:
  5.0 30.4 %collective-permute-start.1 = (bf16[160,1024]{1,0:T(8,128)(2,1)}, bf16[160,1024]{1,0:T(8,128)(2,1)S(1)}, u32[]{:S(2)}, u32[]{:S(2)}) collective-permute-start(bf16[160,1024]{1,0:T(8,128)(2,1)} %get-tuple-element.36), channel_id=1, source_target_pairs={{4,0},{8,4},{12,8},{16,12},{20,16},{24,20},{28,24},{5,1},{9,5},{13... | collective-permute-start | bytes 983048 | tf_op jit(solution)/shard_map/ppermute | solution.py:24
  6.3 29.1 %collective-permute-start = (bf16[152,1024]{1,0:T(8,128)(2,1)}, bf16[152,1024]{1,0:T(8,128)(2,1)}, u32[]{:S(2)}, u32[]{:S(2)}) collective-permute-start(bf16[152,1024]{1,0:T(8,128)(2,1)} %get-tuple-element.35), channel_id=1, source_target_pairs={{0,4},{4,8},{8,12},{12,16},{16,20},{20,24},{24,28},{1,5},{5,9},{9,... | collective-permute-start | bytes 933896 | tf_op jit(solution)/shard_map/ppermute | solution.py:24
  12.5 30.1 %all-to-all-start = ((bf16[8,16,2048]{2,1,0:T(8,128)(2,1)}), bf16[8,16,2048]{2,1,0:T(8,128)(2,1)}, u32[]{:S(2)}, u32[]{:S(2)}) async-start(bf16[8,16,2048]{2,1,0:T(8,128)(2,1)} %get-tuple-element.44), calls=%async_computation | async-start | bytes 1048576 | tf_op jit(solution)/shard_map/all_to_all | solution.py:389
  30.1 1.0 copy-start
  35.4 0.7 copy-start.4
  36.1 20.3 %collective-permute-start.3 = (bf16[160,1024]{1,0:T(8,128)(2,1)}, bf16[160,1024]{1,0:T(8,128)(2,1)S(1)}, u32[]{:S(2)}, u32[]{:S(2)}) collective-permute-start(bf16[160,1024]{1,0:T(8,128)(2,1)} %get-tuple-element.38), channel_id=1, source_target_pairs={{4,0},{8,4},{12,8},{16,12},{20,16},{24,20},{28,24},{5,1},{9,5},{13... | collective-permute-start | bytes 983048 | tf_op jit(solution)/shard_map/ppermute | solution.py:24
  37.4 19.0 %collective-permute-start.2 = (bf16[152,1024]{1,0:T(8,128)(2,1)}, bf16[152,1024]{1,0:T(8,128)(2,1)}, u32[]{:S(2)}, u32[]{:S(2)}) collective-permute-start(bf16[152,1024]{1,0:T(8,128)(2,1)} %get-tuple-element.37), channel_id=1, source_target_pairs={{0,4},{4,8},{8,12},{12,16},{16,20},{20,24},{24,28},{1,5},{5,9},{9,... | collective-permute-start | bytes 933896 | tf_op jit(solution)/shard_map/ppermute | solution.py:24
  42.7 1.2 %copy-start.1 = (bf16[256,2048]{1,0:T(8,128)(2,1)S(1)}, bf16[256,2048]{1,0:T(8,128)(2,1)}, u32[]{:S(2)}) copy-start(bf16[256,2048]{1,0:T(8,128)(2,1)} %copy-done) | copy-start | bytes 3145732
  43.9 1.0 copy-start.5
  68.0 1.0 copy-start.2
  68.9 20.9 %all-to-all-start.1 = ((bf16[8,160,256]{2,1,0:T(8,128)(2,1)}), bf16[8,160,256]{2,1,0:T(8,128)(2,1)S(1)}, u32[]{:S(2)}, u32[]{:S(2)}) async-start(bf16[8,160,256]{2,1,0:T(8,128)(2,1)} %get-tuple-element.50), calls=%async_computation.1 | async-start | bytes 1310720 | tf_op jit(solution)/shard_map/all_to_all | solution.py:448
  74.2 1.2 %copy-start.3 = (bf16[256,2048]{1,0:T(8,128)(2,1)S(1)}, bf16[256,2048]{1,0:T(8,128)(2,1)}, u32[]{:S(2)}) copy-start(bf16[256,2048]{1,0:T(8,128)(2,1)} %copy-done.2) | copy-start | bytes 3145732
  90.8 16.9 %all-to-all-start.2 = ((bf16[32,24,256]{2,1,0:T(8,128)(2,1)}), bf16[32,24,256]{2,1,0:T(8,128)(2,1)S(1)}, u32[]{:S(2)}, u32[]{:S(2)}) async-start(bf16[32,24,256]{2,1,0:T(8,128)(2,1)} %get-tuple-element.59), calls=%async_computation.2 | async-start | bytes 786432 | tf_op jit(solution)/shard_map/all_to_all | solution.py:462

commit v7 on v6

--- a/solution.py
+++ b/solution.py
@@ -14,8 +14,9 @@
 FK = 7
 BF16 = jnp.bfloat16
 F32 = jnp.float32
-CHUNKS = 2
+CHUNKS = 1
 SHORT = 32
+STEP = 64
 
 
 def from_behind(value, axis, by):
@@ -66,9 +67,26 @@
     return jnp.where(position == column, 1.0, 0.0).astype(BF16)
 
 
+def lanes_of(width):
+    return [slice(at, at + 128) for at in range(0, width, 128)]
+
+
+def featurized(x, taps, lane, row, rows):
+    total = None
+    for lag in range(FK):
+        at = row + 8 * (FK - 1 - lag)
+        part = x[at : at + rows, lane].reshape(rows // 8, 8, 128) * taps[lag]
+        total = part if total is None else total + part
+    return total
+
+
+def spread_taps(short, i, lane):
+    return [jnp.broadcast_to(short[i, lag : lag + 1, lane], (8, 128)) for lag in range(FK)]
+
+
 def edges_kernel(proj, cot, short, *refs):
-    forward, backward = refs[-4:-2]
-    p_tail, p_head = refs[-2:]
+    forward, backward = refs[-8:-6]
+    p_tail, p_head, first, second, zeroth, held = refs[-6:]
     length, width = cot.shape
     tail, head = 16, 17
 
@@ -77,22 +95,26 @@
         p_tail[...] = picked(tail, length - 128, length)
         p_head[...] = picked(head, 0, length)
 
-
-    def conv(x, taps, count):
-        x = x.reshape(-1, 8, width)
-        total = taps[0:1] * x[FK - 1 : FK - 1 + count]
-        for lag in range(1, FK):
-            total = total + taps[lag : lag + 1] * x[FK - 1 - lag : FK - 1 - lag + count]
-        return total
-
-    mixed = conv(mm(p_tail[...], proj[1]), short[1], tail) * conv(mm(p_tail[...], proj[2]), short[2], tail)
+    first[...] = mm(p_tail[...], proj[1])
+    second[...] = mm(p_tail[...], proj[2])
+    zeroth[...] = mm(p_head[...], proj[0])
+    held[...] = mm(p_head[(FK - 1) * 8 :, :], cot[...])
+    for lane in lanes_of(width):
+        taps = [spread_taps(short, i, lane) for i in range(3)]
+        for r in range(0, 8 * tail, STEP):
+            mixed = featurized(first, taps[1], lane, r, STEP) * featurized(second, taps[2], lane, r, STEP)
+            forward[r : r + STEP, lane] = mixed.reshape(STEP, 128).astype(BF16)
+        for r in range(0, 8 * head, STEP):
+            rows = min(STEP, 8 * head - r)
+            grad = featurized(zeroth, taps[0], lane, r, rows).reshape(rows, 128) * held[r : r + rows, lane]
+            if rows < STEP:
+                starts = [ref[:16, lane].astype(F32)[:8] for ref in (cot, proj.at[1], proj.at[2])]
+                backward[r:, lane] = jnp.concatenate([grad] + starts, axis=0).astype(BF16)
+            else:
+                backward[r : r + rows, lane] = grad.astype(BF16)
     ends = [proj[i, length - 16 :, :].astype(F32)[8:] for i in range(3)]
-    forward[...] = jnp.concatenate([mixed.reshape(tail * 8, width)] + ends, axis=0).astype(BF16)
-    gate = conv(mm(p_head[...], proj[0]), short[0], head).reshape(head * 8, width)
-    grad = gate * mm(p_head[(FK - 1) * 8 :, :], cot[...])
-    starts = [ref[:16, :].astype(F32)[:8] for ref in (cot, proj.at[1], proj.at[2])]
-    backward[...] = jnp.concatenate([grad] + starts, axis=0).astype(BF16)
-    if len(refs) > 4:
+    forward[8 * tail :, :] = jnp.concatenate(ends, axis=0).astype(BF16)
+    if len(refs) > 8:
         taps, spread = refs[:2]
         spread[...] = jnp.broadcast_to(taps[...].astype(BF16)[None], spread.shape)
 
@@ -106,36 +128,37 @@
     return total
 
 
-def own_kernel(proj, cot, short, e_own, p_in, feat, px, cots, m_part, g_part):
+def own_kernel(proj, cot, short, e_own, p_in, feat, px, cots, m_part, g_part, x, moved, mixed, grads):
     length, width = cot.shape
-    span = length // 8
     edge = FK - 1
-    step = 8
     for i in range(3):
-        x = mm(p_in[...], proj[i])
-        px[i] = x[edge * 8 :].astype(BF16)
-        x = x.reshape(span + edge, 8, width)
-        for at in range(0, width, 128):
-            lane = slice(at, at + 128)
-            weights = [jnp.broadcast_to(short[i, lag : lag + 1, lane], (8, 128)) for lag in range(FK)]
-            for r in range(0, span, step):
-                total = weights[0] * x[r + edge : r + edge + step, :, lane]
-                for lag in range(1, FK):
-                    total = total + weights[lag] * x[r + edge - lag : r + edge - lag + step, :, lane]
-                feat[i, r * 8 : (r + step) * 8, lane] = total.reshape(step * 8, 128)
-    moved = mm(p_in[edge * 8 :, :], cot[...])
-    cots[...] = moved.astype(BF16)
-    mixed = (feat[1] * feat[2]).astype(BF16)
-    m_part[...] = mm(e_own[...], jnp.concatenate([mixed, mixed], axis=0))
-    grad = (moved * feat[0]).astype(BF16)
-    g_part[...] = mm(e_own[...], jnp.concatenate([grad, grad], axis=0))
+        x[i] = mm(p_in[...], proj[i])
+    moved[...] = mm(p_in[edge * 8 :, :], cot[...])
+    for lane in lanes_of(width):
+        taps = [spread_taps(short, i, lane) for i in range(3)]
+        for r in range(0, length, STEP):
+            rows = slice(r, r + STEP)
+            parts = []
+            for i in range(3):
+                px[i, rows, lane] = x[i, r + 8 * edge : r + 8 * edge + STEP, lane].astype(BF16)
+                part = featurized(x.at[i], taps[i], lane, r, STEP).reshape(STEP, 128)
+                feat[i, rows, lane] = part
+                parts.append(part)
+            here = moved[rows, lane]
+            cots[rows, lane] = here.astype(BF16)
+            mixed[rows, lane] = (parts[1] * parts[2]).astype(BF16)
+            grads[rows, lane] = (here * parts[0]).astype(BF16)
+    for out, value in ((m_part, mixed), (g_part, grads)):
+        value = value[...]
+        out[...] = mm(e_own[...], jnp.concatenate([value, value], axis=0))
 
 
 def finish_kernel(
     first, prev, later, feat, px, cots, m_part, g_part, taps, ends, starts, short, decay,
     e_prev, e_next, e_first, e_taps, s_own, s_lags, *refs,
 ):
-    product, grad, sums_out, filter_held, short_held, done = refs[-6:]
+    product, grad, sums_out, filter_held, short_held, done = refs[-17:-11]
+    fixed, ms, gs, hs, ks, ys, zs, cs, filtered, grad_mixed, decays = refs[-11:]
     length, width = cots.shape
     span = length // 8
     edge = FK - 1
@@ -159,7 +182,9 @@
             moved = pltpu.roll(fixes[i], 8 - r, 0) if r else fixes[i]
             rows.append(part + jnp.where(row8 == 0, moved, 0.0))
         heads.append((jnp.concatenate(rows, axis=0), natural))
-    features = lambda i: jnp.concatenate([heads[i][0], feat[i, edge * 8 :, :]], axis=0)
+    for i in range(3):
+        fixed[i, : 8 * edge] = heads[i][0]
+        fixed[i, 8 * edge :] = feat[i, 8 * edge : STEP, :]
     inside = row8 < edge
     (first1, first2), (fix1, fix2) = (heads[1][1], heads[2][1]), fixes[1:]
     mixed_fix = jnp.where(inside, (first1 + fix1) * (first2 + fix2) - first1 * first2, 0.0)
@@ -174,36 +199,51 @@
     mixed_edge = jnp.concatenate([before[:128], feat_next[1] * feat_next[2], mixed_fix], axis=0).astype(BF16)
     grad_first = jnp.concatenate([grad_fix, jnp.zeros((8, width), F32)], axis=0).astype(BF16)
 
-    m_spec = m_part[...] + mm(e_prev[...], mixed_edge)
-    g_own = g_part[...] + mm(e_first[...], grad_first)
-    g_spec = g_part[...] + mm(e_next[...], grad_edge)
-
+    ms[...] = mm(e_prev[...], mixed_edge)
+    hs[...] = mm(e_first[...], grad_first)
+    gs[...] = mm(e_next[...], grad_edge)
     lags = lax.broadcasted_iota(jnp.int32, (taps.shape[0], width), 0).astype(F32)
-    falloff = jnp.exp(-decay[...] * lags)
-    kernel = taps[...].astype(F32) * falloff
+    decays[...] = jnp.exp(-decay[...] * lags)
+    kernel = taps[...].astype(F32) * decays[...]
     high = kernel.astype(BF16)
     low = (kernel - high.astype(F32)).astype(BF16)
-    k_spec = mm(e_taps[...], jnp.concatenate([high, high, low], axis=0))
-
-    half = k_spec.shape[0] // 2
-    parts = lambda value: (value[:half], value[half:])
-    (kr, ki), (mr, mi), (gr, gi), (hr, hi) = parts(k_spec), parts(m_spec), parts(g_spec), parts(g_own)
-
-    def back_to(matrix, real, imaginary):
-        spectrum = jnp.concatenate([real, imaginary], axis=0).astype(BF16)
+    ks[...] = mm(e_taps[...], jnp.concatenate([high, high, low], axis=0))
+
+    half = ks.shape[0] // 2
+    for lane in lanes_of(width):
+        for f in range(0, half, 32):
+            real, imag = slice(f, f + 32), slice(half + f, half + f + 32)
+            kr, ki = ks[real, lane], ks[imag, lane]
+            mr, mi = m_part[real, lane] + ms[real, lane], m_part[imag, lane] + ms[imag, lane]
+            ys[real, lane] = (mr * kr - mi * ki).astype(BF16)
+            ys[imag, lane] = (mr * ki + mi * kr).astype(BF16)
+            pr, pi = g_part[real, lane], g_part[imag, lane]
+            hr, hi = pr + hs[real, lane], pi + hs[imag, lane]
+            cs[real, lane] = (hr * mr + hi * mi).astype(BF16)
+            cs[imag, lane] = (hi * mr - hr * mi).astype(BF16)
+            gr, gi = pr + gs[real, lane], pi + gs[imag, lane]
+            zs[real, lane] = (gr * kr + gi * ki).astype(BF16)
+            zs[imag, lane] = (gi * kr - gr * ki).astype(BF16)
+
+    def back_to(matrix, spectrum):
+        spectrum = spectrum[...]
         return mm(matrix[...], jnp.concatenate([spectrum, spectrum], axis=0))
 
-    filtered = back_to(s_own, mr * kr - mi * ki, mr * ki + mi * kr)
-    grad_mixed = back_to(s_own, gr * kr + gi * ki, gi * kr - gr * ki)
-    filter_sums = back_to(s_lags, hr * mr + hi * mi, hi * mr - hr * mi) * falloff
-
-    own, back = filtered[:length], grad_mixed[:length]
-    product[...] = (features(0) * own).astype(BF16)
-    grad[0, :length] = cots[...].astype(F32) * own
-    grad[1, :length] = back * features(2)
-    grad[2, :length] = back * features(1)
-    back_next = grad_mixed[length:]
-    edge_next = [cot_next * filtered[length:], back_next * feat_next[2], back_next * feat_next[1]]
+    filtered[...] = back_to(s_own, ys)
+    grad_mixed[...] = back_to(s_own, zs)
+    filter_sums = back_to(s_lags, cs) * decays[...]
+
+    for lane in lanes_of(width):
+        for r in range(0, length, STEP):
+            rows = slice(r, r + STEP)
+            features = [fixed[i, :, lane] if r == 0 else feat[i, rows, lane] for i in range(3)]
+            own, back = filtered[rows, lane], grad_mixed[rows, lane]
+            product[rows, lane] = (features[0] * own).astype(BF16)
+            grad[0, rows, lane] = cots[rows, lane].astype(F32) * own
+            grad[1, rows, lane] = back * features[2]
+            grad[2, rows, lane] = back * features[1]
+    own_next, back_next = filtered[length:, :], grad_mixed[length:, :]
+    edge_next = [cot_next * own_next, back_next * feat_next[2], back_next * feat_next[1]]
     for i in range(3):
         for k in range(edge):
             at = length + 8 * k
@@ -264,25 +304,19 @@
             copy.wait()
 
 
-def outputs_kernel(product, grad, short, p_out, gated, grad_proj):
+def outputs_kernel(product, grad, short, p_out, gated, grad_proj, held):
     length, width = product.shape
     gated[...] = mm(p_out[...], product[...]).astype(BF16)
-    chunk = 64
     for i in range(3):
-        columns = []
-        for at in range(0, width, 128):
-            lane = slice(at, at + 128)
-            weights = [jnp.broadcast_to(short[i, lag : lag + 1, lane], (8, 128)) for lag in range(FK)]
-            chunks = []
-            for r in range(0, length, chunk):
-                total = jnp.zeros((chunk // 8, 8, 128), F32)
+        for lane in lanes_of(width):
+            taps = spread_taps(short, i, lane)
+            for r in range(0, length, STEP):
+                total = None
                 for lag in range(FK):
-                    value = grad[i, r + 8 * lag : r + 8 * lag + chunk, lane].reshape(chunk // 8, 8, 128)
-                    total = total + weights[lag] * value
-                chunks.append(total.reshape(chunk, 128))
-            columns.append(jnp.concatenate(chunks, axis=0))
-        result = jnp.concatenate(columns, axis=1).astype(BF16)
-        grad_proj[i] = mm(p_out[...], result).astype(BF16)
+                    part = grad[i, r + 8 * lag : r + 8 * lag + STEP, lane].reshape(STEP // 8, 8, 128) * taps[lag]
+                    total = part if total is None else total + part
+                held[i, r : r + STEP, lane] = total.reshape(STEP, 128).astype(BF16)
+        grad_proj[i] = mm(p_out[...], held[i]).astype(BF16)
 
 
 def whole(array):
@@ -299,7 +333,7 @@
     aliases = {len(operands) + len(constants) + at: at for at in range(len(held))}
     constants = [pltpu.with_memory_space_constraint(jnp.asarray(constant), pltpu.HBM) for constant in constants]
     operands = [
-        (pltpu.with_memory_space_constraint(array, pltpu.HBM) if array.dtype == F32 else array, rows)
+        (array if isinstance(rows, pl.BlockSpec) else pltpu.with_memory_space_constraint(array, pltpu.HBM), rows)
         for array, rows in operands
     ]
     return pl.pallas_call(
@@ -367,7 +401,7 @@
         for array in (jnp.transpose(projected, (1, 0, 2)), cotangent, short_taps, decay[None])
     )
     floats = lambda *shape: pltpu.HBM(shape + (channels,), F32)
-    halves_of = lambda *shape: jax.ShapeDtypeStruct(shape + (channels,), BF16)
+    halves_of = lambda *shape: pltpu.HBM(shape + (channels,), BF16)
     own = interleaved(span)
     after = length + np.arange(8)
 
@@ -383,7 +417,8 @@
             results.insert(0, (pltpu.HBM((ranks, rows, channels), BF16), columns((ranks, rows), channels // blocks)))
         *spread, forward, backward = call(
             edges_kernel, "edges", operands, results, width, cost=1, first=k * blocks, blocks=blocks,
-            scratch_shapes=[pltpu.VMEM(((at + FK - 1) * 8, length), BF16) for at in (16, 17)],
+            scratch_shapes=[pltpu.VMEM(((at + FK - 1) * 8, length), BF16) for at in (16, 17)]
+            + [pltpu.VMEM((at * 8, width), F32) for at in (15 + FK, 15 + FK, 16 + FK, 17)],
         )
         if k == 0:
             taps = lax.all_to_all(spread[0], "seq", 0, 0).reshape(count, channels)
@@ -402,6 +437,10 @@
         width,
         [np.concatenate(list(analysis(own, size)), axis=1), pick(interleaved(span, 0, 1 - FK), length)],
         cost=10,
+        scratch_shapes=[
+            pltpu.VMEM((3, extended, width), F32), pltpu.VMEM((length, width), F32),
+            pltpu.VMEM((length, width), BF16), pltpu.VMEM((length, width), BF16),
+        ],
     )
 
     k_high, k_low = analysis(np.arange(count), size)
@@ -420,7 +459,7 @@
             functools.partial(finish_kernel, first), "finish",
             [
                 (prev[k], columns((152,), width)), (later[k], columns((160,), width)), (feat, (3, length)),
-                (px, (3, length)), (cots, (length,)), (m_part, (size,)), (g_part, (size,)), (taps, (count,)),
+                (px, (3, length)), (cots, (length,)), (m_part, (size,)), (g_part, (size,)), (taps, columns((count,), width, first)),
                 (proj, pl.BlockSpec((3, 16, width), lambda c, first=first: (0, length // 16 - 1, first + c))),
                 (cot, (16,)), (short, (3, FK)), (decay, (1,)),
             ],
@@ -436,14 +475,16 @@
                 pltpu.VMEM((ranks, slot, width), BF16),
                 pltpu.VMEM((ranks * width // channels, SHORT, width), BF16),
                 pltpu.SemaphoreType.DMA((2,)),
-            ],
+                pltpu.VMEM((3, STEP, width), F32),
+            ] + [pltpu.VMEM((size, width), F32)] * 4 + [pltpu.VMEM((size, width), BF16)] * 3
+            + [pltpu.VMEM((length + 8, width), F32)] * 2 + [pltpu.VMEM((count, width), F32)],
         )
     product, grad, sums = held
     gated, grad_proj = call(
         outputs_kernel, "outputs",
         [(product, (length,)), (grad, (3, extended)), (short, (3, FK))],
         [(halves_of(length), (length,)), (halves_of(3, length), (3, length))],
-        width, [pick(own, length).T], cost=8,
+        width, [pick(own, length).T], cost=8, scratch_shapes=[pltpu.VMEM((3, length, width), BF16)],
     )
     sums, gated, grad_proj = lax.optimization_barrier((lax.all_to_all(sums, "seq", 0, 0), gated, grad_proj))
 

time: 110 us -> 111 us (level)
  waiting for transfers between devices: 18.5 us -> 34.3 us
  starting transfers between devices: 28.6 us -> 22.4 us
  local copies, waits for them, and re-layouts: 6.08 us -> 0.9 us
  Pallas kernels: 55.2 us -> 51 us
    ppermute x4 -> x2, waiting for transfers between devices: 0.01 us -> 12.3 us  [from_behind(): return lax.ppermute(value, axis, pairs)]
    ppermute x4 -> x2, starting transfers between devices: 14.1 us -> 6.82 us  [from_behind(): return lax.ppermute(value, axis, pairs)]
    unnamed x12 -> x2, local copies, waits for them, and re-layouts: 6.08 us -> 0.9 us
    pallas_call x6 -> x4, Pallas kernels: 52.8 us -> 48.7 us  [call(): pl.pallas_call(kernel, grid=(blocks or operands[0][0].shape[-1] // width,...]
    all_to_all x1, waiting for transfers between devices: 5.34 us -> 7.56 us  [shards(): lax.all_to_all(sums, 'seq', 0, 0)]
    all_to_all x1, waiting for transfers between devices: 0.01 us -> 1.41 us  [shards(): taps = lax.all_to_all(spread[0], 'seq', 0, 0).reshape(count, channels)]
  transfers between devices with their start and end apart: 7 -> 5, of which waited for: 2 -> 4; matrix products, arithmetic and copies ran while one was open for 0% -> 0% of each run, Pallas kernels for 34% -> 20%
where the time goes in v7:
time: 111 us; the launch traced here: 109 us
  Pallas kernels  51 us (46%)
  waiting for transfers between devices  34.3 us (31%)
  starting transfers between devices  22.4 us (20%)
    pallas_call x4, Pallas kernels, call(): pl.pallas_call(kernel, grid=(blocks or operands[0][0].shape[-1] // width,...  48.7 us
    all_to_all x1, waiting for transfers between devices, shards(): gathered = lax.all_to_all(payload, ('seq', 'ch'), 0, 0)  13.1 us
    ppermute x2, waiting for transfers between devices, from_behind(): return lax.ppermute(value, axis, pairs)  12.3 us
    all_to_all x1, waiting for transfers between devices, shards(): lax.all_to_all(sums, 'seq', 0, 0)  7.56 us
    ppermute x2, starting transfers between devices, from_behind(): return lax.ppermute(value, axis, pairs)  6.82 us
    all_to_all x1, starting transfers between devices, shards(): taps = lax.all_to_all(spread[0], 'seq', 0, 0).reshape(count, channels)  6.19 us
    all_to_all x1, starting transfers between devices, shards(): lax.all_to_all(sums, 'seq', 0, 0)  5.69 us
    all_to_all x1, starting transfers between devices, shards(): gathered = lax.all_to_all(payload, ('seq', 'ch'), 0, 0)  3.66 us
  transfers between devices with their start and end apart: 5, of which 4 were waited for; matrix products, arithmetic and copies ran while one was open for 0% of the time, Pallas kernels for 20%

profile of v7, /device:TPU:0, one launch (start us, length us, event | category | flops | bytes accessed | tf_op | source)
XLA Modules:
  0.0 109.4 jit_solution(4600298190102673553)
XLA Ops:
  0.6 0.0 copy-start
  0.6 0.9 copy-done
  1.5 7.2 %edges.1 = (bf16[8,16,2048]{2,1,0:T(8,128)(2,1)}, bf16[152,2048]{1,0:T(8,128)(2,1)S(1)}, bf16[160,2048]{1,0:T(8,128)(2,1)S(1)}) custom-call(bf16[3,256,2048]{2,1,0:T(8,128)(2,1)} %bitcast.6, bf16[256,2048]{1,0:T(8,128)(2,1)} %starts.1, f32[3,7,2048]{2,1,0:T(8,128)} %short.7, f32[16,2048]{1,0:T(8,128)S(1)} %copy-done), custom_call_target="tpu_custom_call" | custom-call | flops 1000000000 | bytes 1000000 | tf_op jit(solution)/shard_map/edges/pallas_call | solution.py:339
  8.8 1.3 %collective-permute-start.1 = (bf16[160,2048]{1,0:T(8,128)(2,1)S(1)}, bf16[160,2048]{1,0:T(8,128)(2,1)S(1)}, u32[]{:S(2)}, u32[]{:S(2)}) collective-permute-start(bf16[160,2048]{1,0:T(8,128)(2,1)S(1)} %get-tuple-element.25), channel_id=1, source_target_pairs={{4,0},{8,4},{12,8},{16,12},{20,16},{24,20},{28,24},{5,1},{9,5},{13... | collective-permute-start | bytes 1966088 | tf_op jit(solution)/shard_map/ppermute | solution.py:25
  10.0 5.5 %collective-permute-start = (bf16[152,2048]{1,0:T(8,128)(2,1)S(1)}, bf16[152,2048]{1,0:T(8,128)(2,1)S(1)}, u32[]{:S(2)}, u32[]{:S(2)}) collective-permute-start(bf16[152,2048]{1,0:T(8,128)(2,1)S(1)} %get-tuple-element.24), channel_id=1, source_target_pairs={{0,4},{4,8},{8,12},{12,16},{16,20},{20,24},{24,28},{1,5},{5,9},{9,... | collective-permute-start | bytes 1867784 | tf_op jit(solution)/shard_map/ppermute | solution.py:25
  15.6 6.2 %all-to-all-start = ((bf16[8,16,2048]{2,1,0:T(8,128)(2,1)}), bf16[8,16,2048]{2,1,0:T(8,128)(2,1)S(1)}, u32[]{:S(2)}, u32[]{:S(2)}) async-start(bf16[8,16,2048]{2,1,0:T(8,128)(2,1)} %get-tuple-element.31), calls=%async_computation | async-start | bytes 1048576 | tf_op jit(solution)/shard_map/all_to_all | solution.py:424
  21.8 12.1 %own.1 = (f32[3,256,2048]{2,1,0:T(8,128)}, bf16[3,256,2048]{2,1,0:T(8,128)(2,1)}, bf16[256,2048]{1,0:T(8,128)(2,1)}, f32[512,2048]{1,0:T(8,128)}, f32[512,2048]{1,0:T(8,128)}) custom-call(bf16[3,256,2048]{2,1,0:T(8,128)(2,1)} %bitcast.7, bf16[256,2048]{1,0:T(8,128)(2,1)} %starts.1, f32[3,7,2048]{2,1,0:T(8,128)} %short.7, ...), custom_call_target="tpu_custom_call" | custom-call | flops 10000000000 | bytes 1000000 | tf_op jit(solution)/shard_map/own/pallas_call | solution.py:339
  33.9 12.2 %collective-permute-done.prev = bf16[152,2048]{1,0:T(8,128)(2,1)S(1)} collective-permute-done((bf16[152,2048]{1,0:T(8,128)(2,1)S(1)}, bf16[152,2048]{1,0:T(8,128)(2,1)S(1)}, u32[]{:S(2)}, u32[]{:S(2)}) %collective-permute-start) | collective-permute-done | bytes 622624 | tf_op jit(solution)/shard_map/ppermute | solution.py:25
  46.1 0.0 collective-permute-done.1.later
  46.1 1.4 %all-to-all-done = bf16[8,16,2048]{2,1,0:T(8,128)(2,1)S(1)} async-done(((bf16[8,16,2048]{2,1,0:T(8,128)(2,1)}), bf16[8,16,2048]{2,1,0:T(8,128)(2,1)S(1)}, u32[]{:S(2)}, u32[]{:S(2)}) %all-to-all-start) | async-done | bytes 524320 | tf_op jit(solution)/shard_map/all_to_all | solution.py:424
  47.6 19.5 %finish.1 = (bf16[256,2048]{1,0:T(8,128)(2,1)}, f32[3,304,2048]{2,1,0:T(8,128)}, bf16[8,160,256]{2,1,0:T(8,128)(2,1)}) custom-call(bf16[152,2048]{1,0:T(8,128)(2,1)S(1)} %collective-permute-done.prev, bf16[160,2048]{1,0:T(8,128)(2,1)S(1)} %collective-permute-done.1.later, f32[3,256,2048]{2,1,0:T(8,128)} %get-tuple-element.26.feat, ...), custom_call_target="tpu_custom_call" | custom-call | flops 6000000000 | bytes 1000000 | tf_op jit(solution)/shard_map/finish/pallas_call | solution.py:339
  67.0 5.7 %all-to-all-start.1 = ((bf16[8,160,256]{2,1,0:T(8,128)(2,1)}), bf16[8,160,256]{2,1,0:T(8,128)(2,1)S(1)}, u32[]{:S(2)}, u32[]{:S(2)}) async-start(bf16[8,160,256]{2,1,0:T(8,128)(2,1)} %get-tuple-element.32), calls=%async_computation.1 | async-start | bytes 1310720 | tf_op jit(solution)/shard_map/all_to_all | solution.py:489
  72.7 9.9 %outputs.1 = (bf16[256,2048]{1,0:T(8,128)(2,1)}, bf16[3,256,2048]{2,1,0:T(8,128)(2,1)}) custom-call(bf16[256,2048]{1,0:T(8,128)(2,1)} %get-tuple-element.33.product, f32[3,304,2048]{2,1,0:T(8,128)} %get-tuple-element.34.grad, f32[3,7,2048]{2,1,0:T(8,128)} %short.7, bf16[256,256]{1,0:T(8,128)(2,1)} %constant.32.clone.p_out), custom_call_target="tpu_custom_call" | custom-call | flops 8000000000 | bytes 1000000 | tf_op jit(solution)/shard_map/outputs/pallas_call | solution.py:339
  82.6 7.6 %all-to-all-done.1.sums = bf16[8,160,256]{2,1,0:T(8,128)(2,1)S(1)} async-done(((bf16[8,160,256]{2,1,0:T(8,128)(2,1)}), bf16[8,160,256]{2,1,0:T(8,128)(2,1)S(1)}, u32[]{:S(2)}, u32[]{:S(2)}) %all-to-all-start.1) | async-done | bytes 655392 | tf_op jit(solution)/shard_map/all_to_all | solution.py:489
  90.2 1.0 squares.1
  91.2 3.7 %all-to-all-start.2 = ((bf16[32,24,256]{2,1,0:T(8,128)(2,1)}), bf16[32,24,256]{2,1,0:T(8,128)(2,1)S(1)}, u32[]{:S(2)}, u32[]{:S(2)}) async-start(bf16[32,24,256]{2,1,0:T(8,128)(2,1)} %get-tuple-element.41), calls=%async_computation.2 | async-start | bytes 786432 | tf_op jit(solution)/shard_map/all_to_all | solution.py:503
  94.9 0.1 pad_add_fusion.mine
  94.9 13.1 %all-to-all-done.2.gathered = bf16[32,24,256]{2,1,0:T(8,128)(2,1)S(1)} async-done(((bf16[32,24,256]{2,1,0:T(8,128)(2,1)}), bf16[32,24,256]{2,1,0:T(8,128)(2,1)S(1)}, u32[]{:S(2)}, u32[]{:S(2)}) %all-to-all-start.2) | async-done | bytes 393248 | tf_op jit(solution)/shard_map/all_to_all | solution.py:503
  108.0 1.4 %scale.1 = (f32[3,7,2048]{2,1,0:T(8,128)}, f32[16,2048]{1,0:T(8,128)}) custom-call(s32[2]{0:T(128)S(1)} %pad_add_fusion.mine, f32[16,2048]{1,0:T(8,128)S(1)} %get-tuple-element.40.raw, bf16[32,24,256]{2,1,0:T(8,128)(2,1)S(1)} %all-to-all-done.2.gathered), custom_call_target="tpu_custom_call" | custom-call | tf_op jit(solution)/shard_map/scale/pallas_call | solution.py:506
Async XLA Ops:
  0.6 0.9 copy-start
  8.8 37.4 %collective-permute-start.1 = (bf16[160,2048]{1,0:T(8,128)(2,1)S(1)}, bf16[160,2048]{1,0:T(8,128)(2,1)S(1)}, u32[]{:S(2)}, u32[]{:S(2)}) collective-permute-start(bf16[160,2048]{1,0:T(8,128)(2,1)S(1)} %get-tuple-element.25), channel_id=1, source_target_pairs={{4,0},{8,4},{12,8},{16,12},{20,16},{24,20},{28,24},{5,1},{9,5},{13... | collective-permute-start | bytes 1966088 | tf_op jit(solution)/shard_map/ppermute | solution.py:25
  10.0 36.1 %collective-permute-start = (bf16[152,2048]{1,0:T(8,128)(2,1)S(1)}, bf16[152,2048]{1,0:T(8,128)(2,1)S(1)}, u32[]{:S(2)}, u32[]{:S(2)}) collective-permute-start(bf16[152,2048]{1,0:T(8,128)(2,1)S(1)} %get-tuple-element.24), channel_id=1, source_target_pairs={{0,4},{4,8},{8,12},{12,16},{16,20},{20,24},{24,28},{1,5},{5,9},{9,... | collective-permute-start | bytes 1867784 | tf_op jit(solution)/shard_map/ppermute | solution.py:25
  15.6 32.0 %all-to-all-start = ((bf16[8,16,2048]{2,1,0:T(8,128)(2,1)}), bf16[8,16,2048]{2,1,0:T(8,128)(2,1)S(1)}, u32[]{:S(2)}, u32[]{:S(2)}) async-start(bf16[8,16,2048]{2,1,0:T(8,128)(2,1)} %get-tuple-element.31), calls=%async_computation | async-start | bytes 1048576 | tf_op jit(solution)/shard_map/all_to_all | solution.py:424
  67.0 23.2 %all-to-all-start.1 = ((bf16[8,160,256]{2,1,0:T(8,128)(2,1)}), bf16[8,160,256]{2,1,0:T(8,128)(2,1)S(1)}, u32[]{:S(2)}, u32[]{:S(2)}) async-start(bf16[8,160,256]{2,1,0:T(8,128)(2,1)} %get-tuple-element.32), calls=%async_computation.1 | async-start | bytes 1310720 | tf_op jit(solution)/shard_map/all_to_all | solution.py:489
  91.2 16.8 %all-to-all-start.2 = ((bf16[32,24,256]{2,1,0:T(8,128)(2,1)}), bf16[32,24,256]{2,1,0:T(8,128)(2,1)S(1)}, u32[]{:S(2)}, u32[]{:S(2)}) async-start(bf16[32,24,256]{2,1,0:T(8,128)(2,1)} %get-tuple-element.41), calls=%async_computation.2 | async-start | bytes 786432 | tf_op jit(solution)/shard_map/all_to_all | solution.py:503

commit v8 on v7

--- a/solution.py
+++ b/solution.py
@@ -14,7 +14,6 @@
 FK = 7
 BF16 = jnp.bfloat16
 F32 = jnp.float32
-CHUNKS = 1
 SHORT = 32
 STEP = 64
 
@@ -84,39 +83,73 @@
     return [jnp.broadcast_to(short[i, lag : lag + 1, lane], (8, 128)) for lag in range(FK)]
 
 
-def edges_kernel(proj, cot, short, *refs):
-    forward, backward = refs[-8:-6]
-    p_tail, p_head, first, second, zeroth, held = refs[-6:]
-    length, width = cot.shape
+def fetch(pairs, semaphores):
+    copies = [pltpu.make_async_copy(source, into, semaphores.at[at]) for at, (source, into) in enumerate(pairs)]
+    for copy in copies:
+        copy.start()
+    return copies
+
+
+def window(block, width):
+    return pl.ds(pl.multiple_of(block * width, width), width)
+
+
+def edges_kernel(
+    proj, cot, short, forward, backward,
+    tails, heads, few, taps_held, p_tail, p_head, first, second, zeroth, held, semaphores,
+):
+    length, channels = cot.shape
+    some, width = p_tail.shape[1], first.shape[1]
     tail, head = 16, 17
-
-    @pl.when(pl.program_id(0) == 0)
-    def _():
-        p_tail[...] = picked(tail, length - 128, length)
-        p_head[...] = picked(head, 0, length)
-
-    first[...] = mm(p_tail[...], proj[1])
-    second[...] = mm(p_tail[...], proj[2])
-    zeroth[...] = mm(p_head[...], proj[0])
-    held[...] = mm(p_head[(FK - 1) * 8 :, :], cot[...])
-    for lane in lanes_of(width):
-        taps = [spread_taps(short, i, lane) for i in range(3)]
-        for r in range(0, 8 * tail, STEP):
-            mixed = featurized(first, taps[1], lane, r, STEP) * featurized(second, taps[2], lane, r, STEP)
-            forward[r : r + STEP, lane] = mixed.reshape(STEP, 128).astype(BF16)
-        for r in range(0, 8 * head, STEP):
-            rows = min(STEP, 8 * head - r)
-            grad = featurized(zeroth, taps[0], lane, r, rows).reshape(rows, 128) * held[r : r + rows, lane]
-            if rows < STEP:
-                starts = [ref[:16, lane].astype(F32)[:8] for ref in (cot, proj.at[1], proj.at[2])]
-                backward[r:, lane] = jnp.concatenate([grad] + starts, axis=0).astype(BF16)
-            else:
-                backward[r : r + rows, lane] = grad.astype(BF16)
-    ends = [proj[i, length - 16 :, :].astype(F32)[8:] for i in range(3)]
-    forward[8 * tail :, :] = jnp.concatenate(ends, axis=0).astype(BF16)
-    if len(refs) > 8:
-        taps, spread = refs[:2]
-        spread[...] = jnp.broadcast_to(taps[...].astype(BF16)[None], spread.shape)
+    copies = fetch(
+        [
+            (proj.at[1, length - some :, :], tails.at[0]),
+            (proj.at[2, length - some :, :], tails.at[1]),
+            (proj.at[0, :some, :], heads.at[0]),
+            (cot.at[:some, :], heads.at[1]),
+            (proj.at[0, length - 16 :, :], few.at[0]),
+            (proj.at[1, :16, :], few.at[1]),
+            (proj.at[2, :16, :], few.at[2]),
+            (short, taps_held),
+        ],
+        semaphores,
+    )
+    p_tail[...] = picked(tail, some - 128, some)
+    p_head[...] = picked(head, 0, some)
+    for copy in copies:
+        copy.wait()
+
+    def block(c, _):
+        columns = window(c, width)
+        first[...] = mm(p_tail[...], tails[0, :, columns])
+        second[...] = mm(p_tail[...], tails[1, :, columns])
+        zeroth[...] = mm(p_head[...], heads[0, :, columns])
+        held[...] = mm(p_head[(FK - 1) * 8 :, :], heads[1, :, columns])
+        for lane in lanes_of(width):
+            wide = pl.ds(pl.multiple_of(c * width + lane.start, 128), 128)
+            taps = [spread_taps(taps_held, i, wide) for i in range(3)]
+            for r in range(0, 8 * tail, STEP):
+                mixed = featurized(first, taps[1], lane, r, STEP) * featurized(second, taps[2], lane, r, STEP)
+                forward[r : r + STEP, wide] = mixed.reshape(STEP, 128).astype(BF16)
+            ends = [few[0, :, wide], tails[0, some - 16 :, wide], tails[1, some - 16 :, wide]]
+            ends = [end.astype(F32)[8:] for end in ends]
+            forward[8 * tail :, wide] = jnp.concatenate(ends, axis=0).astype(BF16)
+            for r in range(0, 8 * head, STEP):
+                rows = min(STEP, 8 * head - r)
+                grad = featurized(zeroth, taps[0], lane, r, rows).reshape(rows, 128) * held[r : r + rows, lane]
+                if rows < STEP:
+                    starts = [heads[1, :16, wide], few[1, :, wide], few[2, :, wide]]
+                    starts = [start.astype(F32)[:8] for start in starts]
+                    backward[r:, wide] = jnp.concatenate([grad] + starts, axis=0).astype(BF16)
+                else:
+                    backward[r : r + rows, wide] = grad.astype(BF16)
+        return 0
+
+    lax.fori_loop(0, channels // width, block, 0)
+
+
+def spread_kernel(taps, spread):
+    spread[...] = jnp.broadcast_to(taps[...].astype(BF16)[None], spread.shape)
 
 
 def conv8(last, first, taps):
@@ -128,41 +161,91 @@
     return total
 
 
-def own_kernel(proj, cot, short, e_own, p_in, feat, px, cots, m_part, g_part, x, moved, mixed, grads):
-    length, width = cot.shape
+def own_kernel(
+    proj_far, cot_far, short_far, e_own_far, p_in_far, feat, px, cots, m_part, g_part,
+    proj, cot, short, e_own, p_in, x, moved, mixed, grads, semaphores,
+):
+    length, channels = cot.shape
+    width = x.shape[2]
     edge = FK - 1
-    for i in range(3):
-        x[i] = mm(p_in[...], proj[i])
-    moved[...] = mm(p_in[edge * 8 :, :], cot[...])
-    for lane in lanes_of(width):
-        taps = [spread_taps(short, i, lane) for i in range(3)]
-        for r in range(0, length, STEP):
-            rows = slice(r, r + STEP)
-            parts = []
-            for i in range(3):
-                px[i, rows, lane] = x[i, r + 8 * edge : r + 8 * edge + STEP, lane].astype(BF16)
-                part = featurized(x.at[i], taps[i], lane, r, STEP).reshape(STEP, 128)
-                feat[i, rows, lane] = part
-                parts.append(part)
-            here = moved[rows, lane]
-            cots[rows, lane] = here.astype(BF16)
-            mixed[rows, lane] = (parts[1] * parts[2]).astype(BF16)
-            grads[rows, lane] = (here * parts[0]).astype(BF16)
-    for out, value in ((m_part, mixed), (g_part, grads)):
-        value = value[...]
-        out[...] = mm(e_own[...], jnp.concatenate([value, value], axis=0))
+    copies = fetch(
+        [(proj_far.at[i], proj.at[i]) for i in range(3)]
+        + [(cot_far, cot), (short_far, short), (p_in_far, p_in), (e_own_far, e_own)],
+        semaphores,
+    )
+    for copy in copies:
+        copy.wait()
+
+    def block(c, _):
+        columns = window(c, width)
+        for i in range(3):
+            x[i] = mm(p_in[...], proj[i, :, columns])
+        moved[...] = mm(p_in[edge * 8 :, :], cot[:, columns])
+        for lane in lanes_of(width):
+            wide = pl.ds(pl.multiple_of(c * width + lane.start, 128), 128)
+            taps = [spread_taps(short, i, wide) for i in range(3)]
+            for r in range(0, length, STEP):
+                rows = slice(r, r + STEP)
+                parts = []
+                for i in range(3):
+                    px[c, i, rows, lane] = x[i, r + 8 * edge : r + 8 * edge + STEP, lane].astype(BF16)
+                    part = featurized(x.at[i], taps[i], lane, r, STEP).reshape(STEP, 128)
+                    feat[c, i, rows, lane] = part
+                    parts.append(part)
+                here = moved[rows, lane]
+                cots[c, rows, lane] = here.astype(BF16)
+                mixed[rows, lane] = (parts[1] * parts[2]).astype(BF16)
+                grads[rows, lane] = (here * parts[0]).astype(BF16)
+        for out, value in ((m_part, mixed), (g_part, grads)):
+            value = value[...]
+            out[c] = mm(e_own[...], jnp.concatenate([value, value], axis=0))
+        return 0
+
+    lax.fori_loop(0, channels // width, block, 0)
 
 
 def finish_kernel(
-    first, prev, later, feat, px, cots, m_part, g_part, taps, ends, starts, short, decay,
-    e_prev, e_next, e_first, e_taps, s_own, s_lags, *refs,
+    prev_all, later_all, feat_all, px_all, cots_all, m_all, g_all, taps_all, proj_far, cot_far, short_far, decay_far,
+    e_prev_far, e_next_far, e_first_far, e_taps_far, s_own_far, s_lags_far,
+    product_all, grad_all, sums_out,
+    ends_all, starts_all, short_all, decay_all, e_prev, e_next, e_first, e_taps, s_own, s_lags,
+    fixed, ms, gs, hs, ks, ys, zs, cs, filtered, grad_mixed, decays, semaphores,
 ):
-    product, grad, sums_out, filter_held, short_held, done = refs[-17:-11]
-    fixed, ms, gs, hs, ks, ys, zs, cs, filtered, grad_mixed, decays = refs[-11:]
-    length, width = cots.shape
-    span = length // 8
+    length, width = cots_all.shape[1:]
+    pairs = [
+        (proj_far.at[:, length - 16 :, :], ends_all), (cot_far.at[:16, :], starts_all), (short_far, short_all),
+        (decay_far, decay_all), (e_prev_far, e_prev), (e_first_far, e_first), (e_next_far, e_next),
+        (e_taps_far, e_taps), (s_own_far, s_own), (s_lags_far, s_lags),
+    ]
+    copies = fetch(pairs, semaphores)
+    for copy in copies:
+        copy.wait()
+
+    def block(c, _):
+        columns = window(c, width)
+        narrow = [prev_all, later_all, taps_all, starts_all, decay_all]
+        prev, later, taps, starts, decay = [ref.at[:, columns] for ref in narrow]
+        ends, short = ends_all.at[:, :, columns], short_all.at[:, :, columns]
+        feat, px, cots, m_part, g_part, product, grad = [
+            ref.at[c] for ref in (feat_all, px_all, cots_all, m_all, g_all, product_all, grad_all)
+        ]
+        finish_block(
+            c, prev, later, feat, px, cots, m_part, g_part, taps, ends, starts, short, decay,
+            e_prev, e_next, e_first, e_taps, s_own, s_lags, product, grad, sums_out,
+            fixed, ms, gs, hs, ks, ys, zs, cs, filtered, grad_mixed, decays,
+        )
+        return 0
+
+    lax.fori_loop(0, cots_all.shape[0], block, 0)
+
+
+def finish_block(
+    block, prev, later, feat, px, cots, m_part, g_part, taps, ends, starts, short, decay,
+    e_prev, e_next, e_first, e_taps, s_own, s_lags, product, grad, sums_out,
+    fixed, ms, gs, hs, ks, ys, zs, cs, filtered, grad_mixed, decays,
+):
+    length, width = 8 * (grad.shape[1] // 8 - FK + 1), ms.shape[1]
     edge = FK - 1
-    step, steps = pl.program_id(0), pl.num_programs(0)
     row8 = lax.broadcasted_iota(jnp.int32, (8, width), 0)
     before = prev[...].astype(F32)
     after = later[...].astype(F32)
@@ -171,6 +254,7 @@
     next8 = [None, after[144:152], after[152:160]]
     ends8 = [ends[i].astype(F32)[8:] for i in range(3)]
     cot_first = starts[...].astype(F32)[:8]
+    short = [short[i] for i in range(3)]
 
     fixes = [conv8(prev8[i], None, short[i]) for i in range(3)]
     heads = []
@@ -202,7 +286,7 @@
     ms[...] = mm(e_prev[...], mixed_edge)
     hs[...] = mm(e_first[...], grad_first)
     gs[...] = mm(e_next[...], grad_edge)
-    lags = lax.broadcasted_iota(jnp.int32, (taps.shape[0], width), 0).astype(F32)
+    lags = lax.broadcasted_iota(jnp.int32, decays.shape, 0).astype(F32)
     decays[...] = jnp.exp(-decay[...] * lags)
     kernel = taps[...].astype(F32) * decays[...]
     high = kernel.astype(BF16)
@@ -266,54 +350,35 @@
                 rows[lag].append(jnp.sum(sums[lag], axis=0, keepdims=True))
         short_rows += [jnp.concatenate(row, axis=1) for row in rows]
 
-    ranks, slot, _ = filter_held.shape
-    per, share, block = filter_sums.shape[0] // ranks, short_held.shape[0], first + step
-    copies = [
-        pltpu.make_async_copy(
-            filter_held, sums_out.at[:, pl.ds(pl.multiple_of(block * slot, slot), slot), :], done.at[0]
-        ),
-        pltpu.make_async_copy(
-            short_held,
-            sums_out.at[pl.ds(block * share, share), pl.ds(sums_out.shape[1] - SHORT, SHORT), :],
-            done.at[1],
-        ),
-    ]
-
-    @pl.when(step > 0)
-    def _():
-        for copy in copies:
-            copy.wait()
-
+    ranks, total, _ = sums_out.shape
+    per = filter_sums.shape[0] // ranks
+    slot = -(-per // 16) * 16
+    share = ranks * slot // (total - SHORT)
     if per % 8 == 0:
         by_rank = filter_sums.reshape(ranks, per, width)
     else:
         by_rank = jnp.stack([filter_sums[rank * per : rank * per + per] for rank in range(ranks)])
     if slot > per:
         by_rank = jnp.concatenate([by_rank, jnp.zeros((ranks, slot - per, width), F32)], axis=1)
-    filter_held[...] = by_rank.astype(BF16)
+    sums_out[:, pl.ds(pl.multiple_of(block * slot, slot), slot), :] = by_rank.astype(BF16)
     sums = jnp.concatenate(short_rows + [jnp.zeros((SHORT - len(short_rows), width), F32)], axis=0)
     for rank in range(share):
         held = pltpu.roll(sums, width - rank * (width // share), 1) if rank else sums
-        short_held[rank] = held.astype(BF16)
-    for copy in copies:
-        copy.start()
-
-    @pl.when(step == steps - 1)
-    def _():
-        for copy in copies:
-            copy.wait()
+        sums_out[block * share + rank, total - SHORT :, :] = held.astype(BF16)
 
 
 def outputs_kernel(product, grad, short, p_out, gated, grad_proj, held):
-    length, width = product.shape
-    gated[...] = mm(p_out[...], product[...]).astype(BF16)
+    c = pl.program_id(0)
+    length, width = product.shape[1:]
+    gated[...] = mm(p_out[...], product[c]).astype(BF16)
     for i in range(3):
         for lane in lanes_of(width):
             taps = spread_taps(short, i, lane)
             for r in range(0, length, STEP):
                 total = None
                 for lag in range(FK):
-                    part = grad[i, r + 8 * lag : r + 8 * lag + STEP, lane].reshape(STEP // 8, 8, 128) * taps[lag]
+                    at = slice(r + 8 * lag, r + 8 * lag + STEP)
+                    part = grad[c, i, at, lane].reshape(STEP // 8, 8, 128) * taps[lag]
                     total = part if total is None else total + part
                 held[i, r : r + STEP, lane] = total.reshape(STEP, 128).astype(BF16)
         grad_proj[i] = mm(p_out[...], held[i]).astype(BF16)
@@ -328,27 +393,20 @@
     return pl.BlockSpec(tuple(rows) + (width,), lambda c: lead + (first + c,))
 
 
-def call(kernel, name, operands, outputs, width, constants=(), cost=1, first=0, blocks=None, held=(), **options):
-    spec = lambda rows: rows if isinstance(rows, pl.BlockSpec) else columns(rows, width, first)
-    aliases = {len(operands) + len(constants) + at: at for at in range(len(held))}
-    constants = [pltpu.with_memory_space_constraint(jnp.asarray(constant), pltpu.HBM) for constant in constants]
-    operands = [
-        (array if isinstance(rows, pl.BlockSpec) else pltpu.with_memory_space_constraint(array, pltpu.HBM), rows)
-        for array, rows in operands
-    ]
+def call(kernel, name, operands, outputs, cost=1, limit=24, **options):
+    vmem, far = pl.BlockSpec(memory_space=pltpu.VMEM), pl.BlockSpec(memory_space=pl.ANY)
+    if "in_specs" not in options:
+        options["in_specs"] = [far if stays else vmem for _, stays in operands]
+        options["out_specs"] = [vmem] * len(outputs)
+    arrays = [pltpu.with_memory_space_constraint(array, pltpu.HBM) if stays else array for array, stays in operands]
     return pl.pallas_call(
         kernel,
-        grid=(blocks or operands[0][0].shape[-1] // width,),
-        in_specs=[spec(rows) for _, rows in operands] + [whole(constant) for constant in constants]
-        + [pl.BlockSpec(memory_space=pl.ANY)] * len(held),
-        out_specs=[spec(rows) for _, rows in outputs],
-        out_shape=[shape for shape, _ in outputs],
-        compiler_params=pltpu.CompilerParams(vmem_limit_bytes=40 << 20),
+        out_shape=outputs,
+        compiler_params=pltpu.CompilerParams(vmem_limit_bytes=limit << 20),
         cost_estimate=pl.CostEstimate(flops=cost * 10**9, bytes_accessed=10**6, transcendentals=0),
-        input_output_aliases=aliases,
         name=name,
         **options,
-    )(*[array for array, _ in operands], *constants, *held)
+    )(*arrays)
 
 
 def squares_kernel(rows, share, sums, raw, payload):
@@ -391,55 +449,53 @@
     ranks, groups = lax.axis_size("seq"), lax.axis_size("ch")
     rows = filter_taps.shape[0]
     count = rows * ranks
-    width = min(256, channels // CHUNKS)
+    width = min(256, channels)
+    blocks = channels // width
     share = channels // ranks
     slot = -(-rows // 16) * 16
     size, span = 2 * length, length // 8
     extended = length + 8 * (FK - 1)
-    proj, cot, short, decay = (
-        pltpu.with_memory_space_constraint(array, pltpu.HBM)
-        for array in (jnp.transpose(projected, (1, 0, 2)), cotangent, short_taps, decay[None])
-    )
-    floats = lambda *shape: pltpu.HBM(shape + (channels,), F32)
-    halves_of = lambda *shape: pltpu.HBM(shape + (channels,), BF16)
+    some = 144
+    proj, cot, short, decay = jnp.transpose(projected, (1, 0, 2)), cotangent, short_taps, decay[None]
+    full = lambda kind, *shape: jax.ShapeDtypeStruct(shape, kind)
+    vmem = lambda kind, *shape: pltpu.VMEM(shape, kind)
+    copied = lambda array: pltpu.VMEM(array.shape, array.dtype)
+    semaphores = pltpu.SemaphoreType.DMA((10,))
     own = interleaved(span)
     after = length + np.arange(8)
 
-    blocks = channels // width // CHUNKS
-    prev, later, taps = [], [], None
-    for k in range(CHUNKS):
-        operands = [(proj, (3, length)), (cot, (length,)), (short, (3, FK))]
-        results = [
-            (jax.ShapeDtypeStruct((count, blocks * width), BF16), columns((count,), width)) for count in (152, 160)
-        ]
-        if k == 0:
-            operands.append((filter_taps, columns((rows,), channels // blocks)))
-            results.insert(0, (pltpu.HBM((ranks, rows, channels), BF16), columns((ranks, rows), channels // blocks)))
-        *spread, forward, backward = call(
-            edges_kernel, "edges", operands, results, width, cost=1, first=k * blocks, blocks=blocks,
-            scratch_shapes=[pltpu.VMEM(((at + FK - 1) * 8, length), BF16) for at in (16, 17)]
-            + [pltpu.VMEM((at * 8, width), F32) for at in (15 + FK, 15 + FK, 16 + FK, 17)],
-        )
-        if k == 0:
-            taps = lax.all_to_all(spread[0], "seq", 0, 0).reshape(count, channels)
-        else:
-            forward, backward, prev[-1], later[-1] = lax.optimization_barrier((forward, backward, prev[-1], later[-1]))
-        prev.append(from_behind(forward, "seq", 1))
-        later.append(from_behind(backward, "seq", -1))
-
+    forward, backward = call(
+        edges_kernel, "edges", [(proj, True), (cot, True), (short, True)],
+        [full(BF16, 152, channels), full(BF16, 160, channels)],
+        scratch_shapes=[
+            vmem(BF16, 2, some, channels), vmem(BF16, 2, some, channels), vmem(BF16, 3, 16, channels), copied(short),
+            vmem(BF16, 8 * (15 + FK), some), vmem(BF16, 8 * (16 + FK), some), vmem(F32, 8 * (15 + FK), width),
+            vmem(F32, 8 * (15 + FK), width), vmem(F32, 8 * (16 + FK), width), vmem(F32, 8 * 17, width), semaphores,
+        ],
+    )
+    filter_taps, forward = lax.optimization_barrier((filter_taps, forward))
+    prev = from_behind(forward, "seq", 1)
+    later = from_behind(backward, "seq", -1)
+    spread = pl.pallas_call(
+        spread_kernel,
+        out_shape=pltpu.HBM((ranks, rows, channels), BF16),
+        cost_estimate=pl.CostEstimate(flops=0, bytes_accessed=10**6, transcendentals=0),
+        name="spread",
+    )(filter_taps)
+    taps = lax.all_to_all(spread, "seq", 0, 0).reshape(count, channels)
+
+    e_own = jnp.asarray(np.concatenate(list(analysis(own, size)), axis=1))
+    p_in = jnp.asarray(pick(interleaved(span, 0, 1 - FK), length))
     feat, px, cots, m_part, g_part = call(
-        own_kernel, "own",
-        [(proj, (3, length)), (cot, (length,)), (short, (3, FK))],
+        own_kernel, "own", [(array, True) for array in (proj, cot, short, e_own, p_in)],
         [
-            (floats(3, length), (3, length)), (halves_of(3, length), (3, length)), (halves_of(length), (length,)),
-            (floats(size), (size,)), (floats(size), (size,)),
-        ],
-        width,
-        [np.concatenate(list(analysis(own, size)), axis=1), pick(interleaved(span, 0, 1 - FK), length)],
+            full(F32, blocks, 3, length, width), full(BF16, blocks, 3, length, width),
+            full(BF16, blocks, length, width), full(F32, blocks, size, width), full(F32, blocks, size, width),
+        ],
         cost=10,
-        scratch_shapes=[
-            pltpu.VMEM((3, extended, width), F32), pltpu.VMEM((length, width), F32),
-            pltpu.VMEM((length, width), BF16), pltpu.VMEM((length, width), BF16),
+        scratch_shapes=[copied(array) for array in (proj, cot, short, e_own, p_in)] + [
+            vmem(F32, 3, extended, width), vmem(F32, length, width), vmem(BF16, length, width),
+            vmem(BF16, length, width), semaphores,
         ],
     )
 
@@ -452,39 +508,29 @@
         np.concatenate(list(synthesis(np.concatenate([own, after]), size)), axis=1),
         np.concatenate(list(synthesis(np.arange(count), size)), axis=1),
     ]
-    held = ()
-    for k in range(CHUNKS):
-        first = k * blocks
-        held = call(
-            functools.partial(finish_kernel, first), "finish",
-            [
-                (prev[k], columns((152,), width)), (later[k], columns((160,), width)), (feat, (3, length)),
-                (px, (3, length)), (cots, (length,)), (m_part, (size,)), (g_part, (size,)), (taps, columns((count,), width, first)),
-                (proj, pl.BlockSpec((3, 16, width), lambda c, first=first: (0, length // 16 - 1, first + c))),
-                (cot, (16,)), (short, (3, FK)), (decay, (1,)),
-            ],
-            [
-                (halves_of(length), (length,)), (floats(3, extended), (3, extended)),
-                (
-                    pltpu.HBM((ranks, channels // width * slot + SHORT, width), BF16),
-                    pl.BlockSpec(memory_space=pl.ANY),
-                ),
-            ],
-            width, constants, cost=6, first=first, blocks=blocks, held=held,
-            scratch_shapes=[
-                pltpu.VMEM((ranks, slot, width), BF16),
-                pltpu.VMEM((ranks * width // channels, SHORT, width), BF16),
-                pltpu.SemaphoreType.DMA((2,)),
-                pltpu.VMEM((3, STEP, width), F32),
-            ] + [pltpu.VMEM((size, width), F32)] * 4 + [pltpu.VMEM((size, width), BF16)] * 3
-            + [pltpu.VMEM((length + 8, width), F32)] * 2 + [pltpu.VMEM((count, width), F32)],
-        )
-    product, grad, sums = held
+    constants = [jnp.asarray(constant) for constant in constants]
+    product, grad, sums = call(
+        finish_kernel, "finish",
+        [(array, False) for array in (prev, later, feat, px, cots, m_part, g_part, taps)]
+        + [(array, True) for array in [proj, cot, short, decay] + constants],
+        [
+            full(BF16, blocks, length, width), full(F32, blocks, 3, extended, width),
+            full(BF16, ranks, blocks * slot + SHORT, width),
+        ],
+        cost=12,
+        scratch_shapes=[vmem(BF16, 3, 16, channels), vmem(BF16, 16, channels), copied(short), copied(decay)]
+        + [copied(constant) for constant in constants]
+        + [vmem(F32, 3, STEP, width)] + [vmem(F32, size, width)] * 4 + [vmem(BF16, size, width)] * 3
+        + [vmem(F32, length + 8, width)] * 2 + [vmem(F32, count, width), semaphores],
+    )
+    p_out = jnp.asarray(pick(own, length).T)
+    inside = pl.BlockSpec(memory_space=pltpu.VMEM)
     gated, grad_proj = call(
-        outputs_kernel, "outputs",
-        [(product, (length,)), (grad, (3, extended)), (short, (3, FK))],
-        [(halves_of(length), (length,)), (halves_of(3, length), (3, length))],
-        width, [pick(own, length).T], cost=8, scratch_shapes=[pltpu.VMEM((3, length, width), BF16)],
+        outputs_kernel, "outputs", [(product, False), (grad, False), (short, True), (p_out, True)],
+        [full(BF16, length, channels), full(BF16, 3, length, channels)], cost=8,
+        grid=(blocks,), in_specs=[inside, inside, columns((3, FK), width), whole(p_out)],
+        out_specs=[columns((length,), width), columns((3, length), width)],
+        scratch_shapes=[vmem(BF16, 3, length, width)],
     )
     sums, gated, grad_proj = lax.optimization_barrier((lax.all_to_all(sums, "seq", 0, 0), gated, grad_proj))
 

time: 111 us -> 118 us (1.063)
  local copies, waits for them, and re-layouts: 0.9 us -> 25.8 us
  waiting for transfers between devices: 34.3 us -> 24.5 us
  Pallas kernels: 51 us -> 44.8 us
    unnamed x2 -> x24, local copies, waits for them, and re-layouts: 0.9 us -> 25.8 us
    ppermute x2, waiting for transfers between devices: 12.3 us -> 3.7 us  [from_behind(): return lax.ppermute(value, axis, pairs)]
    pallas_call x4 -> x5, Pallas kernels: 48.7 us -> 42.5 us  [the longest x4 40.7 us: call(): pl.pallas_call(kernel, out_shape=outputs, compiler_params=pltpu.CompilerP...]
    all_to_all x1, starting transfers between devices: 6.19 us -> 4.84 us  [shards(): taps = lax.all_to_all(spread, 'seq', 0, 0).reshape(count, channels)]
  transfers between devices with their start and end apart: 5 -> 5, of which waited for: 4 -> 4; matrix products, arithmetic and copies ran while one was open for 0% -> 0% of each run, Pallas kernels for 20% -> 17%
where the time goes in v8:
time: 118 us; the launch traced here: 117 us
  Pallas kernels  44.8 us (38%)
  local copies, waits for them, and re-layouts  25.8 us (22%)
  waiting for transfers between devices  24.5 us (21%)
  starting transfers between devices  21.3 us (18%)
    pallas_call x4, Pallas kernels, call(): pl.pallas_call(kernel, out_shape=outputs, compiler_params=pltpu.CompilerP...  40.7 us
    unnamed x24, local copies, waits for them, and re-layouts  25.8 us
    all_to_all x1, waiting for transfers between devices, shards(): gathered = lax.all_to_all(payload, ('seq', 'ch'), 0, 0)  13.1 us
    all_to_all x1, waiting for transfers between devices, shards(): lax.all_to_all(sums, 'seq', 0, 0)  6.92 us
    all_to_all x1, starting transfers between devices, shards(): lax.all_to_all(sums, 'seq', 0, 0)  6.64 us
    ppermute x2, starting transfers between devices, from_behind(): return lax.ppermute(value, axis, pairs)  6.19 us
    all_to_all x1, starting transfers between devices, shards(): taps = lax.all_to_all(spread, 'seq', 0, 0).reshape(count, channels)  4.84 us
    ppermute x2, waiting for transfers between devices, from_behind(): return lax.ppermute(value, axis, pairs)  3.7 us
  transfers between devices with their start and end apart: 5, of which 4 were waited for; matrix products, arithmetic and copies ran while one was open for 0% of the time, Pallas kernels for 17%

profile of v8, /device:TPU:0, one launch (start us, length us, event | category | flops | bytes accessed | tf_op | source)
XLA Modules:
  0.0 117.2 jit_solution(4886358012340157921)
XLA Ops:
  0.6 4.8 %edges.1 = (bf16[152,2048]{1,0:T(8,128)(2,1)S(1)}, bf16[160,2048]{1,0:T(8,128)(2,1)S(1)}) custom-call(bf16[3,256,2048]{2,1,0:T(8,128)(2,1)} %bitcast.6, bf16[256,2048]{1,0:T(8,128)(2,1)} %cot_far.3, f32[3,7,2048]{2,1,0:T(8,128)} %short.3), custom_call_target="tpu_custom_call" | custom-call | flops 1000000000 | bytes 1000000 | tf_op jit(solution)/shard_map/edges/pallas_call | solution.py:402
  5.5 4.9 %collective-permute-start = (bf16[152,2048]{1,0:T(8,128)(2,1)S(1)}, bf16[152,2048]{1,0:T(8,128)(2,1)S(1)}, u32[]{:S(2)}, u32[]{:S(2)}) collective-permute-start(bf16[152,2048]{1,0:T(8,128)(2,1)S(1)} %get-tuple-element.26), channel_id=1, source_target_pairs={{0,4},{4,8},{8,12},{12,16},{16,20},{20,24},{24,28},{1,5},{5,9},{9,... | collective-permute-start | bytes 1867784 | tf_op jit(solution)/shard_map/ppermute | solution.py:24
  10.4 1.7 %spread.1 = bf16[8,16,2048]{2,1,0:T(8,128)(2,1)} custom-call(f32[16,2048]{1,0:T(8,128)} %taps), custom_call_target="tpu_custom_call" | custom-call | bytes 1000000 | tf_op jit(solution)/shard_map/spread/pallas_call | solution.py:479
  12.1 4.8 %all-to-all-start = ((bf16[8,16,2048]{2,1,0:T(8,128)(2,1)}), bf16[8,16,2048]{2,1,0:T(8,128)(2,1)S(1)}, u32[]{:S(2)}, u32[]{:S(2)}) async-start(bf16[8,16,2048]{2,1,0:T(8,128)(2,1)} %spread.1), calls=%async_computation | async-start | bytes 1048576 | tf_op jit(solution)/shard_map/all_to_all | solution.py:485
  17.0 1.3 %collective-permute-start.1 = (bf16[160,2048]{1,0:T(8,128)(2,1)S(1)}, bf16[160,2048]{1,0:T(8,128)(2,1)S(1)}, u32[]{:S(2)}, u32[]{:S(2)}) collective-permute-start(bf16[160,2048]{1,0:T(8,128)(2,1)S(1)} %get-tuple-element.27), channel_id=1, source_target_pairs={{4,0},{8,4},{12,8},{16,12},{20,16},{24,20},{28,24},{5,1},{9,5},{13... | collective-permute-start | bytes 1966088 | tf_op jit(solution)/shard_map/ppermute | solution.py:24
  18.3 11.2 %own.1 = (f32[8,3,256,256]{3,2,1,0:T(8,128)S(1)}, bf16[8,3,256,256]{3,2,1,0:T(8,128)(2,1)S(1)}, bf16[8,256,256]{2,1,0:T(8,128)(2,1)S(1)}, f32[8,512,256]{2,1,0:T(8,128)S(1)}, f32[8,512,256]{2,1,0:T(8,128)S(1)}) custom-call(bf16[3,256,2048]{2,1,0:T(8,128)(2,1)} %bitcast.7, bf16[256,2048]{1,0:T(8,128)(2,1)} %cot_far.3, f32[3,7,2048]{2,1,0:T(8,128)} %short.3, ...), custom_call_target="tpu_custom_call" | custom-call | flops 10000000000 | bytes 1000000 | tf_op jit(solution)/shard_map/own/pallas_call | solution.py:402
  29.5 0.0 copy-start.2
  29.5 2.6 %copy-done.2 = f32[8,3,256,256]{3,2,1,0:T(8,128)} copy-done((f32[8,3,256,256]{3,2,1,0:T(8,128)}, f32[8,3,256,256]{3,2,1,0:T(8,128)S(1)}, u32[]{:S(2)}) %copy-start.2) | copy-done | bytes 6291480
  32.1 0.0 copy-start.4
  32.1 2.1 %copy-done.4 = f32[8,512,256]{2,1,0:T(8,128)} copy-done((f32[8,512,256]{2,1,0:T(8,128)}, f32[8,512,256]{2,1,0:T(8,128)S(1)}, u32[]{:S(2)}) %copy-start.4) | copy-done | bytes 4194328
  34.2 0.0 copy-start.6
  34.2 2.1 %copy-done.6 = f32[8,512,256]{2,1,0:T(8,128)} copy-done((f32[8,512,256]{2,1,0:T(8,128)}, f32[8,512,256]{2,1,0:T(8,128)S(1)}, u32[]{:S(2)}) %copy-start.6) | copy-done | bytes 4194328
  36.3 0.0 copy-start.8
  36.3 1.7 %copy-done.8 = bf16[8,3,256,256]{3,2,1,0:T(8,128)(2,1)} copy-done((bf16[8,3,256,256]{3,2,1,0:T(8,128)(2,1)}, bf16[8,3,256,256]{3,2,1,0:T(8,128)(2,1)S(1)}, u32[]{:S(2)}) %copy-start.8) | copy-done | bytes 3145752
  37.9 0.0 copy-start.10
  37.9 1.0 copy-done.10
  38.9 3.7 %collective-permute-done.prev_all = bf16[152,2048]{1,0:T(8,128)(2,1)S(1)} collective-permute-done((bf16[152,2048]{1,0:T(8,128)(2,1)S(1)}, bf16[152,2048]{1,0:T(8,128)(2,1)S(1)}, u32[]{:S(2)}, u32[]{:S(2)}) %collective-permute-start) | collective-permute-done | bytes 622624 | tf_op jit(solution)/shard_map/ppermute | solution.py:24
  42.6 0.0 collective-permute-done.1.later_all
  42.6 0.8 all-to-all-done
  43.4 0.0 copy-start.3
  43.4 2.8 %copy-done.3 = f32[8,3,256,256]{3,2,1,0:T(8,128)S(1)} copy-done((f32[8,3,256,256]{3,2,1,0:T(8,128)S(1)}, f32[8,3,256,256]{3,2,1,0:T(8,128)}, u32[]{:S(2)}) %copy-start.3) | copy-done | bytes 6291480
  46.2 0.0 copy-start.5
  46.2 2.2 %copy-done.5 = f32[8,512,256]{2,1,0:T(8,128)S(1)} copy-done((f32[8,512,256]{2,1,0:T(8,128)S(1)}, f32[8,512,256]{2,1,0:T(8,128)}, u32[]{:S(2)}) %copy-start.5) | copy-done | bytes 4194328
  48.4 0.0 copy-start.7
  48.4 2.2 %copy-done.7 = f32[8,512,256]{2,1,0:T(8,128)S(1)} copy-done((f32[8,512,256]{2,1,0:T(8,128)S(1)}, f32[8,512,256]{2,1,0:T(8,128)}, u32[]{:S(2)}) %copy-start.7) | copy-done | bytes 4194328
  50.6 0.0 copy-start.9
  50.6 1.9 %copy-done.9 = bf16[8,3,256,256]{3,2,1,0:T(8,128)(2,1)S(1)} copy-done((bf16[8,3,256,256]{3,2,1,0:T(8,128)(2,1)S(1)}, bf16[8,3,256,256]{3,2,1,0:T(8,128)(2,1)}, u32[]{:S(2)}) %copy-start.9) | copy-done | bytes 3145752
  52.5 0.0 copy-start.11
  52.5 1.2 %copy-done.11 = bf16[8,256,256]{2,1,0:T(8,128)(2,1)S(1)} copy-done((bf16[8,256,256]{2,1,0:T(8,128)(2,1)S(1)}, bf16[8,256,256]{2,1,0:T(8,128)(2,1)}, u32[]{:S(2)}) %copy-start.11) | copy-done | bytes 1048600
  53.7 17.3 %finish.1 = (bf16[8,256,256]{2,1,0:T(8,128)(2,1)S(1)}, f32[8,3,304,256]{3,2,1,0:T(8,128)S(1)}, bf16[8,160,256]{2,1,0:T(8,128)(2,1)}) custom-call(bf16[152,2048]{1,0:T(8,128)(2,1)S(1)} %collective-permute-done.prev_all, bf16[160,2048]{1,0:T(8,128)(2,1)S(1)} %collective-permute-done.1.later_all, f32[8,3,256,256]{3,2,1,0:T(8,128)S(1)} %copy-done.3, ...), custom_call_target="tpu_custom_call" | custom-call | flops 12000000000 | bytes 1000000 | tf_op jit(solution)/shard_map/finish/pallas_call | solution.py:402
  71.0 0.0 copy-start
  71.0 3.0 %copy-done = f32[8,3,304,256]{3,2,1,0:T(8,128)} copy-done((f32[8,3,304,256]{3,2,1,0:T(8,128)}, f32[8,3,304,256]{3,2,1,0:T(8,128)S(1)}, u32[]{:S(2)}) %copy-start) | copy-done | bytes 7471128
  73.9 6.6 %all-to-all-start.1 = ((bf16[8,160,256]{2,1,0:T(8,128)(2,1)}), bf16[8,160,256]{2,1,0:T(8,128)(2,1)S(1)}, u32[]{:S(2)}, u32[]{:S(2)}) async-start(bf16[8,160,256]{2,1,0:T(8,128)(2,1)} %get-tuple-element.34), calls=%async_computation.1 | async-start | bytes 1310720 | tf_op jit(solution)/shard_map/all_to_all | solution.py:535
  80.6 0.0 copy-start.1
  80.6 3.1 %copy-done.1 = f32[8,3,304,256]{3,2,1,0:T(8,128)S(1)} copy-done((f32[8,3,304,256]{3,2,1,0:T(8,128)S(1)}, f32[8,3,304,256]{3,2,1,0:T(8,128)}, u32[]{:S(2)}) %copy-start.1) | copy-done | bytes 7471128
  83.7 7.4 %outputs.1 = (bf16[256,2048]{1,0:T(8,128)(2,1)}, bf16[3,256,2048]{2,1,0:T(8,128)(2,1)}) custom-call(bf16[8,256,256]{2,1,0:T(8,128)(2,1)S(1)} %get-tuple-element.35.product, f32[8,3,304,256]{3,2,1,0:T(8,128)S(1)} %copy-done.1, f32[3,7,2048]{2,1,0:T(8,128)} %short.3, bf16[256,256]{1,0:T(8,128)(2,1)} %constant.32.clone.p_out), custom_call_target="tpu_custom_call" | custom-call | flops 8000000000 | bytes 1000000 | tf_op jit(solution)/shard_map/outputs/pallas_call | solution.py:402
  91.1 6.9 %all-to-all-done.1.sums = bf16[8,160,256]{2,1,0:T(8,128)(2,1)S(1)} async-done(((bf16[8,160,256]{2,1,0:T(8,128)(2,1)}), bf16[8,160,256]{2,1,0:T(8,128)(2,1)S(1)}, u32[]{:S(2)}, u32[]{:S(2)}) %all-to-all-start.1) | async-done | bytes 655392 | tf_op jit(solution)/shard_map/all_to_all | solution.py:535
  98.0 1.0 squares.1
  99.0 3.7 %all-to-all-start.2 = ((bf16[32,24,256]{2,1,0:T(8,128)(2,1)}), bf16[32,24,256]{2,1,0:T(8,128)(2,1)S(1)}, u32[]{:S(2)}, u32[]{:S(2)}) async-start(bf16[32,24,256]{2,1,0:T(8,128)(2,1)} %get-tuple-element.43), calls=%async_computation.2 | async-start | bytes 786432 | tf_op jit(solution)/shard_map/all_to_all | solution.py:549
  102.7 0.1 pad_add_fusion.mine
  102.8 13.1 %all-to-all-done.2.gathered = bf16[32,24,256]{2,1,0:T(8,128)(2,1)S(1)} async-done(((bf16[32,24,256]{2,1,0:T(8,128)(2,1)}), bf16[32,24,256]{2,1,0:T(8,128)(2,1)S(1)}, u32[]{:S(2)}, u32[]{:S(2)}) %all-to-all-start.2) | async-done | bytes 393248 | tf_op jit(solution)/shard_map/all_to_all | solution.py:549
  115.9 1.4 %scale.1 = (f32[3,7,2048]{2,1,0:T(8,128)}, f32[16,2048]{1,0:T(8,128)}) custom-call(s32[2]{0:T(128)S(1)} %pad_add_fusion.mine, f32[16,2048]{1,0:T(8,128)S(1)} %get-tuple-element.42.raw, bf16[32,24,256]{2,1,0:T(8,128)(2,1)S(1)} %all-to-all-done.2.gathered), custom_call_target="tpu_custom_call" | custom-call | tf_op jit(solution)/shard_map/scale/pallas_call | solution.py:552
Async XLA Ops:
  5.5 37.1 %collective-permute-start = (bf16[152,2048]{1,0:T(8,128)(2,1)S(1)}, bf16[152,2048]{1,0:T(8,128)(2,1)S(1)}, u32[]{:S(2)}, u32[]{:S(2)}) collective-permute-start(bf16[152,2048]{1,0:T(8,128)(2,1)S(1)} %get-tuple-element.26), channel_id=1, source_target_pairs={{0,4},{4,8},{8,12},{12,16},{16,20},{20,24},{24,28},{1,5},{5,9},{9,... | collective-permute-start | bytes 1867784 | tf_op jit(solution)/shard_map/ppermute | solution.py:24
  12.1 31.3 %all-to-all-start = ((bf16[8,16,2048]{2,1,0:T(8,128)(2,1)}), bf16[8,16,2048]{2,1,0:T(8,128)(2,1)S(1)}, u32[]{:S(2)}, u32[]{:S(2)}) async-start(bf16[8,16,2048]{2,1,0:T(8,128)(2,1)} %spread.1), calls=%async_computation | async-start | bytes 1048576 | tf_op jit(solution)/shard_map/all_to_all | solution.py:485
  17.0 25.6 %collective-permute-start.1 = (bf16[160,2048]{1,0:T(8,128)(2,1)S(1)}, bf16[160,2048]{1,0:T(8,128)(2,1)S(1)}, u32[]{:S(2)}, u32[]{:S(2)}) collective-permute-start(bf16[160,2048]{1,0:T(8,128)(2,1)S(1)} %get-tuple-element.27), channel_id=1, source_target_pairs={{4,0},{8,4},{12,8},{16,12},{20,16},{24,20},{28,24},{5,1},{9,5},{13... | collective-permute-start | bytes 1966088 | tf_op jit(solution)/shard_map/ppermute | solution.py:24
  29.5 2.7 %copy-start.2 = (f32[8,3,256,256]{3,2,1,0:T(8,128)}, f32[8,3,256,256]{3,2,1,0:T(8,128)S(1)}, u32[]{:S(2)}) copy-start(f32[8,3,256,256]{3,2,1,0:T(8,128)S(1)} %get-tuple-element.28.feat_all) | copy-start | bytes 18874372
  32.1 2.1 %copy-start.4 = (f32[8,512,256]{2,1,0:T(8,128)}, f32[8,512,256]{2,1,0:T(8,128)S(1)}, u32[]{:S(2)}) copy-start(f32[8,512,256]{2,1,0:T(8,128)S(1)} %get-tuple-element.31.m_all) | copy-start | bytes 12582916
  34.2 2.1 %copy-start.6 = (f32[8,512,256]{2,1,0:T(8,128)}, f32[8,512,256]{2,1,0:T(8,128)S(1)}, u32[]{:S(2)}) copy-start(f32[8,512,256]{2,1,0:T(8,128)S(1)} %get-tuple-element.32.g_all) | copy-start | bytes 12582916
  36.3 1.7 %copy-start.8 = (bf16[8,3,256,256]{3,2,1,0:T(8,128)(2,1)}, bf16[8,3,256,256]{3,2,1,0:T(8,128)(2,1)S(1)}, u32[]{:S(2)}) copy-start(bf16[8,3,256,256]{3,2,1,0:T(8,128)(2,1)S(1)} %get-tuple-element.29.px_all) | copy-start | bytes 9437188
  37.9 1.0 copy-start.10
  43.4 2.8 %copy-start.3 = (f32[8,3,256,256]{3,2,1,0:T(8,128)S(1)}, f32[8,3,256,256]{3,2,1,0:T(8,128)}, u32[]{:S(2)}) copy-start(f32[8,3,256,256]{3,2,1,0:T(8,128)} %copy-done.2) | copy-start | bytes 18874372
  46.2 2.2 %copy-start.5 = (f32[8,512,256]{2,1,0:T(8,128)S(1)}, f32[8,512,256]{2,1,0:T(8,128)}, u32[]{:S(2)}) copy-start(f32[8,512,256]{2,1,0:T(8,128)} %copy-done.4) | copy-start | bytes 12582916
  48.4 2.2 %copy-start.7 = (f32[8,512,256]{2,1,0:T(8,128)S(1)}, f32[8,512,256]{2,1,0:T(8,128)}, u32[]{:S(2)}) copy-start(f32[8,512,256]{2,1,0:T(8,128)} %copy-done.6) | copy-start | bytes 12582916
  50.6 1.9 %copy-start.9 = (bf16[8,3,256,256]{3,2,1,0:T(8,128)(2,1)S(1)}, bf16[8,3,256,256]{3,2,1,0:T(8,128)(2,1)}, u32[]{:S(2)}) copy-start(bf16[8,3,256,256]{3,2,1,0:T(8,128)(2,1)} %copy-done.8) | copy-start | bytes 9437188
  52.5 1.2 %copy-start.11 = (bf16[8,256,256]{2,1,0:T(8,128)(2,1)S(1)}, bf16[8,256,256]{2,1,0:T(8,128)(2,1)}, u32[]{:S(2)}) copy-start(bf16[8,256,256]{2,1,0:T(8,128)(2,1)} %copy-done.10) | copy-start | bytes 3145732
  71.0 3.0 %copy-start = (f32[8,3,304,256]{3,2,1,0:T(8,128)}, f32[8,3,304,256]{3,2,1,0:T(8,128)S(1)}, u32[]{:S(2)}) copy-start(f32[8,3,304,256]{3,2,1,0:T(8,128)S(1)} %get-tuple-element.36.grad) | copy-start | bytes 22413316
  73.9 24.1 %all-to-all-start.1 = ((bf16[8,160,256]{2,1,0:T(8,128)(2,1)}), bf16[8,160,256]{2,1,0:T(8,128)(2,1)S(1)}, u32[]{:S(2)}, u32[]{:S(2)}) async-start(bf16[8,160,256]{2,1,0:T(8,128)(2,1)} %get-tuple-element.34), calls=%async_computation.1 | async-start | bytes 1310720 | tf_op jit(solution)/shard_map/all_to_all | solution.py:535
  80.6 3.1 %copy-start.1 = (f32[8,3,304,256]{3,2,1,0:T(8,128)S(1)}, f32[8,3,304,256]{3,2,1,0:T(8,128)}, u32[]{:S(2)}) copy-start(f32[8,3,304,256]{3,2,1,0:T(8,128)} %copy-done) | copy-start | bytes 22413316
  99.0 16.8 %all-to-all-start.2 = ((bf16[32,24,256]{2,1,0:T(8,128)(2,1)}), bf16[32,24,256]{2,1,0:T(8,128)(2,1)S(1)}, u32[]{:S(2)}, u32[]{:S(2)}) async-start(bf16[32,24,256]{2,1,0:T(8,128)(2,1)} %get-tuple-element.43), calls=%async_computation.2 | async-start | bytes 786432 | tf_op jit(solution)/shard_map/all_to_all | solution.py:549

commit v9 on v8

--- a/solution.py
+++ b/solution.py
@@ -90,13 +90,20 @@
     return copies
 
 
+def fetch_first(pairs, semaphores, when):
+    @pl.when(when)
+    def _():
+        for copy in fetch(pairs, semaphores):
+            copy.wait()
+
+
 def window(block, width):
     return pl.ds(pl.multiple_of(block * width, width), width)
 
 
 def edges_kernel(
-    proj, cot, short, forward, backward,
-    tails, heads, few, taps_held, p_tail, p_head, first, second, zeroth, held, semaphores,
+    proj, cot, short, taps, forward, backward, spread,
+    all_taps, all_spread, tails, heads, few, taps_held, p_tail, p_head, first, second, zeroth, held, semaphores,
 ):
     length, channels = cot.shape
     some, width = p_tail.shape[1], first.shape[1]
@@ -111,11 +118,16 @@
             (proj.at[1, :16, :], few.at[1]),
             (proj.at[2, :16, :], few.at[2]),
             (short, taps_held),
+            (taps, all_taps),
         ],
         semaphores,
     )
     p_tail[...] = picked(tail, some - 128, some)
     p_head[...] = picked(head, 0, some)
+    copies.pop().wait()
+    all_spread[...] = jnp.broadcast_to(all_taps[...].astype(BF16)[None], all_spread.shape)
+    sent = pltpu.make_async_copy(all_spread, spread, semaphores.at[9])
+    sent.start()
     for copy in copies:
         copy.wait()
 
@@ -146,10 +158,7 @@
         return 0
 
     lax.fori_loop(0, channels // width, block, 0)
-
-
-def spread_kernel(taps, spread):
-    spread[...] = jnp.broadcast_to(taps[...].astype(BF16)[None], spread.shape)
+    sent.wait()
 
 
 def conv8(last, first, taps):
@@ -168,81 +177,76 @@
     length, channels = cot.shape
     width = x.shape[2]
     edge = FK - 1
-    copies = fetch(
+    c = pl.program_id(0)
+    fetch_first(
         [(proj_far.at[i], proj.at[i]) for i in range(3)]
         + [(cot_far, cot), (short_far, short), (p_in_far, p_in), (e_own_far, e_own)],
         semaphores,
-    )
-    for copy in copies:
-        copy.wait()
-
-    def block(c, _):
-        columns = window(c, width)
-        for i in range(3):
-            x[i] = mm(p_in[...], proj[i, :, columns])
-        moved[...] = mm(p_in[edge * 8 :, :], cot[:, columns])
-        for lane in lanes_of(width):
-            wide = pl.ds(pl.multiple_of(c * width + lane.start, 128), 128)
-            taps = [spread_taps(short, i, wide) for i in range(3)]
-            for r in range(0, length, STEP):
-                rows = slice(r, r + STEP)
-                parts = []
-                for i in range(3):
-                    px[c, i, rows, lane] = x[i, r + 8 * edge : r + 8 * edge + STEP, lane].astype(BF16)
-                    part = featurized(x.at[i], taps[i], lane, r, STEP).reshape(STEP, 128)
-                    feat[c, i, rows, lane] = part
-                    parts.append(part)
-                here = moved[rows, lane]
-                cots[c, rows, lane] = here.astype(BF16)
-                mixed[rows, lane] = (parts[1] * parts[2]).astype(BF16)
-                grads[rows, lane] = (here * parts[0]).astype(BF16)
-        for out, value in ((m_part, mixed), (g_part, grads)):
-            value = value[...]
-            out[c] = mm(e_own[...], jnp.concatenate([value, value], axis=0))
-        return 0
-
-    lax.fori_loop(0, channels // width, block, 0)
+        c == 0,
+    )
+    columns = window(c, width)
+    for i in range(3):
+        x[i] = mm(p_in[...], proj[i, :, columns])
+    moved[...] = mm(p_in[edge * 8 :, :], cot[:, columns])
+    for lane in lanes_of(width):
+        wide = pl.ds(pl.multiple_of(c * width + lane.start, 128), 128)
+        taps = [spread_taps(short, i, wide) for i in range(3)]
+        for r in range(0, length, STEP):
+            rows = slice(r, r + STEP)
+            parts = []
+            for i in range(3):
+                px[0, i, rows, lane] = x[i, r + 8 * edge : r + 8 * edge + STEP, lane].astype(BF16)
+                part = featurized(x.at[i], taps[i], lane, r, STEP).reshape(STEP, 128)
+                feat[0, i, rows, lane] = part
+                parts.append(part)
+            here = moved[rows, lane]
+            cots[0, rows, lane] = here.astype(BF16)
+            mixed[rows, lane] = (parts[1] * parts[2]).astype(BF16)
+            grads[rows, lane] = (here * parts[0]).astype(BF16)
+    for out, value in ((m_part, mixed), (g_part, grads)):
+        value = value[...]
+        out[0] = mm(e_own[...], jnp.concatenate([value, value], axis=0))
+
+
+def taps_kernel(taps, decay, e_taps, k_spec, decays):
+    lags = lax.broadcasted_iota(jnp.int32, taps.shape, 0).astype(F32)
+    falloff = jnp.exp(-decay[...] * lags)
+    decays[0] = falloff
+    kernel = taps[...].astype(F32) * falloff
+    high = kernel.astype(BF16)
+    low = (kernel - high.astype(F32)).astype(BF16)
+    k_spec[0] = mm(e_taps[...], jnp.concatenate([high, high, low], axis=0))
 
 
 def finish_kernel(
-    prev_all, later_all, feat_all, px_all, cots_all, m_all, g_all, taps_all, proj_far, cot_far, short_far, decay_far,
-    e_prev_far, e_next_far, e_first_far, e_taps_far, s_own_far, s_lags_far,
-    product_all, grad_all, sums_out,
-    ends_all, starts_all, short_all, decay_all, e_prev, e_next, e_first, e_taps, s_own, s_lags,
-    fixed, ms, gs, hs, ks, ys, zs, cs, filtered, grad_mixed, decays, semaphores,
+    prev_all, later_all, feat, px, cots, m_part, g_part, ks, decays, proj_far, cot_far, short_far,
+    e_prev_far, e_next_far, e_first_far, s_own_far, s_lags_far,
+    product, grad, sums_out,
+    ends_all, starts_all, short_all, e_prev, e_next, e_first, s_own, s_lags, semaphores, *held,
 ):
-    length, width = cots_all.shape[1:]
+    length, width = cots.shape[1:]
+    c = pl.program_id(0)
     pairs = [
         (proj_far.at[:, length - 16 :, :], ends_all), (cot_far.at[:16, :], starts_all), (short_far, short_all),
-        (decay_far, decay_all), (e_prev_far, e_prev), (e_first_far, e_first), (e_next_far, e_next),
-        (e_taps_far, e_taps), (s_own_far, s_own), (s_lags_far, s_lags),
+        (e_prev_far, e_prev), (e_first_far, e_first), (e_next_far, e_next), (s_own_far, s_own), (s_lags_far, s_lags),
     ]
-    copies = fetch(pairs, semaphores)
-    for copy in copies:
-        copy.wait()
-
-    def block(c, _):
-        columns = window(c, width)
-        narrow = [prev_all, later_all, taps_all, starts_all, decay_all]
-        prev, later, taps, starts, decay = [ref.at[:, columns] for ref in narrow]
-        ends, short = ends_all.at[:, :, columns], short_all.at[:, :, columns]
-        feat, px, cots, m_part, g_part, product, grad = [
-            ref.at[c] for ref in (feat_all, px_all, cots_all, m_all, g_all, product_all, grad_all)
-        ]
-        finish_block(
-            c, prev, later, feat, px, cots, m_part, g_part, taps, ends, starts, short, decay,
-            e_prev, e_next, e_first, e_taps, s_own, s_lags, product, grad, sums_out,
-            fixed, ms, gs, hs, ks, ys, zs, cs, filtered, grad_mixed, decays,
-        )
-        return 0
-
-    lax.fori_loop(0, cots_all.shape[0], block, 0)
+    fetch_first(pairs, semaphores, c == 0)
+    columns = window(c, width)
+    prev, later, starts = [ref.at[:, columns] for ref in (prev_all, later_all, starts_all)]
+    ends, short = ends_all.at[:, :, columns], short_all.at[:, :, columns]
+    feat, px, cots, m_part, g_part, ks, decays, product, grad = [
+        ref.at[0] for ref in (feat, px, cots, m_part, g_part, ks, decays, product, grad)
+    ]
+    finish_block(
+        c, prev, later, feat, px, cots, m_part, g_part, ks, decays, ends, starts, short,
+        e_prev, e_next, e_first, s_own, s_lags, product, grad, sums_out, *held,
+    )
 
 
 def finish_block(
-    block, prev, later, feat, px, cots, m_part, g_part, taps, ends, starts, short, decay,
-    e_prev, e_next, e_first, e_taps, s_own, s_lags, product, grad, sums_out,
-    fixed, ms, gs, hs, ks, ys, zs, cs, filtered, grad_mixed, decays,
+    block, prev, later, feat, px, cots, m_part, g_part, ks, decays, ends, starts, short,
+    e_prev, e_next, e_first, s_own, s_lags, product, grad, sums_out,
+    fixed, ms, gs, hs, ys, zs, cs, filtered, grad_mixed,
 ):
     length, width = 8 * (grad.shape[1] // 8 - FK + 1), ms.shape[1]
     edge = FK - 1
@@ -286,13 +290,6 @@
     ms[...] = mm(e_prev[...], mixed_edge)
     hs[...] = mm(e_first[...], grad_first)
     gs[...] = mm(e_next[...], grad_edge)
-    lags = lax.broadcasted_iota(jnp.int32, decays.shape, 0).astype(F32)
-    decays[...] = jnp.exp(-decay[...] * lags)
-    kernel = taps[...].astype(F32) * decays[...]
-    high = kernel.astype(BF16)
-    low = (kernel - high.astype(F32)).astype(BF16)
-    ks[...] = mm(e_taps[...], jnp.concatenate([high, high, low], axis=0))
-
     half = ks.shape[0] // 2
     for lane in lanes_of(width):
         for f in range(0, half, 32):
@@ -368,9 +365,8 @@
 
 
 def outputs_kernel(product, grad, short, p_out, gated, grad_proj, held):
-    c = pl.program_id(0)
     length, width = product.shape[1:]
-    gated[...] = mm(p_out[...], product[c]).astype(BF16)
+    gated[...] = mm(p_out[...], product[0]).astype(BF16)
     for i in range(3):
         for lane in lanes_of(width):
             taps = spread_taps(short, i, lane)
@@ -378,7 +374,7 @@
                 total = None
                 for lag in range(FK):
                     at = slice(r + 8 * lag, r + 8 * lag + STEP)
-                    part = grad[c, i, at, lane].reshape(STEP // 8, 8, 128) * taps[lag]
+                    part = grad[0, i, at, lane].reshape(STEP // 8, 8, 128) * taps[lag]
                     total = part if total is None else total + part
                 held[i, r : r + STEP, lane] = total.reshape(STEP, 128).astype(BF16)
         grad_proj[i] = mm(p_out[...], held[i]).astype(BF16)
@@ -388,21 +384,30 @@
     return pl.BlockSpec(array.shape, lambda c: (0,) * array.ndim)
 
 
-def columns(rows, width, first=0):
+def columns(rows, width):
     lead = (0,) * len(rows)
-    return pl.BlockSpec(tuple(rows) + (width,), lambda c: lead + (first + c,))
-
-
-def call(kernel, name, operands, outputs, cost=1, limit=24, **options):
-    vmem, far = pl.BlockSpec(memory_space=pltpu.VMEM), pl.BlockSpec(memory_space=pl.ANY)
-    if "in_specs" not in options:
-        options["in_specs"] = [far if stays else vmem for _, stays in operands]
-        options["out_specs"] = [vmem] * len(outputs)
-    arrays = [pltpu.with_memory_space_constraint(array, pltpu.HBM) if stays else array for array, stays in operands]
+    return pl.BlockSpec(tuple(rows) + (width,), lambda c: lead + (c,))
+
+
+def one_of(array):
+    tail = (0,) * (len(array.shape) - 1)
+    return pl.BlockSpec((1,) + tuple(array.shape[1:]), lambda c: (c,) + tail)
+
+
+IN_VMEM = pl.BlockSpec(memory_space=pltpu.VMEM)
+FAR = pl.BlockSpec(memory_space=pl.ANY)
+
+
+def call(kernel, name, operands, outputs, cost=1, **options):
+    arrays = [
+        array if spec is IN_VMEM else pltpu.with_memory_space_constraint(array, pltpu.HBM) for array, spec in operands
+    ]
     return pl.pallas_call(
         kernel,
-        out_shape=outputs,
-        compiler_params=pltpu.CompilerParams(vmem_limit_bytes=limit << 20),
+        in_specs=[spec for _, spec in operands],
+        out_specs=[spec for _, spec in outputs],
+        out_shape=[shape for shape, _ in outputs],
+        compiler_params=pltpu.CompilerParams(vmem_limit_bytes=32 << 20),
         cost_estimate=pl.CostEstimate(flops=cost * 10**9, bytes_accessed=10**6, transcendentals=0),
         name=name,
         **options,
@@ -457,79 +462,87 @@
     extended = length + 8 * (FK - 1)
     some = 144
     proj, cot, short, decay = jnp.transpose(projected, (1, 0, 2)), cotangent, short_taps, decay[None]
-    full = lambda kind, *shape: jax.ShapeDtypeStruct(shape, kind)
+    full = lambda kind, *shape: (jax.ShapeDtypeStruct(shape, kind), IN_VMEM)
+    by_block = lambda kind, *shape: (pltpu.HBM((blocks,) + shape, kind), one_of(np.empty((blocks,) + shape, np.bool_)))
     vmem = lambda kind, *shape: pltpu.VMEM(shape, kind)
     copied = lambda array: pltpu.VMEM(array.shape, array.dtype)
+    far = lambda *arrays: [(array, FAR) for array in arrays]
+    pieces = lambda *arrays: [(array, one_of(array)) for array in arrays]
     semaphores = pltpu.SemaphoreType.DMA((10,))
     own = interleaved(span)
     after = length + np.arange(8)
 
-    forward, backward = call(
-        edges_kernel, "edges", [(proj, True), (cot, True), (short, True)],
-        [full(BF16, 152, channels), full(BF16, 160, channels)],
+    forward, backward, spread = call(
+        edges_kernel, "edges", far(proj, cot, short, filter_taps),
+        [full(BF16, 152, channels), full(BF16, 160, channels), (pltpu.HBM((ranks, rows, channels), BF16), FAR)],
         scratch_shapes=[
+            copied(filter_taps), vmem(BF16, ranks, rows, channels),
             vmem(BF16, 2, some, channels), vmem(BF16, 2, some, channels), vmem(BF16, 3, 16, channels), copied(short),
             vmem(BF16, 8 * (15 + FK), some), vmem(BF16, 8 * (16 + FK), some), vmem(F32, 8 * (15 + FK), width),
             vmem(F32, 8 * (15 + FK), width), vmem(F32, 8 * (16 + FK), width), vmem(F32, 8 * 17, width), semaphores,
         ],
     )
-    filter_taps, forward = lax.optimization_barrier((filter_taps, forward))
     prev = from_behind(forward, "seq", 1)
     later = from_behind(backward, "seq", -1)
-    spread = pl.pallas_call(
-        spread_kernel,
-        out_shape=pltpu.HBM((ranks, rows, channels), BF16),
-        cost_estimate=pl.CostEstimate(flops=0, bytes_accessed=10**6, transcendentals=0),
-        name="spread",
-    )(filter_taps)
     taps = lax.all_to_all(spread, "seq", 0, 0).reshape(count, channels)
 
     e_own = jnp.asarray(np.concatenate(list(analysis(own, size)), axis=1))
     p_in = jnp.asarray(pick(interleaved(span, 0, 1 - FK), length))
+    inputs = (proj, cot, short, e_own, p_in)
     feat, px, cots, m_part, g_part = call(
-        own_kernel, "own", [(array, True) for array in (proj, cot, short, e_own, p_in)],
+        own_kernel, "own", far(*inputs),
         [
-            full(F32, blocks, 3, length, width), full(BF16, blocks, 3, length, width),
-            full(BF16, blocks, length, width), full(F32, blocks, size, width), full(F32, blocks, size, width),
+            by_block(F32, 3, length, width), by_block(BF16, 3, length, width), by_block(BF16, length, width),
+            by_block(F32, size, width), by_block(F32, size, width),
         ],
         cost=10,
-        scratch_shapes=[copied(array) for array in (proj, cot, short, e_own, p_in)] + [
+        grid=(blocks,),
+        scratch_shapes=[copied(array) for array in inputs] + [
             vmem(F32, 3, extended, width), vmem(F32, length, width), vmem(BF16, length, width),
             vmem(BF16, length, width), semaphores,
         ],
     )
 
+    taps, cots = lax.optimization_barrier((taps, cots))
     k_high, k_low = analysis(np.arange(count), size)
+    e_taps = jnp.asarray(np.concatenate([k_high, k_low, k_high], axis=1))
+    k_spec, decays = call(
+        taps_kernel, "taps",
+        [(taps, columns((count,), width)), (decay, columns((1,), width)), (e_taps, whole(e_taps))],
+        [by_block(F32, size, width), by_block(F32, count, width)],
+        cost=3,
+        grid=(blocks,),
+    )
     constants = [
         analysis(np.concatenate([interleaved(16, -128), after, np.arange(8)]), size)[0],
         analysis(np.concatenate([interleaved(17, length), np.arange(8)]), size)[0],
         analysis(np.arange(8), size, 8)[0],
-        np.concatenate([k_high, k_low, k_high], axis=1),
         np.concatenate(list(synthesis(np.concatenate([own, after]), size)), axis=1),
         np.concatenate(list(synthesis(np.arange(count), size)), axis=1),
     ]
     constants = [jnp.asarray(constant) for constant in constants]
     product, grad, sums = call(
         finish_kernel, "finish",
-        [(array, False) for array in (prev, later, feat, px, cots, m_part, g_part, taps)]
-        + [(array, True) for array in [proj, cot, short, decay] + constants],
+        [(prev, IN_VMEM), (later, IN_VMEM)] + pieces(feat, px, cots, m_part, g_part, k_spec, decays)
+        + far(proj, cot, short, *constants),
+        [by_block(BF16, length, width), by_block(F32, 3, extended, width), full(BF16, ranks, blocks * slot + SHORT, width)],
+        cost=12,
+        grid=(blocks,),
+        scratch_shapes=[vmem(BF16, 3, 16, channels), vmem(BF16, 16, channels), copied(short)]
+        + [copied(constant) for constant in constants] + [semaphores]
+        + [vmem(F32, 3, STEP, width)] + [vmem(F32, size, width)] * 3 + [vmem(BF16, size, width)] * 3
+        + [vmem(F32, length + 8, width)] * 2,
+    )
+    p_out = jnp.asarray(pick(own, length).T)
+    gated, grad_proj = call(
+        outputs_kernel, "outputs",
+        pieces(product, grad) + [(short, columns((3, FK), width)), (p_out, whole(p_out))],
         [
-            full(BF16, blocks, length, width), full(F32, blocks, 3, extended, width),
-            full(BF16, ranks, blocks * slot + SHORT, width),
-        ],
-        cost=12,
-        scratch_shapes=[vmem(BF16, 3, 16, channels), vmem(BF16, 16, channels), copied(short), copied(decay)]
-        + [copied(constant) for constant in constants]
-        + [vmem(F32, 3, STEP, width)] + [vmem(F32, size, width)] * 4 + [vmem(BF16, size, width)] * 3
-        + [vmem(F32, length + 8, width)] * 2 + [vmem(F32, count, width), semaphores],
-    )
-    p_out = jnp.asarray(pick(own, length).T)
-    inside = pl.BlockSpec(memory_space=pltpu.VMEM)
-    gated, grad_proj = call(
-        outputs_kernel, "outputs", [(product, False), (grad, False), (short, True), (p_out, True)],
-        [full(BF16, length, channels), full(BF16, 3, length, channels)], cost=8,
-        grid=(blocks,), in_specs=[inside, inside, columns((3, FK), width), whole(p_out)],
-        out_specs=[columns((length,), width), columns((3, length), width)],
+            (jax.ShapeDtypeStruct((length, channels), BF16), columns((length,), width)),
+            (jax.ShapeDtypeStruct((3, length, channels), BF16), columns((3, length), width)),
+        ],
+        cost=8,
+        grid=(blocks,),
         scratch_shapes=[vmem(BF16, 3, length, width)],
     )
     sums, gated, grad_proj = lax.optimization_barrier((lax.all_to_all(sums, "seq", 0, 0), gated, grad_proj))

time: 118 us -> 109 us (0.924)
  local copies, waits for them, and re-layouts: 25.8 us -> 0.78 us
  Pallas kernels: 44.8 us -> 54.6 us
  waiting for transfers between devices: 24.5 us -> 28.7 us
  starting transfers between devices: 21.3 us -> 23.1 us
    unnamed x24 -> x2, local copies, waits for them, and re-layouts: 25.8 us -> 0.78 us
    pallas_call x5, Pallas kernels: 42.5 us -> 52.3 us  [call(): pl.pallas_call(kernel, in_specs=[spec for _, spec in operands], out_specs...]
    ppermute x2, waiting for transfers between devices: 3.7 us -> 8.34 us  [from_behind(): return lax.ppermute(value, axis, pairs)]
    all_to_all x1, starting transfers between devices: 4.84 us -> 7.29 us  [shards(): taps = lax.all_to_all(spread, 'seq', 0, 0).reshape(count, channels)]
  transfers between devices with their start and end apart: 5 -> 5, of which waited for: 4 -> 3; matrix products, arithmetic and copies ran while one was open for 0% -> 0% of each run, Pallas kernels for 17% -> 27%
where the time goes in v9:
time: 109 us; the launch traced here: 108 us
  Pallas kernels  54.6 us (50%)
  waiting for transfers between devices  28.7 us (26%)
  starting transfers between devices  23.1 us (21%)
    pallas_call x5, Pallas kernels, call(): pl.pallas_call(kernel, in_specs=[spec for _, spec in operands], out_specs...  52.3 us
    all_to_all x1, waiting for transfers between devices, shards(): gathered = lax.all_to_all(payload, ('seq', 'ch'), 0, 0)  13.1 us
    ppermute x2, waiting for transfers between devices, from_behind(): return lax.ppermute(value, axis, pairs)  8.34 us
    all_to_all x1, starting transfers between devices, shards(): taps = lax.all_to_all(spread, 'seq', 0, 0).reshape(count, channels)  7.29 us
    all_to_all x1, waiting for transfers between devices, shards(): lax.all_to_all(sums, 'seq', 0, 0)  7.29 us
    all_to_all x1, starting transfers between devices, shards(): lax.all_to_all(sums, 'seq', 0, 0)  6.27 us
    ppermute x2, starting transfers between devices, from_behind(): return lax.ppermute(value, axis, pairs)  5.87 us
    all_to_all x1, starting transfers between devices, shards(): gathered = lax.all_to_all(payload, ('seq', 'ch'), 0, 0)  3.65 us
  transfers between devices with their start and end apart: 5, of which 3 were waited for; matrix products, arithmetic and copies ran while one was open for 0% of the time, Pallas kernels for 27%

profile of v9, /device:TPU:0, one launch (start us, length us, event | category | flops | bytes accessed | tf_op | source)
XLA Modules:
  0.0 108.0 jit_solution(9287351182649893700)
XLA Ops:
  0.6 5.0 %edges.1 = (bf16[152,2048]{1,0:T(8,128)(2,1)S(1)}, bf16[160,2048]{1,0:T(8,128)(2,1)S(1)}, bf16[8,16,2048]{2,1,0:T(8,128)(2,1)}) custom-call(bf16[3,256,2048]{2,1,0:T(8,128)(2,1)} %bitcast.5, bf16[256,2048]{1,0:T(8,128)(2,1)} %cot_far.3, f32[3,7,2048]{2,1,0:T(8,128)} %short.3, f32[16,2048]{1,0:T(8,128)} %taps.2), custom_call_target="tpu_custom_call" | custom-call | flops 1000000000 | bytes 1000000 | tf_op jit(solution)/shard_map/edges/pallas_call | solution.py:405
  5.6 7.3 %all-to-all-start = ((bf16[8,16,2048]{2,1,0:T(8,128)(2,1)}), bf16[8,16,2048]{2,1,0:T(8,128)(2,1)S(1)}, u32[]{:S(2)}, u32[]{:S(2)}) async-start(bf16[8,16,2048]{2,1,0:T(8,128)(2,1)} %get-tuple-element.32), calls=%async_computation | async-start | bytes 1048576 | tf_op jit(solution)/shard_map/all_to_all | solution.py:487
  12.9 1.3 %collective-permute-start.1 = (bf16[160,2048]{1,0:T(8,128)(2,1)S(1)}, bf16[160,2048]{1,0:T(8,128)(2,1)S(1)}, u32[]{:S(2)}, u32[]{:S(2)}) collective-permute-start(bf16[160,2048]{1,0:T(8,128)(2,1)S(1)} %get-tuple-element.29), channel_id=1, source_target_pairs={{4,0},{8,4},{12,8},{16,12},{20,16},{24,20},{28,24},{5,1},{9,5},{13... | collective-permute-start | bytes 1966088 | tf_op jit(solution)/shard_map/ppermute | solution.py:24
  14.2 4.6 %collective-permute-start = (bf16[152,2048]{1,0:T(8,128)(2,1)S(1)}, bf16[152,2048]{1,0:T(8,128)(2,1)S(1)}, u32[]{:S(2)}, u32[]{:S(2)}) collective-permute-start(bf16[152,2048]{1,0:T(8,128)(2,1)S(1)} %get-tuple-element.28), channel_id=1, source_target_pairs={{0,4},{4,8},{8,12},{12,16},{16,20},{20,24},{24,28},{1,5},{5,9},{9,... | collective-permute-start | bytes 1867784 | tf_op jit(solution)/shard_map/ppermute | solution.py:24
  18.8 12.4 %own.1 = (f32[8,3,256,256]{3,2,1,0:T(8,128)}, bf16[8,3,256,256]{3,2,1,0:T(8,128)(2,1)}, bf16[8,256,256]{2,1,0:T(8,128)(2,1)}, f32[8,512,256]{2,1,0:T(8,128)}, f32[8,512,256]{2,1,0:T(8,128)}) custom-call(bf16[3,256,2048]{2,1,0:T(8,128)(2,1)} %bitcast.6, bf16[256,2048]{1,0:T(8,128)(2,1)} %cot_far.3, f32[3,7,2048]{2,1,0:T(8,128)} %short.3, ...), custom_call_target="tpu_custom_call" | custom-call | flops 10000000000 | bytes 1000000 | tf_op jit(solution)/shard_map/own/pallas_call | solution.py:405
  31.1 0.0 all-to-all-done
  31.1 0.0 copy-start
  31.2 0.8 copy-done
  31.9 6.7 %taps.3 = (f32[8,512,256]{2,1,0:T(8,128)}, f32[8,128,256]{2,1,0:T(8,128)}) custom-call(bf16[128,2048]{1,0:T(8,128)(2,1)} %bitcast.8, f32[1,2048]{1,0:T(1,128)} %bitcast.9, bf16[512,384]{1,0:T(8,128)(2,1)} %constant.26.clone.e_taps), custom_call_target="tpu_custom_call" | custom-call | flops 3000000000 | bytes 1000000 | tf_op jit(solution)/shard_map/taps/pallas_call | solution.py:405
  38.7 8.3 %collective-permute-done.prev_all = bf16[152,2048]{1,0:T(8,128)(2,1)S(1)} collective-permute-done((bf16[152,2048]{1,0:T(8,128)(2,1)S(1)}, bf16[152,2048]{1,0:T(8,128)(2,1)S(1)}, u32[]{:S(2)}, u32[]{:S(2)}) %collective-permute-start) | collective-permute-done | bytes 622624 | tf_op jit(solution)/shard_map/ppermute | solution.py:24
  47.0 0.0 collective-permute-done.1.later_all
  47.0 18.3 %finish.1 = (bf16[8,256,256]{2,1,0:T(8,128)(2,1)}, f32[8,3,304,256]{3,2,1,0:T(8,128)}, bf16[8,160,256]{2,1,0:T(8,128)(2,1)}) custom-call(bf16[152,2048]{1,0:T(8,128)(2,1)S(1)} %collective-permute-done.prev_all, bf16[160,2048]{1,0:T(8,128)(2,1)S(1)} %collective-permute-done.1.later_all, f32[8,3,256,256]{3,2,1,0:T(8,128)} %get-tuple-element.30.feat, ...), custom_call_target="tpu_custom_call" | custom-call | flops 12000000000 | bytes 1000000 | tf_op jit(solution)/shard_map/finish/pallas_call | solution.py:405
  65.4 6.3 %all-to-all-start.1 = ((bf16[8,160,256]{2,1,0:T(8,128)(2,1)}), bf16[8,160,256]{2,1,0:T(8,128)(2,1)S(1)}, u32[]{:S(2)}, u32[]{:S(2)}) async-start(bf16[8,160,256]{2,1,0:T(8,128)(2,1)} %get-tuple-element.40), calls=%async_computation.1 | async-start | bytes 1310720 | tf_op jit(solution)/shard_map/all_to_all | solution.py:548
  71.6 9.9 %outputs.1 = (bf16[256,2048]{1,0:T(8,128)(2,1)}, bf16[3,256,2048]{2,1,0:T(8,128)(2,1)}) custom-call(bf16[8,256,256]{2,1,0:T(8,128)(2,1)} %get-tuple-element.41.product, f32[8,3,304,256]{3,2,1,0:T(8,128)} %get-tuple-element.42.grad, f32[3,7,2048]{2,1,0:T(8,128)} %short.3, bf16[256,256]{1,0:T(8,128)(2,1)} %constant.32.clone.p_out), custom_call_target="tpu_custom_call" | custom-call | flops 8000000000 | bytes 1000000 | tf_op jit(solution)/shard_map/outputs/pallas_call | solution.py:405
  81.5 7.3 %all-to-all-done.1.sums = bf16[8,160,256]{2,1,0:T(8,128)(2,1)S(1)} async-done(((bf16[8,160,256]{2,1,0:T(8,128)(2,1)}), bf16[8,160,256]{2,1,0:T(8,128)(2,1)S(1)}, u32[]{:S(2)}, u32[]{:S(2)}) %all-to-all-start.1) | async-done | bytes 655392 | tf_op jit(solution)/shard_map/all_to_all | solution.py:548
  88.8 1.0 squares.1
  89.8 3.6 %all-to-all-start.2 = ((bf16[32,24,256]{2,1,0:T(8,128)(2,1)}), bf16[32,24,256]{2,1,0:T(8,128)(2,1)S(1)}, u32[]{:S(2)}, u32[]{:S(2)}) async-start(bf16[32,24,256]{2,1,0:T(8,128)(2,1)} %get-tuple-element.49), calls=%async_computation.2 | async-start | bytes 786432 | tf_op jit(solution)/shard_map/all_to_all | solution.py:562
  93.5 0.1 pad_add_fusion.mine
  93.5 13.1 %all-to-all-done.2.gathered = bf16[32,24,256]{2,1,0:T(8,128)(2,1)S(1)} async-done(((bf16[32,24,256]{2,1,0:T(8,128)(2,1)}), bf16[32,24,256]{2,1,0:T(8,128)(2,1)S(1)}, u32[]{:S(2)}, u32[]{:S(2)}) %all-to-all-start.2) | async-done | bytes 393248 | tf_op jit(solution)/shard_map/all_to_all | solution.py:562
  106.6 1.4 %scale.1 = (f32[3,7,2048]{2,1,0:T(8,128)}, f32[16,2048]{1,0:T(8,128)}) custom-call(s32[2]{0:T(128)S(1)} %pad_add_fusion.mine, f32[16,2048]{1,0:T(8,128)S(1)} %get-tuple-element.48.raw, bf16[32,24,256]{2,1,0:T(8,128)(2,1)S(1)} %all-to-all-done.2.gathered), custom_call_target="tpu_custom_call" | custom-call | tf_op jit(solution)/shard_map/scale/pallas_call | solution.py:565
Async XLA Ops:
  5.6 25.5 %all-to-all-start = ((bf16[8,16,2048]{2,1,0:T(8,128)(2,1)}), bf16[8,16,2048]{2,1,0:T(8,128)(2,1)S(1)}, u32[]{:S(2)}, u32[]{:S(2)}) async-start(bf16[8,16,2048]{2,1,0:T(8,128)(2,1)} %get-tuple-element.32), calls=%async_computation | async-start | bytes 1048576 | tf_op jit(solution)/shard_map/all_to_all | solution.py:487
  12.9 34.1 %collective-permute-start.1 = (bf16[160,2048]{1,0:T(8,128)(2,1)S(1)}, bf16[160,2048]{1,0:T(8,128)(2,1)S(1)}, u32[]{:S(2)}, u32[]{:S(2)}) collective-permute-start(bf16[160,2048]{1,0:T(8,128)(2,1)S(1)} %get-tuple-element.29), channel_id=1, source_target_pairs={{4,0},{8,4},{12,8},{16,12},{20,16},{24,20},{28,24},{5,1},{9,5},{13... | collective-permute-start | bytes 1966088 | tf_op jit(solution)/shard_map/ppermute | solution.py:24
  14.2 32.9 %collective-permute-start = (bf16[152,2048]{1,0:T(8,128)(2,1)S(1)}, bf16[152,2048]{1,0:T(8,128)(2,1)S(1)}, u32[]{:S(2)}, u32[]{:S(2)}) collective-permute-start(bf16[152,2048]{1,0:T(8,128)(2,1)S(1)} %get-tuple-element.28), channel_id=1, source_target_pairs={{0,4},{4,8},{8,12},{12,16},{16,20},{20,24},{24,28},{1,5},{5,9},{9,... | collective-permute-start | bytes 1867784 | tf_op jit(solution)/shard_map/ppermute | solution.py:24
  31.1 0.8 copy-start
  65.4 23.4 %all-to-all-start.1 = ((bf16[8,160,256]{2,1,0:T(8,128)(2,1)}), bf16[8,160,256]{2,1,0:T(8,128)(2,1)S(1)}, u32[]{:S(2)}, u32[]{:S(2)}) async-start(bf16[8,160,256]{2,1,0:T(8,128)(2,1)} %get-tuple-element.40), calls=%async_computation.1 | async-start | bytes 1310720 | tf_op jit(solution)/shard_map/all_to_all | solution.py:548
  89.8 16.8 %all-to-all-start.2 = ((bf16[32,24,256]{2,1,0:T(8,128)(2,1)}), bf16[32,24,256]{2,1,0:T(8,128)(2,1)S(1)}, u32[]{:S(2)}, u32[]{:S(2)}) async-start(bf16[32,24,256]{2,1,0:T(8,128)(2,1)} %get-tuple-element.49), calls=%async_computation.2 | async-start | bytes 786432 | tf_op jit(solution)/shard_map/all_to_all | solution.py:562

commit v10 on v9

--- a/solution.py
+++ b/solution.py
@@ -208,173 +208,212 @@
         out[0] = mm(e_own[...], jnp.concatenate([value, value], axis=0))
 
 
-def taps_kernel(taps, decay, e_taps, k_spec, decays):
+def started(part, fix, rows):
+    row8 = lax.broadcasted_iota(jnp.int32, fix.shape, 0)
+    groups, natural = [], jnp.zeros(fix.shape, F32)
+    for r in range(FK - 1):
+        here = part[8 * r : 8 * r + 8, :]
+        natural = natural + jnp.where(row8 == r, pltpu.roll(here, r, 0) if r else here, 0.0)
+        groups.append(here + jnp.where(row8 == 0, pltpu.roll(fix, 8 - r, 0) if r else fix, 0.0))
+    rest = [part[8 * (FK - 1) : rows, :]]
+    return jnp.concatenate(groups + rest, axis=0), natural
+
+
+def short_sums(px, grad, length):
+    width = px.shape[-1]
+    rows = [[] for _ in range(FK)]
+    for lane in lanes_of(width):
+        sums = [jnp.zeros((8, 128), F32)] * FK
+        for r in range(0, length, STEP):
+            here = px[r : r + STEP, lane].astype(F32).reshape(STEP // 8, 8, 128)
+            for lag in range(FK):
+                value = grad[r + 8 * lag : r + 8 * lag + STEP, lane].reshape(STEP // 8, 8, 128)
+                sums[lag] = sums[lag] + jnp.sum(here * value, axis=0)
+        for lag in range(FK):
+            rows[lag].append(jnp.sum(sums[lag], axis=0, keepdims=True))
+    return [jnp.concatenate(row, axis=1) for row in rows]
+
+
+def back_to(matrix, spectrum):
+    spectrum = spectrum[...]
+    return mm(matrix[...], jnp.concatenate([spectrum, spectrum], axis=0))
+
+
+def forwards_kernel(
+    prev_all, feat0, feat1, feat2, px0, cots, m_part, g_part, taps, decay, cot_far, short_far,
+    e_prev_far, e_first_far, e_taps_far, s_own_far, s_lags_far,
+    product, grad0, grad0_end, filter_out, short0, next_out, k_out,
+    starts_all, short_all, e_prev, e_first, e_taps, s_own, s_lags, semaphores,
+    fixed, ms, hs, ys, cs, filtered, grad,
+):
+    length, width = cots.shape[1:]
+    edge = FK - 1
+    c = pl.program_id(0)
+    pairs = [
+        (cot_far.at[:16, :], starts_all), (short_far, short_all), (e_prev_far, e_prev), (e_first_far, e_first),
+        (e_taps_far, e_taps), (s_own_far, s_own), (s_lags_far, s_lags),
+    ]
+    fetch_first(pairs, semaphores, c == 0)
+    columns = window(c, width)
+    row8 = lax.broadcasted_iota(jnp.int32, (8, width), 0)
+    before = prev_all[:, columns].astype(F32)
+    fixes = [conv8(before[128 + 8 * i : 136 + 8 * i], None, short_all[i, :, columns]) for i in range(3)]
+    fixed[...], _ = started(feat0.at[0, 0], fixes[0], STEP)
+    first1, first2 = [started(ref.at[0, 0], fix, STEP)[1] for ref, fix in ((feat1, fixes[1]), (feat2, fixes[2]))]
+    inside = row8 < edge
+    mixed_fix = jnp.where(inside, (first1 + fixes[1]) * (first2 + fixes[2]) - first1 * first2, 0.0)
+    grad_fix = jnp.where(inside, starts_all[:, columns].astype(F32)[:8] * fixes[0], 0.0)
+    empty = jnp.zeros((8, width), F32)
+    ms[...] = mm(e_prev[...], jnp.concatenate([before[:128], mixed_fix, empty], axis=0).astype(BF16))
+    hs[...] = mm(e_first[...], jnp.concatenate([grad_fix, empty], axis=0).astype(BF16))
+
     lags = lax.broadcasted_iota(jnp.int32, taps.shape, 0).astype(F32)
     falloff = jnp.exp(-decay[...] * lags)
-    decays[0] = falloff
     kernel = taps[...].astype(F32) * falloff
     high = kernel.astype(BF16)
     low = (kernel - high.astype(F32)).astype(BF16)
-    k_spec[0] = mm(e_taps[...], jnp.concatenate([high, high, low], axis=0))
-
-
-def finish_kernel(
-    prev_all, later_all, feat, px, cots, m_part, g_part, ks, decays, proj_far, cot_far, short_far,
-    e_prev_far, e_next_far, e_first_far, s_own_far, s_lags_far,
-    product, grad, sums_out,
-    ends_all, starts_all, short_all, e_prev, e_next, e_first, s_own, s_lags, semaphores, *held,
-):
-    length, width = cots.shape[1:]
-    c = pl.program_id(0)
-    pairs = [
-        (proj_far.at[:, length - 16 :, :], ends_all), (cot_far.at[:16, :], starts_all), (short_far, short_all),
-        (e_prev_far, e_prev), (e_first_far, e_first), (e_next_far, e_next), (s_own_far, s_own), (s_lags_far, s_lags),
-    ]
-    fetch_first(pairs, semaphores, c == 0)
-    columns = window(c, width)
-    prev, later, starts = [ref.at[:, columns] for ref in (prev_all, later_all, starts_all)]
-    ends, short = ends_all.at[:, :, columns], short_all.at[:, :, columns]
-    feat, px, cots, m_part, g_part, ks, decays, product, grad = [
-        ref.at[0] for ref in (feat, px, cots, m_part, g_part, ks, decays, product, grad)
-    ]
-    finish_block(
-        c, prev, later, feat, px, cots, m_part, g_part, ks, decays, ends, starts, short,
-        e_prev, e_next, e_first, s_own, s_lags, product, grad, sums_out, *held,
-    )
-
-
-def finish_block(
-    block, prev, later, feat, px, cots, m_part, g_part, ks, decays, ends, starts, short,
-    e_prev, e_next, e_first, s_own, s_lags, product, grad, sums_out,
-    fixed, ms, gs, hs, ys, zs, cs, filtered, grad_mixed,
-):
-    length, width = 8 * (grad.shape[1] // 8 - FK + 1), ms.shape[1]
-    edge = FK - 1
-    row8 = lax.broadcasted_iota(jnp.int32, (8, width), 0)
-    before = prev[...].astype(F32)
-    after = later[...].astype(F32)
-    prev8 = [before[128 + 8 * i : 136 + 8 * i] for i in range(3)]
-    cot_next = after[136:144]
-    next8 = [None, after[144:152], after[152:160]]
-    ends8 = [ends[i].astype(F32)[8:] for i in range(3)]
-    cot_first = starts[...].astype(F32)[:8]
-    short = [short[i] for i in range(3)]
-
-    fixes = [conv8(prev8[i], None, short[i]) for i in range(3)]
-    heads = []
-    for i in range(3):
-        rows, natural = [], jnp.zeros((8, width), F32)
-        for r in range(edge):
-            part = feat[i, 8 * r : 8 * r + 8, :]
-            natural = natural + jnp.where(row8 == r, pltpu.roll(part, r, 0) if r else part, 0.0)
-            moved = pltpu.roll(fixes[i], 8 - r, 0) if r else fixes[i]
-            rows.append(part + jnp.where(row8 == 0, moved, 0.0))
-        heads.append((jnp.concatenate(rows, axis=0), natural))
-    for i in range(3):
-        fixed[i, : 8 * edge] = heads[i][0]
-        fixed[i, 8 * edge :] = feat[i, 8 * edge : STEP, :]
-    inside = row8 < edge
-    (first1, first2), (fix1, fix2) = (heads[1][1], heads[2][1]), fixes[1:]
-    mixed_fix = jnp.where(inside, (first1 + fix1) * (first2 + fix2) - first1 * first2, 0.0)
-    grad_fix = jnp.where(inside, cot_first * fixes[0], 0.0)
-
-    feat_next = [None] + [conv8(ends8[i], next8[i], short[i]) for i in (1, 2)]
-    fix = cot_next * conv8(ends8[0], None, short[0])
-    rows = [after[8 * r : 8 * r + 8] for r in range(17)]
-    for r in range(edge):
-        rows[r] = rows[r] + jnp.where(row8 == 0, pltpu.roll(fix, (8 - r) % 8, 0), 0.0)
-    grad_edge = jnp.concatenate(rows + [grad_fix], axis=0).astype(BF16)
-    mixed_edge = jnp.concatenate([before[:128], feat_next[1] * feat_next[2], mixed_fix], axis=0).astype(BF16)
-    grad_first = jnp.concatenate([grad_fix, jnp.zeros((8, width), F32)], axis=0).astype(BF16)
-
-    ms[...] = mm(e_prev[...], mixed_edge)
-    hs[...] = mm(e_first[...], grad_first)
-    gs[...] = mm(e_next[...], grad_edge)
-    half = ks.shape[0] // 2
+    k_out[0] = mm(e_taps[...], jnp.concatenate([high, high, low], axis=0))
+
+    half = ms.shape[0] // 2
     for lane in lanes_of(width):
         for f in range(0, half, 32):
             real, imag = slice(f, f + 32), slice(half + f, half + f + 32)
-            kr, ki = ks[real, lane], ks[imag, lane]
-            mr, mi = m_part[real, lane] + ms[real, lane], m_part[imag, lane] + ms[imag, lane]
+            kr, ki = k_out[0, real, lane], k_out[0, imag, lane]
+            mr, mi = m_part[0, real, lane] + ms[real, lane], m_part[0, imag, lane] + ms[imag, lane]
             ys[real, lane] = (mr * kr - mi * ki).astype(BF16)
             ys[imag, lane] = (mr * ki + mi * kr).astype(BF16)
-            pr, pi = g_part[real, lane], g_part[imag, lane]
-            hr, hi = pr + hs[real, lane], pi + hs[imag, lane]
+            hr, hi = g_part[0, real, lane] + hs[real, lane], g_part[0, imag, lane] + hs[imag, lane]
             cs[real, lane] = (hr * mr + hi * mi).astype(BF16)
             cs[imag, lane] = (hi * mr - hr * mi).astype(BF16)
-            gr, gi = pr + gs[real, lane], pi + gs[imag, lane]
-            zs[real, lane] = (gr * kr + gi * ki).astype(BF16)
-            zs[imag, lane] = (gi * kr - gr * ki).astype(BF16)
-
-    def back_to(matrix, spectrum):
-        spectrum = spectrum[...]
-        return mm(matrix[...], jnp.concatenate([spectrum, spectrum], axis=0))
-
     filtered[...] = back_to(s_own, ys)
-    grad_mixed[...] = back_to(s_own, zs)
-    filter_sums = back_to(s_lags, cs) * decays[...]
+    filter_sums = back_to(s_lags, cs) * falloff
 
     for lane in lanes_of(width):
         for r in range(0, length, STEP):
             rows = slice(r, r + STEP)
-            features = [fixed[i, :, lane] if r == 0 else feat[i, rows, lane] for i in range(3)]
-            own, back = filtered[rows, lane], grad_mixed[rows, lane]
-            product[rows, lane] = (features[0] * own).astype(BF16)
-            grad[0, rows, lane] = cots[rows, lane].astype(F32) * own
-            grad[1, rows, lane] = back * features[2]
-            grad[2, rows, lane] = back * features[1]
-    own_next, back_next = filtered[length:, :], grad_mixed[length:, :]
-    edge_next = [cot_next * own_next, back_next * feat_next[2], back_next * feat_next[1]]
-    for i in range(3):
-        for k in range(edge):
-            at = length + 8 * k
-            moved = pltpu.roll(grad[i, 8 * k : 8 * k + 8, :], 7, 0)
-            grad[i, at : at + 8, :] = jnp.where(row8 == 7, pltpu.roll(edge_next[i], 7 - k, 0), moved)
-
-    short_rows = []
-    chunk = 64
-    for i in range(3):
-        rows = [[] for _ in range(FK)]
-        for at in range(0, width, 128):
-            lane = slice(at, at + 128)
-            sums = [jnp.zeros((8, 128), F32)] * FK
-            for r in range(0, length, chunk):
-                here = px[i, r : r + chunk, lane].astype(F32).reshape(chunk // 8, 8, 128)
-                for lag in range(FK):
-                    value = grad[i, r + 8 * lag : r + 8 * lag + chunk, lane].reshape(chunk // 8, 8, 128)
-                    sums[lag] = sums[lag] + jnp.sum(here * value, axis=0)
-            for lag in range(FK):
-                rows[lag].append(jnp.sum(sums[lag], axis=0, keepdims=True))
-        short_rows += [jnp.concatenate(row, axis=1) for row in rows]
-
-    ranks, total, _ = sums_out.shape
+            own = filtered[rows, lane]
+            feature = fixed[:, lane] if r == 0 else feat0[0, 0, rows, lane]
+            product[0, rows, lane] = (feature * own).astype(BF16)
+            value = cots[0, rows, lane].astype(F32) * own
+            grad[rows, lane] = value
+            grad0[0, rows, lane] = value
+    next_out[0] = filtered[length:, :]
+    for k in range(edge):
+        at = slice(8 * k, 8 * k + 8)
+        value = jnp.where(row8 == 7, 0.0, pltpu.roll(grad[at, :], 7, 0))
+        grad[length + at.start : length + at.stop, :] = value
+        grad0_end[0, at, :] = value
+    short0[0] = jnp.concatenate(short_sums(px0.at[0, 0], grad, length) + [empty[:1]], axis=0)
+
+    ranks, slot = filter_out.shape[1:3]
     per = filter_sums.shape[0] // ranks
-    slot = -(-per // 16) * 16
-    share = ranks * slot // (total - SHORT)
     if per % 8 == 0:
         by_rank = filter_sums.reshape(ranks, per, width)
     else:
         by_rank = jnp.stack([filter_sums[rank * per : rank * per + per] for rank in range(ranks)])
     if slot > per:
         by_rank = jnp.concatenate([by_rank, jnp.zeros((ranks, slot - per, width), F32)], axis=1)
-    sums_out[:, pl.ds(pl.multiple_of(block * slot, slot), slot), :] = by_rank.astype(BF16)
+    filter_out[0] = by_rank.astype(BF16)
+
+
+def backwards_kernel(
+    prev_all, later_all, feat1, feat2, px1, px2, g_part, k_spec, grad0_end, filter_in, short0, next_in, taps, decay,
+    proj_far, cot_far, short_far, e_next_far, s_own_far,
+    grad, grad0_out, sums_out,
+    ends_all, starts_all, short_all, e_next, s_own, semaphores,
+    fixed, gs, zs, grad_mixed,
+):
+    length, width = feat1.shape[2:]
+    edge = FK - 1
+    c = pl.program_id(0)
+    pairs = [
+        (proj_far.at[:, length - 16 :, :], ends_all), (cot_far.at[:16, :], starts_all), (short_far, short_all),
+        (e_next_far, e_next), (s_own_far, s_own),
+    ]
+    fetch_first(pairs, semaphores, c == 0)
+    columns = window(c, width)
+    row8 = lax.broadcasted_iota(jnp.int32, (8, width), 0)
+    before = prev_all[:, columns].astype(F32)[128:]
+    after = later_all[:, columns].astype(F32)
+    cot_next, next8 = after[136:144], [None, after[144:152], after[152:160]]
+    short = [short_all[i, :, columns] for i in range(3)]
+    ends8 = [ends_all[i, :, columns].astype(F32)[8:] for i in range(3)]
+    fixes = [conv8(before[8 * i : 8 * i + 8], None, short[i]) for i in range(3)]
+    for i, ref in ((0, feat1), (1, feat2)):
+        fixed[i], _ = started(ref.at[0, 0], fixes[i + 1], STEP)
+    grad_fix = jnp.where(row8 < edge, starts_all[:, columns].astype(F32)[:8] * fixes[0], 0.0)
+
+    feat_next = [None] + [conv8(ends8[i], next8[i], short[i]) for i in (1, 2)]
+    fix = cot_next * conv8(ends8[0], None, short[0])
+    rows = [after[8 * r : 8 * r + 8] for r in range(17)]
+    for r in range(edge):
+        rows[r] = rows[r] + jnp.where(row8 == 0, pltpu.roll(fix, (8 - r) % 8, 0), 0.0)
+    gs[...] = mm(e_next[...], jnp.concatenate(rows + [grad_fix], axis=0).astype(BF16))
+
+    half = gs.shape[0] // 2
+    for lane in lanes_of(width):
+        for f in range(0, half, 32):
+            real, imag = slice(f, f + 32), slice(half + f, half + f + 32)
+            kr, ki = k_spec[0, real, lane], k_spec[0, imag, lane]
+            gr, gi = g_part[0, real, lane] + gs[real, lane], g_part[0, imag, lane] + gs[imag, lane]
+            zs[real, lane] = (gr * kr + gi * ki).astype(BF16)
+            zs[imag, lane] = (gi * kr - gr * ki).astype(BF16)
+    grad_mixed[...] = back_to(s_own, zs)
+
+    for lane in lanes_of(width):
+        for r in range(0, length, STEP):
+            at = slice(r, r + STEP)
+            back = grad_mixed[at, lane]
+            one, two = [fixed[i, :, lane] if r == 0 else ref[0, 0, at, lane] for i, ref in ((0, feat1), (1, feat2))]
+            grad[0, 0, at, lane] = back * two
+            grad[0, 1, at, lane] = back * one
+
+    own_next, mixed_next = next_in[0], feat_next[1] * feat_next[2]
+    for lag in range(edge):
+        tap = taps[...].astype(F32)[lag : lag + 1] * jnp.exp(-decay[...] * float(lag))
+        moved = pltpu.roll(mixed_next, lag, 0) if lag else mixed_next
+        own_next = own_next + tap * jnp.where(row8 >= lag, moved, 0.0)
+    back_next = grad_mixed[length:, :]
+    edge_next = [cot_next * own_next, back_next * feat_next[2], back_next * feat_next[1]]
+    for k in range(edge):
+        at = slice(8 * k, 8 * k + 8)
+        grad0_out[0, at, :] = jnp.where(row8 == 7, pltpu.roll(edge_next[0], 7 - k, 0), grad0_end[0, at, :])
+        for i in range(2):
+            moved = pltpu.roll(grad[0, i, at, :], 7, 0)
+            value = jnp.where(row8 == 7, pltpu.roll(edge_next[i + 1], 7 - k, 0), moved)
+            grad[0, i, length + at.start : length + at.stop, :] = value
+
+    short_rows = [short0[0, :1, :]]
+    for lag in range(1, FK):
+        pair = jnp.where(row8 < lag, pltpu.roll(ends8[0], lag, 0), 0.0) * edge_next[0]
+        short_rows.append(short0[0, lag : lag + 1, :] + jnp.sum(pair, axis=0, keepdims=True))
+    for i, px in ((0, px1), (1, px2)):
+        short_rows += short_sums(px.at[0, 0], grad.at[0, i], length)
+
+    ranks, total, _ = sums_out.shape
+    slot = filter_in.shape[2]
+    share = ranks * slot // (total - SHORT)
+    sums_out[:, pl.ds(pl.multiple_of(c * slot, slot), slot), :] = filter_in[0]
     sums = jnp.concatenate(short_rows + [jnp.zeros((SHORT - len(short_rows), width), F32)], axis=0)
     for rank in range(share):
         held = pltpu.roll(sums, width - rank * (width // share), 1) if rank else sums
-        sums_out[block * share + rank, total - SHORT :, :] = held.astype(BF16)
-
-
-def outputs_kernel(product, grad, short, p_out, gated, grad_proj, held):
+        sums_out[c * share + rank, total - SHORT :, :] = held.astype(BF16)
+
+
+def outputs_kernel(product, grad0, grad0_end, grad, short, p_out, gated, grad_proj, plane, held):
     length, width = product.shape[1:]
     gated[...] = mm(p_out[...], product[0]).astype(BF16)
+    plane[:length] = grad0[0]
+    plane[length:] = grad0_end[0]
     for i in range(3):
+        source = plane if i == 0 else grad.at[0, i - 1]
         for lane in lanes_of(width):
             taps = spread_taps(short, i, lane)
             for r in range(0, length, STEP):
                 total = None
                 for lag in range(FK):
                     at = slice(r + 8 * lag, r + 8 * lag + STEP)
-                    part = grad[0, i, at, lane].reshape(STEP // 8, 8, 128) * taps[lag]
+                    part = source[at, lane].reshape(STEP // 8, 8, 128) * taps[lag]
                     total = part if total is None else total + part
                 held[i, r : r + STEP, lane] = total.reshape(STEP, 128).astype(BF16)
         grad_proj[i] = mm(p_out[...], held[i]).astype(BF16)
@@ -483,6 +522,7 @@
         ],
     )
     prev = from_behind(forward, "seq", 1)
+    prev, backward = lax.optimization_barrier((prev, backward))
     later = from_behind(backward, "seq", -1)
     taps = lax.all_to_all(spread, "seq", 0, 0).reshape(count, channels)
 
@@ -503,47 +543,66 @@
         ],
     )
 
-    taps, cots = lax.optimization_barrier((taps, cots))
     k_high, k_low = analysis(np.arange(count), size)
-    e_taps = jnp.asarray(np.concatenate([k_high, k_low, k_high], axis=1))
-    k_spec, decays = call(
-        taps_kernel, "taps",
-        [(taps, columns((count,), width)), (decay, columns((1,), width)), (e_taps, whole(e_taps))],
-        [by_block(F32, size, width), by_block(F32, count, width)],
-        cost=3,
+    e_prev = analysis(np.concatenate([interleaved(16, -128), np.arange(8)]), size, 8)[0]
+    e_next = analysis(np.concatenate([interleaved(17, length), np.arange(8)]), size)[0]
+    e_first = analysis(np.arange(8), size, 8)[0]
+    e_taps = np.concatenate([k_high, k_low, k_high], axis=1)
+    s_own = np.concatenate(list(synthesis(np.concatenate([own, after]), size)), axis=1)
+    s_lags = np.concatenate(list(synthesis(np.arange(count), size)), axis=1)
+    e_prev, e_next, e_first, e_taps, s_own, s_lags = [
+        jnp.asarray(constant) for constant in (e_prev, e_next, e_first, e_taps, s_own, s_lags)
+    ]
+
+    def plane(array, i, some=length):
+        return [(array, pl.BlockSpec((1, 1, some, width), lambda c: (c, i, 0, 0)))]
+
+    few = [(taps, columns((16,), width)), (decay, columns((1,), width))]
+    constants = (e_prev, e_first, e_taps, s_own, s_lags)
+    product, grad0, grad0_end, filter_sums, short0, filtered_next, k_spec = call(
+        forwards_kernel, "forwards",
+        [(prev, IN_VMEM)] + plane(feat, 0) + plane(feat, 1, STEP) + plane(feat, 2, STEP) + plane(px, 0)
+        + pieces(cots, m_part, g_part) + [(taps, columns((count,), width)), (decay, columns((1,), width))]
+        + far(cot, short, *constants),
+        [
+            by_block(BF16, length, width), by_block(F32, length, width), by_block(F32, extended - length, width),
+            by_block(BF16, ranks, slot, width), by_block(F32, 8, width), by_block(F32, 8, width),
+            by_block(F32, size, width),
+        ],
+        cost=10,
         grid=(blocks,),
-    )
-    constants = [
-        analysis(np.concatenate([interleaved(16, -128), after, np.arange(8)]), size)[0],
-        analysis(np.concatenate([interleaved(17, length), np.arange(8)]), size)[0],
-        analysis(np.arange(8), size, 8)[0],
-        np.concatenate(list(synthesis(np.concatenate([own, after]), size)), axis=1),
-        np.concatenate(list(synthesis(np.arange(count), size)), axis=1),
-    ]
-    constants = [jnp.asarray(constant) for constant in constants]
-    product, grad, sums = call(
-        finish_kernel, "finish",
-        [(prev, IN_VMEM), (later, IN_VMEM)] + pieces(feat, px, cots, m_part, g_part, k_spec, decays)
-        + far(proj, cot, short, *constants),
-        [by_block(BF16, length, width), by_block(F32, 3, extended, width), full(BF16, ranks, blocks * slot + SHORT, width)],
-        cost=12,
+        scratch_shapes=[vmem(BF16, 16, channels), copied(short)] + [copied(constant) for constant in constants]
+        + [semaphores, vmem(F32, STEP, width)] + [vmem(F32, size, width)] * 2 + [vmem(BF16, size, width)] * 2
+        + [vmem(F32, length + 8, width), vmem(F32, extended, width)],
+    )
+    grad, grad0_end, sums = call(
+        backwards_kernel, "backwards",
+        [(prev, IN_VMEM), (later, IN_VMEM)] + plane(feat, 1) + plane(feat, 2) + plane(px, 1) + plane(px, 2)
+        + pieces(g_part, k_spec, grad0_end, filter_sums, short0, filtered_next) + few
+        + far(proj, cot, short, e_next, s_own),
+        [
+            by_block(F32, 2, extended, width), by_block(F32, extended - length, width),
+            full(BF16, ranks, blocks * slot + SHORT, width),
+        ],
+        cost=10,
         grid=(blocks,),
-        scratch_shapes=[vmem(BF16, 3, 16, channels), vmem(BF16, 16, channels), copied(short)]
-        + [copied(constant) for constant in constants] + [semaphores]
-        + [vmem(F32, 3, STEP, width)] + [vmem(F32, size, width)] * 3 + [vmem(BF16, size, width)] * 3
-        + [vmem(F32, length + 8, width)] * 2,
+        scratch_shapes=[
+            vmem(BF16, 3, 16, channels), vmem(BF16, 16, channels), copied(short), copied(e_next), copied(s_own),
+            semaphores, vmem(F32, 2, STEP, width), vmem(F32, size, width), vmem(BF16, size, width),
+            vmem(F32, length + 8, width),
+        ],
     )
     p_out = jnp.asarray(pick(own, length).T)
     gated, grad_proj = call(
         outputs_kernel, "outputs",
-        pieces(product, grad) + [(short, columns((3, FK), width)), (p_out, whole(p_out))],
+        pieces(product, grad0, grad0_end, grad) + [(short, columns((3, FK), width)), (p_out, whole(p_out))],
         [
             (jax.ShapeDtypeStruct((length, channels), BF16), columns((length,), width)),
             (jax.ShapeDtypeStruct((3, length, channels), BF16), columns((3, length), width)),
         ],
         cost=8,
         grid=(blocks,),
-        scratch_shapes=[vmem(BF16, 3, length, width)],
+        scratch_shapes=[vmem(F32, extended, width), vmem(BF16, 3, length, width)],
     )
     sums, gated, grad_proj = lax.optimization_barrier((lax.all_to_all(sums, "seq", 0, 0), gated, grad_proj))
 

time: 109 us -> 109 us (level)
  waiting for transfers between devices: 28.7 us -> 20.3 us
  Pallas kernels: 54.6 us -> 59.1 us
  starting transfers between devices: 23.1 us -> 27.1 us
    ppermute x2, waiting for transfers between devices: 8.34 us -> 0.93 us  [from_behind(): return lax.ppermute(value, axis, pairs)]
    all_to_all x1, starting transfers between devices: 6.27 us -> 12.4 us  [shards(): lax.all_to_all(sums, 'seq', 0, 0)]
    pallas_call x5, Pallas kernels: 52.3 us -> 56.8 us  [call(): pl.pallas_call(kernel, in_specs=[spec for _, spec in operands], out_specs...]
    all_to_all x1, starting transfers between devices: 7.29 us -> 4.86 us  [shards(): taps = lax.all_to_all(spread, 'seq', 0, 0).reshape(count, channels)]
  transfers between devices with their start and end apart: 5 -> 5, of which waited for: 3 -> 3; matrix products, arithmetic and copies ran while one was open for 0% -> 0% of each run, Pallas kernels for 27% -> 34%
where the time goes in v10:
time: 109 us; the launch traced here: 108 us
  Pallas kernels  59.1 us (54%)
  starting transfers between devices  27.1 us (25%)
  waiting for transfers between devices  20.3 us (19%)
    pallas_call x5, Pallas kernels, call(): pl.pallas_call(kernel, in_specs=[spec for _, spec in operands], out_specs...  56.8 us
    all_to_all x1, waiting for transfers between devices, shards(): gathered = lax.all_to_all(payload, ('seq', 'ch'), 0, 0)  13.1 us
    all_to_all x1, starting transfers between devices, shards(): lax.all_to_all(sums, 'seq', 0, 0)  12.4 us
    all_to_all x1, waiting for transfers between devices, shards(): lax.all_to_all(sums, 'seq', 0, 0)  6.29 us
    ppermute x2, starting transfers between devices, from_behind(): return lax.ppermute(value, axis, pairs)  6.19 us
    all_to_all x1, starting transfers between devices, shards(): taps = lax.all_to_all(spread, 'seq', 0, 0).reshape(count, channels)  4.86 us
    all_to_all x1, starting transfers between devices, shards(): gathered = lax.all_to_all(payload, ('seq', 'ch'), 0, 0)  3.66 us
  transfers between devices with their start and end apart: 5, of which 3 were waited for; matrix products, arithmetic and copies ran while one was open for 0% of the time, Pallas kernels for 34%

profile of v10, /device:TPU:0, one launch (start us, length us, event | category | flops | bytes accessed | tf_op | source)
XLA Modules:
  0.0 108.2 jit_solution(1508960580857708511)
XLA Ops:
  0.6 4.9 %edges.1 = (bf16[152,2048]{1,0:T(8,128)(2,1)S(1)}, bf16[160,2048]{1,0:T(8,128)(2,1)S(1)}, bf16[8,16,2048]{2,1,0:T(8,128)(2,1)}) custom-call(bf16[3,256,2048]{2,1,0:T(8,128)(2,1)} %bitcast.5, bf16[256,2048]{1,0:T(8,128)(2,1)} %cot_far.5, f32[3,7,2048]{2,1,0:T(8,128)} %short.3, f32[16,2048]{1,0:T(8,128)} %taps.1), custom_call_target="tpu_custom_call" | custom-call | flops 1000000000 | bytes 1000000 | tf_op jit(solution)/shard_map/edges/pallas_call | solution.py:444
  5.6 4.9 %collective-permute-start = (bf16[152,2048]{1,0:T(8,128)(2,1)S(1)}, bf16[152,2048]{1,0:T(8,128)(2,1)S(1)}, u32[]{:S(2)}, u32[]{:S(2)}) collective-permute-start(bf16[152,2048]{1,0:T(8,128)(2,1)S(1)} %get-tuple-element.33), channel_id=1, source_target_pairs={{0,4},{4,8},{8,12},{12,16},{16,20},{20,24},{24,28},{1,5},{5,9},{9,... | collective-permute-start | bytes 1867784 | tf_op jit(solution)/shard_map/ppermute | solution.py:24
  10.5 4.9 %all-to-all-start = ((bf16[8,16,2048]{2,1,0:T(8,128)(2,1)}), bf16[8,16,2048]{2,1,0:T(8,128)(2,1)S(1)}, u32[]{:S(2)}, u32[]{:S(2)}) async-start(bf16[8,16,2048]{2,1,0:T(8,128)(2,1)} %get-tuple-element.42), calls=%async_computation | async-start | bytes 1048576 | tf_op jit(solution)/shard_map/all_to_all | solution.py:527
  15.3 12.4 %own.1 = (f32[8,3,256,256]{3,2,1,0:T(8,128)}, bf16[8,3,256,256]{3,2,1,0:T(8,128)(2,1)}, bf16[8,256,256]{2,1,0:T(8,128)(2,1)}, f32[8,512,256]{2,1,0:T(8,128)}, f32[8,512,256]{2,1,0:T(8,128)}) custom-call(bf16[3,256,2048]{2,1,0:T(8,128)(2,1)} %bitcast.6, bf16[256,2048]{1,0:T(8,128)(2,1)} %cot_far.5, f32[3,7,2048]{2,1,0:T(8,128)} %short.3, ...), custom_call_target="tpu_custom_call" | custom-call | flops 10000000000 | bytes 1000000 | tf_op jit(solution)/shard_map/own/pallas_call | solution.py:444
  27.7 0.9 collective-permute-done.prev_all
  28.6 1.3 %collective-permute-start.1 = (bf16[160,2048]{1,0:T(8,128)(2,1)S(1)}, bf16[160,2048]{1,0:T(8,128)(2,1)S(1)}, u32[]{:S(2)}, u32[]{:S(2)}) collective-permute-start(bf16[160,2048]{1,0:T(8,128)(2,1)S(1)} %get-tuple-element.36), channel_id=1, source_target_pairs={{4,0},{8,4},{12,8},{16,12},{20,16},{24,20},{28,24},{5,1},{9,5},{13... | collective-permute-start | bytes 1966088 | tf_op jit(solution)/shard_map/ppermute | solution.py:24
  29.9 0.0 all-to-all-done
  29.9 0.0 copy-start
  29.9 0.8 copy-done
  30.7 14.9 %forwards.1 = (bf16[8,256,256]{2,1,0:T(8,128)(2,1)}, f32[8,256,256]{2,1,0:T(8,128)}, f32[8,48,256]{2,1,0:T(8,128)}, bf16[8,8,16,256]{3,2,1,0:T(8,128)(2,1)}, f32...) custom-call(bf16[152,2048]{1,0:T(8,128)(2,1)S(1)} %collective-permute-done.prev_all, ...), custom_call_target="tpu_custom_call" | custom-call | flops 10000000000 | bytes 1000000 | tf_op jit(solution)/shard_map/forwards/pallas_call | solution.py:444
  45.7 0.0 collective-permute-done.1.later_all
  45.7 14.6 %backwards.1 = (f32[8,2,304,256]{3,2,1,0:T(8,128)}, f32[8,48,256]{2,1,0:T(8,128)}, bf16[8,160,256]{2,1,0:T(8,128)(2,1)}) custom-call(bf16[152,2048]{1,0:T(8,128)(2,1)S(1)} %collective-permute-done.prev_all, bf16[160,2048]{1,0:T(8,128)(2,1)S(1)} %collective-permute-done.1.later_all, f32[8,3,256,256]{3,2,1,0:T(8,128)} %get-tuple-element.37.feat0.feat1.feat2, ...), custom_call_target="tpu_custom_call" | custom-call | flops 10000000000 | bytes 1000000 | tf_op jit(solution)/shard_map/backwards/pallas_call | solution.py:444
  60.3 12.4 %all-to-all-start.1 = ((bf16[8,160,256]{2,1,0:T(8,128)(2,1)}), bf16[8,160,256]{2,1,0:T(8,128)(2,1)S(1)}, u32[]{:S(2)}, u32[]{:S(2)}) async-start(bf16[8,160,256]{2,1,0:T(8,128)(2,1)} %get-tuple-element.48), calls=%async_computation.1 | async-start | bytes 1310720 | tf_op jit(solution)/shard_map/all_to_all | solution.py:607
  72.8 9.9 %outputs.1 = (bf16[256,2048]{1,0:T(8,128)(2,1)}, bf16[3,256,2048]{2,1,0:T(8,128)(2,1)}) custom-call(bf16[8,256,256]{2,1,0:T(8,128)(2,1)} %get-tuple-element.49.product, f32[8,256,256]{2,1,0:T(8,128)} %get-tuple-element.50.grad0, f32[8,48,256]{2,1,0:T(8,128)} %get-tuple-element.51.grad0_end, f32[8,2,304,256]{3,2,1,0:T(8,128)} %get-tuple-element.52.grad, ...), custom_call_target="tpu_custom_call" | custom-call | flops 8000000000 | bytes 1000000 | tf_op jit(solution)/shard_map/outputs/pallas_call | solution.py:444
  82.7 6.3 %all-to-all-done.1.sums = bf16[8,160,256]{2,1,0:T(8,128)(2,1)S(1)} async-done(((bf16[8,160,256]{2,1,0:T(8,128)(2,1)}), bf16[8,160,256]{2,1,0:T(8,128)(2,1)S(1)}, u32[]{:S(2)}, u32[]{:S(2)}) %all-to-all-start.1) | async-done | bytes 655392 | tf_op jit(solution)/shard_map/all_to_all | solution.py:607
  89.0 1.0 squares.1
  89.9 3.7 %all-to-all-start.2 = ((bf16[32,24,256]{2,1,0:T(8,128)(2,1)}), bf16[32,24,256]{2,1,0:T(8,128)(2,1)S(1)}, u32[]{:S(2)}, u32[]{:S(2)}) async-start(bf16[32,24,256]{2,1,0:T(8,128)(2,1)} %get-tuple-element.59), calls=%async_computation.2 | async-start | bytes 786432 | tf_op jit(solution)/shard_map/all_to_all | solution.py:621
  93.6 0.1 pad_add_fusion.mine
  93.7 13.1 %all-to-all-done.2.gathered = bf16[32,24,256]{2,1,0:T(8,128)(2,1)S(1)} async-done(((bf16[32,24,256]{2,1,0:T(8,128)(2,1)}), bf16[32,24,256]{2,1,0:T(8,128)(2,1)S(1)}, u32[]{:S(2)}, u32[]{:S(2)}) %all-to-all-start.2) | async-done | bytes 393248 | tf_op jit(solution)/shard_map/all_to_all | solution.py:621
  106.8 1.4 %scale.1 = (f32[3,7,2048]{2,1,0:T(8,128)}, f32[16,2048]{1,0:T(8,128)}) custom-call(s32[2]{0:T(128)S(1)} %pad_add_fusion.mine, f32[16,2048]{1,0:T(8,128)S(1)} %get-tuple-element.58.raw, bf16[32,24,256]{2,1,0:T(8,128)(2,1)S(1)} %all-to-all-done.2.gathered), custom_call_target="tpu_custom_call" | custom-call | tf_op jit(solution)/shard_map/scale/pallas_call | solution.py:624
Async XLA Ops:
  5.6 23.1 %collective-permute-start = (bf16[152,2048]{1,0:T(8,128)(2,1)S(1)}, bf16[152,2048]{1,0:T(8,128)(2,1)S(1)}, u32[]{:S(2)}, u32[]{:S(2)}) collective-permute-start(bf16[152,2048]{1,0:T(8,128)(2,1)S(1)} %get-tuple-element.33), channel_id=1, source_target_pairs={{0,4},{4,8},{8,12},{12,16},{16,20},{20,24},{24,28},{1,5},{5,9},{9,... | collective-permute-start | bytes 1867784 | tf_op jit(solution)/shard_map/ppermute | solution.py:24
  10.5 19.4 %all-to-all-start = ((bf16[8,16,2048]{2,1,0:T(8,128)(2,1)}), bf16[8,16,2048]{2,1,0:T(8,128)(2,1)S(1)}, u32[]{:S(2)}, u32[]{:S(2)}) async-start(bf16[8,16,2048]{2,1,0:T(8,128)(2,1)} %get-tuple-element.42), calls=%async_computation | async-start | bytes 1048576 | tf_op jit(solution)/shard_map/all_to_all | solution.py:527
  28.6 17.0 %collective-permute-start.1 = (bf16[160,2048]{1,0:T(8,128)(2,1)S(1)}, bf16[160,2048]{1,0:T(8,128)(2,1)S(1)}, u32[]{:S(2)}, u32[]{:S(2)}) collective-permute-start(bf16[160,2048]{1,0:T(8,128)(2,1)S(1)} %get-tuple-element.36), channel_id=1, source_target_pairs={{4,0},{8,4},{12,8},{16,12},{20,16},{24,20},{28,24},{5,1},{9,5},{13... | collective-permute-start | bytes 1966088 | tf_op jit(solution)/shard_map/ppermute | solution.py:24
  29.9 0.8 copy-start
  60.3 28.6 %all-to-all-start.1 = ((bf16[8,160,256]{2,1,0:T(8,128)(2,1)}), bf16[8,160,256]{2,1,0:T(8,128)(2,1)S(1)}, u32[]{:S(2)}, u32[]{:S(2)}) async-start(bf16[8,160,256]{2,1,0:T(8,128)(2,1)} %get-tuple-element.48), calls=%async_computation.1 | async-start | bytes 1310720 | tf_op jit(solution)/shard_map/all_to_all | solution.py:607
  89.9 16.8 %all-to-all-start.2 = ((bf16[32,24,256]{2,1,0:T(8,128)(2,1)}), bf16[32,24,256]{2,1,0:T(8,128)(2,1)S(1)}, u32[]{:S(2)}, u32[]{:S(2)}) async-start(bf16[32,24,256]{2,1,0:T(8,128)(2,1)} %get-tuple-element.59), calls=%async_computation.2 | async-start | bytes 786432 | tf_op jit(solution)/shard_map/all_to_all | solution.py:621

commit v11 on v4

--- a/solution.py
+++ b/solution.py
@@ -16,6 +16,7 @@
 F32 = jnp.float32
 CHUNKS = 2
 SHORT = 32
+STEP = 64
 
 
 def from_behind(value, axis, by):
@@ -66,36 +67,103 @@
     return jnp.where(position == column, 1.0, 0.0).astype(BF16)
 
 
-def edges_kernel(proj, cot, short, forward, backward):
-    length, width = cot.shape
+def lanes_of(width):
+    return [slice(at, at + 128) for at in range(0, width, 128)]
+
+
+def featurized(x, taps, lane, row, rows):
+    total = None
+    for lag in range(FK):
+        at = row + 8 * (FK - 1 - lag)
+        part = x[at : at + rows, lane].reshape(rows // 8, 8, 128) * taps[lag]
+        total = part if total is None else total + part
+    return total
+
+
+def spread_taps(short, i, lane):
+    return [jnp.broadcast_to(short[i, lag : lag + 1, lane], (8, 128)) for lag in range(FK)]
+
+
+def fetch(pairs, semaphores):
+    copies = [pltpu.make_async_copy(source, into, semaphores.at[at]) for at, (source, into) in enumerate(pairs)]
+    for copy in copies:
+        copy.start()
+    return copies
+
+
+def window(block, width):
+    return pl.ds(pl.multiple_of(block * width, width), width)
+
+
+def edges_kernel(at, proj, cot, short, *refs):
+    tails, heads, few, taps_held, p_tail, p_head, first, second, zeroth, held, semaphores = refs[-11:]
+    with_taps = len(refs) > 13
+    if with_taps:
+        taps, forward, backward, spread, all_taps, all_spread = refs[:6]
+    else:
+        forward, backward = refs[:2]
+    length, channels = cot.shape[0], forward.shape[1]
+    here = pl.ds(at, channels)
+    some, width = p_tail.shape[1], first.shape[1]
     tail, head = 16, 17
-    p_tail, p_head = picked(tail, length - 128, length), picked(head, 0, length)
-
-    def conv(x, taps, count):
-        x = x.reshape(-1, 8, width)
-        total = taps[0:1] * x[FK - 1 : FK - 1 + count]
-        for lag in range(1, FK):
-            total = total + taps[lag : lag + 1] * x[FK - 1 - lag : FK - 1 - lag + count]
-        return total
-
-    mixed = conv(mm(p_tail, proj[1]), short[1], tail) * conv(mm(p_tail, proj[2]), short[2], tail)
-    ends = [proj[i, length - 16 :, :].astype(F32)[8:] for i in range(3)]
-    forward[...] = jnp.concatenate([mixed.reshape(tail * 8, width)] + ends, axis=0).astype(BF16)
-    gate = conv(mm(p_head, proj[0]), short[0], head).reshape(head * 8, width)
-    grad = gate * mm(p_head[(FK - 1) * 8 :], cot[...])
-    starts = [ref[:16, :].astype(F32)[:8] for ref in (cot, proj.at[1], proj.at[2])]
-    backward[...] = jnp.concatenate([grad] + starts, axis=0).astype(BF16)
-
-
-def spread_kernel(taps, spread):
-    spread[...] = jnp.broadcast_to(taps[...].astype(BF16)[None], spread.shape)
-
-
-def main_kernel(
+    pairs = [
+        (proj.at[1, length - some :, here], tails.at[0]),
+        (proj.at[2, length - some :, here], tails.at[1]),
+        (proj.at[0, :some, here], heads.at[0]),
+        (cot.at[:some, here], heads.at[1]),
+        (proj.at[0, length - 16 :, here], few.at[0]),
+        (proj.at[1, :16, here], few.at[1]),
+        (proj.at[2, :16, here], few.at[2]),
+        (short.at[:, :, here], taps_held),
+    ]
+    copies = fetch(pairs + [(taps, all_taps)] if with_taps else pairs, semaphores)
+    p_tail[...] = picked(tail, some - 128, some)
+    p_head[...] = picked(head, 0, some)
+    if with_taps:
+        copies.pop().wait()
+        all_spread[...] = jnp.broadcast_to(all_taps[...].astype(BF16)[None], all_spread.shape)
+        sent = pltpu.make_async_copy(all_spread, spread, semaphores.at[9])
+        sent.start()
+    for copy in copies:
+        copy.wait()
+
+    def block(c, _):
+        columns = window(c, width)
+        first[...] = mm(p_tail[...], tails[0, :, columns])
+        second[...] = mm(p_tail[...], tails[1, :, columns])
+        zeroth[...] = mm(p_head[...], heads[0, :, columns])
+        held[...] = mm(p_head[(FK - 1) * 8 :, :], heads[1, :, columns])
+        for lane in lanes_of(width):
+            wide = pl.ds(pl.multiple_of(c * width + lane.start, 128), 128)
+            taps = [spread_taps(taps_held, i, wide) for i in range(3)]
+            for r in range(0, 8 * tail, STEP):
+                mixed = featurized(first, taps[1], lane, r, STEP) * featurized(second, taps[2], lane, r, STEP)
+                forward[r : r + STEP, wide] = mixed.reshape(STEP, 128).astype(BF16)
+            ends = [few[0, :, wide], tails[0, some - 16 :, wide], tails[1, some - 16 :, wide]]
+            ends = [end.astype(F32)[8:] for end in ends]
+            forward[8 * tail :, wide] = jnp.concatenate(ends, axis=0).astype(BF16)
+            for r in range(0, 8 * head, STEP):
+                rows = min(STEP, 8 * head - r)
+                grad = featurized(zeroth, taps[0], lane, r, rows).reshape(rows, 128) * held[r : r + rows, lane]
+                if rows < STEP:
+                    starts = [heads[1, :16, wide], few[1, :, wide], few[2, :, wide]]
+                    starts = [start.astype(F32)[:8] for start in starts]
+                    backward[r:, wide] = jnp.concatenate([grad] + starts, axis=0).astype(BF16)
+                else:
+                    backward[r : r + rows, wide] = grad.astype(BF16)
+        return 0
+
+    lax.fori_loop(0, channels // width, block, 0)
+    if with_taps:
+        sent.wait()
+
+
+def operator_kernel(
     first, proj, cot, prev, later, short, taps, decay,
-    e_own, e_prev, e_next, e_taps, s_own, s_lags, p_in, p_out, *refs,
+    e_own, e_prev, e_next, e_taps, s_own, s_lags, p_in, *refs,
 ):
-    gated, grad_proj, sums_out, px, feat, grad, cots, filter_held, short_held, done = refs[-10:]
+    product, grad, sums_out, px, feat, cots, filter_held, short_held, done = refs[-9:]
+    grad = grad.at[0]
     length, width = cot.shape
     span = length // 8
     edge = FK - 1
@@ -170,7 +238,7 @@
     filter_sums = back_to(s_lags, hr * mr + hi * mi, hi * mr - hr * mi) * falloff
 
     own = filtered[:length].reshape(span, 8, width)
-    gated[...] = mm(p_out[...], flat(feat[0] * own).astype(BF16)).astype(BF16)
+    product[0] = flat(feat[0] * own).astype(BF16)
     back = grad_mixed[:length].reshape(span, 8, width)
     grad[0, :span] = cots[...] * own
     grad[1, :span] = back * feat[2]
@@ -183,25 +251,17 @@
 
     short_rows = []
     for i in range(3):
-        columns, rows = [], [[] for _ in range(FK)]
+        rows = [[] for _ in range(FK)]
         for lane in lanes:
-            weights = [jnp.broadcast_to(short[i, lag : lag + 1, lane], (8, 128)) for lag in range(FK)]
             sums = [jnp.zeros((8, 128), F32)] * FK
-            chunks = []
             for r in range(0, span, step):
-                total = jnp.zeros((step, 8, 128), F32)
                 here = px[i, r + edge : r + edge + step, :, lane]
                 for lag in range(FK):
                     value = grad[i, r + lag : r + lag + step, :, lane]
-                    total = total + weights[lag] * value
                     sums[lag] = sums[lag] + jnp.sum(here * value, axis=0)
-                chunks.append(total)
-            columns.append(jnp.concatenate(chunks, axis=0))
             for lag in range(FK):
                 rows[lag].append(jnp.sum(sums[lag], axis=0, keepdims=True))
         short_rows += [jnp.concatenate(row, axis=1) for row in rows]
-        result = flat(jnp.concatenate(columns, axis=2)).astype(BF16)
-        grad_proj[i] = mm(p_out[...], result).astype(BF16)
 
     step, block = pl.program_id(0), first + pl.program_id(0)
     ranks, slot, _ = filter_held.shape
@@ -241,6 +301,26 @@
             copy.wait()
 
 
+def outputs_kernel(product, grad, short, p_out, gated, grad_proj):
+    length, width = product.shape[1:]
+    span = length // 8
+    gated[...] = mm(p_out[...], product[0]).astype(BF16)
+    for i in range(3):
+        lanes = []
+        for lane in lanes_of(width):
+            taps = spread_taps(short, i, lane)
+            chunks = []
+            for r in range(0, span, 8):
+                total = None
+                for lag in range(FK):
+                    part = grad[0, i, r + lag : r + lag + 8, :, lane] * taps[lag]
+                    total = part if total is None else total + part
+                chunks.append(total)
+            lanes.append(jnp.concatenate(chunks, axis=0))
+        result = jnp.concatenate(lanes, axis=2).reshape(length, width).astype(BF16)
+        grad_proj[i] = mm(p_out[...], result).astype(BF16)
+
+
 def whole(array):
     return pl.BlockSpec(array.shape, lambda c: (0,) * array.ndim)
 
@@ -250,78 +330,31 @@
     return pl.BlockSpec(tuple(rows) + (width,), lambda c: lead + (first + c,))
 
 
-def edges(proj, cot, short, width, first, blocks):
-    length = cot.shape[0]
+def one_of(array, first=0):
+    tail = (0,) * (len(array.shape) - 1)
+    return pl.BlockSpec((1,) + tuple(array.shape[1:]), lambda c: (first + c,) + tail)
+
+
+IN_VMEM = pl.BlockSpec(memory_space=pltpu.VMEM)
+FAR = pl.BlockSpec(memory_space=pl.ANY)
+
+
+def call(kernel, name, operands, outputs, cost=1, held=(), free=(), **options):
+    arrays = [
+        array if at in free else pltpu.with_memory_space_constraint(array, pltpu.HBM)
+        for at, (array, _) in enumerate(operands)
+    ]
     return pl.pallas_call(
-        edges_kernel,
-        grid=(blocks,),
-        in_specs=[
-            columns((3, length), width, first), columns((length,), width, first), columns((3, FK), width, first),
-        ],
-        out_specs=[columns((152,), width), columns((160,), width)],
-        out_shape=[jax.ShapeDtypeStruct((rows, blocks * width), BF16) for rows in (152, 160)],
-        compiler_params=pltpu.CompilerParams(vmem_limit_bytes=32 << 20),
-        cost_estimate=pl.CostEstimate(flops=0, bytes_accessed=blocks * width * 10000, transcendentals=0),
-        name="edges",
-    )(proj, cot, short)
-
-
-def main(proj, cot, prev, later, short, taps, decay, width, first, blocks, ranks, slot, held):
-    length, channels = cot.shape
-    count = taps.shape[0]
-    size = 2 * length
-    span = length // 8
-    share = ranks * width // channels
-    own = interleaved(span)
-    high, low = analysis(own, size)
-    k_high, k_low = analysis(np.arange(count), size)
-    constants = [
-        np.concatenate([high, low], axis=1),
-        analysis(np.concatenate([interleaved(16, -128), length + np.arange(8)]), size, 8)[0],
-        analysis(interleaved(17, length), size, 8)[0],
-        np.concatenate([k_high, k_low, k_high], axis=1),
-        np.concatenate(list(synthesis(np.concatenate([own, length + np.arange(8)]), size)), axis=1),
-        np.concatenate(list(synthesis(np.arange(count), size)), axis=1),
-        pick(interleaved(span, 0, 1 - FK), length),
-        pick(own, length).T,
-    ]
-    constants = [pltpu.with_memory_space_constraint(jnp.asarray(constant), pltpu.HBM) for constant in constants]
-    operands = [proj, cot, prev, later, short, taps, decay] + constants
-    aliases = {}
-    for index, value in enumerate(held):
-        if value is not None:
-            aliases[len(operands)] = index
-            operands.append(value)
-    return pl.pallas_call(
-        functools.partial(main_kernel, first),
-        grid=(blocks,),
-        in_specs=[
-            columns((3, length), width, first), columns((length,), width, first), columns((prev.shape[0],), width),
-            columns((later.shape[0],), width), columns((3, FK), width, first), columns((count,), width, first),
-            columns((1,), width, first),
-        ] + [whole(constant) for constant in constants] + [pl.BlockSpec(memory_space=pl.ANY)] * len(aliases),
-        out_specs=[
-            columns((length,), width, first), columns((3, length), width, first), pl.BlockSpec(memory_space=pl.ANY),
-        ],
-        out_shape=[
-            jax.ShapeDtypeStruct((length, channels), BF16),
-            jax.ShapeDtypeStruct((3, length, channels), BF16),
-            pltpu.HBM((ranks, channels // width * slot + SHORT, width), BF16),
-        ],
-        scratch_shapes=[
-            pltpu.VMEM((3, span + FK - 1, 8, width), F32),
-            pltpu.VMEM((3, span, 8, width), F32),
-            pltpu.VMEM((3, span + FK - 1, 8, width), F32),
-            pltpu.VMEM((span, 8, width), F32),
-            pltpu.VMEM((ranks, slot, width), BF16),
-            pltpu.VMEM((share, SHORT, width), BF16),
-            pltpu.SemaphoreType.DMA((2,)),
-        ],
-        input_output_aliases=aliases,
+        kernel,
+        in_specs=[spec for _, spec in operands] + [FAR] * len(held),
+        out_specs=[spec for _, spec in outputs],
+        out_shape=[shape for shape, _ in outputs],
+        input_output_aliases={len(operands) + at: at for at in range(len(held))},
         compiler_params=pltpu.CompilerParams(vmem_limit_bytes=40 << 20),
-        cost_estimate=pl.CostEstimate(flops=blocks * 4 * 10**9, bytes_accessed=blocks * 2 * 10**6, transcendentals=0),
-        name="operator",
-    )(*operands)
+        cost_estimate=pl.CostEstimate(flops=cost * 10**9, bytes_accessed=10**6, transcendentals=0),
+        name=name,
+        **options,
+    )(*arrays, *held)
 
 
 def squares_kernel(rows, share, sums, raw, payload):
@@ -363,42 +396,97 @@
     length, _, channels = projected.shape
     ranks, groups = lax.axis_size("seq"), lax.axis_size("ch")
     rows = filter_taps.shape[0]
+    count = rows * ranks
     width = min(256, channels // CHUNKS)
-    blocks = channels // width // CHUNKS
-    proj = jnp.transpose(projected, (1, 0, 2))
-    proj, cotangent, short_taps, decay = (
-        pltpu.with_memory_space_constraint(array, pltpu.HBM)
-        for array in (proj, cotangent, short_taps, decay[None])
-    )
-
+    share = channels // ranks
     slot = -(-rows // 16) * 16
-    share = channels // ranks
-
-    def constrained(*values):
-        return lax.optimization_barrier(values)
-
-    prev, later = [], []
+    size, span = 2 * length, length // 8
+    some = 144
+    proj, cot, short, decay = jnp.transpose(projected, (1, 0, 2)), cotangent, short_taps, decay[None]
+    full = lambda kind, *shape: (jax.ShapeDtypeStruct(shape, kind), IN_VMEM)
+    vmem = lambda kind, *shape: pltpu.VMEM(shape, kind)
+    far = lambda *arrays: [(array, FAR) for array in arrays]
+    semaphores = pltpu.SemaphoreType.DMA((10,))
+    own = interleaved(span)
+    after = length + np.arange(8)
+    chunk = channels // CHUNKS
+    blocks = chunk // width
+
+    prev, later, taps = [], [], None
     for k in range(CHUNKS):
-        forward, backward = edges(proj, cotangent, short_taps, width, k * blocks, blocks)
-        if k:
-            forward, backward, later[-1] = constrained(forward, backward, later[-1])
+        operands = far(proj, cot, short)
+        results = [full(BF16, 152, chunk), full(BF16, 160, chunk)]
+        scratch = [
+            vmem(BF16, 2, some, chunk), vmem(BF16, 2, some, chunk), vmem(BF16, 3, 16, chunk), vmem(F32, 3, FK, chunk),
+            vmem(BF16, 8 * (15 + FK), some), vmem(BF16, 8 * (16 + FK), some), vmem(F32, 8 * (15 + FK), width),
+            vmem(F32, 8 * (15 + FK), width), vmem(F32, 8 * (16 + FK), width), vmem(F32, 8 * 17, width), semaphores,
+        ]
+        if k == 0:
+            operands += far(filter_taps)
+            results.append((pltpu.HBM((ranks, rows, channels), BF16), FAR))
+            scratch = [vmem(F32, rows, channels), vmem(BF16, ranks, rows, channels)] + scratch
+        forward, backward, *spread = call(
+            functools.partial(edges_kernel, k * chunk), "edges", operands, results, scratch_shapes=scratch
+        )
+        if k == 0:
+            taps = lax.all_to_all(spread[0], "seq", 0, 0).reshape(count, channels)
+        else:
+            forward, backward, prev[-1], later[-1] = lax.optimization_barrier((forward, backward, prev[-1], later[-1]))
         prev.append(from_behind(forward, "seq", 1))
         later.append(from_behind(backward, "seq", -1))
-    filter_taps, prev[0] = constrained(filter_taps, prev[0])
-    spread = pl.pallas_call(
-        spread_kernel,
-        out_shape=pltpu.HBM((ranks, rows, channels), BF16),
-        name="spread",
-    )(filter_taps)
-    taps = lax.all_to_all(spread, "seq", 0, 0).reshape(rows * ranks, channels)
-
-    held = [None] * 3
+
+    high, low = analysis(own, size)
+    k_high, k_low = analysis(np.arange(count), size)
+    constants = [
+        np.concatenate([high, low], axis=1),
+        analysis(np.concatenate([interleaved(16, -128), after]), size, 8)[0],
+        analysis(interleaved(17, length), size, 8)[0],
+        np.concatenate([k_high, k_low, k_high], axis=1),
+        np.concatenate(list(synthesis(np.concatenate([own, after]), size)), axis=1),
+        np.concatenate(list(synthesis(np.arange(count), size)), axis=1),
+        pick(interleaved(span, 0, 1 - FK), length),
+    ]
+    constants = [(jnp.asarray(constant), whole(constant)) for constant in constants]
+    held = ()
     for k in range(CHUNKS):
-        held = main(
-            proj, cotangent, prev[k], later[k], short_taps, taps, decay, width, k * blocks, blocks, ranks, slot, held
+        first = k * blocks
+        results = [
+            pltpu.HBM((CHUNKS * blocks, length, width), BF16),
+            pltpu.HBM((CHUNKS * blocks, 3, span + FK - 1, 8, width), F32),
+        ]
+        held = call(
+            functools.partial(operator_kernel, first), "operator",
+            [
+                (proj, columns((3, length), width, first)), (cot, columns((length,), width, first)),
+                (prev[k], columns((152,), width)), (later[k], columns((160,), width)),
+                (short, columns((3, FK), width, first)), (taps, columns((count,), width, first)),
+                (decay, columns((1,), width, first)),
+            ] + constants,
+            [(result, one_of(result, first)) for result in results]
+            + [(pltpu.HBM((ranks, CHUNKS * blocks * slot + SHORT, width), BF16), FAR)],
+            cost=12,
+            held=held,
+            free=(2, 3, 5),
+            grid=(blocks,),
+            scratch_shapes=[
+                vmem(F32, 3, span + FK - 1, 8, width), vmem(F32, 3, span, 8, width), vmem(F32, span, 8, width),
+                vmem(BF16, ranks, slot, width), vmem(BF16, ranks * width // channels, SHORT, width),
+                pltpu.SemaphoreType.DMA((2,)),
+            ],
         )
-    gated, grad_proj, sums = held
-    sums = lax.all_to_all(sums, "seq", 0, 0)
+    product, grad, sums = held
+    p_out = jnp.asarray(pick(own, length).T)
+    gated, grad_proj = call(
+        outputs_kernel, "outputs",
+        [(product, one_of(product)), (grad, one_of(grad)), (short, columns((3, FK), width)), (p_out, whole(p_out))],
+        [
+            (jax.ShapeDtypeStruct((length, channels), BF16), columns((length,), width)),
+            (jax.ShapeDtypeStruct((3, length, channels), BF16), columns((3, length), width)),
+        ],
+        cost=8,
+        grid=(CHUNKS * blocks,),
+    )
+    sums, gated, grad_proj = lax.optimization_barrier((lax.all_to_all(sums, "seq", 0, 0), gated, grad_proj))
 
     vmem = pl.BlockSpec(memory_space=pltpu.VMEM)
     raw, payload = pl.pallas_call(

time: 116 us -> 104 us (0.90)
  blocking collectives: 22.7 us -> 0 us
  starting transfers between devices: 24.3 us -> 29 us
  Pallas kernels: 37.4 us -> 41.1 us
  waiting for transfers between devices: 30 us -> 32.8 us
    all_to_all x1 -> x0, blocking collectives: 22.7 us -> none  [shards(): sums = lax.all_to_all(sums, 'seq', 0, 0)]
    all_to_all x1 -> x2, waiting for transfers between devices: 0.01 us -> 7.87 us  [the longest x1 7.87 us: shards(): lax.all_to_all(sums, 'seq', 0, 0)]
    all_to_all x1 -> x2, starting transfers between devices: 6.8 us -> 13.2 us  [the longest x1 7.29 us: shards(): taps = lax.all_to_all(spread[0], 'seq', 0, 0).reshape(count, channels)]
    ppermute x4, waiting for transfers between devices: 16.9 us -> 11.9 us  [from_behind(): return lax.ppermute(value, axis, pairs)]
    pallas_call x5, Pallas kernels: 35 us -> 38.7 us  [call(): pl.pallas_call(kernel, in_specs=[spec for _, spec in operands] + [FAR] *...]
    ppermute x4, starting transfers between devices: 14.3 us -> 12.2 us  [from_behind(): return lax.ppermute(value, axis, pairs)]
  transfers between devices with their start and end apart: 6 -> 7, of which waited for: 3 -> 4; matrix products, arithmetic and copies ran while one was open for 0% -> 0% of each run, Pallas kernels for 14% -> 23%
where the time goes in v11:
time: 104 us
  Pallas kernels  41.1 us (40%)
  waiting for transfers between devices  32.8 us (32%)
  starting transfers between devices  29 us (28%)
    pallas_call x5, Pallas kernels, call(): pl.pallas_call(kernel, in_specs=[spec for _, spec in operands] + [FAR] *...  38.7 us
    all_to_all x1, waiting for transfers between devices, shards(): gathered = lax.all_to_all(payload, ('seq', 'ch'), 0, 0)  13.1 us
    ppermute x4, starting transfers between devices, from_behind(): return lax.ppermute(value, axis, pairs)  12.2 us
    ppermute x4, waiting for transfers between devices, from_behind(): return lax.ppermute(value, axis, pairs)  11.9 us
    all_to_all x1, waiting for transfers between devices, shards(): lax.all_to_all(sums, 'seq', 0, 0)  7.87 us
    all_to_all x1, starting transfers between devices, shards(): taps = lax.all_to_all(spread[0], 'seq', 0, 0).reshape(count, channels)  7.29 us
    all_to_all x1, starting transfers between devices, shards(): lax.all_to_all(sums, 'seq', 0, 0)  5.88 us
    all_to_all x1, starting transfers between devices, shards(): gathered = lax.all_to_all(payload, ('seq', 'ch'), 0, 0)  3.65 us
  transfers between devices with their start and end apart: 7, of which 4 were waited for; matrix products, arithmetic and copies ran while one was open for 0% of the time, Pallas kernels for 23%

profile of v11, /device:TPU:0, one launch (start us, length us, event | category | flops | bytes accessed | tf_op | source)
XLA Modules:
  0.0 103.7 jit_solution(738761255151448249)
XLA Ops:
  0.6 3.0 %edges.3 = (bf16[152,1024]{1,0:T(8,128)(2,1)S(1)}, bf16[160,1024]{1,0:T(8,128)(2,1)S(1)}, bf16[8,16,2048]{2,1,0:T(8,128)(2,1)}) custom-call(bf16[3,256,2048]{2,1,0:T(8,128)(2,1)} %bitcast.7, bf16[256,2048]{1,0:T(8,128)(2,1)} %cot.7, f32[3,7,2048]{2,1,0:T(8,128)} %short.9, f32[16,2048]{1,0:T(8,128)} %refs_0_.1), custom_call_target="tpu_custom_call" | custom-call | flops 1000000000 | bytes 1000000 | tf_op jit(solution)/shard_map/edges/pallas_call | solution.py:347
  3.6 7.3 %all-to-all-start = ((bf16[8,16,2048]{2,1,0:T(8,128)(2,1)}), bf16[8,16,2048]{2,1,0:T(8,128)(2,1)S(1)}, u32[]{:S(2)}, u32[]{:S(2)}) async-start(bf16[8,16,2048]{2,1,0:T(8,128)(2,1)} %get-tuple-element.34), calls=%async_computation | async-start | bytes 1048576 | tf_op jit(solution)/shard_map/all_to_all | solution.py:432
  10.9 1.3 %collective-permute-start.1 = (bf16[160,1024]{1,0:T(8,128)(2,1)S(1)}, bf16[160,1024]{1,0:T(8,128)(2,1)S(1)}, u32[]{:S(2)}, u32[]{:S(2)}) collective-permute-start(bf16[160,1024]{1,0:T(8,128)(2,1)S(1)} %get-tuple-element.31), channel_id=1, source_target_pairs={{4,0},{8,4},{12,8},{16,12},{20,16},{24,20},{28,24},{5,1},{9,5},{13... | collective-permute-start | bytes 983048 | tf_op jit(solution)/shard_map/ppermute | solution.py:25
  12.2 4.6 %collective-permute-start = (bf16[152,1024]{1,0:T(8,128)(2,1)S(1)}, bf16[152,1024]{1,0:T(8,128)(2,1)S(1)}, u32[]{:S(2)}, u32[]{:S(2)}) collective-permute-start(bf16[152,1024]{1,0:T(8,128)(2,1)S(1)} %get-tuple-element.30), channel_id=1, source_target_pairs={{0,4},{4,8},{8,12},{12,16},{16,20},{20,24},{24,28},{1,5},{5,9},{9,... | collective-permute-start | bytes 933896 | tf_op jit(solution)/shard_map/ppermute | solution.py:25
  16.8 2.9 %edges.2 = (bf16[152,1024]{1,0:T(8,128)(2,1)S(1)}, bf16[160,1024]{1,0:T(8,128)(2,1)S(1)}) custom-call(bf16[3,256,2048]{2,1,0:T(8,128)(2,1)} %bitcast.8, bf16[256,2048]{1,0:T(8,128)(2,1)} %cot.7, f32[3,7,2048]{2,1,0:T(8,128)} %short.9), custom_call_target="tpu_custom_call" | custom-call | flops 1000000000 | bytes 1000000 | tf_op jit(solution)/shard_map/edges/pallas_call | solution.py:347
  19.7 11.7 %collective-permute-done.prev = bf16[152,1024]{1,0:T(8,128)(2,1)S(1)} collective-permute-done((bf16[152,1024]{1,0:T(8,128)(2,1)S(1)}, bf16[152,1024]{1,0:T(8,128)(2,1)S(1)}, u32[]{:S(2)}, u32[]{:S(2)}) %collective-permute-start) | collective-permute-done | bytes 311328 | tf_op jit(solution)/shard_map/ppermute | solution.py:25
  31.4 0.0 collective-permute-done.1.later
  31.4 1.3 %collective-permute-start.3 = (bf16[160,1024]{1,0:T(8,128)(2,1)S(1)}, bf16[160,1024]{1,0:T(8,128)(2,1)S(1)}, u32[]{:S(2)}, u32[]{:S(2)}) collective-permute-start(bf16[160,1024]{1,0:T(8,128)(2,1)S(1)} %get-tuple-element.33), channel_id=1, source_target_pairs={{4,0},{8,4},{12,8},{16,12},{20,16},{24,20},{28,24},{5,1},{9,5},{13... | collective-permute-start | bytes 983048 | tf_op jit(solution)/shard_map/ppermute | solution.py:25
  32.7 5.0 %collective-permute-start.2 = (bf16[152,1024]{1,0:T(8,128)(2,1)S(1)}, bf16[152,1024]{1,0:T(8,128)(2,1)S(1)}, u32[]{:S(2)}, u32[]{:S(2)}) collective-permute-start(bf16[152,1024]{1,0:T(8,128)(2,1)S(1)} %get-tuple-element.32), channel_id=1, source_target_pairs={{0,4},{4,8},{8,12},{12,16},{16,20},{20,24},{24,28},{1,5},{5,9},{9,... | collective-permute-start | bytes 933896 | tf_op jit(solution)/shard_map/ppermute | solution.py:25
  37.7 0.0 all-to-all-done
  37.7 11.7 %operator.2 = (bf16[8,256,256]{2,1,0:T(8,128)(2,1)}, f32[8,3,38,8,256]{4,3,2,1,0:T(8,128)}, bf16[8,160,256]{2,1,0:T(8,128)(2,1)}) custom-call(bf16[3,256,2048]{2,1,0:T(8,128)(2,1)} %bitcast.9, bf16[256,2048]{1,0:T(8,128)(2,1)} %cot.7, bf16[152,1024]{1,0:T(8,128)(2,1)S(1)} %collective-permute-done.prev, bf16[160,1024]{1,0:T(8,128)(2,1)S(1)} %collective-permute-done.1.later, ...), custom_call_target="tpu_custom_call" | custom-call | flops 12000000000 | bytes 1000000 | tf_op jit(solution)/shard_map/operator/pallas_call | solution.py:347
  49.5 0.2 collective-permute-done.2.prev
  49.7 0.0 collective-permute-done.3.later
  49.7 11.7 %operator.3 = (bf16[8,256,256]{2,1,0:T(8,128)(2,1)}, f32[8,3,38,8,256]{4,3,2,1,0:T(8,128)}, bf16[8,160,256]{2,1,0:T(8,128)(2,1)}) custom-call(bf16[3,256,2048]{2,1,0:T(8,128)(2,1)} %bitcast.10, bf16[256,2048]{1,0:T(8,128)(2,1)} %cot.7, ...), custom_call_target="tpu_custom_call", output_to_operand_aliasing={{0}: (14, {}), {1}: (15, {}), {2}: (16, {})} | custom-call | flops 12000000000 | bytes 1000000 | tf_op jit(solution)/shard_map/operator/pallas_call | solution.py:347
  61.4 5.9 %all-to-all-start.1 = ((bf16[8,160,256]{2,1,0:T(8,128)(2,1)}), bf16[8,160,256]{2,1,0:T(8,128)(2,1)S(1)}, u32[]{:S(2)}, u32[]{:S(2)}) async-start(bf16[8,160,256]{2,1,0:T(8,128)(2,1)} %get-tuple-element.40), calls=%async_computation.1 | async-start | bytes 1310720 | tf_op jit(solution)/shard_map/all_to_all | solution.py:489
  67.3 9.3 %outputs.1 = (bf16[256,2048]{1,0:T(8,128)(2,1)}, bf16[3,256,2048]{2,1,0:T(8,128)(2,1)}) custom-call(bf16[8,256,256]{2,1,0:T(8,128)(2,1)} %get-tuple-element.41.product, f32[8,3,38,8,256]{4,3,2,1,0:T(8,128)} %get-tuple-element.42.grad, f32[3,7,2048]{2,1,0:T(8,128)} %short.9, bf16[256,256]{1,0:T(8,128)(2,1)} %constant.29.clone.p_out), custom_call_target="tpu_custom_call" | custom-call | flops 8000000000 | bytes 1000000 | tf_op jit(solution)/shard_map/outputs/pallas_call | solution.py:347
  76.6 7.9 %all-to-all-done.1.sums = bf16[8,160,256]{2,1,0:T(8,128)(2,1)S(1)} async-done(((bf16[8,160,256]{2,1,0:T(8,128)(2,1)}), bf16[8,160,256]{2,1,0:T(8,128)(2,1)S(1)}, u32[]{:S(2)}, u32[]{:S(2)}) %all-to-all-start.1) | async-done | bytes 655392 | tf_op jit(solution)/shard_map/all_to_all | solution.py:489
  84.5 1.0 squares.1
  85.5 3.6 %all-to-all-start.2 = ((bf16[32,24,256]{2,1,0:T(8,128)(2,1)}), bf16[32,24,256]{2,1,0:T(8,128)(2,1)S(1)}, u32[]{:S(2)}, u32[]{:S(2)}) async-start(bf16[32,24,256]{2,1,0:T(8,128)(2,1)} %get-tuple-element.49), calls=%async_computation.2 | async-start | bytes 786432 | tf_op jit(solution)/shard_map/all_to_all | solution.py:503
  89.2 0.1 pad_add_fusion.mine
  89.2 13.1 %all-to-all-done.2.gathered = bf16[32,24,256]{2,1,0:T(8,128)(2,1)S(1)} async-done(((bf16[32,24,256]{2,1,0:T(8,128)(2,1)}), bf16[32,24,256]{2,1,0:T(8,128)(2,1)S(1)}, u32[]{:S(2)}, u32[]{:S(2)}) %all-to-all-start.2) | async-done | bytes 393248 | tf_op jit(solution)/shard_map/all_to_all | solution.py:503
  102.3 1.4 %scale.1 = (f32[3,7,2048]{2,1,0:T(8,128)}, f32[16,2048]{1,0:T(8,128)}) custom-call(s32[2]{0:T(128)S(1)} %pad_add_fusion.mine, f32[16,2048]{1,0:T(8,128)S(1)} %get-tuple-element.48.raw, bf16[32,24,256]{2,1,0:T(8,128)(2,1)S(1)} %all-to-all-done.2.gathered), custom_call_target="tpu_custom_call" | custom-call | tf_op jit(solution)/shard_map/scale/pallas_call | solution.py:506
Async XLA Ops:
  3.6 34.1 %all-to-all-start = ((bf16[8,16,2048]{2,1,0:T(8,128)(2,1)}), bf16[8,16,2048]{2,1,0:T(8,128)(2,1)S(1)}, u32[]{:S(2)}, u32[]{:S(2)}) async-start(bf16[8,16,2048]{2,1,0:T(8,128)(2,1)} %get-tuple-element.34), calls=%async_computation | async-start | bytes 1048576 | tf_op jit(solution)/shard_map/all_to_all | solution.py:432
  10.9 20.4 %collective-permute-start.1 = (bf16[160,1024]{1,0:T(8,128)(2,1)S(1)}, bf16[160,1024]{1,0:T(8,128)(2,1)S(1)}, u32[]{:S(2)}, u32[]{:S(2)}) collective-permute-start(bf16[160,1024]{1,0:T(8,128)(2,1)S(1)} %get-tuple-element.31), channel_id=1, source_target_pairs={{4,0},{8,4},{12,8},{16,12},{20,16},{24,20},{28,24},{5,1},{9,5},{13... | collective-permute-start | bytes 983048 | tf_op jit(solution)/shard_map/ppermute | solution.py:25
  12.2 19.2 %collective-permute-start = (bf16[152,1024]{1,0:T(8,128)(2,1)S(1)}, bf16[152,1024]{1,0:T(8,128)(2,1)S(1)}, u32[]{:S(2)}, u32[]{:S(2)}) collective-permute-start(bf16[152,1024]{1,0:T(8,128)(2,1)S(1)} %get-tuple-element.30), channel_id=1, source_target_pairs={{0,4},{4,8},{8,12},{12,16},{16,20},{20,24},{24,28},{1,5},{5,9},{9,... | collective-permute-start | bytes 933896 | tf_op jit(solution)/shard_map/ppermute | solution.py:25
  31.4 18.3 %collective-permute-start.3 = (bf16[160,1024]{1,0:T(8,128)(2,1)S(1)}, bf16[160,1024]{1,0:T(8,128)(2,1)S(1)}, u32[]{:S(2)}, u32[]{:S(2)}) collective-permute-start(bf16[160,1024]{1,0:T(8,128)(2,1)S(1)} %get-tuple-element.33), channel_id=1, source_target_pairs={{4,0},{8,4},{12,8},{16,12},{20,16},{24,20},{28,24},{5,1},{9,5},{13... | collective-permute-start | bytes 983048 | tf_op jit(solution)/shard_map/ppermute | solution.py:25
  32.7 17.0 %collective-permute-start.2 = (bf16[152,1024]{1,0:T(8,128)(2,1)S(1)}, bf16[152,1024]{1,0:T(8,128)(2,1)S(1)}, u32[]{:S(2)}, u32[]{:S(2)}) collective-permute-start(bf16[152,1024]{1,0:T(8,128)(2,1)S(1)} %get-tuple-element.32), channel_id=1, source_target_pairs={{0,4},{4,8},{8,12},{12,16},{16,20},{20,24},{24,28},{1,5},{5,9},{9,... | collective-permute-start | bytes 933896 | tf_op jit(solution)/shard_map/ppermute | solution.py:25
  61.4 23.1 %all-to-all-start.1 = ((bf16[8,160,256]{2,1,0:T(8,128)(2,1)}), bf16[8,160,256]{2,1,0:T(8,128)(2,1)S(1)}, u32[]{:S(2)}, u32[]{:S(2)}) async-start(bf16[8,160,256]{2,1,0:T(8,128)(2,1)} %get-tuple-element.40), calls=%async_computation.1 | async-start | bytes 1310720 | tf_op jit(solution)/shard_map/all_to_all | solution.py:489
  85.5 16.8 %all-to-all-start.2 = ((bf16[32,24,256]{2,1,0:T(8,128)(2,1)}), bf16[32,24,256]{2,1,0:T(8,128)(2,1)S(1)}, u32[]{:S(2)}, u32[]{:S(2)}) async-start(bf16[32,24,256]{2,1,0:T(8,128)(2,1)} %get-tuple-element.49), calls=%async_computation.2 | async-start | bytes 786432 | tf_op jit(solution)/shard_map/all_to_all | solution.py:503

commit v12 on v11

--- a/solution.py
+++ b/solution.py
@@ -426,7 +426,8 @@
             results.append((pltpu.HBM((ranks, rows, channels), BF16), FAR))
             scratch = [vmem(F32, rows, channels), vmem(BF16, ranks, rows, channels)] + scratch
         forward, backward, *spread = call(
-            functools.partial(edges_kernel, k * chunk), "edges", operands, results, scratch_shapes=scratch
+            functools.partial(edges_kernel, k * chunk), "edges", operands, results, cost=10 if k else 1,
+            scratch_shapes=scratch,
         )
         if k == 0:
             taps = lax.all_to_all(spread[0], "seq", 0, 0).reshape(count, channels)

time: 104 us -> 101 us (0.971)
  waiting for transfers between devices: 32.8 us -> 29.2 us
    ppermute x4, waiting for transfers between devices: 11.9 us -> 7.97 us  [from_behind(): return lax.ppermute(value, axis, pairs)]
    all_to_all x1, starting transfers between devices: 7.29 us -> 6.21 us  [shards(): taps = lax.all_to_all(spread[0], 'seq', 0, 0).reshape(count, channels)]
  transfers between devices with their start and end apart: 7 -> 7, of which waited for: 4 -> 4; matrix products, arithmetic and copies ran while one was open for 0% -> 0% of each run, Pallas kernels for 23% -> 24%
where the time goes in v12:
time: 101 us
  Pallas kernels  41.1 us (41%)
  starting transfers between devices  29.5 us (29%)
  waiting for transfers between devices  29.2 us (29%)
    pallas_call x5, Pallas kernels, call(): pl.pallas_call(kernel, in_specs=[spec for _, spec in operands] + [FAR] *...  38.7 us
    ppermute x4, starting transfers between devices, from_behind(): return lax.ppermute(value, axis, pairs)  13.1 us
    all_to_all x1, waiting for transfers between devices, shards(): gathered = lax.all_to_all(payload, ('seq', 'ch'), 0, 0)  13.1 us
    all_to_all x1, waiting for transfers between devices, shards(): lax.all_to_all(sums, 'seq', 0, 0)  8.14 us
    ppermute x4, waiting for transfers between devices, from_behind(): return lax.ppermute(value, axis, pairs)  7.97 us
    all_to_all x1, starting transfers between devices, shards(): lax.all_to_all(sums, 'seq', 0, 0)  6.5 us
    all_to_all x1, starting transfers between devices, shards(): taps = lax.all_to_all(spread[0], 'seq', 0, 0).reshape(count, channels)  6.21 us
    all_to_all x1, starting transfers between devices, shards(): gathered = lax.all_to_all(payload, ('seq', 'ch'), 0, 0)  3.65 us
  transfers between devices with their start and end apart: 7, of which 4 were waited for; matrix products, arithmetic and copies ran while one was open for 0% of the time, Pallas kernels for 24%

profile of v12, /device:TPU:0, one launch (start us, length us, event | category | flops | bytes accessed | tf_op | source)
XLA Modules:
  0.0 100.6 jit_solution(4160672762480581789)
XLA Ops:
  0.6 3.0 %edges.3 = (bf16[152,1024]{1,0:T(8,128)(2,1)S(1)}, bf16[160,1024]{1,0:T(8,128)(2,1)S(1)}, bf16[8,16,2048]{2,1,0:T(8,128)(2,1)}) custom-call(bf16[3,256,2048]{2,1,0:T(8,128)(2,1)} %bitcast.7, bf16[256,2048]{1,0:T(8,128)(2,1)} %cot.7, f32[3,7,2048]{2,1,0:T(8,128)} %short.9, f32[16,2048]{1,0:T(8,128)} %refs_0_.1), custom_call_target="tpu_custom_call" | custom-call | flops 1000000000 | bytes 1000000 | tf_op jit(solution)/shard_map/edges/pallas_call | solution.py:347
  3.6 1.3 %collective-permute-start.1 = (bf16[160,1024]{1,0:T(8,128)(2,1)S(1)}, bf16[160,1024]{1,0:T(8,128)(2,1)S(1)}, u32[]{:S(2)}, u32[]{:S(2)}) collective-permute-start(bf16[160,1024]{1,0:T(8,128)(2,1)S(1)} %get-tuple-element.31), channel_id=1, source_target_pairs={{4,0},{8,4},{12,8},{16,12},{20,16},{24,20},{28,24},{5,1},{9,5},{13... | collective-permute-start | bytes 983048 | tf_op jit(solution)/shard_map/ppermute | solution.py:25
  4.9 5.5 %collective-permute-start = (bf16[152,1024]{1,0:T(8,128)(2,1)S(1)}, bf16[152,1024]{1,0:T(8,128)(2,1)S(1)}, u32[]{:S(2)}, u32[]{:S(2)}) collective-permute-start(bf16[152,1024]{1,0:T(8,128)(2,1)S(1)} %get-tuple-element.30), channel_id=1, source_target_pairs={{0,4},{4,8},{8,12},{12,16},{16,20},{20,24},{24,28},{1,5},{5,9},{9,... | collective-permute-start | bytes 933896 | tf_op jit(solution)/shard_map/ppermute | solution.py:25
  10.5 6.2 %all-to-all-start = ((bf16[8,16,2048]{2,1,0:T(8,128)(2,1)}), bf16[8,16,2048]{2,1,0:T(8,128)(2,1)S(1)}, u32[]{:S(2)}, u32[]{:S(2)}) async-start(bf16[8,16,2048]{2,1,0:T(8,128)(2,1)} %get-tuple-element.34), calls=%async_computation | async-start | bytes 1048576 | tf_op jit(solution)/shard_map/all_to_all | solution.py:433
  16.7 2.9 %edges.2 = (bf16[152,1024]{1,0:T(8,128)(2,1)S(1)}, bf16[160,1024]{1,0:T(8,128)(2,1)S(1)}) custom-call(bf16[3,256,2048]{2,1,0:T(8,128)(2,1)} %bitcast.8, bf16[256,2048]{1,0:T(8,128)(2,1)} %cot.7, f32[3,7,2048]{2,1,0:T(8,128)} %short.9), custom_call_target="tpu_custom_call" | custom-call | flops 10000000000 | bytes 1000000 | tf_op jit(solution)/shard_map/edges/pallas_call | solution.py:347
  19.6 7.0 %collective-permute-done.prev = bf16[152,1024]{1,0:T(8,128)(2,1)S(1)} collective-permute-done((bf16[152,1024]{1,0:T(8,128)(2,1)S(1)}, bf16[152,1024]{1,0:T(8,128)(2,1)S(1)}, u32[]{:S(2)}, u32[]{:S(2)}) %collective-permute-start) | collective-permute-done | bytes 311328 | tf_op jit(solution)/shard_map/ppermute | solution.py:25
  26.6 0.0 collective-permute-done.1.later
  26.7 1.3 %collective-permute-start.3 = (bf16[160,1024]{1,0:T(8,128)(2,1)S(1)}, bf16[160,1024]{1,0:T(8,128)(2,1)S(1)}, u32[]{:S(2)}, u32[]{:S(2)}) collective-permute-start(bf16[160,1024]{1,0:T(8,128)(2,1)S(1)} %get-tuple-element.33), channel_id=1, source_target_pairs={{4,0},{8,4},{12,8},{16,12},{20,16},{24,20},{28,24},{5,1},{9,5},{13... | collective-permute-start | bytes 983048 | tf_op jit(solution)/shard_map/ppermute | solution.py:25
  27.9 5.0 %collective-permute-start.2 = (bf16[152,1024]{1,0:T(8,128)(2,1)S(1)}, bf16[152,1024]{1,0:T(8,128)(2,1)S(1)}, u32[]{:S(2)}, u32[]{:S(2)}) collective-permute-start(bf16[152,1024]{1,0:T(8,128)(2,1)S(1)} %get-tuple-element.32), channel_id=1, source_target_pairs={{0,4},{4,8},{8,12},{12,16},{16,20},{20,24},{24,28},{1,5},{5,9},{9,... | collective-permute-start | bytes 933896 | tf_op jit(solution)/shard_map/ppermute | solution.py:25
  33.0 0.0 all-to-all-done
  33.0 11.7 %operator.2 = (bf16[8,256,256]{2,1,0:T(8,128)(2,1)}, f32[8,3,38,8,256]{4,3,2,1,0:T(8,128)}, bf16[8,160,256]{2,1,0:T(8,128)(2,1)}) custom-call(bf16[3,256,2048]{2,1,0:T(8,128)(2,1)} %bitcast.9, bf16[256,2048]{1,0:T(8,128)(2,1)} %cot.7, bf16[152,1024]{1,0:T(8,128)(2,1)S(1)} %collective-permute-done.prev, bf16[160,1024]{1,0:T(8,128)(2,1)S(1)} %collective-permute-done.1.later, ...), custom_call_target="tpu_custom_call" | custom-call | flops 12000000000 | bytes 1000000 | tf_op jit(solution)/shard_map/operator/pallas_call | solution.py:347
  44.7 0.9 collective-permute-done.2.prev
  45.6 0.0 collective-permute-done.3.later
  45.6 11.7 %operator.3 = (bf16[8,256,256]{2,1,0:T(8,128)(2,1)}, f32[8,3,38,8,256]{4,3,2,1,0:T(8,128)}, bf16[8,160,256]{2,1,0:T(8,128)(2,1)}) custom-call(bf16[3,256,2048]{2,1,0:T(8,128)(2,1)} %bitcast.10, bf16[256,2048]{1,0:T(8,128)(2,1)} %cot.7, ...), custom_call_target="tpu_custom_call", output_to_operand_aliasing={{0}: (14, {}), {1}: (15, {}), {2}: (16, {})} | custom-call | flops 12000000000 | bytes 1000000 | tf_op jit(solution)/shard_map/operator/pallas_call | solution.py:347
  57.4 6.5 %all-to-all-start.1 = ((bf16[8,160,256]{2,1,0:T(8,128)(2,1)}), bf16[8,160,256]{2,1,0:T(8,128)(2,1)S(1)}, u32[]{:S(2)}, u32[]{:S(2)}) async-start(bf16[8,160,256]{2,1,0:T(8,128)(2,1)} %get-tuple-element.40), calls=%async_computation.1 | async-start | bytes 1310720 | tf_op jit(solution)/shard_map/all_to_all | solution.py:490
  63.9 9.3 %outputs.1 = (bf16[256,2048]{1,0:T(8,128)(2,1)}, bf16[3,256,2048]{2,1,0:T(8,128)(2,1)}) custom-call(bf16[8,256,256]{2,1,0:T(8,128)(2,1)} %get-tuple-element.41.product, f32[8,3,38,8,256]{4,3,2,1,0:T(8,128)} %get-tuple-element.42.grad, f32[3,7,2048]{2,1,0:T(8,128)} %short.9, bf16[256,256]{1,0:T(8,128)(2,1)} %constant.29.clone.p_out), custom_call_target="tpu_custom_call" | custom-call | flops 8000000000 | bytes 1000000 | tf_op jit(solution)/shard_map/outputs/pallas_call | solution.py:347
  73.2 8.1 %all-to-all-done.1.sums = bf16[8,160,256]{2,1,0:T(8,128)(2,1)S(1)} async-done(((bf16[8,160,256]{2,1,0:T(8,128)(2,1)}), bf16[8,160,256]{2,1,0:T(8,128)(2,1)S(1)}, u32[]{:S(2)}, u32[]{:S(2)}) %all-to-all-start.1) | async-done | bytes 655392 | tf_op jit(solution)/shard_map/all_to_all | solution.py:490
  81.4 1.0 %squares.1 = (f32[16,2048]{1,0:T(8,128)S(1)}, bf16[32,24,256]{2,1,0:T(8,128)(2,1)}) custom-call(bf16[8,160,256]{2,1,0:T(8,128)(2,1)S(1)} %all-to-all-done.1.sums), custom_call_target="tpu_custom_call" | custom-call | tf_op jit(solution)/shard_map/squares/pallas_call | solution.py:493
  82.4 3.6 %all-to-all-start.2 = ((bf16[32,24,256]{2,1,0:T(8,128)(2,1)}), bf16[32,24,256]{2,1,0:T(8,128)(2,1)S(1)}, u32[]{:S(2)}, u32[]{:S(2)}) async-start(bf16[32,24,256]{2,1,0:T(8,128)(2,1)} %get-tuple-element.49), calls=%async_computation.2 | async-start | bytes 786432 | tf_op jit(solution)/shard_map/all_to_all | solution.py:504
  86.1 0.1 pad_add_fusion.mine
  86.1 13.1 %all-to-all-done.2.gathered = bf16[32,24,256]{2,1,0:T(8,128)(2,1)S(1)} async-done(((bf16[32,24,256]{2,1,0:T(8,128)(2,1)}), bf16[32,24,256]{2,1,0:T(8,128)(2,1)S(1)}, u32[]{:S(2)}, u32[]{:S(2)}) %all-to-all-start.2) | async-done | bytes 393248 | tf_op jit(solution)/shard_map/all_to_all | solution.py:504
  99.2 1.4 %scale.1 = (f32[3,7,2048]{2,1,0:T(8,128)}, f32[16,2048]{1,0:T(8,128)}) custom-call(s32[2]{0:T(128)S(1)} %pad_add_fusion.mine, f32[16,2048]{1,0:T(8,128)S(1)} %get-tuple-element.48.raw, bf16[32,24,256]{2,1,0:T(8,128)(2,1)S(1)} %all-to-all-done.2.gathered), custom_call_target="tpu_custom_call" | custom-call | tf_op jit(solution)/shard_map/scale/pallas_call | solution.py:507
Async XLA Ops:
  3.6 23.0 %collective-permute-start.1 = (bf16[160,1024]{1,0:T(8,128)(2,1)S(1)}, bf16[160,1024]{1,0:T(8,128)(2,1)S(1)}, u32[]{:S(2)}, u32[]{:S(2)}) collective-permute-start(bf16[160,1024]{1,0:T(8,128)(2,1)S(1)} %get-tuple-element.31), channel_id=1, source_target_pairs={{4,0},{8,4},{12,8},{16,12},{20,16},{24,20},{28,24},{5,1},{9,5},{13... | collective-permute-start | bytes 983048 | tf_op jit(solution)/shard_map/ppermute | solution.py:25
  4.9 21.7 %collective-permute-start = (bf16[152,1024]{1,0:T(8,128)(2,1)S(1)}, bf16[152,1024]{1,0:T(8,128)(2,1)S(1)}, u32[]{:S(2)}, u32[]{:S(2)}) collective-permute-start(bf16[152,1024]{1,0:T(8,128)(2,1)S(1)} %get-tuple-element.30), channel_id=1, source_target_pairs={{0,4},{4,8},{8,12},{12,16},{16,20},{20,24},{24,28},{1,5},{5,9},{9,... | collective-permute-start | bytes 933896 | tf_op jit(solution)/shard_map/ppermute | solution.py:25
  10.5 22.5 %all-to-all-start = ((bf16[8,16,2048]{2,1,0:T(8,128)(2,1)}), bf16[8,16,2048]{2,1,0:T(8,128)(2,1)S(1)}, u32[]{:S(2)}, u32[]{:S(2)}) async-start(bf16[8,16,2048]{2,1,0:T(8,128)(2,1)} %get-tuple-element.34), calls=%async_computation | async-start | bytes 1048576 | tf_op jit(solution)/shard_map/all_to_all | solution.py:433
  26.7 19.0 %collective-permute-start.3 = (bf16[160,1024]{1,0:T(8,128)(2,1)S(1)}, bf16[160,1024]{1,0:T(8,128)(2,1)S(1)}, u32[]{:S(2)}, u32[]{:S(2)}) collective-permute-start(bf16[160,1024]{1,0:T(8,128)(2,1)S(1)} %get-tuple-element.33), channel_id=1, source_target_pairs={{4,0},{8,4},{12,8},{16,12},{20,16},{24,20},{28,24},{5,1},{9,5},{13... | collective-permute-start | bytes 983048 | tf_op jit(solution)/shard_map/ppermute | solution.py:25
  27.9 17.7 %collective-permute-start.2 = (bf16[152,1024]{1,0:T(8,128)(2,1)S(1)}, bf16[152,1024]{1,0:T(8,128)(2,1)S(1)}, u32[]{:S(2)}, u32[]{:S(2)}) collective-permute-start(bf16[152,1024]{1,0:T(8,128)(2,1)S(1)} %get-tuple-element.32), channel_id=1, source_target_pairs={{0,4},{4,8},{8,12},{12,16},{16,20},{20,24},{24,28},{1,5},{5,9},{9,... | collective-permute-start | bytes 933896 | tf_op jit(solution)/shard_map/ppermute | solution.py:25
  57.4 24.0 %all-to-all-start.1 = ((bf16[8,160,256]{2,1,0:T(8,128)(2,1)}), bf16[8,160,256]{2,1,0:T(8,128)(2,1)S(1)}, u32[]{:S(2)}, u32[]{:S(2)}) async-start(bf16[8,160,256]{2,1,0:T(8,128)(2,1)} %get-tuple-element.40), calls=%async_computation.1 | async-start | bytes 1310720 | tf_op jit(solution)/shard_map/all_to_all | solution.py:490
  82.4 16.8 %all-to-all-start.2 = ((bf16[32,24,256]{2,1,0:T(8,128)(2,1)}), bf16[32,24,256]{2,1,0:T(8,128)(2,1)S(1)}, u32[]{:S(2)}, u32[]{:S(2)}) async-start(bf16[32,24,256]{2,1,0:T(8,128)(2,1)} %get-tuple-element.49), calls=%async_computation.2 | async-start | bytes 786432 | tf_op jit(solution)/shard_map/all_to_all | solution.py:504

commit v13 on v12

--- a/solution.py
+++ b/solution.py
@@ -431,8 +431,6 @@
         )
         if k == 0:
             taps = lax.all_to_all(spread[0], "seq", 0, 0).reshape(count, channels)
-        else:
-            forward, backward, prev[-1], later[-1] = lax.optimization_barrier((forward, backward, prev[-1], later[-1]))
         prev.append(from_behind(forward, "seq", 1))
         later.append(from_behind(backward, "seq", -1))
 

time: 101 us -> 105 us (1.040)
  waiting for transfers between devices: 29.2 us -> 32.9 us
    ppermute x4, waiting for transfers between devices: 7.97 us -> 12.8 us  [from_behind(): return lax.ppermute(value, axis, pairs)]
    all_to_all x1, waiting for transfers between devices: 8.14 us -> 7.01 us  [shards(): lax.all_to_all(sums, 'seq', 0, 0)]
    all_to_all x1, starting transfers between devices: 6.21 us -> 7.29 us  [shards(): taps = lax.all_to_all(spread[0], 'seq', 0, 0).reshape(count, channels)]
  transfers between devices with their start and end apart: 7 -> 7, of which waited for: 4 -> 3; matrix products, arithmetic and copies ran while one was open for 0% -> 0% of each run, Pallas kernels for 24% -> 23%
where the time goes in v13:
time: 105 us; the launch traced here: 104 us
  Pallas kernels  41.1 us (39%)
  waiting for transfers between devices  32.9 us (31%)
  starting transfers between devices  29.4 us (28%)
    pallas_call x5, Pallas kernels, call(): pl.pallas_call(kernel, in_specs=[spec for _, spec in operands] + [FAR] *...  38.7 us
    all_to_all x1, waiting for transfers between devices, shards(): gathered = lax.all_to_all(payload, ('seq', 'ch'), 0, 0)  13.1 us
    ppermute x4, waiting for transfers between devices, from_behind(): return lax.ppermute(value, axis, pairs)  12.8 us
    ppermute x4, starting transfers between devices, from_behind(): return lax.ppermute(value, axis, pairs)  12.6 us
    all_to_all x1, starting transfers between devices, shards(): taps = lax.all_to_all(spread[0], 'seq', 0, 0).reshape(count, channels)  7.29 us
    all_to_all x1, waiting for transfers between devices, shards(): lax.all_to_all(sums, 'seq', 0, 0)  7.01 us
    all_to_all x1, starting transfers between devices, shards(): lax.all_to_all(sums, 'seq', 0, 0)  5.86 us
    all_to_all x1, starting transfers between devices, shards(): gathered = lax.all_to_all(payload, ('seq', 'ch'), 0, 0)  3.65 us
  transfers between devices with their start and end apart: 7, of which 3 were waited for; matrix products, arithmetic and copies ran while one was open for 0% of the time, Pallas kernels for 23%

profile of v13, /device:TPU:0, one launch (start us, length us, event | category | flops | bytes accessed | tf_op | source)
XLA Modules:
  0.0 104.3 jit_solution(4055363227146841811)
XLA Ops:
  0.6 3.0 %edges.3 = (bf16[152,1024]{1,0:T(8,128)(2,1)S(1)}, bf16[160,1024]{1,0:T(8,128)(2,1)S(1)}, bf16[8,16,2048]{2,1,0:T(8,128)(2,1)}) custom-call(bf16[3,256,2048]{2,1,0:T(8,128)(2,1)} %bitcast.7, bf16[256,2048]{1,0:T(8,128)(2,1)} %cot.7, f32[3,7,2048]{2,1,0:T(8,128)} %short.9, f32[16,2048]{1,0:T(8,128)} %refs_0_.1), custom_call_target="tpu_custom_call" | custom-call | flops 1000000000 | bytes 1000000 | tf_op jit(solution)/shard_map/edges/pallas_call | solution.py:347
  3.6 7.3 %all-to-all-start = ((bf16[8,16,2048]{2,1,0:T(8,128)(2,1)}), bf16[8,16,2048]{2,1,0:T(8,128)(2,1)S(1)}, u32[]{:S(2)}, u32[]{:S(2)}) async-start(bf16[8,16,2048]{2,1,0:T(8,128)(2,1)} %get-tuple-element.26), calls=%async_computation | async-start | bytes 1048576 | tf_op jit(solution)/shard_map/all_to_all | solution.py:433
  10.9 1.3 %collective-permute-start.3 = (bf16[160,1024]{1,0:T(8,128)(2,1)S(1)}, bf16[160,1024]{1,0:T(8,128)(2,1)S(1)}, u32[]{:S(2)}, u32[]{:S(2)}) collective-permute-start(bf16[160,1024]{1,0:T(8,128)(2,1)S(1)} %get-tuple-element.28), channel_id=1, source_target_pairs={{4,0},{8,4},{12,8},{16,12},{20,16},{24,20},{28,24},{5,1},{9,5},{13... | collective-permute-start | bytes 983048 | tf_op jit(solution)/shard_map/ppermute | solution.py:25
  12.2 4.6 %collective-permute-start.2 = (bf16[152,1024]{1,0:T(8,128)(2,1)S(1)}, bf16[152,1024]{1,0:T(8,128)(2,1)S(1)}, u32[]{:S(2)}, u32[]{:S(2)}) collective-permute-start(bf16[152,1024]{1,0:T(8,128)(2,1)S(1)} %get-tuple-element.27), channel_id=1, source_target_pairs={{0,4},{4,8},{8,12},{12,16},{16,20},{20,24},{24,28},{1,5},{5,9},{9,... | collective-permute-start | bytes 933896 | tf_op jit(solution)/shard_map/ppermute | solution.py:25
  16.8 2.9 %edges.2 = (bf16[152,1024]{1,0:T(8,128)(2,1)S(1)}, bf16[160,1024]{1,0:T(8,128)(2,1)S(1)}) custom-call(bf16[3,256,2048]{2,1,0:T(8,128)(2,1)} %bitcast.8, bf16[256,2048]{1,0:T(8,128)(2,1)} %cot.7, f32[3,7,2048]{2,1,0:T(8,128)} %short.9), custom_call_target="tpu_custom_call" | custom-call | flops 10000000000 | bytes 1000000 | tf_op jit(solution)/shard_map/edges/pallas_call | solution.py:347
  19.7 1.3 %collective-permute-start.1 = (bf16[160,1024]{1,0:T(8,128)(2,1)S(1)}, bf16[160,1024]{1,0:T(8,128)(2,1)S(1)}, u32[]{:S(2)}, u32[]{:S(2)}) collective-permute-start(bf16[160,1024]{1,0:T(8,128)(2,1)S(1)} %get-tuple-element.25), channel_id=1, source_target_pairs={{4,0},{8,4},{12,8},{16,12},{20,16},{24,20},{28,24},{5,1},{9,5},{13... | collective-permute-start | bytes 983048 | tf_op jit(solution)/shard_map/ppermute | solution.py:25
  21.0 5.5 %collective-permute-start = (bf16[152,1024]{1,0:T(8,128)(2,1)S(1)}, bf16[152,1024]{1,0:T(8,128)(2,1)S(1)}, u32[]{:S(2)}, u32[]{:S(2)}) collective-permute-start(bf16[152,1024]{1,0:T(8,128)(2,1)S(1)} %get-tuple-element.24), channel_id=1, source_target_pairs={{0,4},{4,8},{8,12},{12,16},{16,20},{20,24},{24,28},{1,5},{5,9},{9,... | collective-permute-start | bytes 933896 | tf_op jit(solution)/shard_map/ppermute | solution.py:25
  26.5 12.8 %collective-permute-done.2.prev = bf16[152,1024]{1,0:T(8,128)(2,1)S(1)} collective-permute-done((bf16[152,1024]{1,0:T(8,128)(2,1)S(1)}, bf16[152,1024]{1,0:T(8,128)(2,1)S(1)}, u32[]{:S(2)}, u32[]{:S(2)}) %collective-permute-start.2) | collective-permute-done | bytes 311328 | tf_op jit(solution)/shard_map/ppermute | solution.py:25
  39.3 0.0 collective-permute-done.3.later
  39.3 0.0 all-to-all-done
  39.3 11.7 %operator.2 = (bf16[8,256,256]{2,1,0:T(8,128)(2,1)}, f32[8,3,38,8,256]{4,3,2,1,0:T(8,128)}, bf16[8,160,256]{2,1,0:T(8,128)(2,1)}) custom-call(bf16[3,256,2048]{2,1,0:T(8,128)(2,1)} %bitcast.9, bf16[256,2048]{1,0:T(8,128)(2,1)} %cot.7, bf16[152,1024]{1,0:T(8,128)(2,1)S(1)} %collective-permute-done.2.prev, bf16[160,1024]{1,0:T(8,128)(2,1)S(1)} %collective-permute-done.3.later, ...), custom_call_target="tpu_custom_call" | custom-call | flops 12000000000 | bytes 1000000 | tf_op jit(solution)/shard_map/operator/pallas_call | solution.py:347
  51.0 0.0 collective-permute-done.prev
  51.1 0.0 collective-permute-done.1.later
  51.1 11.8 %operator.3 = (bf16[8,256,256]{2,1,0:T(8,128)(2,1)}, f32[8,3,38,8,256]{4,3,2,1,0:T(8,128)}, bf16[8,160,256]{2,1,0:T(8,128)(2,1)}) custom-call(bf16[3,256,2048]{2,1,0:T(8,128)(2,1)} %bitcast.10, bf16[256,2048]{1,0:T(8,128)(2,1)} %cot.7, ...), custom_call_target="tpu_custom_call", output_to_operand_aliasing={{0}: (14, {}), {1}: (15, {}), {2}: (16, {})} | custom-call | flops 12000000000 | bytes 1000000 | tf_op jit(solution)/shard_map/operator/pallas_call | solution.py:347
  62.8 5.9 %all-to-all-start.1 = ((bf16[8,160,256]{2,1,0:T(8,128)(2,1)}), bf16[8,160,256]{2,1,0:T(8,128)(2,1)S(1)}, u32[]{:S(2)}, u32[]{:S(2)}) async-start(bf16[8,160,256]{2,1,0:T(8,128)(2,1)} %get-tuple-element.32), calls=%async_computation.1 | async-start | bytes 1310720 | tf_op jit(solution)/shard_map/all_to_all | solution.py:488
  68.7 9.3 %outputs.1 = (bf16[256,2048]{1,0:T(8,128)(2,1)}, bf16[3,256,2048]{2,1,0:T(8,128)(2,1)}) custom-call(bf16[8,256,256]{2,1,0:T(8,128)(2,1)} %get-tuple-element.33.product, f32[8,3,38,8,256]{4,3,2,1,0:T(8,128)} %get-tuple-element.34.grad, f32[3,7,2048]{2,1,0:T(8,128)} %short.9, bf16[256,256]{1,0:T(8,128)(2,1)} %constant.29.clone.p_out), custom_call_target="tpu_custom_call" | custom-call | flops 8000000000 | bytes 1000000 | tf_op jit(solution)/shard_map/outputs/pallas_call | solution.py:347
  78.0 7.0 %all-to-all-done.1.sums = bf16[8,160,256]{2,1,0:T(8,128)(2,1)S(1)} async-done(((bf16[8,160,256]{2,1,0:T(8,128)(2,1)}), bf16[8,160,256]{2,1,0:T(8,128)(2,1)S(1)}, u32[]{:S(2)}, u32[]{:S(2)}) %all-to-all-start.1) | async-done | bytes 655392 | tf_op jit(solution)/shard_map/all_to_all | solution.py:488
  85.1 1.0 squares.1
  86.1 3.6 %all-to-all-start.2 = ((bf16[32,24,256]{2,1,0:T(8,128)(2,1)}), bf16[32,24,256]{2,1,0:T(8,128)(2,1)S(1)}, u32[]{:S(2)}, u32[]{:S(2)}) async-start(bf16[32,24,256]{2,1,0:T(8,128)(2,1)} %get-tuple-element.41), calls=%async_computation.2 | async-start | bytes 786432 | tf_op jit(solution)/shard_map/all_to_all | solution.py:502
  89.7 0.1 pad_add_fusion.mine
  89.8 13.1 %all-to-all-done.2.gathered = bf16[32,24,256]{2,1,0:T(8,128)(2,1)S(1)} async-done(((bf16[32,24,256]{2,1,0:T(8,128)(2,1)}), bf16[32,24,256]{2,1,0:T(8,128)(2,1)S(1)}, u32[]{:S(2)}, u32[]{:S(2)}) %all-to-all-start.2) | async-done | bytes 393248 | tf_op jit(solution)/shard_map/all_to_all | solution.py:502
  102.9 1.4 %scale.1 = (f32[3,7,2048]{2,1,0:T(8,128)}, f32[16,2048]{1,0:T(8,128)}) custom-call(s32[2]{0:T(128)S(1)} %pad_add_fusion.mine, f32[16,2048]{1,0:T(8,128)S(1)} %get-tuple-element.40.raw, bf16[32,24,256]{2,1,0:T(8,128)(2,1)S(1)} %all-to-all-done.2.gathered), custom_call_target="tpu_custom_call" | custom-call | tf_op jit(solution)/shard_map/scale/pallas_call | solution.py:505
Async XLA Ops:
  3.6 35.7 %all-to-all-start = ((bf16[8,16,2048]{2,1,0:T(8,128)(2,1)}), bf16[8,16,2048]{2,1,0:T(8,128)(2,1)S(1)}, u32[]{:S(2)}, u32[]{:S(2)}) async-start(bf16[8,16,2048]{2,1,0:T(8,128)(2,1)} %get-tuple-element.26), calls=%async_computation | async-start | bytes 1048576 | tf_op jit(solution)/shard_map/all_to_all | solution.py:433
  10.9 28.4 %collective-permute-start.3 = (bf16[160,1024]{1,0:T(8,128)(2,1)S(1)}, bf16[160,1024]{1,0:T(8,128)(2,1)S(1)}, u32[]{:S(2)}, u32[]{:S(2)}) collective-permute-start(bf16[160,1024]{1,0:T(8,128)(2,1)S(1)} %get-tuple-element.28), channel_id=1, source_target_pairs={{4,0},{8,4},{12,8},{16,12},{20,16},{24,20},{28,24},{5,1},{9,5},{13... | collective-permute-start | bytes 983048 | tf_op jit(solution)/shard_map/ppermute | solution.py:25
  12.2 27.1 %collective-permute-start.2 = (bf16[152,1024]{1,0:T(8,128)(2,1)S(1)}, bf16[152,1024]{1,0:T(8,128)(2,1)S(1)}, u32[]{:S(2)}, u32[]{:S(2)}) collective-permute-start(bf16[152,1024]{1,0:T(8,128)(2,1)S(1)} %get-tuple-element.27), channel_id=1, source_target_pairs={{0,4},{4,8},{8,12},{12,16},{16,20},{20,24},{24,28},{1,5},{5,9},{9,... | collective-permute-start | bytes 933896 | tf_op jit(solution)/shard_map/ppermute | solution.py:25
  19.7 31.3 %collective-permute-start.1 = (bf16[160,1024]{1,0:T(8,128)(2,1)S(1)}, bf16[160,1024]{1,0:T(8,128)(2,1)S(1)}, u32[]{:S(2)}, u32[]{:S(2)}) collective-permute-start(bf16[160,1024]{1,0:T(8,128)(2,1)S(1)} %get-tuple-element.25), channel_id=1, source_target_pairs={{4,0},{8,4},{12,8},{16,12},{20,16},{24,20},{28,24},{5,1},{9,5},{13... | collective-permute-start | bytes 983048 | tf_op jit(solution)/shard_map/ppermute | solution.py:25
  21.0 30.0 %collective-permute-start = (bf16[152,1024]{1,0:T(8,128)(2,1)S(1)}, bf16[152,1024]{1,0:T(8,128)(2,1)S(1)}, u32[]{:S(2)}, u32[]{:S(2)}) collective-permute-start(bf16[152,1024]{1,0:T(8,128)(2,1)S(1)} %get-tuple-element.24), channel_id=1, source_target_pairs={{0,4},{4,8},{8,12},{12,16},{16,20},{20,24},{24,28},{1,5},{5,9},{9,... | collective-permute-start | bytes 933896 | tf_op jit(solution)/shard_map/ppermute | solution.py:25
  62.8 22.2 %all-to-all-start.1 = ((bf16[8,160,256]{2,1,0:T(8,128)(2,1)}), bf16[8,160,256]{2,1,0:T(8,128)(2,1)S(1)}, u32[]{:S(2)}, u32[]{:S(2)}) async-start(bf16[8,160,256]{2,1,0:T(8,128)(2,1)} %get-tuple-element.32), calls=%async_computation.1 | async-start | bytes 1310720 | tf_op jit(solution)/shard_map/all_to_all | solution.py:488
  86.1 16.8 %all-to-all-start.2 = ((bf16[32,24,256]{2,1,0:T(8,128)(2,1)}), bf16[32,24,256]{2,1,0:T(8,128)(2,1)S(1)}, u32[]{:S(2)}, u32[]{:S(2)}) async-start(bf16[32,24,256]{2,1,0:T(8,128)(2,1)} %get-tuple-element.41), calls=%async_computation.2 | async-start | bytes 786432 | tf_op jit(solution)/shard_map/all_to_all | solution.py:502

commit v14 on v13

--- a/solution.py
+++ b/solution.py
@@ -421,7 +421,7 @@
             vmem(BF16, 8 * (15 + FK), some), vmem(BF16, 8 * (16 + FK), some), vmem(F32, 8 * (15 + FK), width),
             vmem(F32, 8 * (15 + FK), width), vmem(F32, 8 * (16 + FK), width), vmem(F32, 8 * 17, width), semaphores,
         ]
-        if k == 0:
+        if k == CHUNKS - 1:
             operands += far(filter_taps)
             results.append((pltpu.HBM((ranks, rows, channels), BF16), FAR))
             scratch = [vmem(F32, rows, channels), vmem(BF16, ranks, rows, channels)] + scratch
@@ -429,8 +429,10 @@
             functools.partial(edges_kernel, k * chunk), "edges", operands, results, cost=10 if k else 1,
             scratch_shapes=scratch,
         )
-        if k == 0:
+        if k == CHUNKS - 1:
             taps = lax.all_to_all(spread[0], "seq", 0, 0).reshape(count, channels)
+        if k:
+            forward, backward, prev[-1], later[-1] = lax.optimization_barrier((forward, backward, prev[-1], later[-1]))
         prev.append(from_behind(forward, "seq", 1))
         later.append(from_behind(backward, "seq", -1))
 

time: 105 us -> 106 us (level)
  waiting for transfers between devices: 32.9 us -> 34.4 us
  transfers between devices with their start and end apart: 7 -> 7, of which waited for: 3 -> 4; matrix products, arithmetic and copies ran while one was open for 0% -> 0% of each run, Pallas kernels for 23% -> 23%
where the time goes in v14:
time: 106 us; the launch traced here: 105 us
  Pallas kernels  41.1 us (39%)
  waiting for transfers between devices  34.4 us (32%)
  starting transfers between devices  28.8 us (27%)
    pallas_call x5, Pallas kernels, call(): pl.pallas_call(kernel, in_specs=[spec for _, spec in operands] + [FAR] *...  38.7 us
    ppermute x4, waiting for transfers between devices, from_behind(): return lax.ppermute(value, axis, pairs)  13.6 us
    all_to_all x1, waiting for transfers between devices, shards(): gathered = lax.all_to_all(payload, ('seq', 'ch'), 0, 0)  13.1 us
    ppermute x4, starting transfers between devices, from_behind(): return lax.ppermute(value, axis, pairs)  12.2 us
    all_to_all x1, waiting for transfers between devices, shards(): lax.all_to_all(sums, 'seq', 0, 0)  7.75 us
    all_to_all x1, starting transfers between devices, shards(): taps = lax.all_to_all(spread[0], 'seq', 0, 0).reshape(count, channels)  7.29 us
    all_to_all x1, starting transfers between devices, shards(): lax.all_to_all(sums, 'seq', 0, 0)  5.73 us
    all_to_all x1, starting transfers between devices, shards(): gathered = lax.all_to_all(payload, ('seq', 'ch'), 0, 0)  3.65 us
  transfers between devices with their start and end apart: 7, of which 4 were waited for; matrix products, arithmetic and copies ran while one was open for 0% of the time, Pallas kernels for 23%

profile of v14, /device:TPU:0, one launch (start us, length us, event | category | flops | bytes accessed | tf_op | source)
XLA Modules:
  0.0 105.2 jit_solution(15705766548257225270)
XLA Ops:
  0.6 3.0 %edges.2 = (bf16[152,1024]{1,0:T(8,128)(2,1)S(1)}, bf16[160,1024]{1,0:T(8,128)(2,1)S(1)}, bf16[8,16,2048]{2,1,0:T(8,128)(2,1)}) custom-call(bf16[3,256,2048]{2,1,0:T(8,128)(2,1)} %bitcast.7, bf16[256,2048]{1,0:T(8,128)(2,1)} %cot.7, f32[3,7,2048]{2,1,0:T(8,128)} %short.9, f32[16,2048]{1,0:T(8,128)} %refs_0_.1), custom_call_target="tpu_custom_call" | custom-call | flops 10000000000 | bytes 1000000 | tf_op jit(solution)/shard_map/edges/pallas_call | solution.py:347
  3.6 7.3 %all-to-all-start = ((bf16[8,16,2048]{2,1,0:T(8,128)(2,1)}), bf16[8,16,2048]{2,1,0:T(8,128)(2,1)S(1)}, u32[]{:S(2)}, u32[]{:S(2)}) async-start(bf16[8,16,2048]{2,1,0:T(8,128)(2,1)} %get-tuple-element.34), calls=%async_computation | async-start | bytes 1048576 | tf_op jit(solution)/shard_map/all_to_all | solution.py:433
  10.9 2.9 %edges.3 = (bf16[152,1024]{1,0:T(8,128)(2,1)S(1)}, bf16[160,1024]{1,0:T(8,128)(2,1)S(1)}) custom-call(bf16[3,256,2048]{2,1,0:T(8,128)(2,1)} %bitcast.8, bf16[256,2048]{1,0:T(8,128)(2,1)} %cot.7, f32[3,7,2048]{2,1,0:T(8,128)} %short.9), custom_call_target="tpu_custom_call" | custom-call | flops 1000000000 | bytes 1000000 | tf_op jit(solution)/shard_map/edges/pallas_call | solution.py:347
  13.9 1.3 %collective-permute-start.1 = (bf16[160,1024]{1,0:T(8,128)(2,1)S(1)}, bf16[160,1024]{1,0:T(8,128)(2,1)S(1)}, u32[]{:S(2)}, u32[]{:S(2)}) collective-permute-start(bf16[160,1024]{1,0:T(8,128)(2,1)S(1)} %get-tuple-element.31), channel_id=1, source_target_pairs={{4,0},{8,4},{12,8},{16,12},{20,16},{24,20},{28,24},{5,1},{9,5},{13... | collective-permute-start | bytes 983048 | tf_op jit(solution)/shard_map/ppermute | solution.py:25
  15.2 4.6 %collective-permute-start = (bf16[152,1024]{1,0:T(8,128)(2,1)S(1)}, bf16[152,1024]{1,0:T(8,128)(2,1)S(1)}, u32[]{:S(2)}, u32[]{:S(2)}) collective-permute-start(bf16[152,1024]{1,0:T(8,128)(2,1)S(1)} %get-tuple-element.30), channel_id=1, source_target_pairs={{0,4},{4,8},{8,12},{12,16},{16,20},{20,24},{24,28},{1,5},{5,9},{9,... | collective-permute-start | bytes 933896 | tf_op jit(solution)/shard_map/ppermute | solution.py:25
  19.7 13.2 %collective-permute-done.prev = bf16[152,1024]{1,0:T(8,128)(2,1)S(1)} collective-permute-done((bf16[152,1024]{1,0:T(8,128)(2,1)S(1)}, bf16[152,1024]{1,0:T(8,128)(2,1)S(1)}, u32[]{:S(2)}, u32[]{:S(2)}) %collective-permute-start) | collective-permute-done | bytes 311328 | tf_op jit(solution)/shard_map/ppermute | solution.py:25
  32.9 0.0 collective-permute-done.1.later
  32.9 1.3 %collective-permute-start.3 = (bf16[160,1024]{1,0:T(8,128)(2,1)S(1)}, bf16[160,1024]{1,0:T(8,128)(2,1)S(1)}, u32[]{:S(2)}, u32[]{:S(2)}) collective-permute-start(bf16[160,1024]{1,0:T(8,128)(2,1)S(1)} %get-tuple-element.33), channel_id=1, source_target_pairs={{4,0},{8,4},{12,8},{16,12},{20,16},{24,20},{28,24},{5,1},{9,5},{13... | collective-permute-start | bytes 983048 | tf_op jit(solution)/shard_map/ppermute | solution.py:25
  34.2 5.0 %collective-permute-start.2 = (bf16[152,1024]{1,0:T(8,128)(2,1)S(1)}, bf16[152,1024]{1,0:T(8,128)(2,1)S(1)}, u32[]{:S(2)}, u32[]{:S(2)}) collective-permute-start(bf16[152,1024]{1,0:T(8,128)(2,1)S(1)} %get-tuple-element.32), channel_id=1, source_target_pairs={{0,4},{4,8},{8,12},{12,16},{16,20},{20,24},{24,28},{1,5},{5,9},{9,... | collective-permute-start | bytes 933896 | tf_op jit(solution)/shard_map/ppermute | solution.py:25
  39.3 0.0 all-to-all-done
  39.3 11.7 %operator.2 = (bf16[8,256,256]{2,1,0:T(8,128)(2,1)}, f32[8,3,38,8,256]{4,3,2,1,0:T(8,128)}, bf16[8,160,256]{2,1,0:T(8,128)(2,1)}) custom-call(bf16[3,256,2048]{2,1,0:T(8,128)(2,1)} %bitcast.9, bf16[256,2048]{1,0:T(8,128)(2,1)} %cot.7, bf16[152,1024]{1,0:T(8,128)(2,1)S(1)} %collective-permute-done.prev, bf16[160,1024]{1,0:T(8,128)(2,1)S(1)} %collective-permute-done.1.later, ...), custom_call_target="tpu_custom_call" | custom-call | flops 12000000000 | bytes 1000000 | tf_op jit(solution)/shard_map/operator/pallas_call | solution.py:347
  51.0 0.4 collective-permute-done.2.prev
  51.4 0.0 collective-permute-done.3.later
  51.4 11.7 %operator.3 = (bf16[8,256,256]{2,1,0:T(8,128)(2,1)}, f32[8,3,38,8,256]{4,3,2,1,0:T(8,128)}, bf16[8,160,256]{2,1,0:T(8,128)(2,1)}) custom-call(bf16[3,256,2048]{2,1,0:T(8,128)(2,1)} %bitcast.10, bf16[256,2048]{1,0:T(8,128)(2,1)} %cot.7, ...), custom_call_target="tpu_custom_call", output_to_operand_aliasing={{0}: (14, {}), {1}: (15, {}), {2}: (16, {})} | custom-call | flops 12000000000 | bytes 1000000 | tf_op jit(solution)/shard_map/operator/pallas_call | solution.py:347
  63.1 5.7 %all-to-all-start.1 = ((bf16[8,160,256]{2,1,0:T(8,128)(2,1)}), bf16[8,160,256]{2,1,0:T(8,128)(2,1)S(1)}, u32[]{:S(2)}, u32[]{:S(2)}) async-start(bf16[8,160,256]{2,1,0:T(8,128)(2,1)} %get-tuple-element.40), calls=%async_computation.1 | async-start | bytes 1310720 | tf_op jit(solution)/shard_map/all_to_all | solution.py:490
  68.9 9.3 %outputs.1 = (bf16[256,2048]{1,0:T(8,128)(2,1)}, bf16[3,256,2048]{2,1,0:T(8,128)(2,1)}) custom-call(bf16[8,256,256]{2,1,0:T(8,128)(2,1)} %get-tuple-element.41.product, f32[8,3,38,8,256]{4,3,2,1,0:T(8,128)} %get-tuple-element.42.grad, f32[3,7,2048]{2,1,0:T(8,128)} %short.9, bf16[256,256]{1,0:T(8,128)(2,1)} %constant.29.clone.p_out), custom_call_target="tpu_custom_call" | custom-call | flops 8000000000 | bytes 1000000 | tf_op jit(solution)/shard_map/outputs/pallas_call | solution.py:347
  78.2 7.7 %all-to-all-done.1.sums = bf16[8,160,256]{2,1,0:T(8,128)(2,1)S(1)} async-done(((bf16[8,160,256]{2,1,0:T(8,128)(2,1)}), bf16[8,160,256]{2,1,0:T(8,128)(2,1)S(1)}, u32[]{:S(2)}, u32[]{:S(2)}) %all-to-all-start.1) | async-done | bytes 655392 | tf_op jit(solution)/shard_map/all_to_all | solution.py:490
  86.0 1.0 squares.1
  87.0 3.6 %all-to-all-start.2 = ((bf16[32,24,256]{2,1,0:T(8,128)(2,1)}), bf16[32,24,256]{2,1,0:T(8,128)(2,1)S(1)}, u32[]{:S(2)}, u32[]{:S(2)}) async-start(bf16[32,24,256]{2,1,0:T(8,128)(2,1)} %get-tuple-element.49), calls=%async_computation.2 | async-start | bytes 786432 | tf_op jit(solution)/shard_map/all_to_all | solution.py:504
  90.6 0.1 pad_add_fusion.mine
  90.7 13.1 %all-to-all-done.2.gathered = bf16[32,24,256]{2,1,0:T(8,128)(2,1)S(1)} async-done(((bf16[32,24,256]{2,1,0:T(8,128)(2,1)}), bf16[32,24,256]{2,1,0:T(8,128)(2,1)S(1)}, u32[]{:S(2)}, u32[]{:S(2)}) %all-to-all-start.2) | async-done | bytes 393248 | tf_op jit(solution)/shard_map/all_to_all | solution.py:504
  103.8 1.4 %scale.1 = (f32[3,7,2048]{2,1,0:T(8,128)}, f32[16,2048]{1,0:T(8,128)}) custom-call(s32[2]{0:T(128)S(1)} %pad_add_fusion.mine, f32[16,2048]{1,0:T(8,128)S(1)} %get-tuple-element.48.raw, bf16[32,24,256]{2,1,0:T(8,128)(2,1)S(1)} %all-to-all-done.2.gathered), custom_call_target="tpu_custom_call" | custom-call | tf_op jit(solution)/shard_map/scale/pallas_call | solution.py:507
Async XLA Ops:
  3.6 35.6 %all-to-all-start = ((bf16[8,16,2048]{2,1,0:T(8,128)(2,1)}), bf16[8,16,2048]{2,1,0:T(8,128)(2,1)S(1)}, u32[]{:S(2)}, u32[]{:S(2)}) async-start(bf16[8,16,2048]{2,1,0:T(8,128)(2,1)} %get-tuple-element.34), calls=%async_computation | async-start | bytes 1048576 | tf_op jit(solution)/shard_map/all_to_all | solution.py:433
  13.9 19.1 %collective-permute-start.1 = (bf16[160,1024]{1,0:T(8,128)(2,1)S(1)}, bf16[160,1024]{1,0:T(8,128)(2,1)S(1)}, u32[]{:S(2)}, u32[]{:S(2)}) collective-permute-start(bf16[160,1024]{1,0:T(8,128)(2,1)S(1)} %get-tuple-element.31), channel_id=1, source_target_pairs={{4,0},{8,4},{12,8},{16,12},{20,16},{24,20},{28,24},{5,1},{9,5},{13... | collective-permute-start | bytes 983048 | tf_op jit(solution)/shard_map/ppermute | solution.py:25
  15.2 17.8 %collective-permute-start = (bf16[152,1024]{1,0:T(8,128)(2,1)S(1)}, bf16[152,1024]{1,0:T(8,128)(2,1)S(1)}, u32[]{:S(2)}, u32[]{:S(2)}) collective-permute-start(bf16[152,1024]{1,0:T(8,128)(2,1)S(1)} %get-tuple-element.30), channel_id=1, source_target_pairs={{0,4},{4,8},{8,12},{12,16},{16,20},{20,24},{24,28},{1,5},{5,9},{9,... | collective-permute-start | bytes 933896 | tf_op jit(solution)/shard_map/ppermute | solution.py:25
  32.9 18.5 %collective-permute-start.3 = (bf16[160,1024]{1,0:T(8,128)(2,1)S(1)}, bf16[160,1024]{1,0:T(8,128)(2,1)S(1)}, u32[]{:S(2)}, u32[]{:S(2)}) collective-permute-start(bf16[160,1024]{1,0:T(8,128)(2,1)S(1)} %get-tuple-element.33), channel_id=1, source_target_pairs={{4,0},{8,4},{12,8},{16,12},{20,16},{24,20},{28,24},{5,1},{9,5},{13... | collective-permute-start | bytes 983048 | tf_op jit(solution)/shard_map/ppermute | solution.py:25
  34.2 17.2 %collective-permute-start.2 = (bf16[152,1024]{1,0:T(8,128)(2,1)S(1)}, bf16[152,1024]{1,0:T(8,128)(2,1)S(1)}, u32[]{:S(2)}, u32[]{:S(2)}) collective-permute-start(bf16[152,1024]{1,0:T(8,128)(2,1)S(1)} %get-tuple-element.32), channel_id=1, source_target_pairs={{0,4},{4,8},{8,12},{12,16},{16,20},{20,24},{24,28},{1,5},{5,9},{9,... | collective-permute-start | bytes 933896 | tf_op jit(solution)/shard_map/ppermute | solution.py:25
  63.1 22.8 %all-to-all-start.1 = ((bf16[8,160,256]{2,1,0:T(8,128)(2,1)}), bf16[8,160,256]{2,1,0:T(8,128)(2,1)S(1)}, u32[]{:S(2)}, u32[]{:S(2)}) async-start(bf16[8,160,256]{2,1,0:T(8,128)(2,1)} %get-tuple-element.40), calls=%async_computation.1 | async-start | bytes 1310720 | tf_op jit(solution)/shard_map/all_to_all | solution.py:490
  87.0 16.8 %all-to-all-start.2 = ((bf16[32,24,256]{2,1,0:T(8,128)(2,1)}), bf16[32,24,256]{2,1,0:T(8,128)(2,1)S(1)}, u32[]{:S(2)}, u32[]{:S(2)}) async-start(bf16[32,24,256]{2,1,0:T(8,128)(2,1)} %get-tuple-element.49), calls=%async_computation.2 | async-start | bytes 786432 | tf_op jit(solution)/shard_map/all_to_all | solution.py:504

commit v15 on v12

--- a/solution.py
+++ b/solution.py
@@ -15,6 +15,7 @@
 BF16 = jnp.bfloat16
 F32 = jnp.float32
 CHUNKS = 2
+PAIR = 2
 SHORT = 32
 STEP = 64
 
@@ -158,12 +159,10 @@
         sent.wait()
 
 
-def operator_kernel(
-    first, proj, cot, prev, later, short, taps, decay,
-    e_own, e_prev, e_next, e_taps, s_own, s_lags, p_in, *refs,
+def operator_block(
+    proj, cot, prev, later, short, taps, decay,
+    e_own, e_prev, e_next, e_taps, s_own, s_lags, p_in, product, grad, px, feat, cots,
 ):
-    product, grad, sums_out, px, feat, cots, filter_held, short_held, done = refs[-9:]
-    grad = grad.at[0]
     length, width = cot.shape
     span = length // 8
     edge = FK - 1
@@ -190,6 +189,7 @@
             px[i, edge - k] = jnp.where(row8 == 0, pltpu.roll(prev8[i], k, 0), x[edge - k])
     cots[...] = mm(p_in[edge * 8 :, :], cot[...]).reshape(span, 8, width)
 
+    yield
     step = 8
     for i in range(3):
         for lane in lanes:
@@ -221,24 +221,30 @@
     flat = lambda value: value.reshape(length, width)
     mixed = flat(feat[1] * feat[2]).astype(BF16)
     grad_own = flat(cots[...] * feat[0]).astype(BF16)
+    yield
     m_spec = mm(e_own[...], jnp.concatenate([mixed, mixed], axis=0)) + mm(e_prev[...], mixed_edge)
     g_own = mm(e_own[...], jnp.concatenate([grad_own, grad_own], axis=0))
     g_spec = g_own + mm(e_next[...], grad_next)
 
+    yield
     half = k_spec.shape[0] // 2
     parts = lambda value: (value[:half], value[half:])
     (kr, ki), (mr, mi), (gr, gi), (hr, hi) = parts(k_spec), parts(m_spec), parts(g_spec), parts(g_own)
 
-    def back_to(matrix, real, imaginary):
+    def joined(real, imaginary):
         spectrum = jnp.concatenate([real, imaginary], axis=0).astype(BF16)
-        return mm(matrix[...], jnp.concatenate([spectrum, spectrum], axis=0))
-
-    filtered = back_to(s_own, mr * kr - mi * ki, mr * ki + mi * kr)
-    grad_mixed = back_to(s_own, gr * kr + gi * ki, gi * kr - gr * ki)
-    filter_sums = back_to(s_lags, hr * mr + hi * mi, hi * mr - hr * mi) * falloff
+        return jnp.concatenate([spectrum, spectrum], axis=0)
+
+    filtered = joined(mr * kr - mi * ki, mr * ki + mi * kr)
+    grad_mixed = joined(gr * kr + gi * ki, gi * kr - gr * ki)
+    filter_sums = joined(hr * mr + hi * mi, hi * mr - hr * mi)
+    yield
+    filtered, grad_mixed = mm(s_own[...], filtered), mm(s_own[...], grad_mixed)
+    filter_sums = mm(s_lags[...], filter_sums) * falloff
+    yield
 
     own = filtered[:length].reshape(span, 8, width)
-    product[0] = flat(feat[0] * own).astype(BF16)
+    product[...] = flat(feat[0] * own).astype(BF16)
     back = grad_mixed[:length].reshape(span, 8, width)
     grad[0, :span] = cots[...] * own
     grad[1, :span] = back * feat[2]
@@ -262,36 +268,56 @@
             for lag in range(FK):
                 rows[lag].append(jnp.sum(sums[lag], axis=0, keepdims=True))
         short_rows += [jnp.concatenate(row, axis=1) for row in rows]
-
-    step, block = pl.program_id(0), first + pl.program_id(0)
-    ranks, slot, _ = filter_held.shape
-    per, share = filter_sums.shape[0] // ranks, short_held.shape[0]
-    copies = [
-        pltpu.make_async_copy(
-            filter_held, sums_out.at[:, pl.ds(pl.multiple_of(block * slot, slot), slot), :], done.at[0]
-        ),
-        pltpu.make_async_copy(
-            short_held,
-            sums_out.at[pl.ds(block * share, share), pl.ds(sums_out.shape[1] - SHORT, SHORT), :],
-            done.at[1],
-        ),
-    ]
+    yield filter_sums, short_rows
+
+
+def operator_kernel(first, proj, cot, prev, later, short, taps, decay, *refs):
+    constants, (product, grad, sums_out, px, feat, cots, filter_held, short_held, done) = refs[:7], refs[-9:]
+    width = px.shape[-1]
+    pair = []
+    for at in range(PAIR):
+        here = slice(at * width, (at + 1) * width)
+        views = [proj.at[:, :, here], cot.at[:, here], prev.at[:, here], later.at[:, here], short.at[:, :, here]]
+        views += [taps.at[:, here], decay.at[:, here], *constants]
+        pair.append(operator_block(*views, product.at[at], grad.at[at], px.at[at], feat.at[at], cots.at[at]))
+    results = [None] * PAIR
+    for turn in range(6 + PAIR - 1):
+        for at in range(PAIR):
+            if 0 <= turn - at < 6:
+                results[at] = next(pair[at])
+
+    step = pl.program_id(0)
+    _, ranks, slot, width = filter_held.shape
+    per, share = results[0][0].shape[0] // ranks, short_held.shape[1]
+    copies = []
+    for at in range(PAIR):
+        block = first + PAIR * step + at
+        rows = pl.ds(pl.multiple_of(block * slot, slot), slot)
+        few = pl.ds(sums_out.shape[1] - SHORT, SHORT)
+        copies += [
+            pltpu.make_async_copy(filter_held.at[at], sums_out.at[:, rows, :], done.at[2 * at]),
+            pltpu.make_async_copy(
+                short_held.at[at], sums_out.at[pl.ds(block * share, share), few, :], done.at[2 * at + 1]
+            ),
+        ]
 
     @pl.when(step > 0)
     def _():
         for copy in copies:
             copy.wait()
 
-    by_rank = filter_sums.reshape(ranks, per, width) if per % 8 == 0 else jnp.stack(
-        [filter_sums[rank * per : rank * per + per] for rank in range(ranks)]
-    )
-    if slot > per:
-        by_rank = jnp.concatenate([by_rank, jnp.zeros((ranks, slot - per, width), F32)], axis=1)
-    filter_held[...] = by_rank.astype(BF16)
-    sums = jnp.concatenate(short_rows + [jnp.zeros((SHORT - len(short_rows), width), F32)], axis=0)
-    for rank in range(share):
-        held = pltpu.roll(sums, width - rank * (width // share), 1) if rank else sums
-        short_held[rank] = held.astype(BF16)
+    for at, (filter_sums, short_rows) in enumerate(results):
+        if per % 8 == 0:
+            by_rank = filter_sums.reshape(ranks, per, width)
+        else:
+            by_rank = jnp.stack([filter_sums[rank * per : rank * per + per] for rank in range(ranks)])
+        if slot > per:
+            by_rank = jnp.concatenate([by_rank, jnp.zeros((ranks, slot - per, width), F32)], axis=1)
+        filter_held[at] = by_rank.astype(BF16)
+        sums = jnp.concatenate(short_rows + [jnp.zeros((SHORT - len(short_rows), width), F32)], axis=0)
+        for rank in range(share):
+            held = pltpu.roll(sums, width - rank * (width // share), 1) if rank else sums
+            short_held[at, rank] = held.astype(BF16)
     for copy in copies:
         copy.start()
 
@@ -330,9 +356,9 @@
     return pl.BlockSpec(tuple(rows) + (width,), lambda c: lead + (first + c,))
 
 
-def one_of(array, first=0):
+def one_of(array, first=0, some=1):
     tail = (0,) * (len(array.shape) - 1)
-    return pl.BlockSpec((1,) + tuple(array.shape[1:]), lambda c: (first + c,) + tail)
+    return pl.BlockSpec((some,) + tuple(array.shape[1:]), lambda c: (first + c,) + tail)
 
 
 IN_VMEM = pl.BlockSpec(memory_space=pltpu.VMEM)
@@ -397,7 +423,7 @@
     ranks, groups = lax.axis_size("seq"), lax.axis_size("ch")
     rows = filter_taps.shape[0]
     count = rows * ranks
-    width = min(256, channels // CHUNKS)
+    width = min(256, channels // CHUNKS // PAIR)
     share = channels // ranks
     slot = -(-rows // 16) * 16
     size, span = 2 * length, length // 8
@@ -450,29 +476,29 @@
     constants = [(jnp.asarray(constant), whole(constant)) for constant in constants]
     held = ()
     for k in range(CHUNKS):
-        first = k * blocks
+        first, wide = k * blocks // PAIR, PAIR * width
         results = [
             pltpu.HBM((CHUNKS * blocks, length, width), BF16),
             pltpu.HBM((CHUNKS * blocks, 3, span + FK - 1, 8, width), F32),
         ]
         held = call(
-            functools.partial(operator_kernel, first), "operator",
+            functools.partial(operator_kernel, k * blocks), "operator",
             [
-                (proj, columns((3, length), width, first)), (cot, columns((length,), width, first)),
-                (prev[k], columns((152,), width)), (later[k], columns((160,), width)),
-                (short, columns((3, FK), width, first)), (taps, columns((count,), width, first)),
-                (decay, columns((1,), width, first)),
+                (proj, columns((3, length), wide, first)), (cot, columns((length,), wide, first)),
+                (prev[k], columns((152,), wide)), (later[k], columns((160,), wide)),
+                (short, columns((3, FK), wide, first)), (taps, columns((count,), wide, first)),
+                (decay, columns((1,), wide, first)),
             ] + constants,
-            [(result, one_of(result, first)) for result in results]
+            [(result, one_of(result, first, PAIR)) for result in results]
             + [(pltpu.HBM((ranks, CHUNKS * blocks * slot + SHORT, width), BF16), FAR)],
             cost=12,
             held=held,
             free=(2, 3, 5),
-            grid=(blocks,),
+            grid=(blocks // PAIR,),
             scratch_shapes=[
-                vmem(F32, 3, span + FK - 1, 8, width), vmem(F32, 3, span, 8, width), vmem(F32, span, 8, width),
-                vmem(BF16, ranks, slot, width), vmem(BF16, ranks * width // channels, SHORT, width),
-                pltpu.SemaphoreType.DMA((2,)),
+                vmem(F32, PAIR, 3, span + FK - 1, 8, width), vmem(F32, PAIR, 3, span, 8, width),
+                vmem(F32, PAIR, span, 8, width), vmem(BF16, PAIR, ranks, slot, width),
+                vmem(BF16, PAIR, ranks * width // channels, SHORT, width), pltpu.SemaphoreType.DMA((2 * PAIR,)),
             ],
         )
     product, grad, sums = held

time: 101 us -> 100 us (0.990)
  Pallas kernels: 41.1 us -> 39.5 us
    pallas_call x5, Pallas kernels: 38.7 us -> 37.2 us  [call(): pl.pallas_call(kernel, in_specs=[spec for _, spec in operands] + [FAR] *...]
  transfers between devices with their start and end apart: 7 -> 7, of which waited for: 4 -> 4; matrix products, arithmetic and copies ran while one was open for 0% -> 0% of each run, Pallas kernels for 24% -> 23%
where the time goes in v15:
time: 100 us; the launch traced here: 99.8 us
  Pallas kernels  39.5 us (40%)
  waiting for transfers between devices  30 us (30%)
  starting transfers between devices  29.5 us (30%)
    pallas_call x5, Pallas kernels, call(): pl.pallas_call(kernel, in_specs=[spec for _, spec in operands] + [FAR] *...  37.2 us
    ppermute x4, starting transfers between devices, from_behind(): return lax.ppermute(value, axis, pairs)  13.1 us
    all_to_all x1, waiting for transfers between devices, shards(): gathered = lax.all_to_all(payload, ('seq', 'ch'), 0, 0)  13.1 us
    ppermute x4, waiting for transfers between devices, from_behind(): return lax.ppermute(value, axis, pairs)  8.75 us
    all_to_all x1, waiting for transfers between devices, shards(): lax.all_to_all(sums, 'seq', 0, 0)  8.14 us
    all_to_all x1, starting transfers between devices, shards(): lax.all_to_all(sums, 'seq', 0, 0)  6.5 us
    all_to_all x1, starting transfers between devices, shards(): taps = lax.all_to_all(spread[0], 'seq', 0, 0).reshape(count, channels)  6.21 us
    all_to_all x1, starting transfers between devices, shards(): gathered = lax.all_to_all(payload, ('seq', 'ch'), 0, 0)  3.65 us
  transfers between devices with their start and end apart: 7, of which 4 were waited for; matrix products, arithmetic and copies ran while one was open for 0% of the time, Pallas kernels for 23%

profile of v15, /device:TPU:0, one launch (start us, length us, event | category | flops | bytes accessed | tf_op | source)
XLA Modules:
  0.0 99.8 jit_solution(4538429240166962665)
XLA Ops:
  0.6 3.0 %edges.3 = (bf16[152,1024]{1,0:T(8,128)(2,1)S(1)}, bf16[160,1024]{1,0:T(8,128)(2,1)S(1)}, bf16[8,16,2048]{2,1,0:T(8,128)(2,1)}) custom-call(bf16[3,256,2048]{2,1,0:T(8,128)(2,1)} %bitcast.7, bf16[256,2048]{1,0:T(8,128)(2,1)} %cot.7, f32[3,7,2048]{2,1,0:T(8,128)} %short.9, f32[16,2048]{1,0:T(8,128)} %refs_0_.3), custom_call_target="tpu_custom_call" | custom-call | flops 1000000000 | bytes 1000000 | tf_op jit(solution)/shard_map/edges/pallas_call | solution.py:373
  3.6 1.3 %collective-permute-start.1 = (bf16[160,1024]{1,0:T(8,128)(2,1)S(1)}, bf16[160,1024]{1,0:T(8,128)(2,1)S(1)}, u32[]{:S(2)}, u32[]{:S(2)}) collective-permute-start(bf16[160,1024]{1,0:T(8,128)(2,1)S(1)} %get-tuple-element.31), channel_id=1, source_target_pairs={{4,0},{8,4},{12,8},{16,12},{20,16},{24,20},{28,24},{5,1},{9,5},{13... | collective-permute-start | bytes 983048 | tf_op jit(solution)/shard_map/ppermute | solution.py:26
  4.9 5.5 %collective-permute-start = (bf16[152,1024]{1,0:T(8,128)(2,1)S(1)}, bf16[152,1024]{1,0:T(8,128)(2,1)S(1)}, u32[]{:S(2)}, u32[]{:S(2)}) collective-permute-start(bf16[152,1024]{1,0:T(8,128)(2,1)S(1)} %get-tuple-element.30), channel_id=1, source_target_pairs={{0,4},{4,8},{8,12},{12,16},{16,20},{20,24},{24,28},{1,5},{5,9},{9,... | collective-permute-start | bytes 933896 | tf_op jit(solution)/shard_map/ppermute | solution.py:26
  10.5 6.2 %all-to-all-start = ((bf16[8,16,2048]{2,1,0:T(8,128)(2,1)}), bf16[8,16,2048]{2,1,0:T(8,128)(2,1)S(1)}, u32[]{:S(2)}, u32[]{:S(2)}) async-start(bf16[8,16,2048]{2,1,0:T(8,128)(2,1)} %get-tuple-element.34), calls=%async_computation | async-start | bytes 1048576 | tf_op jit(solution)/shard_map/all_to_all | solution.py:459
  16.7 2.9 %edges.2 = (bf16[152,1024]{1,0:T(8,128)(2,1)S(1)}, bf16[160,1024]{1,0:T(8,128)(2,1)S(1)}) custom-call(bf16[3,256,2048]{2,1,0:T(8,128)(2,1)} %bitcast.8, bf16[256,2048]{1,0:T(8,128)(2,1)} %cot.7, f32[3,7,2048]{2,1,0:T(8,128)} %short.9), custom_call_target="tpu_custom_call" | custom-call | flops 10000000000 | bytes 1000000 | tf_op jit(solution)/shard_map/edges/pallas_call | solution.py:373
  19.6 7.0 %collective-permute-done.prev = bf16[152,1024]{1,0:T(8,128)(2,1)S(1)} collective-permute-done((bf16[152,1024]{1,0:T(8,128)(2,1)S(1)}, bf16[152,1024]{1,0:T(8,128)(2,1)S(1)}, u32[]{:S(2)}, u32[]{:S(2)}) %collective-permute-start) | collective-permute-done | bytes 311328 | tf_op jit(solution)/shard_map/ppermute | solution.py:26
  26.6 0.0 collective-permute-done.1.later
  26.7 1.3 %collective-permute-start.3 = (bf16[160,1024]{1,0:T(8,128)(2,1)S(1)}, bf16[160,1024]{1,0:T(8,128)(2,1)S(1)}, u32[]{:S(2)}, u32[]{:S(2)}) collective-permute-start(bf16[160,1024]{1,0:T(8,128)(2,1)S(1)} %get-tuple-element.33), channel_id=1, source_target_pairs={{4,0},{8,4},{12,8},{16,12},{20,16},{24,20},{28,24},{5,1},{9,5},{13... | collective-permute-start | bytes 983048 | tf_op jit(solution)/shard_map/ppermute | solution.py:26
  27.9 5.0 %collective-permute-start.2 = (bf16[152,1024]{1,0:T(8,128)(2,1)S(1)}, bf16[152,1024]{1,0:T(8,128)(2,1)S(1)}, u32[]{:S(2)}, u32[]{:S(2)}) collective-permute-start(bf16[152,1024]{1,0:T(8,128)(2,1)S(1)} %get-tuple-element.32), channel_id=1, source_target_pairs={{0,4},{4,8},{8,12},{12,16},{16,20},{20,24},{24,28},{1,5},{5,9},{9,... | collective-permute-start | bytes 933896 | tf_op jit(solution)/shard_map/ppermute | solution.py:26
  33.0 0.0 all-to-all-done
  33.0 10.9 %operator.2 = (bf16[8,256,256]{2,1,0:T(8,128)(2,1)}, f32[8,3,38,8,256]{4,3,2,1,0:T(8,128)}, bf16[8,160,256]{2,1,0:T(8,128)(2,1)}) custom-call(bf16[3,256,2048]{2,1,0:T(8,128)(2,1)} %bitcast.9, bf16[256,2048]{1,0:T(8,128)(2,1)} %cot.7, bf16[152,1024]{1,0:T(8,128)(2,1)S(1)} %collective-permute-done.prev, bf16[160,1024]{1,0:T(8,128)(2,1)S(1)} %collective-permute-done.1.later, ...), custom_call_target="tpu_custom_call" | custom-call | flops 12000000000 | bytes 1000000 | tf_op jit(solution)/shard_map/operator/pallas_call | solution.py:373
  43.9 1.7 %collective-permute-done.2.prev = bf16[152,1024]{1,0:T(8,128)(2,1)S(1)} collective-permute-done((bf16[152,1024]{1,0:T(8,128)(2,1)S(1)}, bf16[152,1024]{1,0:T(8,128)(2,1)S(1)}, u32[]{:S(2)}, u32[]{:S(2)}) %collective-permute-start.2) | collective-permute-done | bytes 311328 | tf_op jit(solution)/shard_map/ppermute | solution.py:26
  45.6 0.0 collective-permute-done.3.later
  45.6 11.0 %operator.3 = (bf16[8,256,256]{2,1,0:T(8,128)(2,1)}, f32[8,3,38,8,256]{4,3,2,1,0:T(8,128)}, bf16[8,160,256]{2,1,0:T(8,128)(2,1)}) custom-call(bf16[3,256,2048]{2,1,0:T(8,128)(2,1)} %bitcast.10, bf16[256,2048]{1,0:T(8,128)(2,1)} %cot.7, ...), custom_call_target="tpu_custom_call", output_to_operand_aliasing={{0}: (14, {}), {1}: (15, {}), {2}: (16, {})} | custom-call | flops 12000000000 | bytes 1000000 | tf_op jit(solution)/shard_map/operator/pallas_call | solution.py:373
  56.6 6.5 %all-to-all-start.1 = ((bf16[8,160,256]{2,1,0:T(8,128)(2,1)}), bf16[8,160,256]{2,1,0:T(8,128)(2,1)S(1)}, u32[]{:S(2)}, u32[]{:S(2)}) async-start(bf16[8,160,256]{2,1,0:T(8,128)(2,1)} %get-tuple-element.40), calls=%async_computation.1 | async-start | bytes 1310720 | tf_op jit(solution)/shard_map/all_to_all | solution.py:516
  63.1 9.3 %outputs.1 = (bf16[256,2048]{1,0:T(8,128)(2,1)}, bf16[3,256,2048]{2,1,0:T(8,128)(2,1)}) custom-call(bf16[8,256,256]{2,1,0:T(8,128)(2,1)} %get-tuple-element.41.product, f32[8,3,38,8,256]{4,3,2,1,0:T(8,128)} %get-tuple-element.42.grad, f32[3,7,2048]{2,1,0:T(8,128)} %short.9, bf16[256,256]{1,0:T(8,128)(2,1)} %constant.29.clone.p_out), custom_call_target="tpu_custom_call" | custom-call | flops 8000000000 | bytes 1000000 | tf_op jit(solution)/shard_map/outputs/pallas_call | solution.py:373
  72.5 8.1 %all-to-all-done.1.sums = bf16[8,160,256]{2,1,0:T(8,128)(2,1)S(1)} async-done(((bf16[8,160,256]{2,1,0:T(8,128)(2,1)}), bf16[8,160,256]{2,1,0:T(8,128)(2,1)S(1)}, u32[]{:S(2)}, u32[]{:S(2)}) %all-to-all-start.1) | async-done | bytes 655392 | tf_op jit(solution)/shard_map/all_to_all | solution.py:516
  80.6 1.0 %squares.1 = (f32[16,2048]{1,0:T(8,128)S(1)}, bf16[32,24,256]{2,1,0:T(8,128)(2,1)}) custom-call(bf16[8,160,256]{2,1,0:T(8,128)(2,1)S(1)} %all-to-all-done.1.sums), custom_call_target="tpu_custom_call" | custom-call | tf_op jit(solution)/shard_map/squares/pallas_call | solution.py:519
  81.6 3.6 %all-to-all-start.2 = ((bf16[32,24,256]{2,1,0:T(8,128)(2,1)}), bf16[32,24,256]{2,1,0:T(8,128)(2,1)S(1)}, u32[]{:S(2)}, u32[]{:S(2)}) async-start(bf16[32,24,256]{2,1,0:T(8,128)(2,1)} %get-tuple-element.49), calls=%async_computation.2 | async-start | bytes 786432 | tf_op jit(solution)/shard_map/all_to_all | solution.py:530
  85.3 0.1 pad_add_fusion.mine
  85.3 13.1 %all-to-all-done.2.gathered = bf16[32,24,256]{2,1,0:T(8,128)(2,1)S(1)} async-done(((bf16[32,24,256]{2,1,0:T(8,128)(2,1)}), bf16[32,24,256]{2,1,0:T(8,128)(2,1)S(1)}, u32[]{:S(2)}, u32[]{:S(2)}) %all-to-all-start.2) | async-done | bytes 393248 | tf_op jit(solution)/shard_map/all_to_all | solution.py:530
  98.4 1.4 %scale.1 = (f32[3,7,2048]{2,1,0:T(8,128)}, f32[16,2048]{1,0:T(8,128)}) custom-call(s32[2]{0:T(128)S(1)} %pad_add_fusion.mine, f32[16,2048]{1,0:T(8,128)S(1)} %get-tuple-element.48.raw, bf16[32,24,256]{2,1,0:T(8,128)(2,1)S(1)} %all-to-all-done.2.gathered), custom_call_target="tpu_custom_call" | custom-call | tf_op jit(solution)/shard_map/scale/pallas_call | solution.py:533
Async XLA Ops:
  3.6 23.0 %collective-permute-start.1 = (bf16[160,1024]{1,0:T(8,128)(2,1)S(1)}, bf16[160,1024]{1,0:T(8,128)(2,1)S(1)}, u32[]{:S(2)}, u32[]{:S(2)}) collective-permute-start(bf16[160,1024]{1,0:T(8,128)(2,1)S(1)} %get-tuple-element.31), channel_id=1, source_target_pairs={{4,0},{8,4},{12,8},{16,12},{20,16},{24,20},{28,24},{5,1},{9,5},{13... | collective-permute-start | bytes 983048 | tf_op jit(solution)/shard_map/ppermute | solution.py:26
  4.9 21.7 %collective-permute-start = (bf16[152,1024]{1,0:T(8,128)(2,1)S(1)}, bf16[152,1024]{1,0:T(8,128)(2,1)S(1)}, u32[]{:S(2)}, u32[]{:S(2)}) collective-permute-start(bf16[152,1024]{1,0:T(8,128)(2,1)S(1)} %get-tuple-element.30), channel_id=1, source_target_pairs={{0,4},{4,8},{8,12},{12,16},{16,20},{20,24},{24,28},{1,5},{5,9},{9,... | collective-permute-start | bytes 933896 | tf_op jit(solution)/shard_map/ppermute | solution.py:26
  10.5 22.5 %all-to-all-start = ((bf16[8,16,2048]{2,1,0:T(8,128)(2,1)}), bf16[8,16,2048]{2,1,0:T(8,128)(2,1)S(1)}, u32[]{:S(2)}, u32[]{:S(2)}) async-start(bf16[8,16,2048]{2,1,0:T(8,128)(2,1)} %get-tuple-element.34), calls=%async_computation | async-start | bytes 1048576 | tf_op jit(solution)/shard_map/all_to_all | solution.py:459
  26.7 19.0 %collective-permute-start.3 = (bf16[160,1024]{1,0:T(8,128)(2,1)S(1)}, bf16[160,1024]{1,0:T(8,128)(2,1)S(1)}, u32[]{:S(2)}, u32[]{:S(2)}) collective-permute-start(bf16[160,1024]{1,0:T(8,128)(2,1)S(1)} %get-tuple-element.33), channel_id=1, source_target_pairs={{4,0},{8,4},{12,8},{16,12},{20,16},{24,20},{28,24},{5,1},{9,5},{13... | collective-permute-start | bytes 983048 | tf_op jit(solution)/shard_map/ppermute | solution.py:26
  27.9 17.7 %collective-permute-start.2 = (bf16[152,1024]{1,0:T(8,128)(2,1)S(1)}, bf16[152,1024]{1,0:T(8,128)(2,1)S(1)}, u32[]{:S(2)}, u32[]{:S(2)}) collective-permute-start(bf16[152,1024]{1,0:T(8,128)(2,1)S(1)} %get-tuple-element.32), channel_id=1, source_target_pairs={{0,4},{4,8},{8,12},{12,16},{16,20},{20,24},{24,28},{1,5},{5,9},{9,... | collective-permute-start | bytes 933896 | tf_op jit(solution)/shard_map/ppermute | solution.py:26
  56.6 24.0 %all-to-all-start.1 = ((bf16[8,160,256]{2,1,0:T(8,128)(2,1)}), bf16[8,160,256]{2,1,0:T(8,128)(2,1)S(1)}, u32[]{:S(2)}, u32[]{:S(2)}) async-start(bf16[8,160,256]{2,1,0:T(8,128)(2,1)} %get-tuple-element.40), calls=%async_computation.1 | async-start | bytes 1310720 | tf_op jit(solution)/shard_map/all_to_all | solution.py:516
  81.6 16.8 %all-to-all-start.2 = ((bf16[32,24,256]{2,1,0:T(8,128)(2,1)}), bf16[32,24,256]{2,1,0:T(8,128)(2,1)S(1)}, u32[]{:S(2)}, u32[]{:S(2)}) async-start(bf16[32,24,256]{2,1,0:T(8,128)(2,1)} %get-tuple-element.49), calls=%async_computation.2 | async-start | bytes 786432 | tf_op jit(solution)/shard_map/all_to_all | solution.py:530

commit v16 on v15

--- a/solution.py
+++ b/solution.py
@@ -458,9 +458,9 @@
         if k == 0:
             taps = lax.all_to_all(spread[0], "seq", 0, 0).reshape(count, channels)
         else:
-            forward, backward, prev[-1], later[-1] = lax.optimization_barrier((forward, backward, prev[-1], later[-1]))
+            backward, prev[-1], later[-1] = lax.optimization_barrier((backward, prev[-1], later[-1]))
+        later.append(from_behind(backward, "seq", -1))
         prev.append(from_behind(forward, "seq", 1))
-        later.append(from_behind(backward, "seq", -1))
 
     high, low = analysis(own, size)
     k_high, k_low = analysis(np.arange(count), size)

time: 100 us -> 97 us (0.970)
  waiting for transfers between devices: 30 us -> 24.1 us
  starting transfers between devices: 29.5 us -> 32 us
    ppermute x4, waiting for transfers between devices: 8.75 us -> 3.86 us  [from_behind(): return lax.ppermute(value, axis, pairs)]
    all_to_all x1, waiting for transfers between devices: 8.14 us -> 4.38 us  [shards(): lax.all_to_all(sums, 'seq', 0, 0)]
    all_to_all x1, starting transfers between devices: 6.5 us -> 10 us  [shards(): lax.all_to_all(sums, 'seq', 0, 0)]
    all_to_all x1, waiting for transfers between devices: 0.01 us -> 2.72 us  [shards(): taps = lax.all_to_all(spread[0], 'seq', 0, 0).reshape(count, channels)]
    ppermute x4, starting transfers between devices: 13.1 us -> 12 us  [from_behind(): return lax.ppermute(value, axis, pairs)]
  transfers between devices with their start and end apart: 7 -> 7, of which waited for: 4 -> 5; matrix products, arithmetic and copies ran while one was open for 0% -> 0% of each run, Pallas kernels for 23% -> 24%
where the time goes in v16:
time: 97 us; the launch traced here: 96.4 us
  Pallas kernels  39.5 us (41%)
  starting transfers between devices  32 us (33%)
  waiting for transfers between devices  24.1 us (25%)
    pallas_call x5, Pallas kernels, call(): pl.pallas_call(kernel, in_specs=[spec for _, spec in operands] + [FAR] *...  37.1 us
    all_to_all x1, waiting for transfers between devices, shards(): gathered = lax.all_to_all(payload, ('seq', 'ch'), 0, 0)  13.1 us
    ppermute x4, starting transfers between devices, from_behind(): return lax.ppermute(value, axis, pairs)  12 us
    all_to_all x1, starting transfers between devices, shards(): lax.all_to_all(sums, 'seq', 0, 0)  10 us
    all_to_all x1, starting transfers between devices, shards(): taps = lax.all_to_all(spread[0], 'seq', 0, 0).reshape(count, channels)  6.21 us
    all_to_all x1, waiting for transfers between devices, shards(): lax.all_to_all(sums, 'seq', 0, 0)  4.38 us
    ppermute x4, waiting for transfers between devices, from_behind(): return lax.ppermute(value, axis, pairs)  3.86 us
    all_to_all x1, starting transfers between devices, shards(): gathered = lax.all_to_all(payload, ('seq', 'ch'), 0, 0)  3.69 us
  transfers between devices with their start and end apart: 7, of which 5 were waited for; matrix products, arithmetic and copies ran while one was open for 0% of the time, Pallas kernels for 24%

profile of v16, /device:TPU:0, one launch (start us, length us, event | category | flops | bytes accessed | tf_op | source)
XLA Modules:
  0.0 96.4 jit_solution(8169051612841246206)
XLA Ops:
  0.6 3.0 %edges.3 = (bf16[152,1024]{1,0:T(8,128)(2,1)S(1)}, bf16[160,1024]{1,0:T(8,128)(2,1)S(1)}, bf16[8,16,2048]{2,1,0:T(8,128)(2,1)}) custom-call(bf16[3,256,2048]{2,1,0:T(8,128)(2,1)} %bitcast.7, bf16[256,2048]{1,0:T(8,128)(2,1)} %cot.7, f32[3,7,2048]{2,1,0:T(8,128)} %short.9, f32[16,2048]{1,0:T(8,128)} %refs_0_.3), custom_call_target="tpu_custom_call" | custom-call | flops 1000000000 | bytes 1000000 | tf_op jit(solution)/shard_map/edges/pallas_call | solution.py:373
  3.6 1.3 %collective-permute-start.2 = (bf16[160,1024]{1,0:T(8,128)(2,1)S(1)}, bf16[160,1024]{1,0:T(8,128)(2,1)S(1)}, u32[]{:S(2)}, u32[]{:S(2)}) collective-permute-start(bf16[160,1024]{1,0:T(8,128)(2,1)S(1)} %get-tuple-element.30), channel_id=1, source_target_pairs={{4,0},{8,4},{12,8},{16,12},{20,16},{24,20},{28,24},{5,1},{9,5},{13... | collective-permute-start | bytes 983048 | tf_op jit(solution)/shard_map/ppermute | solution.py:26
  4.9 5.5 %collective-permute-start.1 = (bf16[152,1024]{1,0:T(8,128)(2,1)S(1)}, bf16[152,1024]{1,0:T(8,128)(2,1)S(1)}, u32[]{:S(2)}, u32[]{:S(2)}) collective-permute-start(bf16[152,1024]{1,0:T(8,128)(2,1)S(1)} %get-tuple-element.29), channel_id=1, source_target_pairs={{0,4},{4,8},{8,12},{12,16},{16,20},{20,24},{24,28},{1,5},{5,9},{9,... | collective-permute-start | bytes 933896 | tf_op jit(solution)/shard_map/ppermute | solution.py:26
  10.5 6.2 %all-to-all-start = ((bf16[8,16,2048]{2,1,0:T(8,128)(2,1)}), bf16[8,16,2048]{2,1,0:T(8,128)(2,1)S(1)}, u32[]{:S(2)}, u32[]{:S(2)}) async-start(bf16[8,16,2048]{2,1,0:T(8,128)(2,1)} %get-tuple-element.32), calls=%async_computation | async-start | bytes 1048576 | tf_op jit(solution)/shard_map/all_to_all | solution.py:459
  16.7 2.9 %edges.2 = (bf16[152,1024]{1,0:T(8,128)(2,1)S(1)}, bf16[160,1024]{1,0:T(8,128)(2,1)S(1)}) custom-call(bf16[3,256,2048]{2,1,0:T(8,128)(2,1)} %bitcast.8, bf16[256,2048]{1,0:T(8,128)(2,1)} %cot.7, f32[3,7,2048]{2,1,0:T(8,128)} %short.9), custom_call_target="tpu_custom_call" | custom-call | flops 10000000000 | bytes 1000000 | tf_op jit(solution)/shard_map/edges/pallas_call | solution.py:373
  19.6 3.9 %collective-permute-start = (bf16[152,1024]{1,0:T(8,128)(2,1)S(1)}, bf16[152,1024]{1,0:T(8,128)(2,1)S(1)}, u32[]{:S(2)}, u32[]{:S(2)}) collective-permute-start(bf16[152,1024]{1,0:T(8,128)(2,1)S(1)} %get-tuple-element.27), channel_id=1, source_target_pairs={{0,4},{4,8},{8,12},{12,16},{16,20},{20,24},{24,28},{1,5},{5,9},{9,... | collective-permute-start | bytes 933896 | tf_op jit(solution)/shard_map/ppermute | solution.py:26
  23.6 3.1 %collective-permute-done.1.prev = bf16[152,1024]{1,0:T(8,128)(2,1)S(1)} collective-permute-done((bf16[152,1024]{1,0:T(8,128)(2,1)S(1)}, bf16[152,1024]{1,0:T(8,128)(2,1)S(1)}, u32[]{:S(2)}, u32[]{:S(2)}) %collective-permute-start.1) | collective-permute-done | bytes 311328 | tf_op jit(solution)/shard_map/ppermute | solution.py:26
  26.6 0.0 collective-permute-done.2.later
  26.7 1.3 %collective-permute-start.3 = (bf16[160,1024]{1,0:T(8,128)(2,1)S(1)}, bf16[160,1024]{1,0:T(8,128)(2,1)S(1)}, u32[]{:S(2)}, u32[]{:S(2)}) collective-permute-start(bf16[160,1024]{1,0:T(8,128)(2,1)S(1)} %get-tuple-element.31), channel_id=1, source_target_pairs={{4,0},{8,4},{12,8},{16,12},{20,16},{24,20},{28,24},{5,1},{9,5},{13... | collective-permute-start | bytes 983048 | tf_op jit(solution)/shard_map/ppermute | solution.py:26
  27.9 2.7 %all-to-all-done = bf16[8,16,2048]{2,1,0:T(8,128)(2,1)S(1)} async-done(((bf16[8,16,2048]{2,1,0:T(8,128)(2,1)}), bf16[8,16,2048]{2,1,0:T(8,128)(2,1)S(1)}, u32[]{:S(2)}, u32[]{:S(2)}) %all-to-all-start) | async-done | bytes 524320 | tf_op jit(solution)/shard_map/all_to_all | solution.py:459
  30.7 10.9 %operator.2 = (bf16[8,256,256]{2,1,0:T(8,128)(2,1)}, f32[8,3,38,8,256]{4,3,2,1,0:T(8,128)}, bf16[8,160,256]{2,1,0:T(8,128)(2,1)}) custom-call(bf16[3,256,2048]{2,1,0:T(8,128)(2,1)} %bitcast.9, bf16[256,2048]{1,0:T(8,128)(2,1)} %cot.7, bf16[152,1024]{1,0:T(8,128)(2,1)S(1)} %collective-permute-done.1.prev, bf16[160,1024]{1,0:T(8,128)(2,1)S(1)} %collective-permute-done.2.later, ...), custom_call_target="tpu_custom_call" | custom-call | flops 12000000000 | bytes 1000000 | tf_op jit(solution)/shard_map/operator/pallas_call | solution.py:373
  41.6 0.8 collective-permute-done.prev
  42.4 0.0 collective-permute-done.3.later
  42.4 11.0 %operator.3 = (bf16[8,256,256]{2,1,0:T(8,128)(2,1)}, f32[8,3,38,8,256]{4,3,2,1,0:T(8,128)}, bf16[8,160,256]{2,1,0:T(8,128)(2,1)}) custom-call(bf16[3,256,2048]{2,1,0:T(8,128)(2,1)} %bitcast.10, bf16[256,2048]{1,0:T(8,128)(2,1)} %cot.7, ...), custom_call_target="tpu_custom_call", output_to_operand_aliasing={{0}: (14, {}), {1}: (15, {}), {2}: (16, {})} | custom-call | flops 12000000000 | bytes 1000000 | tf_op jit(solution)/shard_map/operator/pallas_call | solution.py:373
  53.3 10.0 %all-to-all-start.1 = ((bf16[8,160,256]{2,1,0:T(8,128)(2,1)}), bf16[8,160,256]{2,1,0:T(8,128)(2,1)S(1)}, u32[]{:S(2)}, u32[]{:S(2)}) async-start(bf16[8,160,256]{2,1,0:T(8,128)(2,1)} %get-tuple-element.38), calls=%async_computation.1 | async-start | bytes 1310720 | tf_op jit(solution)/shard_map/all_to_all | solution.py:516
  63.4 9.3 %outputs.1 = (bf16[256,2048]{1,0:T(8,128)(2,1)}, bf16[3,256,2048]{2,1,0:T(8,128)(2,1)}) custom-call(bf16[8,256,256]{2,1,0:T(8,128)(2,1)} %get-tuple-element.39.product, f32[8,3,38,8,256]{4,3,2,1,0:T(8,128)} %get-tuple-element.40.grad, f32[3,7,2048]{2,1,0:T(8,128)} %short.9, bf16[256,256]{1,0:T(8,128)(2,1)} %constant.29.clone.p_out), custom_call_target="tpu_custom_call" | custom-call | flops 8000000000 | bytes 1000000 | tf_op jit(solution)/shard_map/outputs/pallas_call | solution.py:373
  72.7 4.4 %all-to-all-done.1.sums = bf16[8,160,256]{2,1,0:T(8,128)(2,1)S(1)} async-done(((bf16[8,160,256]{2,1,0:T(8,128)(2,1)}), bf16[8,160,256]{2,1,0:T(8,128)(2,1)S(1)}, u32[]{:S(2)}, u32[]{:S(2)}) %all-to-all-start.1) | async-done | bytes 655392 | tf_op jit(solution)/shard_map/all_to_all | solution.py:516
  77.1 1.0 %squares.1 = (f32[16,2048]{1,0:T(8,128)S(1)}, bf16[32,24,256]{2,1,0:T(8,128)(2,1)}) custom-call(bf16[8,160,256]{2,1,0:T(8,128)(2,1)S(1)} %all-to-all-done.1.sums), custom_call_target="tpu_custom_call" | custom-call | tf_op jit(solution)/shard_map/squares/pallas_call | solution.py:519
  78.1 3.7 %all-to-all-start.2 = ((bf16[32,24,256]{2,1,0:T(8,128)(2,1)}), bf16[32,24,256]{2,1,0:T(8,128)(2,1)S(1)}, u32[]{:S(2)}, u32[]{:S(2)}) async-start(bf16[32,24,256]{2,1,0:T(8,128)(2,1)} %get-tuple-element.47), calls=%async_computation.2 | async-start | bytes 786432 | tf_op jit(solution)/shard_map/all_to_all | solution.py:530
  81.8 0.1 pad_add_fusion.mine
  81.9 13.1 %all-to-all-done.2.gathered = bf16[32,24,256]{2,1,0:T(8,128)(2,1)S(1)} async-done(((bf16[32,24,256]{2,1,0:T(8,128)(2,1)}), bf16[32,24,256]{2,1,0:T(8,128)(2,1)S(1)}, u32[]{:S(2)}, u32[]{:S(2)}) %all-to-all-start.2) | async-done | bytes 393248 | tf_op jit(solution)/shard_map/all_to_all | solution.py:530
  95.0 1.4 %scale.1 = (f32[3,7,2048]{2,1,0:T(8,128)}, f32[16,2048]{1,0:T(8,128)}) custom-call(s32[2]{0:T(128)S(1)} %pad_add_fusion.mine, f32[16,2048]{1,0:T(8,128)S(1)} %get-tuple-element.46.raw, bf16[32,24,256]{2,1,0:T(8,128)(2,1)S(1)} %all-to-all-done.2.gathered), custom_call_target="tpu_custom_call" | custom-call | tf_op jit(solution)/shard_map/scale/pallas_call | solution.py:533
Async XLA Ops:
  3.6 23.0 %collective-permute-start.2 = (bf16[160,1024]{1,0:T(8,128)(2,1)S(1)}, bf16[160,1024]{1,0:T(8,128)(2,1)S(1)}, u32[]{:S(2)}, u32[]{:S(2)}) collective-permute-start(bf16[160,1024]{1,0:T(8,128)(2,1)S(1)} %get-tuple-element.30), channel_id=1, source_target_pairs={{4,0},{8,4},{12,8},{16,12},{20,16},{24,20},{28,24},{5,1},{9,5},{13... | collective-permute-start | bytes 983048 | tf_op jit(solution)/shard_map/ppermute | solution.py:26
  4.9 21.7 %collective-permute-start.1 = (bf16[152,1024]{1,0:T(8,128)(2,1)S(1)}, bf16[152,1024]{1,0:T(8,128)(2,1)S(1)}, u32[]{:S(2)}, u32[]{:S(2)}) collective-permute-start(bf16[152,1024]{1,0:T(8,128)(2,1)S(1)} %get-tuple-element.29), channel_id=1, source_target_pairs={{0,4},{4,8},{8,12},{12,16},{16,20},{20,24},{24,28},{1,5},{5,9},{9,... | collective-permute-start | bytes 933896 | tf_op jit(solution)/shard_map/ppermute | solution.py:26
  10.5 20.2 %all-to-all-start = ((bf16[8,16,2048]{2,1,0:T(8,128)(2,1)}), bf16[8,16,2048]{2,1,0:T(8,128)(2,1)S(1)}, u32[]{:S(2)}, u32[]{:S(2)}) async-start(bf16[8,16,2048]{2,1,0:T(8,128)(2,1)} %get-tuple-element.32), calls=%async_computation | async-start | bytes 1048576 | tf_op jit(solution)/shard_map/all_to_all | solution.py:459
  19.6 22.7 %collective-permute-start = (bf16[152,1024]{1,0:T(8,128)(2,1)S(1)}, bf16[152,1024]{1,0:T(8,128)(2,1)S(1)}, u32[]{:S(2)}, u32[]{:S(2)}) collective-permute-start(bf16[152,1024]{1,0:T(8,128)(2,1)S(1)} %get-tuple-element.27), channel_id=1, source_target_pairs={{0,4},{4,8},{8,12},{12,16},{16,20},{20,24},{24,28},{1,5},{5,9},{9,... | collective-permute-start | bytes 933896 | tf_op jit(solution)/shard_map/ppermute | solution.py:26
  26.7 15.7 %collective-permute-start.3 = (bf16[160,1024]{1,0:T(8,128)(2,1)S(1)}, bf16[160,1024]{1,0:T(8,128)(2,1)S(1)}, u32[]{:S(2)}, u32[]{:S(2)}) collective-permute-start(bf16[160,1024]{1,0:T(8,128)(2,1)S(1)} %get-tuple-element.31), channel_id=1, source_target_pairs={{4,0},{8,4},{12,8},{16,12},{20,16},{24,20},{28,24},{5,1},{9,5},{13... | collective-permute-start | bytes 983048 | tf_op jit(solution)/shard_map/ppermute | solution.py:26
  53.3 23.8 %all-to-all-start.1 = ((bf16[8,160,256]{2,1,0:T(8,128)(2,1)}), bf16[8,160,256]{2,1,0:T(8,128)(2,1)S(1)}, u32[]{:S(2)}, u32[]{:S(2)}) async-start(bf16[8,160,256]{2,1,0:T(8,128)(2,1)} %get-tuple-element.38), calls=%async_computation.1 | async-start | bytes 1310720 | tf_op jit(solution)/shard_map/all_to_all | solution.py:516
  78.1 16.9 %all-to-all-start.2 = ((bf16[32,24,256]{2,1,0:T(8,128)(2,1)}), bf16[32,24,256]{2,1,0:T(8,128)(2,1)S(1)}, u32[]{:S(2)}, u32[]{:S(2)}) async-start(bf16[32,24,256]{2,1,0:T(8,128)(2,1)} %get-tuple-element.47), calls=%async_computation.2 | async-start | bytes 786432 | tf_op jit(solution)/shard_map/all_to_all | solution.py:530

commit v17 on v16

--- a/solution.py
+++ b/solution.py
@@ -98,11 +98,14 @@
 
 def edges_kernel(at, proj, cot, short, *refs):
     tails, heads, few, taps_held, p_tail, p_head, first, second, zeroth, held, semaphores = refs[-11:]
-    with_taps = len(refs) > 13
+    with_taps = len(refs) == 17
     if with_taps:
         taps, forward, backward, spread, all_taps, all_spread = refs[:6]
+    elif len(refs) == 16:
+        decay, forward, backward, falloff, all_decay = refs[:5]
     else:
         forward, backward = refs[:2]
+    with_decay = len(refs) == 16
     length, channels = cot.shape[0], forward.shape[1]
     here = pl.ds(at, channels)
     some, width = p_tail.shape[1], first.shape[1]
@@ -117,7 +120,11 @@
         (proj.at[2, :16, here], few.at[2]),
         (short.at[:, :, here], taps_held),
     ]
-    copies = fetch(pairs + [(taps, all_taps)] if with_taps else pairs, semaphores)
+    if with_taps:
+        pairs.append((taps, all_taps))
+    if with_decay:
+        pairs.append((decay, all_decay))
+    copies = fetch(pairs, semaphores)
     p_tail[...] = picked(tail, some - 128, some)
     p_head[...] = picked(head, 0, some)
     if with_taps:
@@ -157,6 +164,15 @@
     lax.fori_loop(0, channels // width, block, 0)
     if with_taps:
         sent.wait()
+    if with_decay:
+
+        def factors(c, _):
+            columns = window(c, width)
+            lags = lax.broadcasted_iota(jnp.int32, (falloff.shape[0], width), 0).astype(F32)
+            falloff[:, columns] = jnp.exp(-all_decay[:, columns] * lags)
+            return 0
+
+        lax.fori_loop(0, falloff.shape[1] // width, factors, 0)
 
 
 def operator_block(
@@ -175,8 +191,7 @@
     cot_next = after[136:144]
     next8 = [None, after[144:152], after[152:160]]
 
-    lags = lax.broadcasted_iota(jnp.int32, (taps.shape[0], width), 0).astype(F32)
-    falloff = jnp.exp(-decay[...] * lags)
+    falloff = decay[...]
     kernel = taps[...].astype(F32) * falloff
     high = kernel.astype(BF16)
     low = (kernel - high.astype(F32)).astype(BF16)
@@ -451,10 +466,16 @@
             operands += far(filter_taps)
             results.append((pltpu.HBM((ranks, rows, channels), BF16), FAR))
             scratch = [vmem(F32, rows, channels), vmem(BF16, ranks, rows, channels)] + scratch
+        elif k == CHUNKS - 1:
+            operands += far(decay)
+            results.append((pltpu.HBM((count, channels), F32), IN_VMEM))
+            scratch = [vmem(F32, 1, channels)] + scratch
         forward, backward, *spread = call(
             functools.partial(edges_kernel, k * chunk), "edges", operands, results, cost=10 if k else 1,
             scratch_shapes=scratch,
         )
+        if k == CHUNKS - 1:
+            falloff = spread[0]
         if k == 0:
             taps = lax.all_to_all(spread[0], "seq", 0, 0).reshape(count, channels)
         else:
@@ -487,7 +508,7 @@
                 (proj, columns((3, length), wide, first)), (cot, columns((length,), wide, first)),
                 (prev[k], columns((152,), wide)), (later[k], columns((160,), wide)),
                 (short, columns((3, FK), wide, first)), (taps, columns((count,), wide, first)),
-                (decay, columns((1,), wide, first)),
+                (falloff, columns((count,), wide, first)),
             ] + constants,
             [(result, one_of(result, first, PAIR)) for result in results]
             + [(pltpu.HBM((ranks, CHUNKS * blocks * slot + SHORT, width), BF16), FAR)],

time: 97 us -> 97.1 us (level)
  waiting for transfers between devices: 24.1 us -> 22.8 us
  Pallas kernels: 39.5 us -> 40.8 us
    pallas_call x5, Pallas kernels: 37.1 us -> 38.4 us  [call(): pl.pallas_call(kernel, in_specs=[spec for _, spec in operands] + [FAR] *...]
    ppermute x4, waiting for transfers between devices: 3.86 us -> 2.63 us  [from_behind(): return lax.ppermute(value, axis, pairs)]
  transfers between devices with their start and end apart: 7 -> 7, of which waited for: 5 -> 5; matrix products, arithmetic and copies ran while one was open for 0% -> 0% of each run, Pallas kernels for 24% -> 25%
where the time goes in v17:
time: 97.1 us; the launch traced here: 96.4 us
  Pallas kernels  40.8 us (42%)
  starting transfers between devices  32 us (33%)
  waiting for transfers between devices  22.8 us (23%)
    pallas_call x5, Pallas kernels, call(): pl.pallas_call(kernel, in_specs=[spec for _, spec in operands] + [FAR] *...  38.4 us
    all_to_all x1, waiting for transfers between devices, shards(): gathered = lax.all_to_all(payload, ('seq', 'ch'), 0, 0)  13.1 us
    ppermute x4, starting transfers between devices, from_behind(): return lax.ppermute(value, axis, pairs)  12 us
    all_to_all x1, starting transfers between devices, shards(): lax.all_to_all(sums, 'seq', 0, 0)  10.1 us
    all_to_all x1, starting transfers between devices, shards(): taps = lax.all_to_all(spread[0], 'seq', 0, 0).reshape(count, channels)  6.21 us
    all_to_all x1, waiting for transfers between devices, shards(): lax.all_to_all(sums, 'seq', 0, 0)  4.36 us
    all_to_all x1, starting transfers between devices, shards(): gathered = lax.all_to_all(payload, ('seq', 'ch'), 0, 0)  3.69 us
    all_to_all x1, waiting for transfers between devices, shards(): taps = lax.all_to_all(spread[0], 'seq', 0, 0).reshape(count, channels)  2.72 us
  transfers between devices with their start and end apart: 7, of which 5 were waited for; matrix products, arithmetic and copies ran while one was open for 0% of the time, Pallas kernels for 25%

profile of v17, /device:TPU:0, one launch (start us, length us, event | category | flops | bytes accessed | tf_op | source)
XLA Modules:
  0.0 96.4 jit_solution(5227759032572625158)
XLA Ops:
  0.6 3.0 %edges.3 = (bf16[152,1024]{1,0:T(8,128)(2,1)S(1)}, bf16[160,1024]{1,0:T(8,128)(2,1)S(1)}, bf16[8,16,2048]{2,1,0:T(8,128)(2,1)}) custom-call(bf16[3,256,2048]{2,1,0:T(8,128)(2,1)} %bitcast.7, bf16[256,2048]{1,0:T(8,128)(2,1)} %cot.7, f32[3,7,2048]{2,1,0:T(8,128)} %short.9, f32[16,2048]{1,0:T(8,128)} %refs_0_.3), custom_call_target="tpu_custom_call" | custom-call | flops 1000000000 | bytes 1000000 | tf_op jit(solution)/shard_map/edges/pallas_call | solution.py:388
  3.6 1.3 %collective-permute-start.2 = (bf16[160,1024]{1,0:T(8,128)(2,1)S(1)}, bf16[160,1024]{1,0:T(8,128)(2,1)S(1)}, u32[]{:S(2)}, u32[]{:S(2)}) collective-permute-start(bf16[160,1024]{1,0:T(8,128)(2,1)S(1)} %get-tuple-element.31), channel_id=1, source_target_pairs={{4,0},{8,4},{12,8},{16,12},{20,16},{24,20},{28,24},{5,1},{9,5},{13... | collective-permute-start | bytes 983048 | tf_op jit(solution)/shard_map/ppermute | solution.py:26
  4.9 5.5 %collective-permute-start.1 = (bf16[152,1024]{1,0:T(8,128)(2,1)S(1)}, bf16[152,1024]{1,0:T(8,128)(2,1)S(1)}, u32[]{:S(2)}, u32[]{:S(2)}) collective-permute-start(bf16[152,1024]{1,0:T(8,128)(2,1)S(1)} %get-tuple-element.30), channel_id=1, source_target_pairs={{0,4},{4,8},{8,12},{12,16},{16,20},{20,24},{24,28},{1,5},{5,9},{9,... | collective-permute-start | bytes 933896 | tf_op jit(solution)/shard_map/ppermute | solution.py:26
  10.5 6.2 %all-to-all-start = ((bf16[8,16,2048]{2,1,0:T(8,128)(2,1)}), bf16[8,16,2048]{2,1,0:T(8,128)(2,1)S(1)}, u32[]{:S(2)}, u32[]{:S(2)}) async-start(bf16[8,16,2048]{2,1,0:T(8,128)(2,1)} %get-tuple-element.33), calls=%async_computation | async-start | bytes 1048576 | tf_op jit(solution)/shard_map/all_to_all | solution.py:480
  16.7 4.1 %edges.2 = (bf16[152,1024]{1,0:T(8,128)(2,1)S(1)}, bf16[160,1024]{1,0:T(8,128)(2,1)S(1)}, f32[128,2048]{1,0:T(8,128)}) custom-call(bf16[3,256,2048]{2,1,0:T(8,128)(2,1)} %bitcast.8, bf16[256,2048]{1,0:T(8,128)(2,1)} %cot.7, f32[3,7,2048]{2,1,0:T(8,128)} %short.9, f32[1,2048]{1,0:T(1,128)} %bitcast.11), custom_call_target="tpu_custom_call" | custom-call | flops 10000000000 | bytes 1000000 | tf_op jit(solution)/shard_map/edges/pallas_call | solution.py:388
  20.8 3.9 %collective-permute-start = (bf16[152,1024]{1,0:T(8,128)(2,1)S(1)}, bf16[152,1024]{1,0:T(8,128)(2,1)S(1)}, u32[]{:S(2)}, u32[]{:S(2)}) collective-permute-start(bf16[152,1024]{1,0:T(8,128)(2,1)S(1)} %get-tuple-element.28), channel_id=1, source_target_pairs={{0,4},{4,8},{8,12},{12,16},{16,20},{20,24},{24,28},{1,5},{5,9},{9,... | collective-permute-start | bytes 933896 | tf_op jit(solution)/shard_map/ppermute | solution.py:26
  24.7 1.9 %collective-permute-done.1.prev = bf16[152,1024]{1,0:T(8,128)(2,1)S(1)} collective-permute-done((bf16[152,1024]{1,0:T(8,128)(2,1)S(1)}, bf16[152,1024]{1,0:T(8,128)(2,1)S(1)}, u32[]{:S(2)}, u32[]{:S(2)}) %collective-permute-start.1) | collective-permute-done | bytes 311328 | tf_op jit(solution)/shard_map/ppermute | solution.py:26
  26.6 0.0 collective-permute-done.2.later
  26.7 1.3 %collective-permute-start.3 = (bf16[160,1024]{1,0:T(8,128)(2,1)S(1)}, bf16[160,1024]{1,0:T(8,128)(2,1)S(1)}, u32[]{:S(2)}, u32[]{:S(2)}) collective-permute-start(bf16[160,1024]{1,0:T(8,128)(2,1)S(1)} %get-tuple-element.32), channel_id=1, source_target_pairs={{4,0},{8,4},{12,8},{16,12},{20,16},{24,20},{28,24},{5,1},{9,5},{13... | collective-permute-start | bytes 983048 | tf_op jit(solution)/shard_map/ppermute | solution.py:26
  27.9 2.7 %all-to-all-done = bf16[8,16,2048]{2,1,0:T(8,128)(2,1)S(1)} async-done(((bf16[8,16,2048]{2,1,0:T(8,128)(2,1)}), bf16[8,16,2048]{2,1,0:T(8,128)(2,1)S(1)}, u32[]{:S(2)}, u32[]{:S(2)}) %all-to-all-start) | async-done | bytes 524320 | tf_op jit(solution)/shard_map/all_to_all | solution.py:480
  30.7 11.0 %operator.2 = (bf16[8,256,256]{2,1,0:T(8,128)(2,1)}, f32[8,3,38,8,256]{4,3,2,1,0:T(8,128)}, bf16[8,160,256]{2,1,0:T(8,128)(2,1)}) custom-call(bf16[3,256,2048]{2,1,0:T(8,128)(2,1)} %bitcast.9, bf16[256,2048]{1,0:T(8,128)(2,1)} %cot.7, bf16[152,1024]{1,0:T(8,128)(2,1)S(1)} %collective-permute-done.1.prev, bf16[160,1024]{1,0:T(8,128)(2,1)S(1)} %collective-permute-done.2.later, ...), custom_call_target="tpu_custom_call" | custom-call | flops 12000000000 | bytes 1000000 | tf_op jit(solution)/shard_map/operator/pallas_call | solution.py:388
  41.6 0.7 collective-permute-done.prev
  42.4 0.0 collective-permute-done.3.later
  42.4 11.0 %operator.3 = (bf16[8,256,256]{2,1,0:T(8,128)(2,1)}, f32[8,3,38,8,256]{4,3,2,1,0:T(8,128)}, bf16[8,160,256]{2,1,0:T(8,128)(2,1)}) custom-call(bf16[3,256,2048]{2,1,0:T(8,128)(2,1)} %bitcast.10, bf16[256,2048]{1,0:T(8,128)(2,1)} %cot.7, ...), custom_call_target="tpu_custom_call", output_to_operand_aliasing={{0}: (14, {}), {1}: (15, {}), {2}: (16, {})} | custom-call | flops 12000000000 | bytes 1000000 | tf_op jit(solution)/shard_map/operator/pallas_call | solution.py:388
  53.4 10.1 %all-to-all-start.1 = ((bf16[8,160,256]{2,1,0:T(8,128)(2,1)}), bf16[8,160,256]{2,1,0:T(8,128)(2,1)S(1)}, u32[]{:S(2)}, u32[]{:S(2)}) async-start(bf16[8,160,256]{2,1,0:T(8,128)(2,1)} %get-tuple-element.40), calls=%async_computation.1 | async-start | bytes 1310720 | tf_op jit(solution)/shard_map/all_to_all | solution.py:537
  63.5 9.3 %outputs.1 = (bf16[256,2048]{1,0:T(8,128)(2,1)}, bf16[3,256,2048]{2,1,0:T(8,128)(2,1)}) custom-call(bf16[8,256,256]{2,1,0:T(8,128)(2,1)} %get-tuple-element.41.product, f32[8,3,38,8,256]{4,3,2,1,0:T(8,128)} %get-tuple-element.42.grad, f32[3,7,2048]{2,1,0:T(8,128)} %short.9, bf16[256,256]{1,0:T(8,128)(2,1)} %constant.29.clone.p_out), custom_call_target="tpu_custom_call" | custom-call | flops 8000000000 | bytes 1000000 | tf_op jit(solution)/shard_map/outputs/pallas_call | solution.py:388
  72.8 4.4 %all-to-all-done.1.sums = bf16[8,160,256]{2,1,0:T(8,128)(2,1)S(1)} async-done(((bf16[8,160,256]{2,1,0:T(8,128)(2,1)}), bf16[8,160,256]{2,1,0:T(8,128)(2,1)S(1)}, u32[]{:S(2)}, u32[]{:S(2)}) %all-to-all-start.1) | async-done | bytes 655392 | tf_op jit(solution)/shard_map/all_to_all | solution.py:537
  77.1 1.0 %squares.1 = (f32[16,2048]{1,0:T(8,128)S(1)}, bf16[32,24,256]{2,1,0:T(8,128)(2,1)}) custom-call(bf16[8,160,256]{2,1,0:T(8,128)(2,1)S(1)} %all-to-all-done.1.sums), custom_call_target="tpu_custom_call" | custom-call | tf_op jit(solution)/shard_map/squares/pallas_call | solution.py:540
  78.2 3.7 %all-to-all-start.2 = ((bf16[32,24,256]{2,1,0:T(8,128)(2,1)}), bf16[32,24,256]{2,1,0:T(8,128)(2,1)S(1)}, u32[]{:S(2)}, u32[]{:S(2)}) async-start(bf16[32,24,256]{2,1,0:T(8,128)(2,1)} %get-tuple-element.49), calls=%async_computation.2 | async-start | bytes 786432 | tf_op jit(solution)/shard_map/all_to_all | solution.py:551
  81.9 0.1 pad_add_fusion.mine
  81.9 13.1 %all-to-all-done.2.gathered = bf16[32,24,256]{2,1,0:T(8,128)(2,1)S(1)} async-done(((bf16[32,24,256]{2,1,0:T(8,128)(2,1)}), bf16[32,24,256]{2,1,0:T(8,128)(2,1)S(1)}, u32[]{:S(2)}, u32[]{:S(2)}) %all-to-all-start.2) | async-done | bytes 393248 | tf_op jit(solution)/shard_map/all_to_all | solution.py:551
  95.0 1.4 %scale.1 = (f32[3,7,2048]{2,1,0:T(8,128)}, f32[16,2048]{1,0:T(8,128)}) custom-call(s32[2]{0:T(128)S(1)} %pad_add_fusion.mine, f32[16,2048]{1,0:T(8,128)S(1)} %get-tuple-element.48.raw, bf16[32,24,256]{2,1,0:T(8,128)(2,1)S(1)} %all-to-all-done.2.gathered), custom_call_target="tpu_custom_call" | custom-call | tf_op jit(solution)/shard_map/scale/pallas_call | solution.py:554
Async XLA Ops:
  3.6 23.0 %collective-permute-start.2 = (bf16[160,1024]{1,0:T(8,128)(2,1)S(1)}, bf16[160,1024]{1,0:T(8,128)(2,1)S(1)}, u32[]{:S(2)}, u32[]{:S(2)}) collective-permute-start(bf16[160,1024]{1,0:T(8,128)(2,1)S(1)} %get-tuple-element.31), channel_id=1, source_target_pairs={{4,0},{8,4},{12,8},{16,12},{20,16},{24,20},{28,24},{5,1},{9,5},{13... | collective-permute-start | bytes 983048 | tf_op jit(solution)/shard_map/ppermute | solution.py:26
  4.9 21.7 %collective-permute-start.1 = (bf16[152,1024]{1,0:T(8,128)(2,1)S(1)}, bf16[152,1024]{1,0:T(8,128)(2,1)S(1)}, u32[]{:S(2)}, u32[]{:S(2)}) collective-permute-start(bf16[152,1024]{1,0:T(8,128)(2,1)S(1)} %get-tuple-element.30), channel_id=1, source_target_pairs={{0,4},{4,8},{8,12},{12,16},{16,20},{20,24},{24,28},{1,5},{5,9},{9,... | collective-permute-start | bytes 933896 | tf_op jit(solution)/shard_map/ppermute | solution.py:26
  10.5 20.2 %all-to-all-start = ((bf16[8,16,2048]{2,1,0:T(8,128)(2,1)}), bf16[8,16,2048]{2,1,0:T(8,128)(2,1)S(1)}, u32[]{:S(2)}, u32[]{:S(2)}) async-start(bf16[8,16,2048]{2,1,0:T(8,128)(2,1)} %get-tuple-element.33), calls=%async_computation | async-start | bytes 1048576 | tf_op jit(solution)/shard_map/all_to_all | solution.py:480
  20.8 21.6 %collective-permute-start = (bf16[152,1024]{1,0:T(8,128)(2,1)S(1)}, bf16[152,1024]{1,0:T(8,128)(2,1)S(1)}, u32[]{:S(2)}, u32[]{:S(2)}) collective-permute-start(bf16[152,1024]{1,0:T(8,128)(2,1)S(1)} %get-tuple-element.28), channel_id=1, source_target_pairs={{0,4},{4,8},{8,12},{12,16},{16,20},{20,24},{24,28},{1,5},{5,9},{9,... | collective-permute-start | bytes 933896 | tf_op jit(solution)/shard_map/ppermute | solution.py:26
  26.7 15.7 %collective-permute-start.3 = (bf16[160,1024]{1,0:T(8,128)(2,1)S(1)}, bf16[160,1024]{1,0:T(8,128)(2,1)S(1)}, u32[]{:S(2)}, u32[]{:S(2)}) collective-permute-start(bf16[160,1024]{1,0:T(8,128)(2,1)S(1)} %get-tuple-element.32), channel_id=1, source_target_pairs={{4,0},{8,4},{12,8},{16,12},{20,16},{24,20},{28,24},{5,1},{9,5},{13... | collective-permute-start | bytes 983048 | tf_op jit(solution)/shard_map/ppermute | solution.py:26
  53.4 23.8 %all-to-all-start.1 = ((bf16[8,160,256]{2,1,0:T(8,128)(2,1)}), bf16[8,160,256]{2,1,0:T(8,128)(2,1)S(1)}, u32[]{:S(2)}, u32[]{:S(2)}) async-start(bf16[8,160,256]{2,1,0:T(8,128)(2,1)} %get-tuple-element.40), calls=%async_computation.1 | async-start | bytes 1310720 | tf_op jit(solution)/shard_map/all_to_all | solution.py:537
  78.2 16.9 %all-to-all-start.2 = ((bf16[32,24,256]{2,1,0:T(8,128)(2,1)}), bf16[32,24,256]{2,1,0:T(8,128)(2,1)S(1)}, u32[]{:S(2)}, u32[]{:S(2)}) async-start(bf16[32,24,256]{2,1,0:T(8,128)(2,1)} %get-tuple-element.49), calls=%async_computation.2 | async-start | bytes 786432 | tf_op jit(solution)/shard_map/all_to_all | solution.py:551

commit v18 on v17

--- a/solution.py
+++ b/solution.py
@@ -479,7 +479,7 @@
         if k == 0:
             taps = lax.all_to_all(spread[0], "seq", 0, 0).reshape(count, channels)
         else:
-            backward, prev[-1], later[-1] = lax.optimization_barrier((backward, prev[-1], later[-1]))
+            backward, prev[-1] = lax.optimization_barrier((backward, prev[-1]))
         later.append(from_behind(backward, "seq", -1))
         prev.append(from_behind(forward, "seq", 1))
 

time: 97.1 us -> 100 us (1.030)
  waiting for transfers between devices: 22.8 us -> 27.3 us
  starting transfers between devices: 32 us -> 30.7 us
    ppermute x4, waiting for transfers between devices: 2.63 us -> 6.83 us  [from_behind(): return lax.ppermute(value, axis, pairs)]
    all_to_all x1, waiting for transfers between devices: 4.36 us -> 7.4 us  [shards(): lax.all_to_all(sums, 'seq', 0, 0)]
    all_to_all x1, waiting for transfers between devices: 2.72 us -> 0.01 us  [shards(): taps = lax.all_to_all(spread[0], 'seq', 0, 0).reshape(count, channels)]
    all_to_all x1, starting transfers between devices: 6.21 us -> 4.88 us  [shards(): taps = lax.all_to_all(spread[0], 'seq', 0, 0).reshape(count, channels)]
  transfers between devices with their start and end apart: 7 -> 7, of which waited for: 5 -> 4; matrix products, arithmetic and copies ran while one was open for 0% -> 0% of each run, Pallas kernels for 25% -> 25%
where the time goes in v18:
time: 100 us; the launch traced here: 99.6 us
  Pallas kernels  40.8 us (41%)
  starting transfers between devices  30.7 us (31%)
  waiting for transfers between devices  27.3 us (27%)
    pallas_call x5, Pallas kernels, call(): pl.pallas_call(kernel, in_specs=[spec for _, spec in operands] + [FAR] *...  38.4 us
    all_to_all x1, waiting for transfers between devices, shards(): gathered = lax.all_to_all(payload, ('seq', 'ch'), 0, 0)  13.1 us
    ppermute x4, starting transfers between devices, from_behind(): return lax.ppermute(value, axis, pairs)  12 us
    all_to_all x1, starting transfers between devices, shards(): lax.all_to_all(sums, 'seq', 0, 0)  10.1 us
    all_to_all x1, waiting for transfers between devices, shards(): lax.all_to_all(sums, 'seq', 0, 0)  7.4 us
    ppermute x4, waiting for transfers between devices, from_behind(): return lax.ppermute(value, axis, pairs)  6.83 us
    all_to_all x1, starting transfers between devices, shards(): taps = lax.all_to_all(spread[0], 'seq', 0, 0).reshape(count, channels)  4.88 us
    all_to_all x1, starting transfers between devices, shards(): gathered = lax.all_to_all(payload, ('seq', 'ch'), 0, 0)  3.65 us
  transfers between devices with their start and end apart: 7, of which 4 were waited for; matrix products, arithmetic and copies ran while one was open for 0% of the time, Pallas kernels for 25%

profile of v18, /device:TPU:0, one launch (start us, length us, event | category | flops | bytes accessed | tf_op | source)
XLA Modules:
  0.0 99.6 jit_solution(12060758164299730345)
XLA Ops:
  0.6 3.0 %edges.3 = (bf16[152,1024]{1,0:T(8,128)(2,1)S(1)}, bf16[160,1024]{1,0:T(8,128)(2,1)S(1)}, bf16[8,16,2048]{2,1,0:T(8,128)(2,1)}) custom-call(bf16[3,256,2048]{2,1,0:T(8,128)(2,1)} %bitcast.7, bf16[256,2048]{1,0:T(8,128)(2,1)} %cot.7, f32[3,7,2048]{2,1,0:T(8,128)} %short.9, f32[16,2048]{1,0:T(8,128)} %refs_0_.3), custom_call_target="tpu_custom_call" | custom-call | flops 1000000000 | bytes 1000000 | tf_op jit(solution)/shard_map/edges/pallas_call | solution.py:388
  3.6 4.9 %collective-permute-start.1 = (bf16[152,1024]{1,0:T(8,128)(2,1)S(1)}, bf16[152,1024]{1,0:T(8,128)(2,1)S(1)}, u32[]{:S(2)}, u32[]{:S(2)}) collective-permute-start(bf16[152,1024]{1,0:T(8,128)(2,1)S(1)} %get-tuple-element.29), channel_id=1, source_target_pairs={{0,4},{4,8},{8,12},{12,16},{16,20},{20,24},{24,28},{1,5},{5,9},{9,... | collective-permute-start | bytes 933896 | tf_op jit(solution)/shard_map/ppermute | solution.py:26
  8.5 4.9 %all-to-all-start = ((bf16[8,16,2048]{2,1,0:T(8,128)(2,1)}), bf16[8,16,2048]{2,1,0:T(8,128)(2,1)S(1)}, u32[]{:S(2)}, u32[]{:S(2)}) async-start(bf16[8,16,2048]{2,1,0:T(8,128)(2,1)} %get-tuple-element.31), calls=%async_computation | async-start | bytes 1048576 | tf_op jit(solution)/shard_map/all_to_all | solution.py:480
  13.4 1.3 %collective-permute-start.3 = (bf16[160,1024]{1,0:T(8,128)(2,1)S(1)}, bf16[160,1024]{1,0:T(8,128)(2,1)S(1)}, u32[]{:S(2)}, u32[]{:S(2)}) collective-permute-start(bf16[160,1024]{1,0:T(8,128)(2,1)S(1)} %get-tuple-element.34), channel_id=1, source_target_pairs={{4,0},{8,4},{12,8},{16,12},{20,16},{24,20},{28,24},{5,1},{9,5},{13... | collective-permute-start | bytes 983048 | tf_op jit(solution)/shard_map/ppermute | solution.py:26
  14.7 4.1 %edges.2 = (bf16[152,1024]{1,0:T(8,128)(2,1)S(1)}, bf16[160,1024]{1,0:T(8,128)(2,1)S(1)}, f32[128,2048]{1,0:T(8,128)}) custom-call(bf16[3,256,2048]{2,1,0:T(8,128)(2,1)} %bitcast.8, bf16[256,2048]{1,0:T(8,128)(2,1)} %cot.7, f32[3,7,2048]{2,1,0:T(8,128)} %short.9, f32[1,2048]{1,0:T(1,128)} %bitcast.11), custom_call_target="tpu_custom_call" | custom-call | flops 10000000000 | bytes 1000000 | tf_op jit(solution)/shard_map/edges/pallas_call | solution.py:388
  18.8 4.6 %collective-permute-start = (bf16[152,1024]{1,0:T(8,128)(2,1)S(1)}, bf16[152,1024]{1,0:T(8,128)(2,1)S(1)}, u32[]{:S(2)}, u32[]{:S(2)}) collective-permute-start(bf16[152,1024]{1,0:T(8,128)(2,1)S(1)} %get-tuple-element.27), channel_id=1, source_target_pairs={{0,4},{4,8},{8,12},{12,16},{16,20},{20,24},{24,28},{1,5},{5,9},{9,... | collective-permute-start | bytes 933896 | tf_op jit(solution)/shard_map/ppermute | solution.py:26
  23.4 0.0 collective-permute-done.1.prev
  23.4 1.3 %collective-permute-start.2 = (bf16[160,1024]{1,0:T(8,128)(2,1)S(1)}, bf16[160,1024]{1,0:T(8,128)(2,1)S(1)}, u32[]{:S(2)}, u32[]{:S(2)}) collective-permute-start(bf16[160,1024]{1,0:T(8,128)(2,1)S(1)} %get-tuple-element.30), channel_id=1, source_target_pairs={{4,0},{8,4},{12,8},{16,12},{20,16},{24,20},{28,24},{5,1},{9,5},{13... | collective-permute-start | bytes 983048 | tf_op jit(solution)/shard_map/ppermute | solution.py:26
  24.7 5.0 %collective-permute-done.3.later = bf16[160,1024]{1,0:T(8,128)(2,1)S(1)} collective-permute-done((bf16[160,1024]{1,0:T(8,128)(2,1)S(1)}, bf16[160,1024]{1,0:T(8,128)(2,1)S(1)}, u32[]{:S(2)}, u32[]{:S(2)}) %collective-permute-start.3) | collective-permute-done | bytes 327712 | tf_op jit(solution)/shard_map/ppermute | solution.py:26
  29.7 0.0 all-to-all-done
  29.7 11.0 %operator.2 = (bf16[8,256,256]{2,1,0:T(8,128)(2,1)}, f32[8,3,38,8,256]{4,3,2,1,0:T(8,128)}, bf16[8,160,256]{2,1,0:T(8,128)(2,1)}) custom-call(bf16[3,256,2048]{2,1,0:T(8,128)(2,1)} %bitcast.9, bf16[256,2048]{1,0:T(8,128)(2,1)} %cot.7, bf16[152,1024]{1,0:T(8,128)(2,1)S(1)} %collective-permute-done.1.prev, bf16[160,1024]{1,0:T(8,128)(2,1)S(1)} %collective-permute-done.3.later, ...), custom_call_target="tpu_custom_call" | custom-call | flops 12000000000 | bytes 1000000 | tf_op jit(solution)/shard_map/operator/pallas_call | solution.py:388
  40.7 1.8 %collective-permute-done.prev = bf16[152,1024]{1,0:T(8,128)(2,1)S(1)} collective-permute-done((bf16[152,1024]{1,0:T(8,128)(2,1)S(1)}, bf16[152,1024]{1,0:T(8,128)(2,1)S(1)}, u32[]{:S(2)}, u32[]{:S(2)}) %collective-permute-start) | collective-permute-done | bytes 311328 | tf_op jit(solution)/shard_map/ppermute | solution.py:26
  42.5 0.0 collective-permute-done.2.later
  42.5 11.0 %operator.3 = (bf16[8,256,256]{2,1,0:T(8,128)(2,1)}, f32[8,3,38,8,256]{4,3,2,1,0:T(8,128)}, bf16[8,160,256]{2,1,0:T(8,128)(2,1)}) custom-call(bf16[3,256,2048]{2,1,0:T(8,128)(2,1)} %bitcast.10, bf16[256,2048]{1,0:T(8,128)(2,1)} %cot.7, ...), custom_call_target="tpu_custom_call", output_to_operand_aliasing={{0}: (14, {}), {1}: (15, {}), {2}: (16, {})} | custom-call | flops 12000000000 | bytes 1000000 | tf_op jit(solution)/shard_map/operator/pallas_call | solution.py:388
  53.5 10.1 %all-to-all-start.1 = ((bf16[8,160,256]{2,1,0:T(8,128)(2,1)}), bf16[8,160,256]{2,1,0:T(8,128)(2,1)S(1)}, u32[]{:S(2)}, u32[]{:S(2)}) async-start(bf16[8,160,256]{2,1,0:T(8,128)(2,1)} %get-tuple-element.38), calls=%async_computation.1 | async-start | bytes 1310720 | tf_op jit(solution)/shard_map/all_to_all | solution.py:537
  63.7 9.3 %outputs.1 = (bf16[256,2048]{1,0:T(8,128)(2,1)}, bf16[3,256,2048]{2,1,0:T(8,128)(2,1)}) custom-call(bf16[8,256,256]{2,1,0:T(8,128)(2,1)} %get-tuple-element.39.product, f32[8,3,38,8,256]{4,3,2,1,0:T(8,128)} %get-tuple-element.40.grad, f32[3,7,2048]{2,1,0:T(8,128)} %short.9, bf16[256,256]{1,0:T(8,128)(2,1)} %constant.29.clone.p_out), custom_call_target="tpu_custom_call" | custom-call | flops 8000000000 | bytes 1000000 | tf_op jit(solution)/shard_map/outputs/pallas_call | solution.py:388
  73.0 7.4 %all-to-all-done.1.sums = bf16[8,160,256]{2,1,0:T(8,128)(2,1)S(1)} async-done(((bf16[8,160,256]{2,1,0:T(8,128)(2,1)}), bf16[8,160,256]{2,1,0:T(8,128)(2,1)S(1)}, u32[]{:S(2)}, u32[]{:S(2)}) %all-to-all-start.1) | async-done | bytes 655392 | tf_op jit(solution)/shard_map/all_to_all | solution.py:537
  80.4 1.0 %squares.1 = (f32[16,2048]{1,0:T(8,128)S(1)}, bf16[32,24,256]{2,1,0:T(8,128)(2,1)}) custom-call(bf16[8,160,256]{2,1,0:T(8,128)(2,1)S(1)} %all-to-all-done.1.sums), custom_call_target="tpu_custom_call" | custom-call | tf_op jit(solution)/shard_map/squares/pallas_call | solution.py:540
  81.4 3.7 %all-to-all-start.2 = ((bf16[32,24,256]{2,1,0:T(8,128)(2,1)}), bf16[32,24,256]{2,1,0:T(8,128)(2,1)S(1)}, u32[]{:S(2)}, u32[]{:S(2)}) async-start(bf16[32,24,256]{2,1,0:T(8,128)(2,1)} %get-tuple-element.47), calls=%async_computation.2 | async-start | bytes 786432 | tf_op jit(solution)/shard_map/all_to_all | solution.py:551
  85.1 0.1 pad_add_fusion.mine
  85.1 13.1 %all-to-all-done.2.gathered = bf16[32,24,256]{2,1,0:T(8,128)(2,1)S(1)} async-done(((bf16[32,24,256]{2,1,0:T(8,128)(2,1)}), bf16[32,24,256]{2,1,0:T(8,128)(2,1)S(1)}, u32[]{:S(2)}, u32[]{:S(2)}) %all-to-all-start.2) | async-done | bytes 393248 | tf_op jit(solution)/shard_map/all_to_all | solution.py:551
  98.2 1.4 %scale.1 = (f32[3,7,2048]{2,1,0:T(8,128)}, f32[16,2048]{1,0:T(8,128)}) custom-call(s32[2]{0:T(128)S(1)} %pad_add_fusion.mine, f32[16,2048]{1,0:T(8,128)S(1)} %get-tuple-element.46.raw, bf16[32,24,256]{2,1,0:T(8,128)(2,1)S(1)} %all-to-all-done.2.gathered), custom_call_target="tpu_custom_call" | custom-call | tf_op jit(solution)/shard_map/scale/pallas_call | solution.py:554
Async XLA Ops:
  3.6 19.8 %collective-permute-start.1 = (bf16[152,1024]{1,0:T(8,128)(2,1)S(1)}, bf16[152,1024]{1,0:T(8,128)(2,1)S(1)}, u32[]{:S(2)}, u32[]{:S(2)}) collective-permute-start(bf16[152,1024]{1,0:T(8,128)(2,1)S(1)} %get-tuple-element.29), channel_id=1, source_target_pairs={{0,4},{4,8},{8,12},{12,16},{16,20},{20,24},{24,28},{1,5},{5,9},{9,... | collective-permute-start | bytes 933896 | tf_op jit(solution)/shard_map/ppermute | solution.py:26
  8.5 21.2 %all-to-all-start = ((bf16[8,16,2048]{2,1,0:T(8,128)(2,1)}), bf16[8,16,2048]{2,1,0:T(8,128)(2,1)S(1)}, u32[]{:S(2)}, u32[]{:S(2)}) async-start(bf16[8,16,2048]{2,1,0:T(8,128)(2,1)} %get-tuple-element.31), calls=%async_computation | async-start | bytes 1048576 | tf_op jit(solution)/shard_map/all_to_all | solution.py:480
  13.4 16.3 %collective-permute-start.3 = (bf16[160,1024]{1,0:T(8,128)(2,1)S(1)}, bf16[160,1024]{1,0:T(8,128)(2,1)S(1)}, u32[]{:S(2)}, u32[]{:S(2)}) collective-permute-start(bf16[160,1024]{1,0:T(8,128)(2,1)S(1)} %get-tuple-element.34), channel_id=1, source_target_pairs={{4,0},{8,4},{12,8},{16,12},{20,16},{24,20},{28,24},{5,1},{9,5},{13... | collective-permute-start | bytes 983048 | tf_op jit(solution)/shard_map/ppermute | solution.py:26
  18.8 23.7 %collective-permute-start = (bf16[152,1024]{1,0:T(8,128)(2,1)S(1)}, bf16[152,1024]{1,0:T(8,128)(2,1)S(1)}, u32[]{:S(2)}, u32[]{:S(2)}) collective-permute-start(bf16[152,1024]{1,0:T(8,128)(2,1)S(1)} %get-tuple-element.27), channel_id=1, source_target_pairs={{0,4},{4,8},{8,12},{12,16},{16,20},{20,24},{24,28},{1,5},{5,9},{9,... | collective-permute-start | bytes 933896 | tf_op jit(solution)/shard_map/ppermute | solution.py:26
  23.4 19.1 %collective-permute-start.2 = (bf16[160,1024]{1,0:T(8,128)(2,1)S(1)}, bf16[160,1024]{1,0:T(8,128)(2,1)S(1)}, u32[]{:S(2)}, u32[]{:S(2)}) collective-permute-start(bf16[160,1024]{1,0:T(8,128)(2,1)S(1)} %get-tuple-element.30), channel_id=1, source_target_pairs={{4,0},{8,4},{12,8},{16,12},{20,16},{24,20},{28,24},{5,1},{9,5},{13... | collective-permute-start | bytes 983048 | tf_op jit(solution)/shard_map/ppermute | solution.py:26
  53.5 26.9 %all-to-all-start.1 = ((bf16[8,160,256]{2,1,0:T(8,128)(2,1)}), bf16[8,160,256]{2,1,0:T(8,128)(2,1)S(1)}, u32[]{:S(2)}, u32[]{:S(2)}) async-start(bf16[8,160,256]{2,1,0:T(8,128)(2,1)} %get-tuple-element.38), calls=%async_computation.1 | async-start | bytes 1310720 | tf_op jit(solution)/shard_map/all_to_all | solution.py:537
  81.4 16.8 %all-to-all-start.2 = ((bf16[32,24,256]{2,1,0:T(8,128)(2,1)}), bf16[32,24,256]{2,1,0:T(8,128)(2,1)S(1)}, u32[]{:S(2)}, u32[]{:S(2)}) async-start(bf16[32,24,256]{2,1,0:T(8,128)(2,1)} %get-tuple-element.47), calls=%async_computation.2 | async-start | bytes 786432 | tf_op jit(solution)/shard_map/all_to_all | solution.py:551

commit v19 on v17

--- a/solution.py
+++ b/solution.py
@@ -194,8 +194,7 @@
     falloff = decay[...]
     kernel = taps[...].astype(F32) * falloff
     high = kernel.astype(BF16)
-    low = (kernel - high.astype(F32)).astype(BF16)
-    k_spec = mm(e_taps[...], jnp.concatenate([high, high, low], axis=0))
+    k_spec = mm(e_taps[...], jnp.concatenate([high, high], axis=0))
 
     for i in range(3):
         x = mm(p_in[...], proj[i]).reshape(span + edge, 8, width)
@@ -246,15 +245,16 @@
     parts = lambda value: (value[:half], value[half:])
     (kr, ki), (mr, mi), (gr, gi), (hr, hi) = parts(k_spec), parts(m_spec), parts(g_spec), parts(g_own)
 
+    twice = lambda spectrum: jnp.concatenate([spectrum, spectrum], axis=0)
+
     def joined(real, imaginary):
-        spectrum = jnp.concatenate([real, imaginary], axis=0).astype(BF16)
-        return jnp.concatenate([spectrum, spectrum], axis=0)
+        return jnp.concatenate([real, imaginary], axis=0).astype(BF16)
 
     filtered = joined(mr * kr - mi * ki, mr * ki + mi * kr)
     grad_mixed = joined(gr * kr + gi * ki, gi * kr - gr * ki)
     filter_sums = joined(hr * mr + hi * mi, hi * mr - hr * mi)
     yield
-    filtered, grad_mixed = mm(s_own[...], filtered), mm(s_own[...], grad_mixed)
+    filtered, grad_mixed = mm(s_own[...], twice(filtered)), mm(s_own[...], twice(grad_mixed))
     filter_sums = mm(s_lags[...], filter_sums) * falloff
     yield
 
@@ -489,9 +489,9 @@
         np.concatenate([high, low], axis=1),
         analysis(np.concatenate([interleaved(16, -128), after]), size, 8)[0],
         analysis(interleaved(17, length), size, 8)[0],
-        np.concatenate([k_high, k_low, k_high], axis=1),
+        np.concatenate([k_high, k_low], axis=1),
         np.concatenate(list(synthesis(np.concatenate([own, after]), size)), axis=1),
-        np.concatenate(list(synthesis(np.arange(count), size)), axis=1),
+        synthesis(np.arange(count), size)[0],
         pick(interleaved(span, 0, 1 - FK), length),
     ]
     constants = [(jnp.asarray(constant), whole(constant)) for constant in constants]

time: 97.1 us -> 96.7 us (level)
  no operation moved by 1% of the time
where the time goes in v19:
time: 96.7 us; the launch traced here: 96.1 us
  Pallas kernels  40.1 us (41%)
  starting transfers between devices  31.7 us (33%)
  waiting for transfers between devices  23.5 us (24%)
    pallas_call x5, Pallas kernels, call(): pl.pallas_call(kernel, in_specs=[spec for _, spec in operands] + [FAR] *...  37.8 us
    all_to_all x1, waiting for transfers between devices, shards(): gathered = lax.all_to_all(payload, ('seq', 'ch'), 0, 0)  13.1 us
    ppermute x4, starting transfers between devices, from_behind(): return lax.ppermute(value, axis, pairs)  12 us
    all_to_all x1, starting transfers between devices, shards(): lax.all_to_all(sums, 'seq', 0, 0)  9.76 us
    all_to_all x1, starting transfers between devices, shards(): taps = lax.all_to_all(spread[0], 'seq', 0, 0).reshape(count, channels)  6.21 us
    all_to_all x1, waiting for transfers between devices, shards(): lax.all_to_all(sums, 'seq', 0, 0)  4.68 us
    all_to_all x1, starting transfers between devices, shards(): gathered = lax.all_to_all(payload, ('seq', 'ch'), 0, 0)  3.7 us
    ppermute x4, waiting for transfers between devices, from_behind(): return lax.ppermute(value, axis, pairs)  2.96 us
  transfers between devices with their start and end apart: 7, of which 5 were waited for; matrix products, arithmetic and copies ran while one was open for 0% of the time, Pallas kernels for 25%

profile of v19, /device:TPU:0, one launch (start us, length us, event | category | flops | bytes accessed | tf_op | source)
XLA Modules:
  0.0 96.1 jit_solution(8262088423069336919)
XLA Ops:
  0.6 3.0 %edges.3 = (bf16[152,1024]{1,0:T(8,128)(2,1)S(1)}, bf16[160,1024]{1,0:T(8,128)(2,1)S(1)}, bf16[8,16,2048]{2,1,0:T(8,128)(2,1)}) custom-call(bf16[3,256,2048]{2,1,0:T(8,128)(2,1)} %bitcast.7, bf16[256,2048]{1,0:T(8,128)(2,1)} %cot.7, f32[3,7,2048]{2,1,0:T(8,128)} %short.9, f32[16,2048]{1,0:T(8,128)} %refs_0_.3), custom_call_target="tpu_custom_call" | custom-call | flops 1000000000 | bytes 1000000 | tf_op jit(solution)/shard_map/edges/pallas_call | solution.py:388
  3.6 1.3 %collective-permute-start.2 = (bf16[160,1024]{1,0:T(8,128)(2,1)S(1)}, bf16[160,1024]{1,0:T(8,128)(2,1)S(1)}, u32[]{:S(2)}, u32[]{:S(2)}) collective-permute-start(bf16[160,1024]{1,0:T(8,128)(2,1)S(1)} %get-tuple-element.31), channel_id=1, source_target_pairs={{4,0},{8,4},{12,8},{16,12},{20,16},{24,20},{28,24},{5,1},{9,5},{13... | collective-permute-start | bytes 983048 | tf_op jit(solution)/shard_map/ppermute | solution.py:26
  4.9 5.5 %collective-permute-start.1 = (bf16[152,1024]{1,0:T(8,128)(2,1)S(1)}, bf16[152,1024]{1,0:T(8,128)(2,1)S(1)}, u32[]{:S(2)}, u32[]{:S(2)}) collective-permute-start(bf16[152,1024]{1,0:T(8,128)(2,1)S(1)} %get-tuple-element.30), channel_id=1, source_target_pairs={{0,4},{4,8},{8,12},{12,16},{16,20},{20,24},{24,28},{1,5},{5,9},{9,... | collective-permute-start | bytes 933896 | tf_op jit(solution)/shard_map/ppermute | solution.py:26
  10.5 6.2 %all-to-all-start = ((bf16[8,16,2048]{2,1,0:T(8,128)(2,1)}), bf16[8,16,2048]{2,1,0:T(8,128)(2,1)S(1)}, u32[]{:S(2)}, u32[]{:S(2)}) async-start(bf16[8,16,2048]{2,1,0:T(8,128)(2,1)} %get-tuple-element.33), calls=%async_computation | async-start | bytes 1048576 | tf_op jit(solution)/shard_map/all_to_all | solution.py:480
  16.7 4.1 %edges.2 = (bf16[152,1024]{1,0:T(8,128)(2,1)S(1)}, bf16[160,1024]{1,0:T(8,128)(2,1)S(1)}, f32[128,2048]{1,0:T(8,128)}) custom-call(bf16[3,256,2048]{2,1,0:T(8,128)(2,1)} %bitcast.8, bf16[256,2048]{1,0:T(8,128)(2,1)} %cot.7, f32[3,7,2048]{2,1,0:T(8,128)} %short.9, f32[1,2048]{1,0:T(1,128)} %bitcast.11), custom_call_target="tpu_custom_call" | custom-call | flops 10000000000 | bytes 1000000 | tf_op jit(solution)/shard_map/edges/pallas_call | solution.py:388
  20.8 3.9 %collective-permute-start = (bf16[152,1024]{1,0:T(8,128)(2,1)S(1)}, bf16[152,1024]{1,0:T(8,128)(2,1)S(1)}, u32[]{:S(2)}, u32[]{:S(2)}) collective-permute-start(bf16[152,1024]{1,0:T(8,128)(2,1)S(1)} %get-tuple-element.28), channel_id=1, source_target_pairs={{0,4},{4,8},{8,12},{12,16},{16,20},{20,24},{24,28},{1,5},{5,9},{9,... | collective-permute-start | bytes 933896 | tf_op jit(solution)/shard_map/ppermute | solution.py:26
  24.7 1.9 %collective-permute-done.1.prev = bf16[152,1024]{1,0:T(8,128)(2,1)S(1)} collective-permute-done((bf16[152,1024]{1,0:T(8,128)(2,1)S(1)}, bf16[152,1024]{1,0:T(8,128)(2,1)S(1)}, u32[]{:S(2)}, u32[]{:S(2)}) %collective-permute-start.1) | collective-permute-done | bytes 311328 | tf_op jit(solution)/shard_map/ppermute | solution.py:26
  26.6 0.0 collective-permute-done.2.later
  26.7 1.3 %collective-permute-start.3 = (bf16[160,1024]{1,0:T(8,128)(2,1)S(1)}, bf16[160,1024]{1,0:T(8,128)(2,1)S(1)}, u32[]{:S(2)}, u32[]{:S(2)}) collective-permute-start(bf16[160,1024]{1,0:T(8,128)(2,1)S(1)} %get-tuple-element.32), channel_id=1, source_target_pairs={{4,0},{8,4},{12,8},{16,12},{20,16},{24,20},{28,24},{5,1},{9,5},{13... | collective-permute-start | bytes 983048 | tf_op jit(solution)/shard_map/ppermute | solution.py:26
  27.9 2.7 %all-to-all-done = bf16[8,16,2048]{2,1,0:T(8,128)(2,1)S(1)} async-done(((bf16[8,16,2048]{2,1,0:T(8,128)(2,1)}), bf16[8,16,2048]{2,1,0:T(8,128)(2,1)S(1)}, u32[]{:S(2)}, u32[]{:S(2)}) %all-to-all-start) | async-done | bytes 524320 | tf_op jit(solution)/shard_map/all_to_all | solution.py:480
  30.7 10.6 %operator.2 = (bf16[8,256,256]{2,1,0:T(8,128)(2,1)}, f32[8,3,38,8,256]{4,3,2,1,0:T(8,128)}, bf16[8,160,256]{2,1,0:T(8,128)(2,1)}) custom-call(bf16[3,256,2048]{2,1,0:T(8,128)(2,1)} %bitcast.9, bf16[256,2048]{1,0:T(8,128)(2,1)} %cot.7, bf16[152,1024]{1,0:T(8,128)(2,1)S(1)} %collective-permute-done.1.prev, bf16[160,1024]{1,0:T(8,128)(2,1)S(1)} %collective-permute-done.2.later, ...), custom_call_target="tpu_custom_call" | custom-call | flops 12000000000 | bytes 1000000 | tf_op jit(solution)/shard_map/operator/pallas_call | solution.py:388
  41.3 1.1 %collective-permute-done.prev = bf16[152,1024]{1,0:T(8,128)(2,1)S(1)} collective-permute-done((bf16[152,1024]{1,0:T(8,128)(2,1)S(1)}, bf16[152,1024]{1,0:T(8,128)(2,1)S(1)}, u32[]{:S(2)}, u32[]{:S(2)}) %collective-permute-start) | collective-permute-done | bytes 311328 | tf_op jit(solution)/shard_map/ppermute | solution.py:26
  42.4 0.0 collective-permute-done.3.later
  42.4 10.7 %operator.3 = (bf16[8,256,256]{2,1,0:T(8,128)(2,1)}, f32[8,3,38,8,256]{4,3,2,1,0:T(8,128)}, bf16[8,160,256]{2,1,0:T(8,128)(2,1)}) custom-call(bf16[3,256,2048]{2,1,0:T(8,128)(2,1)} %bitcast.10, bf16[256,2048]{1,0:T(8,128)(2,1)} %cot.7, ...), custom_call_target="tpu_custom_call", output_to_operand_aliasing={{0}: (14, {}), {1}: (15, {}), {2}: (16, {})} | custom-call | flops 12000000000 | bytes 1000000 | tf_op jit(solution)/shard_map/operator/pallas_call | solution.py:388
  53.0 9.8 %all-to-all-start.1 = ((bf16[8,160,256]{2,1,0:T(8,128)(2,1)}), bf16[8,160,256]{2,1,0:T(8,128)(2,1)S(1)}, u32[]{:S(2)}, u32[]{:S(2)}) async-start(bf16[8,160,256]{2,1,0:T(8,128)(2,1)} %get-tuple-element.40), calls=%async_computation.1 | async-start | bytes 1310720 | tf_op jit(solution)/shard_map/all_to_all | solution.py:537
  62.8 9.3 %outputs.1 = (bf16[256,2048]{1,0:T(8,128)(2,1)}, bf16[3,256,2048]{2,1,0:T(8,128)(2,1)}) custom-call(bf16[8,256,256]{2,1,0:T(8,128)(2,1)} %get-tuple-element.41.product, f32[8,3,38,8,256]{4,3,2,1,0:T(8,128)} %get-tuple-element.42.grad, f32[3,7,2048]{2,1,0:T(8,128)} %short.9, bf16[256,256]{1,0:T(8,128)(2,1)} %constant.29.clone.p_out), custom_call_target="tpu_custom_call" | custom-call | flops 8000000000 | bytes 1000000 | tf_op jit(solution)/shard_map/outputs/pallas_call | solution.py:388
  72.1 4.7 %all-to-all-done.1.sums = bf16[8,160,256]{2,1,0:T(8,128)(2,1)S(1)} async-done(((bf16[8,160,256]{2,1,0:T(8,128)(2,1)}), bf16[8,160,256]{2,1,0:T(8,128)(2,1)S(1)}, u32[]{:S(2)}, u32[]{:S(2)}) %all-to-all-start.1) | async-done | bytes 655392 | tf_op jit(solution)/shard_map/all_to_all | solution.py:537
  76.8 1.0 %squares.1 = (f32[16,2048]{1,0:T(8,128)S(1)}, bf16[32,24,256]{2,1,0:T(8,128)(2,1)}) custom-call(bf16[8,160,256]{2,1,0:T(8,128)(2,1)S(1)} %all-to-all-done.1.sums), custom_call_target="tpu_custom_call" | custom-call | tf_op jit(solution)/shard_map/squares/pallas_call | solution.py:540
  77.8 3.7 %all-to-all-start.2 = ((bf16[32,24,256]{2,1,0:T(8,128)(2,1)}), bf16[32,24,256]{2,1,0:T(8,128)(2,1)S(1)}, u32[]{:S(2)}, u32[]{:S(2)}) async-start(bf16[32,24,256]{2,1,0:T(8,128)(2,1)} %get-tuple-element.49), calls=%async_computation.2 | async-start | bytes 786432 | tf_op jit(solution)/shard_map/all_to_all | solution.py:551
  81.5 0.1 pad_add_fusion.mine
  81.6 13.1 %all-to-all-done.2.gathered = bf16[32,24,256]{2,1,0:T(8,128)(2,1)S(1)} async-done(((bf16[32,24,256]{2,1,0:T(8,128)(2,1)}), bf16[32,24,256]{2,1,0:T(8,128)(2,1)S(1)}, u32[]{:S(2)}, u32[]{:S(2)}) %all-to-all-start.2) | async-done | bytes 393248 | tf_op jit(solution)/shard_map/all_to_all | solution.py:551
  94.7 1.4 %scale.1 = (f32[3,7,2048]{2,1,0:T(8,128)}, f32[16,2048]{1,0:T(8,128)}) custom-call(s32[2]{0:T(128)S(1)} %pad_add_fusion.mine, f32[16,2048]{1,0:T(8,128)S(1)} %get-tuple-element.48.raw, bf16[32,24,256]{2,1,0:T(8,128)(2,1)S(1)} %all-to-all-done.2.gathered), custom_call_target="tpu_custom_call" | custom-call | tf_op jit(solution)/shard_map/scale/pallas_call | solution.py:554
Async XLA Ops:
  3.6 23.0 %collective-permute-start.2 = (bf16[160,1024]{1,0:T(8,128)(2,1)S(1)}, bf16[160,1024]{1,0:T(8,128)(2,1)S(1)}, u32[]{:S(2)}, u32[]{:S(2)}) collective-permute-start(bf16[160,1024]{1,0:T(8,128)(2,1)S(1)} %get-tuple-element.31), channel_id=1, source_target_pairs={{4,0},{8,4},{12,8},{16,12},{20,16},{24,20},{28,24},{5,1},{9,5},{13... | collective-permute-start | bytes 983048 | tf_op jit(solution)/shard_map/ppermute | solution.py:26
  4.9 21.7 %collective-permute-start.1 = (bf16[152,1024]{1,0:T(8,128)(2,1)S(1)}, bf16[152,1024]{1,0:T(8,128)(2,1)S(1)}, u32[]{:S(2)}, u32[]{:S(2)}) collective-permute-start(bf16[152,1024]{1,0:T(8,128)(2,1)S(1)} %get-tuple-element.30), channel_id=1, source_target_pairs={{0,4},{4,8},{8,12},{12,16},{16,20},{20,24},{24,28},{1,5},{5,9},{9,... | collective-permute-start | bytes 933896 | tf_op jit(solution)/shard_map/ppermute | solution.py:26
  10.5 20.2 %all-to-all-start = ((bf16[8,16,2048]{2,1,0:T(8,128)(2,1)}), bf16[8,16,2048]{2,1,0:T(8,128)(2,1)S(1)}, u32[]{:S(2)}, u32[]{:S(2)}) async-start(bf16[8,16,2048]{2,1,0:T(8,128)(2,1)} %get-tuple-element.33), calls=%async_computation | async-start | bytes 1048576 | tf_op jit(solution)/shard_map/all_to_all | solution.py:480
  20.8 21.6 %collective-permute-start = (bf16[152,1024]{1,0:T(8,128)(2,1)S(1)}, bf16[152,1024]{1,0:T(8,128)(2,1)S(1)}, u32[]{:S(2)}, u32[]{:S(2)}) collective-permute-start(bf16[152,1024]{1,0:T(8,128)(2,1)S(1)} %get-tuple-element.28), channel_id=1, source_target_pairs={{0,4},{4,8},{8,12},{12,16},{16,20},{20,24},{24,28},{1,5},{5,9},{9,... | collective-permute-start | bytes 933896 | tf_op jit(solution)/shard_map/ppermute | solution.py:26
  26.7 15.7 %collective-permute-start.3 = (bf16[160,1024]{1,0:T(8,128)(2,1)S(1)}, bf16[160,1024]{1,0:T(8,128)(2,1)S(1)}, u32[]{:S(2)}, u32[]{:S(2)}) collective-permute-start(bf16[160,1024]{1,0:T(8,128)(2,1)S(1)} %get-tuple-element.32), channel_id=1, source_target_pairs={{4,0},{8,4},{12,8},{16,12},{20,16},{24,20},{28,24},{5,1},{9,5},{13... | collective-permute-start | bytes 983048 | tf_op jit(solution)/shard_map/ppermute | solution.py:26
  53.0 23.8 %all-to-all-start.1 = ((bf16[8,160,256]{2,1,0:T(8,128)(2,1)}), bf16[8,160,256]{2,1,0:T(8,128)(2,1)S(1)}, u32[]{:S(2)}, u32[]{:S(2)}) async-start(bf16[8,160,256]{2,1,0:T(8,128)(2,1)} %get-tuple-element.40), calls=%async_computation.1 | async-start | bytes 1310720 | tf_op jit(solution)/shard_map/all_to_all | solution.py:537
  77.8 16.9 %all-to-all-start.2 = ((bf16[32,24,256]{2,1,0:T(8,128)(2,1)}), bf16[32,24,256]{2,1,0:T(8,128)(2,1)S(1)}, u32[]{:S(2)}, u32[]{:S(2)}) async-start(bf16[32,24,256]{2,1,0:T(8,128)(2,1)} %get-tuple-element.49), calls=%async_computation.2 | async-start | bytes 786432 | tf_op jit(solution)/shard_map/all_to_all | solution.py:551
